TPU v7x, 32 devices: a whole 2x2x4 slice. The times are simulated.
32 devices in a mesh: grp: 8 (over z, x), dom: 4 (over y, core).
Axes of the slice: x: 2, y: 2, z: 4, core: 2. Of those that a mesh axis runs over, the one named last changes fastest.
Arguments:
- density: float32 [8, 256, 2048], P('grp', 'dom'), may hold values from -6 to 6
- diffusion: float32 [8, 256, 2048], P('grp', 'dom'), may hold values from 0.05 to 0.22
- drift_speed: float32 [8, 256, 2048], P('grp', 'dom'), may hold values from -0.3 to 0.3
- levels: int32 [8], P('grp'), may hold values from 5 to 8
- coefficient: int32 [8], P('grp'), may hold values from -2 to 2
Outputs:
- combined_field: float32 [8, 256, 2048], P('grp', 'dom')
All inputs are finite; a program needn't handle non-finite values.
Results may differ from a plain program's by a relative error of at most 0.0003.
Values sent between devices are 32-bit elements; how exact they have to be, the bound alone decides.
No kernel may reach another device: no remote copies, remote signals or barrier semaphores. Data moves between devices by JAX's collectives and lax.ppermute only.
A program may use at most 64 MiB of HBM per device.

v0:
```python
import jax
import jax.numpy as jnp
import numpy as np
from jax import lax
from jax.sharding import PartitionSpec as P

STEPS = 4


def extended(array, sides, width):
    for axis, dim in sides:
        devices, length = (lax.axis_size(axis), array.shape[dim])
        up = [(i, (i + 1) % devices) for i in range(devices - 1)]
        down = [(j, i) for i, j in up]
        last = lax.slice_in_dim(array, length - width, length, axis=dim)
        leading = lax.slice_in_dim(array, 0, width, axis=dim)
        before = lax.ppermute(last, axis, up)
        after = lax.ppermute(leading, axis, down)
        array = jnp.concatenate([before, array, after], axis=dim)
    return array


def hier_tables(size):
    to_surplus = np.zeros((size, size), dtype=np.float32)
    to_nodal = np.zeros((size, size), dtype=np.float32)
    node_level = np.zeros((size,), dtype=np.int32)
    depth = size.bit_length() - 1
    spots = np.arange(1, size + 1, dtype=np.float32)
    for index in range(size):
        position = index + 1
        to_surplus[index, index] = 1.0
        if position == size:
            node_level[index] = 0
            to_nodal[:, index] = spots / size
            continue
        stride = 1
        zeros_count = 0
        while position % (2 * stride) == 0:
            stride = stride * 2
            zeros_count = zeros_count + 1
        node_level[index] = depth - zeros_count
        to_nodal[:, index] = np.maximum(0.0, 1.0 - np.abs(spots - position) / stride)
        if position - stride > 0:
            to_surplus[index, position - stride - 1] -= 0.5
        if position + stride <= size:
            to_surplus[index, position + stride - 1] -= 0.5
    return (to_surplus, to_nodal, node_level)


def advance(state, diffuse, drifts, padded):
    above_cell = padded[2:, 1:-1]
    below_cell = padded[:-2, 1:-1]
    right_cell = padded[1:-1, 2:]
    left_cell = padded[1:-1, :-2]
    return (
        state
        + diffuse * (above_cell + below_cell + right_cell + left_cell - 4.0 * state)
        - 0.5 * drifts * (above_cell - below_cell)
    )


def on_device(density, diffusion, drift_speed, levels, coefficient):
    state = density[0]
    diffuse = diffusion[0]
    drifts = drift_speed[0]
    rows_all = state.shape[0] * lax.axis_size("dom")
    to_surplus, to_nodal, node_level = hier_tables(rows_all)
    to_surplus = jnp.asarray(to_surplus)
    to_nodal = jnp.asarray(to_nodal)
    node_level = jnp.asarray(node_level)
    for sweep in range(STEPS):
        padded = extended(state, (("dom", 0),), 1)
        padded = jnp.pad(padded, ((0, 0), (1, 1)))
        state = advance(state, diffuse, drifts, padded)
    poles = lax.all_to_all(state, "dom", split_axis=1, concat_axis=0, tiled=True)
    surplus = jnp.dot(
        to_surplus, poles, precision=lax.Precision.HIGHEST, preferred_element_type=jnp.float32
    )
    member_mask = (node_level <= levels[0]).astype(jnp.float32)[:, None]
    weighted = surplus * (member_mask * coefficient[0].astype(jnp.float32))
    total = lax.psum(weighted, "grp")
    nodal = jnp.dot(
        to_nodal,
        total * member_mask,
        precision=lax.Precision.HIGHEST,
        preferred_element_type=jnp.float32,
    )
    slabs = lax.all_to_all(nodal, "dom", split_axis=0, concat_axis=1, tiled=True)
    return slabs[None]


def solution(mesh):
    return jax.shard_map(
        on_device,
        mesh=mesh,
        in_specs=(
            P("grp", "dom", None),
            P("grp", "dom", None),
            P("grp", "dom", None),
            P("grp"),
            P("grp"),
        ),
        out_specs=P("grp", "dom", None),
        check_vma=False,
    )
```

profile of v0, /device:TPU:0, one launch (start us, length us, event | category | flops | bytes accessed | tf_op | source)
XLA Modules:
  0.0 151.6 jit_solution(15080935413548630595)
XLA Ops:
  6.5 0.9 slice_bitcast_fusion
  7.4 1.3 collective-permute-start
  8.7 3.0 %collective-permute-start.1 = (f32[1,2048]{1,0:T(1,128)S(1)}, f32[1,2048]{1,0:T(1,128)S(1)}, u32[]{:S(2)}, u32[]{:S(2)}) collective-permute-start(f32[1,2048]{1,0:T(1,128)S(1)} %get-tuple-element.11), channel_id=1, source_target_pairs={{0,1},{1,2},{2,3},{4,5},{5,6},{6,7},{8,9},{9,10},{10,11},{12,13},{... | collective-permute-start | bytes 24584 | tf_op jit(solution)/shard_map/ppermute | solution.py:17
  11.8 0.0 collective-permute-done
  11.8 0.8 collective-permute-done.1
  12.6 0.0 copy-start
  12.6 0.0 copy-start.1
  12.6 1.4 select_maximum_fusion.6
  14.0 0.0 copy-done
  14.0 0.0 copy-done.1
  14.0 1.8 %fusion.17 = f32[64,2048]{1,0:T(8,128)S(1)} fusion(f32[64,2048]{1,0:T(8,128)} %bitcast.39, f32[66,2050]{1,0:T(8,128)S(1)} %select_maximum_fusion.6, f32[1,64,2048]{2,1,0:T(8,128)S(1)} %copy-done, f32[1,2048]{1,0:T(1,128)S(1)} %collective-permute-done, f32[1,2048]{1,0:T(1,128)S(1)} %collective-permute-done.1, f32[1,64,2048]{2,1,0:T(8,128)S(1)} %copy-done.1), kind=kLoop, calls=%fused_computation.42 | loop fusion | flops 1703936 | bytes 3162112 | tf_op jit(solution)/shard_map/sub | solution.py:56
  15.8 1.3 collective-permute-start.2
  17.1 5.1 %collective-permute-start.3 = (f32[1,2048]{1,0:T(1,128)S(1)}, f32[1,2048]{1,0:T(1,128)S(1)}, u32[]{:S(2)}, u32[]{:S(2)}) collective-permute-start(f32[1,2048]{1,0:T(1,128)S(1)} %get-tuple-element.9), channel_id=1, source_target_pairs={{0,1},{1,2},{2,3},{4,5},{5,6},{6,7},{8,9},{9,10},{10,11},{12,13},{... | collective-permute-start | bytes 24584 | tf_op jit(solution)/shard_map/ppermute | solution.py:17
  22.2 0.0 collective-permute-done.2
  22.2 0.8 collective-permute-done.3
  23.0 0.3 select_maximum_fusion.4
  23.3 0.4 fusion.13
  23.7 1.3 collective-permute-start.4
  25.0 4.8 %collective-permute-start.5 = (f32[1,2048]{1,0:T(1,128)S(1)}, f32[1,2048]{1,0:T(1,128)S(1)}, u32[]{:S(2)}, u32[]{:S(2)}) collective-permute-start(f32[1,2048]{1,0:T(1,128)S(1)} %get-tuple-element.7), channel_id=1, source_target_pairs={{0,1},{1,2},{2,3},{4,5},{5,6},{6,7},{8,9},{9,10},{10,11},{12,13},{... | collective-permute-start | bytes 24584 | tf_op jit(solution)/shard_map/ppermute | solution.py:17
  29.8 0.0 collective-permute-done.4
  29.8 0.8 collective-permute-done.5
  30.6 0.3 select_maximum_fusion.2
  30.9 0.4 fusion.9
  31.3 1.3 collective-permute-start.6
  32.6 4.8 %collective-permute-start.7 = (f32[1,2048]{1,0:T(1,128)S(1)}, f32[1,2048]{1,0:T(1,128)S(1)}, u32[]{:S(2)}, u32[]{:S(2)}) collective-permute-start(f32[1,2048]{1,0:T(1,128)S(1)} %get-tuple-element.5), channel_id=1, source_target_pairs={{0,1},{1,2},{2,3},{4,5},{5,6},{6,7},{8,9},{9,10},{10,11},{12,13},{... | collective-permute-start | bytes 24584 | tf_op jit(solution)/shard_map/ppermute | solution.py:17
  37.4 0.0 collective-permute-done.6
  37.4 0.8 collective-permute-done.7
  38.2 0.3 select_maximum_fusion
  38.5 0.4 fusion.5
  38.9 0.8 copy.16
  39.7 5.7 %all-to-all-start = ((f32[64,4,512]{2,0,1:T(8,128)}), f32[64,4,512]{2,0,1:T(8,128)S(1)}, u32[]{:S(2)}, u32[]{:S(2)}) async-start(f32[64,4,512]{2,0,1:T(8,128)} %bitcast.35), calls=%async_computation | async-start | bytes 1048576 | tf_op jit(solution)/shard_map/all_to_all | solution.py:75
  45.4 0.0 all-reduce.6.cloned.1.call-start
  46.7 0.0 copy-start.4
  46.7 0.7 copy-done.4
  47.4 6.9 %all-to-all-done = f32[64,4,512]{2,0,1:T(8,128)S(1)} async-done(((f32[64,4,512]{2,0,1:T(8,128)}), f32[64,4,512]{2,0,1:T(8,128)S(1)}, u32[]{:S(2)}, u32[]{:S(2)}) %all-to-all-start) | async-done | bytes 524320 | tf_op jit(solution)/shard_map/all_to_all | solution.py:75
  54.2 0.3 copy.12
  54.6 0.0 copy-start.3
  54.6 0.2 reshape.15
  54.8 0.8 copy-done.3
  55.5 1.8 %fusion = f32[256,512]{0,1:T(8,128)} fusion(f32[256,512]{1,0:T(8,128)S(1)} %reshape.15, f32[256,256]{1,0:T(8,128)S(1)} %copy-done.3, f32[256]{0:T(256)S(1)} %compare_select_fusion), kind=kOutput, calls=%fused_computation.1 | convolution fusion | flops 402784256 | bytes 1311744 | tf_op jit(solution)/shard_map/dot_general | solution.py:76
  57.3 0.0 copy-start.2
  57.3 0.0 all-reduce.6.cloned.1.call-update
  57.4 72.8 %all-reduce.6.cloned.1.call-done = f32[256,512]{0,1:T(8,128)} async-done(((f32[256,512]{0,1:T(8,128)}), f32[256,512]{0,1:T(8,128)}) %all-reduce.6.cloned.1.call-update) | async-done | bytes 524304 | tf_op jit(solution)/shard_map/psum | solution.py:81
  130.2 0.0 copy-done.2
  130.2 1.7 %fusion.18 = f32[256,512]{1,0:T(8,128)S(1)} fusion(f32[256,256]{1,0:T(8,128)S(1)} %copy-done.2, f32[256,512]{0,1:T(8,128)} %all-reduce.6.cloned.1.call-done, f32[256]{0:T(256)S(1)} %compare_convert_fusion), kind=kOutput, calls=%fused_computation.50 | convolution fusion | flops 402784256 | bytes 1311744 | tf_op jit(solution)/shard_map/dot_general | solution.py:82
  131.9 11.4 %all_to_all.35 = f32[4,64,512]{2,1,0:T(8,128)S(1)} all-to-all(f32[4,64,512]{2,1,0:T(8,128)S(1)} %bitcast.40), channel_id=1, replica_groups=mesh['grp'=8,'dom'=4] {'dom'}, dimensions={0} | all-to-all | bytes 1048576 | tf_op jit(solution)/shard_map/all_to_all | solution.py:88
  143.3 0.3 copy.13
  143.6 1.2 broadcast_in_dim.4
  (5 shorter events, 0.0 us)
Async XLA Ops:
  7.4 4.3 %collective-permute-start = (f32[1,2048]{1,0:T(1,128)S(1)}, f32[1,2048]{1,0:T(1,128)S(1)}, u32[]{:S(2)}, u32[]{:S(2)}) collective-permute-start(f32[1,2048]{1,0:T(1,128)S(1)} %get-tuple-element.12), channel_id=1, source_target_pairs={{1,0},{2,1},{3,2},{5,4},{6,5},{7,6},{9,8},{10,9},{11,10},{13,12},{... | collective-permute-start | bytes 24584 | tf_op jit(solution)/shard_map/ppermute | solution.py:18
  8.7 3.8 %collective-permute-start.1 = (f32[1,2048]{1,0:T(1,128)S(1)}, f32[1,2048]{1,0:T(1,128)S(1)}, u32[]{:S(2)}, u32[]{:S(2)}) collective-permute-start(f32[1,2048]{1,0:T(1,128)S(1)} %get-tuple-element.11), channel_id=1, source_target_pairs={{0,1},{1,2},{2,3},{4,5},{5,6},{6,7},{8,9},{9,10},{10,11},{12,13},{... | collective-permute-start | bytes 24584 | tf_op jit(solution)/shard_map/ppermute | solution.py:17
  12.6 1.4 copy-start
  12.6 1.4 copy-start.1
  15.8 6.4 %collective-permute-start.2 = (f32[1,2048]{1,0:T(1,128)S(1)}, f32[1,2048]{1,0:T(1,128)S(1)}, u32[]{:S(2)}, u32[]{:S(2)}) collective-permute-start(f32[1,2048]{1,0:T(1,128)S(1)} %get-tuple-element.10), channel_id=1, source_target_pairs={{1,0},{2,1},{3,2},{5,4},{6,5},{7,6},{9,8},{10,9},{11,10},{13,12},{... | collective-permute-start | bytes 24584 | tf_op jit(solution)/shard_map/ppermute | solution.py:18
  17.1 5.9 %collective-permute-start.3 = (f32[1,2048]{1,0:T(1,128)S(1)}, f32[1,2048]{1,0:T(1,128)S(1)}, u32[]{:S(2)}, u32[]{:S(2)}) collective-permute-start(f32[1,2048]{1,0:T(1,128)S(1)} %get-tuple-element.9), channel_id=1, source_target_pairs={{0,1},{1,2},{2,3},{4,5},{5,6},{6,7},{8,9},{9,10},{10,11},{12,13},{... | collective-permute-start | bytes 24584 | tf_op jit(solution)/shard_map/ppermute | solution.py:17
  23.7 6.1 %collective-permute-start.4 = (f32[1,2048]{1,0:T(1,128)S(1)}, f32[1,2048]{1,0:T(1,128)S(1)}, u32[]{:S(2)}, u32[]{:S(2)}) collective-permute-start(f32[1,2048]{1,0:T(1,128)S(1)} %get-tuple-element.8), channel_id=1, source_target_pairs={{1,0},{2,1},{3,2},{5,4},{6,5},{7,6},{9,8},{10,9},{11,10},{13,12},{... | collective-permute-start | bytes 24584 | tf_op jit(solution)/shard_map/ppermute | solution.py:18
  25.0 5.6 %collective-permute-start.5 = (f32[1,2048]{1,0:T(1,128)S(1)}, f32[1,2048]{1,0:T(1,128)S(1)}, u32[]{:S(2)}, u32[]{:S(2)}) collective-permute-start(f32[1,2048]{1,0:T(1,128)S(1)} %get-tuple-element.7), channel_id=1, source_target_pairs={{0,1},{1,2},{2,3},{4,5},{5,6},{6,7},{8,9},{9,10},{10,11},{12,13},{... | collective-permute-start | bytes 24584 | tf_op jit(solution)/shard_map/ppermute | solution.py:17
  31.3 6.1 %collective-permute-start.6 = (f32[1,2048]{1,0:T(1,128)S(1)}, f32[1,2048]{1,0:T(1,128)S(1)}, u32[]{:S(2)}, u32[]{:S(2)}) collective-permute-start(f32[1,2048]{1,0:T(1,128)S(1)} %get-tuple-element.6), channel_id=1, source_target_pairs={{1,0},{2,1},{3,2},{5,4},{6,5},{7,6},{9,8},{10,9},{11,10},{13,12},{... | collective-permute-start | bytes 24584 | tf_op jit(solution)/shard_map/ppermute | solution.py:18
  32.6 5.6 %collective-permute-start.7 = (f32[1,2048]{1,0:T(1,128)S(1)}, f32[1,2048]{1,0:T(1,128)S(1)}, u32[]{:S(2)}, u32[]{:S(2)}) collective-permute-start(f32[1,2048]{1,0:T(1,128)S(1)} %get-tuple-element.5), channel_id=1, source_target_pairs={{0,1},{1,2},{2,3},{4,5},{5,6},{6,7},{8,9},{9,10},{10,11},{12,13},{... | collective-permute-start | bytes 24584 | tf_op jit(solution)/shard_map/ppermute | solution.py:17
  39.7 14.5 %all-to-all-start = ((f32[64,4,512]{2,0,1:T(8,128)}), f32[64,4,512]{2,0,1:T(8,128)S(1)}, u32[]{:S(2)}, u32[]{:S(2)}) async-start(f32[64,4,512]{2,0,1:T(8,128)} %bitcast.35), calls=%async_computation | async-start | bytes 1048576 | tf_op jit(solution)/shard_map/all_to_all | solution.py:75
  45.4 84.8 %all-reduce.6.cloned.1.call-start = ((), (), s32[]{:S(2)}) async-start(), calls=%async_computation.2 | async-start | bytes 1048576 | tf_op jit(solution)/shard_map/psum | solution.py:81
  46.7 0.7 copy-start.4
  54.6 1.0 copy-start.3
  57.3 72.9 %copy-start.2 = (f32[256,256]{1,0:T(8,128)S(1)}, f32[256,256]{1,0:T(8,128)}, u32[]{:S(2)}) copy-start(f32[256,256]{1,0:T(8,128)} %constant.15.clone) | copy-start | bytes 786436
Sparse Core Ops, SparseCore 0:
  57.5 72.6 all-reduce.5
where the time goes:
time: 152 us
  waiting for transfers between devices  82.9 us (55%)
  starting transfers between devices  28.5 us (19%)
  between operations  14.9 us (10%)
  blocking collectives  11.4 us (8%)
  local copies, waits for them, and re-layouts  5.22 us (3%)
  other arithmetic  5.19 us (3%)
  matrix products  3.47 us (2%)
    psum x1, waiting for transfers between devices, on_device(): total = lax.psum(weighted, 'grp')  72.8 us
    ppermute x4, starting transfers between devices, extended(): before = lax.ppermute(last, axis, up)  17.7 us
    all_to_all x1, blocking collectives, on_device(): lax.all_to_all(nodal, 'dom', split_axis=0, concat_axis=1, tiled=True)  11.4 us
    all_to_all x1, waiting for transfers between devices, on_device(): lax.all_to_all(state, 'dom', split_axis=1, concat_axis=0, tiled=True)  6.86 us
    all_to_all x1, starting transfers between devices, on_device(): lax.all_to_all(state, 'dom', split_axis=1, concat_axis=0, tiled=True)  5.68 us
    ppermute x4, starting transfers between devices, extended(): after = lax.ppermute(leading, axis, down)  5.17 us
    ppermute x4, waiting for transfers between devices, extended(): before = lax.ppermute(last, axis, up)  3.2 us
  transfers between devices with their start and end apart: 10, of which 6 were waited for; matrix products, arithmetic and copies ran while one was open for 0% of the time, Pallas kernels for 0%

commit v1 on v0

v1 whole, which is shorter than its diff:
```python
import functools

import jax
import jax.numpy as jnp
from jax import lax
from jax.experimental import pallas as pl
from jax.experimental.pallas import tpu as pltpu
from jax.sharding import PartitionSpec as P

STEPS = 4
LANES = 128
TILE = 8
VMEM_LIMIT = 40 * 1024 * 1024


def lane_ids(shape):
    return lax.broadcasted_iota(jnp.int32, shape, 1)


def row_in_tile(shape):
    return lax.broadcasted_iota(jnp.int32, shape, 0) % TILE


def run_kernel(
    rows, strips, per_chunk, level_ref, coef_ref, dens_ref, diff_ref, drift_ref, up_ref, dn_ref,
    out_ref, state_a, state_b, center, above_c, below_c, side
):
    tall = rows + 2 * TILE
    lanes = lane_ids((tall, LANES))
    zeros = jnp.zeros((tall, LANES), jnp.float32)
    for buf in (state_a, state_b):
        buf[0] = zeros
        buf[strips + 1] = zeros

    def columns(j):
        return pl.ds(pl.multiple_of(j * LANES, LANES), LANES)

    def first_state(j):
        at = columns(j)
        return jnp.concatenate([up_ref[0:TILE, at], dens_ref[:, at], dn_ref[0:TILE, at]], axis=0)

    def coefficients(j):
        at = columns(j)
        up, dn = up_ref[TILE:, at], dn_ref[TILE:, at]
        diffuse = jnp.concatenate([up, diff_ref[:, at], dn], axis=0)
        drifts = jnp.concatenate(
            [pltpu.roll(up, 4, 0), drift_ref[:, at], pltpu.roll(dn, 4, 0)], axis=0
        )
        half = 0.5 * drifts
        return 1.0 - 4.0 * diffuse, diffuse - half, diffuse + half, diffuse

    def sweep(load, coefs, emit):
        def body(j, carry):
            cur, right_prev, left_cur = carry
            nxt = load(j + 1)
            left_next = pltpu.roll(nxt, LANES - 1, 1)
            right_cur = pltpu.roll(cur, 1, 1)
            left = jnp.where(lanes == 0, right_prev, right_cur)
            right = jnp.where(lanes == LANES - 1, left_next, left_cur)
            above = pltpu.roll(cur, tall - 1, 0)
            below = pltpu.roll(cur, 1, 0)
            c0, ca, cb, cs = coefs(j)
            emit(j, c0 * cur + ca * above + cb * below + cs * (left + right))
            return nxt, right_cur, left_next

        cur = load(0)
        lax.fori_loop(0, strips, body, (cur, zeros, pltpu.roll(cur, LANES - 1, 1)), unroll=2)

    def load_first(j):
        strip = first_state(jnp.minimum(j, strips - 1))
        return jnp.where(j < strips, strip, zeros)

    def coefs_first(j):
        c0, ca, cb, cs = coefficients(j)
        center[j], above_c[j], below_c[j], side[j] = c0, ca, cb, cs
        return c0, ca, cb, cs

    def coefs_kept(j):
        return center[j], above_c[j], below_c[j], side[j]

    def to(buf):
        def emit(j, value):
            buf[j + 1] = value

        return emit

    coef = coef_ref[0].astype(jnp.float32)
    weight = [jnp.where(level_ref[0] >= level, coef, 0.0) for level in (6, 7, 8)]
    row = row_in_tile((tall, LANES))
    is8, is7, is6 = row % 2 == 0, row % 4 == 1, row == 3
    scale = jnp.where(is8, weight[2], jnp.where(is7, weight[1], jnp.where(is6, weight[0], coef)))
    halves = jnp.where(row == 7, 0.0, 0.5)

    def surplus(j, value):
        def both(shift):
            return pltpu.roll(value, shift, 0) + pltpu.roll(value, tall - shift, 0)

        ends = jnp.where(is8, both(1), jnp.where(is7, both(2), both(4)))
        weighted = scale * (value - halves * ends)
        chunk, part = j // per_chunk, lax.rem(j, per_chunk)
        out_ref[chunk, pl.ds(pl.multiple_of(part * rows, TILE), rows), :] = weighted[
            TILE : TILE + rows
        ]
        out_ref[chunk, pl.ds(per_chunk * rows + part, 1), :] = coef * value[TILE - 1 : TILE]

    sweep(load_first, coefs_first, to(state_a))
    src, dst = state_a, state_b
    for step in range(1, STEPS):
        emit = to(dst) if step < STEPS - 1 else surplus
        sweep(lambda j, src=src: src[j + 1], coefs_kept, emit)
        src, dst = dst, src


def sum_kernel(parts_ref, out_ref):
    total = parts_ref[0]
    for g in range(1, parts_ref.shape[0]):
        total = total + parts_ref[g]
    for g in range(out_ref.shape[0]):
        out_ref[g] = total


def nodal_kernel(rows, strips, per_chunk, level_ref, total_ref, out_ref):
    level = level_ref[0]
    keep = [jnp.where(level >= at, 1.0, 0.0) for at in (6, 7, 8)]
    row = row_in_tile((TILE, LANES))
    place = (row + 1).astype(jnp.float32)
    from_next = place / TILE
    from_prev = 1.0 - from_next
    hat6 = keep[0] * jnp.minimum(place, TILE - place) * 0.25
    fine = jnp.where(row >= 4, place - 4, place)
    hat7 = keep[1] * jnp.minimum(fine, 4.0 - fine) * 0.5
    hat8 = jnp.where(row % 2 == 0, keep[2], 0.0)

    def body(j, _):
        chunk, part = j // per_chunk, lax.rem(j, per_chunk)
        top = pl.multiple_of(part * rows, TILE)
        prev = total_ref[chunk, pl.ds(per_chunk * rows + part, 1), :]
        strip = total_ref[chunk, pl.ds(top, rows), :]
        tiles = []
        for t in range(rows // TILE):
            tile = strip[t * TILE : (t + 1) * TILE]
            last = tile[7:8]
            mid = jnp.where(row < 4, tile[1:2], tile[5:6])
            tiles.append(
                from_prev * prev + from_next * last + hat6 * tile[3:4] + hat7 * mid + hat8 * tile
            )
            prev = last
        at = pl.ds(pl.multiple_of(j * LANES, LANES), LANES)
        out_ref[:, at] = jnp.concatenate(tiles, axis=0)
        return 0

    lax.fori_loop(0, strips, body, 0, unroll=2)


def call(kernel, out_shape, operands, in_smem, scratch=()):
    specs = [
        pl.BlockSpec(memory_space=pltpu.SMEM if k < in_smem else pltpu.VMEM)
        for k in range(len(operands))
    ]
    return pl.pallas_call(
        kernel,
        out_shape=jax.ShapeDtypeStruct(out_shape, jnp.float32),
        in_specs=specs,
        out_specs=pl.BlockSpec(memory_space=pltpu.VMEM),
        scratch_shapes=list(scratch),
        compiler_params=pltpu.CompilerParams(vmem_limit_bytes=VMEM_LIMIT),
    )(*operands)


def on_device(density, diffusion, drift_speed, levels, coefficient):
    state, diffuse, drifts = density[0], diffusion[0], drift_speed[0]
    rows, cols = state.shape
    doms, grids = lax.axis_size("dom"), lax.axis_size("grp")
    strips = cols // LANES
    per_chunk = strips // grids
    tall = rows + 2 * TILE
    chunk_rows = per_chunk * rows + -(-per_chunk // TILE) * TILE

    up = [(i, i + 1) for i in range(doms - 1)]
    down = [(j, i) for i, j in up]
    to_next = jnp.concatenate([state[-8:], drifts[-4:], diffuse[-4:]], axis=0)
    to_prev = jnp.concatenate([state[:8], diffuse[:4], drifts[:4]], axis=0)
    before = lax.ppermute(to_next, "dom", up)
    after = lax.ppermute(to_prev, "dom", down)

    packed = (grids, chunk_rows, LANES)
    weighted = call(
        functools.partial(run_kernel, rows, strips, per_chunk),
        packed,
        (levels, coefficient, state, diffuse, drifts, before, after),
        2,
        [pltpu.VMEM((strips + 2, tall, LANES), jnp.float32)] * 2
        + [pltpu.VMEM((strips, tall, LANES), jnp.float32)] * 4,
    )
    parts = lax.all_to_all(weighted, "grp", split_axis=0, concat_axis=0, tiled=True)
    spread = call(sum_kernel, packed, (parts,), 0)
    total = lax.all_to_all(spread, "grp", split_axis=0, concat_axis=0, tiled=True)
    nodal = call(
        functools.partial(nodal_kernel, rows, strips, per_chunk), (rows, cols), (levels, total), 1
    )
    return nodal[None]


def solution(mesh):
    return jax.shard_map(
        on_device,
        mesh=mesh,
        in_specs=(
            P("grp", "dom", None),
            P("grp", "dom", None),
            P("grp", "dom", None),
            P("grp"),
            P("grp"),
        ),
        out_specs=P("grp", "dom", None),
        check_vma=False,
    )
```

time: 152 us -> 58.2 us (0.38)
  waiting for transfers between devices: 82.9 us -> 2.77 us
  blocking collectives: 11.4 us -> 41.6 us
  starting transfers between devices: 28.5 us -> 3.66 us
  between operations: 14.9 us -> 1.35 us
  Pallas kernels: 0 us -> 5.39 us
  other arithmetic: 5.19 us -> 0.05 us
  matrix products: 3.47 us -> 0 us
  local copies, waits for them, and re-layouts: 5.22 us -> 2.98 us
    psum x1 -> x0, waiting for transfers between devices: 72.8 us -> none  [on_device(): total = lax.psum(weighted, 'grp')]
    all_to_all x1 -> x2, blocking collectives: 11.4 us -> 41.6 us  [the longest x1 21.2 us: on_device(): lax.all_to_all(weighted, 'grp', split_axis=0, concat_axis=0, tiled=True)]
    ppermute x8 -> x2, starting transfers between devices: 22.8 us -> 3.66 us  [the longest x1 2.36 us: on_device(): before = lax.ppermute(to_next, 'dom', up)]
    all_to_all x1 -> x0, waiting for transfers between devices: 6.86 us -> none  [on_device(): lax.all_to_all(state, 'dom', split_axis=1, concat_axis=0, tiled=True)]
    all_to_all x1 -> x0, starting transfers between devices: 5.68 us -> none  [on_device(): lax.all_to_all(state, 'dom', split_axis=1, concat_axis=0, tiled=True)]
    pallas_call x0 -> x3, Pallas kernels: none -> 5.39 us  [call(): pl.pallas_call(kernel, out_shape=jax.ShapeDtypeStruct(out_shape, jnp.floa...]
    dot_general x2 -> x0, matrix products: 3.47 us -> none  [the longest x1 1.79 us: on_device(): jnp.dot(to_surplus, poles, precision=lax.Precision.HIGHEST, preferred_ele...]
    sub x4 -> x0, other arithmetic: 3 us -> none  [advance(): state + diffuse * (above_cell + below_cell + right_cell + left_cell - 4.0...]
  transfers between devices with their start and end apart: 10 -> 2, of which waited for: 6 -> 1; matrix products, arithmetic and copies ran while one was open for 0% -> 0% of each run, Pallas kernels for 0% -> 0%
where the time goes in v1:
time: 58.2 us; the launch traced here: 57.8 us
  blocking collectives  41.6 us (71%)
  Pallas kernels  5.39 us (9%)
  starting transfers between devices  3.66 us (6%)
  local copies, waits for them, and re-layouts  2.98 us (5%)
  waiting for transfers between devices  2.77 us (5%)
  between operations  1.35 us (2%)
    all_to_all x1, blocking collectives, on_device(): lax.all_to_all(weighted, 'grp', split_axis=0, concat_axis=0, tiled=True)  21.2 us
    all_to_all x1, blocking collectives, on_device(): lax.all_to_all(spread, 'grp', split_axis=0, concat_axis=0, tiled=True)  20.4 us
    pallas_call x3, Pallas kernels, call(): pl.pallas_call(kernel, out_shape=jax.ShapeDtypeStruct(out_shape, jnp.floa...  5.39 us
    ppermute x1, waiting for transfers between devices, on_device(): after = lax.ppermute(to_prev, 'dom', down)  2.77 us
    ppermute x1, starting transfers between devices, on_device(): before = lax.ppermute(to_next, 'dom', up)  2.36 us
    slice x2, local copies, waits for them, and re-layouts, on_device(): to_prev = jnp.concatenate([state[:8], diffuse[:4], drifts[:4]], axis=0)  1.93 us
    ppermute x1, starting transfers between devices, on_device(): after = lax.ppermute(to_prev, 'dom', down)  1.29 us
  transfers between devices with their start and end apart: 2, of which 1 were waited for; matrix products, arithmetic and copies ran while one was open for 0% of the time, Pallas kernels for 0%

profile of v1, /device:TPU:0, one launch (start us, length us, event | category | flops | bytes accessed | tf_op | source)
XLA Modules:
  0.0 57.8 jit_solution(7756669643666730806)
XLA Ops:
  0.0 0.0 copy-start
  0.0 0.0 copy-start.1
  0.0 1.0 %slice_bitcast_fusion = (f32[8,2048]{1,0:T(8,128)S(1)}, f32[8,2048]{1,0:T(8,128)S(1)}) fusion(f32[1,64,2048]{2,1,0:T(8,128)} %param.5), kind=kLoop, calls=%fused_computation.2 | loop fusion | bytes 262144 | tf_op jit(solution)/shard_map/slice | solution.py:182
  1.0 1.0 %slice_bitcast_fusion.2 = (f32[4,2048]{1,0:T(4,128)S(1)}, f32[4,2048]{1,0:T(4,128)S(1)}, f32[4,2048]{1,0:T(4,128)S(1)}, f32[4,2048]{1,0:T(4,128)S(1)}) fusion(f32[1,64,2048]{2,1,0:T(8,128)} %param.7, f32[1,64,2048]{2,1,0:T(8,128)} %param.6), kind=kLoop, calls=%fused_computation.4 | loop fusion | bytes 262144 | tf_op jit(solution)/shard_map/slice | solution.py:182
  2.0 2.4 %collective-permute-start = (f32[16,2048]{1,0:T(8,128)S(1)}, f32[16,2048]{1,0:T(8,128)S(1)}, u32[]{:S(2)}, u32[]{:S(2)}) collective-permute-start(f32[16,2048]{1,0:T(8,128)S(1)} %pad_maximum_fusion), channel_id=1, source_target_pairs={{0,1},{1,2},{2,3},{4,5},{5,6},{6,7},{8,9},{9,10},{10,11},{12,13},{... | collective-permute-start | bytes 393224 | tf_op jit(solution)/shard_map/ppermute | solution.py:183
  4.4 1.3 %collective-permute-start.1 = (f32[16,2048]{1,0:T(8,128)S(1)}, f32[16,2048]{1,0:T(8,128)S(1)}, u32[]{:S(2)}, u32[]{:S(2)}) collective-permute-start(f32[16,2048]{1,0:T(8,128)S(1)} %pad_maximum_fusion.1), channel_id=1, source_target_pairs={{1,0},{2,1},{3,2},{5,4},{6,5},{7,6},{9,8},{10,9},{11,10},{13,12},{... | collective-permute-start | bytes 393224 | tf_op jit(solution)/shard_map/ppermute | solution.py:184
  7.0 0.0 collective-permute-done.up_ref
  7.0 2.8 %collective-permute-done.1.dn_ref = f32[16,2048]{1,0:T(8,128)S(1)} collective-permute-done((f32[16,2048]{1,0:T(8,128)S(1)}, f32[16,2048]{1,0:T(8,128)S(1)}, u32[]{:S(2)}, u32[]{:S(2)}) %collective-permute-start.1) | collective-permute-done | bytes 131104 | tf_op jit(solution)/shard_map/ppermute | solution.py:184
  9.7 0.0 copy-done
  9.7 0.0 copy-done.1
  9.8 0.0 copy-start.2
  9.8 1.0 %copy-done.2 = f32[1,64,2048]{2,1,0:T(8,128)S(1)} copy-done((f32[1,64,2048]{2,1,0:T(8,128)S(1)}, f32[1,64,2048]{2,1,0:T(8,128)}, u32[]{:S(2)}) %copy-start.2) | copy-done | bytes 524312
  10.8 4.3 %shard_map.55 = f32[8,136,128]{2,1,0:T(8,128)S(1)} custom-call(s32[1]{0:T(128)S(6)} %copy.6.level_ref, s32[1]{0:T(128)S(6)} %copy.7.coef_ref, f32[64,2048]{1,0:T(8,128)S(1)} %bitcast.16, f32[64,2048]{1,0:T(8,128)S(1)} %bitcast.17, f32[64,2048]{1,0:T(8,128)S(1)} %bitcast.18, f32[16,2048]{1,0:T(8,128)S(1)} %collective-permute-done.up_ref, ...), custom_call_target="tpu_custom_call" | custom-call | tf_op jit(solution)/shard_map/pallas_call | solution.py:160
  15.1 21.2 %all_to_all.10.parts_ref = f32[8,136,128]{2,1,0:T(8,128)S(1)} all-to-all(f32[8,136,128]{2,1,0:T(8,128)S(1)} %shard_map.55), channel_id=1, replica_groups=mesh['grp'=8,'dom'=4] {'grp'}, dimensions={0} | all-to-all | bytes 1114112 | tf_op jit(solution)/shard_map/all_to_all | solution.py:195
  36.4 20.4 %all_to_all.11.total_ref = f32[8,136,128]{2,1,0:T(8,128)S(1)} all-to-all(f32[8,136,128]{2,1,0:T(8,128)S(1)} %shard_map.56), channel_id=1, replica_groups=mesh['grp'=8,'dom'=4] {'grp'}, dimensions={0} | all-to-all | bytes 1114112 | tf_op jit(solution)/shard_map/all_to_all | solution.py:197
  56.7 1.1 %shard_map.57 = f32[64,2048]{1,0:T(8,128)} custom-call(s32[1]{0:T(128)S(6)} %copy.6.level_ref, f32[8,136,128]{2,1,0:T(8,128)S(1)} %all_to_all.11.total_ref), custom_call_target="tpu_custom_call" | custom-call | tf_op jit(solution)/shard_map/pallas_call | solution.py:160
  (3 shorter events, 0.1 us)
Async XLA Ops:
  0.0 9.7 %copy-start = (f32[1,64,2048]{2,1,0:T(8,128)S(1)}, f32[1,64,2048]{2,1,0:T(8,128)}, u32[]{:S(2)}) copy-start(f32[1,64,2048]{2,1,0:T(8,128)} %param.5) | copy-start | bytes 1572868
  0.0 9.7 %copy-start.1 = (f32[1,64,2048]{2,1,0:T(8,128)S(1)}, f32[1,64,2048]{2,1,0:T(8,128)}, u32[]{:S(2)}) copy-start(f32[1,64,2048]{2,1,0:T(8,128)} %param.6) | copy-start | bytes 1572868
  2.0 5.0 %collective-permute-start = (f32[16,2048]{1,0:T(8,128)S(1)}, f32[16,2048]{1,0:T(8,128)S(1)}, u32[]{:S(2)}, u32[]{:S(2)}) collective-permute-start(f32[16,2048]{1,0:T(8,128)S(1)} %pad_maximum_fusion), channel_id=1, source_target_pairs={{0,1},{1,2},{2,3},{4,5},{5,6},{6,7},{8,9},{9,10},{10,11},{12,13},{... | collective-permute-start | bytes 393224 | tf_op jit(solution)/shard_map/ppermute | solution.py:183
  4.4 5.4 %collective-permute-start.1 = (f32[16,2048]{1,0:T(8,128)S(1)}, f32[16,2048]{1,0:T(8,128)S(1)}, u32[]{:S(2)}, u32[]{:S(2)}) collective-permute-start(f32[16,2048]{1,0:T(8,128)S(1)} %pad_maximum_fusion.1), channel_id=1, source_target_pairs={{1,0},{2,1},{3,2},{5,4},{6,5},{7,6},{9,8},{10,9},{11,10},{13,12},{... | collective-permute-start | bytes 393224 | tf_op jit(solution)/shard_map/ppermute | solution.py:184
  9.8 1.0 %copy-start.2 = (f32[1,64,2048]{2,1,0:T(8,128)S(1)}, f32[1,64,2048]{2,1,0:T(8,128)}, u32[]{:S(2)}) copy-start(f32[1,64,2048]{2,1,0:T(8,128)} %param.7) | copy-start | bytes 1572868

commit v2 on v1

--- a/solution.py
+++ b/solution.py
@@ -9,6 +9,7 @@
 
 STEPS = 4
 LANES = 128
+SQUARE = 4
 TILE = 8
 VMEM_LIMIT = 40 * 1024 * 1024
 
@@ -115,6 +116,11 @@
     total = parts_ref[0]
     for g in range(1, parts_ref.shape[0]):
         total = total + parts_ref[g]
+    out_ref[...] = total
+
+
+def spread_kernel(mine_ref, theirs_ref, out_ref):
+    total = mine_ref[...] + theirs_ref[...]
     for g in range(out_ref.shape[0]):
         out_ref[g] = total
 
@@ -172,7 +178,8 @@
     rows, cols = state.shape
     doms, grids = lax.axis_size("dom"), lax.axis_size("grp")
     strips = cols // LANES
-    per_chunk = strips // grids
+    squares = [list(range(q, q + SQUARE)) for q in range(0, grids, SQUARE)]
+    per_chunk = strips // SQUARE
     tall = rows + 2 * TILE
     chunk_rows = per_chunk * rows + -(-per_chunk // TILE) * TILE
 
@@ -183,7 +190,7 @@
     before = lax.ppermute(to_next, "dom", up)
     after = lax.ppermute(to_prev, "dom", down)
 
-    packed = (grids, chunk_rows, LANES)
+    packed = (SQUARE, chunk_rows, LANES)
     weighted = call(
         functools.partial(run_kernel, rows, strips, per_chunk),
         packed,
@@ -192,9 +199,24 @@
         [pltpu.VMEM((strips + 2, tall, LANES), jnp.float32)] * 2
         + [pltpu.VMEM((strips, tall, LANES), jnp.float32)] * 4,
     )
-    parts = lax.all_to_all(weighted, "grp", split_axis=0, concat_axis=0, tiled=True)
-    spread = call(sum_kernel, packed, (parts,), 0)
-    total = lax.all_to_all(spread, "grp", split_axis=0, concat_axis=0, tiled=True)
+    exchange = functools.partial(
+        lax.all_to_all,
+        axis_name="grp",
+        split_axis=0,
+        concat_axis=0,
+        axis_index_groups=squares,
+        tiled=True,
+    )
+    total = call(sum_kernel, packed[1:], (exchange(weighted),), 0)
+    apart = SQUARE
+    while apart < grids:
+        swap = [(g, g ^ apart) for g in range(grids)]
+        other = lax.ppermute(total, "grp", swap)
+        apart *= 2
+        if apart < grids:
+            total = total + other
+    spread = call(spread_kernel, packed, (total, other), 0)
+    total = exchange(spread)
     nodal = call(
         functools.partial(nodal_kernel, rows, strips, per_chunk), (rows, cols), (levels, total), 1
     )

time: 58.2 us -> 50.1 us (0.86)
  blocking collectives: 41.6 us -> 23.5 us
  waiting for transfers between devices: 2.77 us -> 10.1 us
  starting transfers between devices: 3.66 us -> 6.31 us
    all_to_all x2, blocking collectives: 41.6 us -> 23.5 us  [the longest x1 11.9 us: on_device(): total = exchange(spread)]
    ppermute x0 -> x1, waiting for transfers between devices: none -> 7.36 us  [on_device(): other = lax.ppermute(total, 'grp', swap)]
    ppermute x0 -> x1, starting transfers between devices: none -> 2.65 us  [on_device(): other = lax.ppermute(total, 'grp', swap)]
    pallas_call x3 -> x4, Pallas kernels: 5.39 us -> 5.41 us  [call(): pl.pallas_call(kernel, out_shape=jax.ShapeDtypeStruct(out_shape, jnp.floa...]
  transfers between devices with their start and end apart: 2 -> 3, of which waited for: 1 -> 2; matrix products, arithmetic and copies ran while one was open for 0% -> 0% of each run, Pallas kernels for 0% -> 0%
where the time goes in v2:
time: 50.1 us; the launch traced here: 49.8 us
  blocking collectives  23.5 us (47%)
  waiting for transfers between devices  10.1 us (20%)
  starting transfers between devices  6.31 us (13%)
  Pallas kernels  5.41 us (11%)
  local copies, waits for them, and re-layouts  2.98 us (6%)
  between operations  1.36 us (3%)
    all_to_all x1, blocking collectives, on_device(): total = exchange(spread)  11.9 us
    all_to_all x1, blocking collectives, on_device(): total = call(sum_kernel, packed[1:], (exchange(weighted),), 0)  11.6 us
    ppermute x1, waiting for transfers between devices, on_device(): other = lax.ppermute(total, 'grp', swap)  7.36 us
    pallas_call x4, Pallas kernels, call(): pl.pallas_call(kernel, out_shape=jax.ShapeDtypeStruct(out_shape, jnp.floa...  5.41 us
    ppermute x1, waiting for transfers between devices, on_device(): after = lax.ppermute(to_prev, 'dom', down)  2.77 us
    ppermute x1, starting transfers between devices, on_device(): other = lax.ppermute(total, 'grp', swap)  2.65 us
    ppermute x1, starting transfers between devices, on_device(): before = lax.ppermute(to_next, 'dom', up)  2.36 us
    slice x2, local copies, waits for them, and re-layouts, on_device(): to_prev = jnp.concatenate([state[:8], diffuse[:4], drifts[:4]], axis=0)  1.93 us
  transfers between devices with their start and end apart: 3, of which 2 were waited for; matrix products, arithmetic and copies ran while one was open for 0% of the time, Pallas kernels for 0%

profile of v2, /device:TPU:0, one launch (start us, length us, event | category | flops | bytes accessed | tf_op | source)
XLA Modules:
  0.0 49.8 jit_solution(8818901732414125881)
XLA Ops:
  0.0 0.0 copy-start
  0.0 0.0 copy-start.1
  0.0 1.0 %slice_bitcast_fusion = (f32[8,2048]{1,0:T(8,128)S(1)}, f32[8,2048]{1,0:T(8,128)S(1)}) fusion(f32[1,64,2048]{2,1,0:T(8,128)} %param.5), kind=kLoop, calls=%fused_computation.2 | loop fusion | bytes 262144 | tf_op jit(solution)/shard_map/slice | solution.py:189
  1.0 1.0 %slice_bitcast_fusion.2 = (f32[4,2048]{1,0:T(4,128)S(1)}, f32[4,2048]{1,0:T(4,128)S(1)}, f32[4,2048]{1,0:T(4,128)S(1)}, f32[4,2048]{1,0:T(4,128)S(1)}) fusion(f32[1,64,2048]{2,1,0:T(8,128)} %param.7, f32[1,64,2048]{2,1,0:T(8,128)} %param.6), kind=kLoop, calls=%fused_computation.4 | loop fusion | bytes 262144 | tf_op jit(solution)/shard_map/slice | solution.py:189
  2.0 2.4 %collective-permute-start = (f32[16,2048]{1,0:T(8,128)S(1)}, f32[16,2048]{1,0:T(8,128)S(1)}, u32[]{:S(2)}, u32[]{:S(2)}) collective-permute-start(f32[16,2048]{1,0:T(8,128)S(1)} %pad_maximum_fusion), channel_id=1, source_target_pairs={{0,1},{1,2},{2,3},{4,5},{5,6},{6,7},{8,9},{9,10},{10,11},{12,13},{... | collective-permute-start | bytes 393224 | tf_op jit(solution)/shard_map/ppermute | solution.py:190
  4.4 1.3 %collective-permute-start.1 = (f32[16,2048]{1,0:T(8,128)S(1)}, f32[16,2048]{1,0:T(8,128)S(1)}, u32[]{:S(2)}, u32[]{:S(2)}) collective-permute-start(f32[16,2048]{1,0:T(8,128)S(1)} %pad_maximum_fusion.1), channel_id=1, source_target_pairs={{1,0},{2,1},{3,2},{5,4},{6,5},{7,6},{9,8},{10,9},{11,10},{13,12},{... | collective-permute-start | bytes 393224 | tf_op jit(solution)/shard_map/ppermute | solution.py:191
  7.0 0.0 collective-permute-done.up_ref
  7.0 2.8 %collective-permute-done.1.dn_ref = f32[16,2048]{1,0:T(8,128)S(1)} collective-permute-done((f32[16,2048]{1,0:T(8,128)S(1)}, f32[16,2048]{1,0:T(8,128)S(1)}, u32[]{:S(2)}, u32[]{:S(2)}) %collective-permute-start.1) | collective-permute-done | bytes 131104 | tf_op jit(solution)/shard_map/ppermute | solution.py:191
  9.7 0.0 copy-done
  9.7 0.0 copy-done.1
  9.8 0.0 copy-start.2
  9.8 1.0 %copy-done.2 = f32[1,64,2048]{2,1,0:T(8,128)S(1)} copy-done((f32[1,64,2048]{2,1,0:T(8,128)S(1)}, f32[1,64,2048]{2,1,0:T(8,128)}, u32[]{:S(2)}) %copy-start.2) | copy-done | bytes 524312
  10.8 4.3 %shard_map.55 = f32[4,264,128]{2,1,0:T(8,128)S(1)} custom-call(s32[1]{0:T(128)S(6)} %copy.6.level_ref, s32[1]{0:T(128)S(6)} %copy.7.coef_ref, f32[64,2048]{1,0:T(8,128)S(1)} %bitcast.16, f32[64,2048]{1,0:T(8,128)S(1)} %bitcast.17, f32[64,2048]{1,0:T(8,128)S(1)} %bitcast.18, f32[16,2048]{1,0:T(8,128)S(1)} %collective-permute-done.up_ref, ...), custom_call_target="tpu_custom_call" | custom-call | tf_op jit(solution)/shard_map/pallas_call | solution.py:166
  15.1 11.6 %all_to_all.10.parts_ref = f32[4,264,128]{2,1,0:T(8,128)S(1)} all-to-all(f32[4,264,128]{2,1,0:T(8,128)S(1)} %shard_map.55), channel_id=1, replica_groups={{0,4,8,12},{16,20,24,28},{1,5,9,13},{17,21,25,29},{2,6,10,14},{18,22,26..., dimensions={0} | all-to-all | bytes 1081344 | tf_op jit(solution)/shard_map/all_to_all | solution.py:210
  26.7 2.7 %collective-permute-start.2 = (f32[264,128]{1,0:T(8,128)S(1)}, f32[264,128]{1,0:T(8,128)S(1)}, u32[]{:S(2)}, u32[]{:S(2)}) collective-permute-start(f32[264,128]{1,0:T(8,128)S(1)} %shard_map.56.mine_ref), channel_id=1, source_target_pairs={{0,16},{4,20},{8,24},{12,28},{16,0},{20,4},{24,8},{28,12},{1,17},{... | collective-permute-start | bytes 405512 | tf_op jit(solution)/shard_map/ppermute | solution.py:214
  29.4 7.4 %collective-permute-done.2.theirs_ref = f32[264,128]{1,0:T(8,128)S(1)} collective-permute-done((f32[264,128]{1,0:T(8,128)S(1)}, f32[264,128]{1,0:T(8,128)S(1)}, u32[]{:S(2)}, u32[]{:S(2)}) %collective-permute-start.2) | collective-permute-done | bytes 135200 | tf_op jit(solution)/shard_map/ppermute | solution.py:214
  36.8 11.9 %all_to_all.11.total_ref = f32[4,264,128]{2,1,0:T(8,128)S(1)} all-to-all(f32[4,264,128]{2,1,0:T(8,128)S(1)} %shard_map.57), channel_id=1, replica_groups={{0,4,8,12},{16,20,24,28},{1,5,9,13},{17,21,25,29},{2,6,10,14},{18,22,26..., dimensions={0} | all-to-all | bytes 1081344 | tf_op jit(solution)/shard_map/all_to_all | solution.py:219
  48.7 1.1 %shard_map.58 = f32[64,2048]{1,0:T(8,128)} custom-call(s32[1]{0:T(128)S(6)} %copy.6.level_ref, f32[4,264,128]{2,1,0:T(8,128)S(1)} %all_to_all.11.total_ref), custom_call_target="tpu_custom_call" | custom-call | tf_op jit(solution)/shard_map/pallas_call | solution.py:166
  (4 shorter events, 0.1 us)
Async XLA Ops:
  0.0 9.7 %copy-start = (f32[1,64,2048]{2,1,0:T(8,128)S(1)}, f32[1,64,2048]{2,1,0:T(8,128)}, u32[]{:S(2)}) copy-start(f32[1,64,2048]{2,1,0:T(8,128)} %param.5) | copy-start | bytes 1572868
  0.0 9.7 %copy-start.1 = (f32[1,64,2048]{2,1,0:T(8,128)S(1)}, f32[1,64,2048]{2,1,0:T(8,128)}, u32[]{:S(2)}) copy-start(f32[1,64,2048]{2,1,0:T(8,128)} %param.6) | copy-start | bytes 1572868
  2.0 5.0 %collective-permute-start = (f32[16,2048]{1,0:T(8,128)S(1)}, f32[16,2048]{1,0:T(8,128)S(1)}, u32[]{:S(2)}, u32[]{:S(2)}) collective-permute-start(f32[16,2048]{1,0:T(8,128)S(1)} %pad_maximum_fusion), channel_id=1, source_target_pairs={{0,1},{1,2},{2,3},{4,5},{5,6},{6,7},{8,9},{9,10},{10,11},{12,13},{... | collective-permute-start | bytes 393224 | tf_op jit(solution)/shard_map/ppermute | solution.py:190
  4.4 5.4 %collective-permute-start.1 = (f32[16,2048]{1,0:T(8,128)S(1)}, f32[16,2048]{1,0:T(8,128)S(1)}, u32[]{:S(2)}, u32[]{:S(2)}) collective-permute-start(f32[16,2048]{1,0:T(8,128)S(1)} %pad_maximum_fusion.1), channel_id=1, source_target_pairs={{1,0},{2,1},{3,2},{5,4},{6,5},{7,6},{9,8},{10,9},{11,10},{13,12},{... | collective-permute-start | bytes 393224 | tf_op jit(solution)/shard_map/ppermute | solution.py:191
  9.8 1.0 %copy-start.2 = (f32[1,64,2048]{2,1,0:T(8,128)S(1)}, f32[1,64,2048]{2,1,0:T(8,128)}, u32[]{:S(2)}) copy-start(f32[1,64,2048]{2,1,0:T(8,128)} %param.7) | copy-start | bytes 1572868
  26.7 10.0 %collective-permute-start.2 = (f32[264,128]{1,0:T(8,128)S(1)}, f32[264,128]{1,0:T(8,128)S(1)}, u32[]{:S(2)}, u32[]{:S(2)}) collective-permute-start(f32[264,128]{1,0:T(8,128)S(1)} %shard_map.56.mine_ref), channel_id=1, source_target_pairs={{0,16},{4,20},{8,24},{12,28},{16,0},{20,4},{24,8},{28,12},{1,17},{... | collective-permute-start | bytes 405512 | tf_op jit(solution)/shard_map/ppermute | solution.py:214

commit v3 on v1

--- a/solution.py
+++ b/solution.py
@@ -9,6 +9,7 @@
 
 STEPS = 4
 LANES = 128
+SQUARE = 4
 TILE = 8
 VMEM_LIMIT = 40 * 1024 * 1024
 
@@ -22,8 +23,8 @@
 
 
 def run_kernel(
-    rows, strips, per_chunk, level_ref, coef_ref, dens_ref, diff_ref, drift_ref, up_ref, dn_ref,
-    out_ref, state_a, state_b, center, above_c, below_c, side
+    rows, strips, per_chunk, me_ref, level_ref, coef_ref, dens_ref, diff_ref, drift_ref, up_ref,
+    dn_ref, own_ref, one_ref, two_ref, three_ref, state_a, state_b, center, above_c, below_c, side
 ):
     tall = rows + 2 * TILE
     lanes = lane_ids((tall, LANES))
@@ -97,11 +98,15 @@
 
         ends = jnp.where(is8, both(1), jnp.where(is7, both(2), both(4)))
         weighted = scale * (value - halves * ends)
-        chunk, part = j // per_chunk, lax.rem(j, per_chunk)
-        out_ref[chunk, pl.ds(pl.multiple_of(part * rows, TILE), rows), :] = weighted[
-            TILE : TILE + rows
-        ]
-        out_ref[chunk, pl.ds(per_chunk * rows + part, 1), :] = coef * value[TILE - 1 : TILE]
+        away = (j // per_chunk) ^ me_ref[0]
+        part = lax.rem(j, per_chunk)
+        for k, ref in enumerate((own_ref, one_ref, two_ref, three_ref)):
+
+            @pl.when(away == k)
+            def _(ref=ref):
+                at = pl.ds(pl.multiple_of(part * rows, TILE), rows)
+                ref[at, :] = weighted[TILE : TILE + rows]
+                ref[pl.ds(per_chunk * rows + part, 1), :] = coef * value[TILE - 1 : TILE]
 
     sweep(load_first, coefs_first, to(state_a))
     src, dst = state_a, state_b
@@ -111,15 +116,16 @@
         src, dst = dst, src
 
 
-def sum_kernel(parts_ref, out_ref):
-    total = parts_ref[0]
-    for g in range(1, parts_ref.shape[0]):
-        total = total + parts_ref[g]
-    for g in range(out_ref.shape[0]):
-        out_ref[g] = total
-
-
-def nodal_kernel(rows, strips, per_chunk, level_ref, total_ref, out_ref):
+def sum_kernel(*refs):
+    *parts, out_ref = refs
+    total = parts[0][...]
+    for part in parts[1:]:
+        total = total + part[...]
+    out_ref[...] = total
+
+
+def nodal_kernel(rows, per_chunk, me_ref, level_ref, *refs):
+    *totals, out_ref = refs
     level = level_ref[0]
     keep = [jnp.where(level >= at, 1.0, 0.0) for at in (6, 7, 8)]
     row = row_in_tile((TILE, LANES))
@@ -131,37 +137,37 @@
     hat7 = keep[1] * jnp.minimum(fine, 4.0 - fine) * 0.5
     hat8 = jnp.where(row % 2 == 0, keep[2], 0.0)
 
-    def body(j, _):
-        chunk, part = j // per_chunk, lax.rem(j, per_chunk)
-        top = pl.multiple_of(part * rows, TILE)
-        prev = total_ref[chunk, pl.ds(per_chunk * rows + part, 1), :]
-        strip = total_ref[chunk, pl.ds(top, rows), :]
-        tiles = []
-        for t in range(rows // TILE):
-            tile = strip[t * TILE : (t + 1) * TILE]
-            last = tile[7:8]
-            mid = jnp.where(row < 4, tile[1:2], tile[5:6])
-            tiles.append(
-                from_prev * prev + from_next * last + hat6 * tile[3:4] + hat7 * mid + hat8 * tile
-            )
-            prev = last
-        at = pl.ds(pl.multiple_of(j * LANES, LANES), LANES)
-        out_ref[:, at] = jnp.concatenate(tiles, axis=0)
-        return 0
-
-    lax.fori_loop(0, strips, body, 0, unroll=2)
-
-
-def call(kernel, out_shape, operands, in_smem, scratch=()):
+    for away, total_ref in enumerate(totals):
+        first = (me_ref[0] ^ away) * per_chunk
+
+        def body(part, _, total_ref=total_ref, first=first):
+            prev = total_ref[pl.ds(per_chunk * rows + part, 1), :]
+            strip = total_ref[pl.ds(pl.multiple_of(part * rows, TILE), rows), :]
+            tiles = []
+            for t in range(rows // TILE):
+                tile = strip[t * TILE : (t + 1) * TILE]
+                last = tile[7:8]
+                mid = jnp.where(row < 4, tile[1:2], tile[5:6])
+                spans = from_prev * prev + from_next * last
+                tiles.append(spans + hat6 * tile[3:4] + hat7 * mid + hat8 * tile)
+                prev = last
+            at = pl.ds(pl.multiple_of((first + part) * LANES, LANES), LANES)
+            out_ref[:, at] = jnp.concatenate(tiles, axis=0)
+            return 0
+
+        lax.fori_loop(0, per_chunk, body, 0, unroll=2)
+
+
+def call(kernel, out_shapes, operands, in_smem, scratch=()):
     specs = [
         pl.BlockSpec(memory_space=pltpu.SMEM if k < in_smem else pltpu.VMEM)
         for k in range(len(operands))
     ]
     return pl.pallas_call(
         kernel,
-        out_shape=jax.ShapeDtypeStruct(out_shape, jnp.float32),
+        out_shape=[jax.ShapeDtypeStruct(shape, jnp.float32) for shape in out_shapes],
         in_specs=specs,
-        out_specs=pl.BlockSpec(memory_space=pltpu.VMEM),
+        out_specs=[pl.BlockSpec(memory_space=pltpu.VMEM) for _ in out_shapes],
         scratch_shapes=list(scratch),
         compiler_params=pltpu.CompilerParams(vmem_limit_bytes=VMEM_LIMIT),
     )(*operands)
@@ -172,7 +178,8 @@
     rows, cols = state.shape
     doms, grids = lax.axis_size("dom"), lax.axis_size("grp")
     strips = cols // LANES
-    per_chunk = strips // grids
+    me = lax.rem(lax.axis_index("grp"), SQUARE).astype(jnp.int32)[None]
+    per_chunk = strips // SQUARE
     tall = rows + 2 * TILE
     chunk_rows = per_chunk * rows + -(-per_chunk // TILE) * TILE
 
@@ -183,20 +190,28 @@
     before = lax.ppermute(to_next, "dom", up)
     after = lax.ppermute(to_prev, "dom", down)
 
-    packed = (grids, chunk_rows, LANES)
-    weighted = call(
+    packed = (chunk_rows, LANES)
+    own, *others = call(
         functools.partial(run_kernel, rows, strips, per_chunk),
-        packed,
-        (levels, coefficient, state, diffuse, drifts, before, after),
-        2,
+        [packed] * SQUARE,
+        (me, levels, coefficient, state, diffuse, drifts, before, after),
+        3,
         [pltpu.VMEM((strips + 2, tall, LANES), jnp.float32)] * 2
         + [pltpu.VMEM((strips, tall, LANES), jnp.float32)] * 4,
     )
-    parts = lax.all_to_all(weighted, "grp", split_axis=0, concat_axis=0, tiled=True)
-    spread = call(sum_kernel, packed, (parts,), 0)
-    total = lax.all_to_all(spread, "grp", split_axis=0, concat_axis=0, tiled=True)
-    nodal = call(
-        functools.partial(nodal_kernel, rows, strips, per_chunk), (rows, cols), (levels, total), 1
+
+    def swap(array, apart):
+        return lax.ppermute(array, "grp", [(g, g ^ apart) for g in range(grids)])
+
+    theirs = [swap(array, apart) for apart, array in enumerate(others, 1)]
+    (total,) = call(sum_kernel, [packed], (own, *theirs), 0)
+    apart = SQUARE
+    while apart < grids:
+        (total,) = call(sum_kernel, [packed], (total, swap(total, apart)), 0)
+        apart *= 2
+    totals = [total] + [swap(total, apart) for apart in range(1, SQUARE)]
+    (nodal,) = call(
+        functools.partial(nodal_kernel, rows, per_chunk), [(rows, cols)], (me, levels, *totals), 2
     )
     return nodal[None]
 

time: 58.2 us -> 46.6 us (0.80)
  blocking collectives: 41.6 us -> 0 us
  waiting for transfers between devices: 2.77 us -> 22.3 us
  starting transfers between devices: 3.66 us -> 13.4 us
  Pallas kernels: 5.39 us -> 6.16 us
    all_to_all x2 -> x0, blocking collectives: 41.6 us -> none  [the longest x1 21.2 us: on_device(): lax.all_to_all(weighted, 'grp', split_axis=0, concat_axis=0, tiled=True)]
    ppermute x0 -> x7, waiting for transfers between devices: none -> 19.6 us  [swap(): return lax.ppermute(array, 'grp', [(g, g ^ apart) for g in range(grids)])]
    ppermute x0 -> x7, starting transfers between devices: none -> 9.76 us  [swap(): return lax.ppermute(array, 'grp', [(g, g ^ apart) for g in range(grids)])]
    pallas_call x3 -> x4, Pallas kernels: 5.39 us -> 6.16 us  [call(): pl.pallas_call(kernel, out_shape=[jax.ShapeDtypeStruct(shape, jnp.float32...]
  transfers between devices with their start and end apart: 2 -> 9, of which waited for: 1 -> 8; matrix products, arithmetic and copies ran while one was open for 0% -> 0% of each run, Pallas kernels for 0% -> 0%
where the time goes in v3:
time: 46.6 us; the launch traced here: 46.3 us
  waiting for transfers between devices  22.3 us (48%)
  starting transfers between devices  13.4 us (29%)
  Pallas kernels  6.16 us (13%)
  local copies, waits for them, and re-layouts  2.98 us (6%)
  between operations  1.36 us (3%)
    ppermute x7, waiting for transfers between devices, swap(): return lax.ppermute(array, 'grp', [(g, g ^ apart) for g in range(grids)])  19.6 us
    ppermute x7, starting transfers between devices, swap(): return lax.ppermute(array, 'grp', [(g, g ^ apart) for g in range(grids)])  9.76 us
    pallas_call x4, Pallas kernels, call(): pl.pallas_call(kernel, out_shape=[jax.ShapeDtypeStruct(shape, jnp.float32...  6.16 us
    ppermute x1, waiting for transfers between devices, on_device(): after = lax.ppermute(to_prev, 'dom', down)  2.76 us
    ppermute x1, starting transfers between devices, on_device(): before = lax.ppermute(to_next, 'dom', up)  2.36 us
    slice x2, local copies, waits for them, and re-layouts, on_device(): to_prev = jnp.concatenate([state[:8], diffuse[:4], drifts[:4]], axis=0)  1.93 us
    ppermute x1, starting transfers between devices, on_device(): after = lax.ppermute(to_prev, 'dom', down)  1.29 us
    unnamed x6, local copies, waits for them, and re-layouts  1.05 us
  transfers between devices with their start and end apart: 9, of which 8 were waited for; matrix products, arithmetic and copies ran while one was open for 0% of the time, Pallas kernels for 0%

profile of v3, /device:TPU:0, one launch (start us, length us, event | category | flops | bytes accessed | tf_op | source)
XLA Modules:
  0.0 46.3 jit_solution(8813550010401804861)
XLA Ops:
  0.0 0.0 copy-start
  0.0 0.0 copy-start.1
  0.0 1.0 %slice_bitcast_fusion = (f32[8,2048]{1,0:T(8,128)S(1)}, f32[8,2048]{1,0:T(8,128)S(1)}) fusion(f32[1,64,2048]{2,1,0:T(8,128)} %param.5), kind=kLoop, calls=%fused_computation.2 | loop fusion | bytes 262144 | tf_op jit(solution)/shard_map/slice | solution.py:189
  1.0 1.0 %slice_bitcast_fusion.2 = (f32[4,2048]{1,0:T(4,128)S(1)}, f32[4,2048]{1,0:T(4,128)S(1)}, f32[4,2048]{1,0:T(4,128)S(1)}, f32[4,2048]{1,0:T(4,128)S(1)}) fusion(f32[1,64,2048]{2,1,0:T(8,128)} %param.7, f32[1,64,2048]{2,1,0:T(8,128)} %param.6), kind=kLoop, calls=%fused_computation.4 | loop fusion | bytes 262144 | tf_op jit(solution)/shard_map/slice | solution.py:189
  2.0 2.4 %collective-permute-start = (f32[16,2048]{1,0:T(8,128)S(1)}, f32[16,2048]{1,0:T(8,128)S(1)}, u32[]{:S(2)}, u32[]{:S(2)}) collective-permute-start(f32[16,2048]{1,0:T(8,128)S(1)} %pad_maximum_fusion), channel_id=1, source_target_pairs={{0,1},{1,2},{2,3},{4,5},{5,6},{6,7},{8,9},{9,10},{10,11},{12,13},{... | collective-permute-start | bytes 393224 | tf_op jit(solution)/shard_map/ppermute | solution.py:190
  4.4 1.3 %collective-permute-start.1 = (f32[16,2048]{1,0:T(8,128)S(1)}, f32[16,2048]{1,0:T(8,128)S(1)}, u32[]{:S(2)}, u32[]{:S(2)}) collective-permute-start(f32[16,2048]{1,0:T(8,128)S(1)} %pad_maximum_fusion.1), channel_id=1, source_target_pairs={{1,0},{2,1},{3,2},{5,4},{6,5},{7,6},{9,8},{10,9},{11,10},{13,12},{... | collective-permute-start | bytes 393224 | tf_op jit(solution)/shard_map/ppermute | solution.py:191
  7.0 0.0 collective-permute-done.up_ref
  7.0 2.8 %collective-permute-done.1.dn_ref = f32[16,2048]{1,0:T(8,128)S(1)} collective-permute-done((f32[16,2048]{1,0:T(8,128)S(1)}, f32[16,2048]{1,0:T(8,128)S(1)}, u32[]{:S(2)}, u32[]{:S(2)}) %collective-permute-start.1) | collective-permute-done | bytes 131104 | tf_op jit(solution)/shard_map/ppermute | solution.py:191
  9.7 0.0 copy-done
  9.7 0.0 copy-done.1
  9.8 0.0 copy-start.2
  9.8 1.0 %copy-done.2 = f32[1,64,2048]{2,1,0:T(8,128)S(1)} copy-done((f32[1,64,2048]{2,1,0:T(8,128)S(1)}, f32[1,64,2048]{2,1,0:T(8,128)}, u32[]{:S(2)}) %copy-start.2) | copy-done | bytes 524312
  10.8 5.1 %shard_map.55 = (f32[264,128]{1,0:T(8,128)S(1)}, f32[264,128]{1,0:T(8,128)S(1)}, f32[264,128]{1,0:T(8,128)S(1)}, f32[264,128]{1,0:T(8,128)S(1)}) custom-call(s32[1]{0:T(128)} %bitcast.me_ref, s32[1]{0:T(128)S(6)} %copy.6.level_ref, s32[1]{0:T(128)S(6)} %copy.7.coef_ref, f32[64,2048]{1,0:T(8,128)S(1)} %bitcast.17, f32[64,2048]{1,0:T(8,128)S(1)} %bitcast.18, ...), custom_call_target="tpu_custom_call" | custom-call | tf_op jit(solution)/shard_map/pallas_call | solution.py:166
  15.9 1.6 %collective-permute-start.2 = (f32[264,128]{1,0:T(8,128)S(1)}, f32[264,128]{1,0:T(8,128)S(1)}, u32[]{:S(2)}, u32[]{:S(2)}) collective-permute-start(f32[264,128]{1,0:T(8,128)S(1)} %get-tuple-element.10), channel_id=1, source_target_pairs={{0,4},{4,0},{8,12},{12,8},{16,20},{20,16},{24,28},{28,24},{1,5},{5... | collective-permute-start | bytes 405512 | tf_op jit(solution)/shard_map/ppermute | solution.py:204
  17.4 1.6 %collective-permute-start.3 = (f32[264,128]{1,0:T(8,128)S(1)}, f32[264,128]{1,0:T(8,128)S(1)}, u32[]{:S(2)}, u32[]{:S(2)}) collective-permute-start(f32[264,128]{1,0:T(8,128)S(1)} %get-tuple-element.11), channel_id=1, source_target_pairs={{0,8},{4,12},{8,0},{12,4},{16,24},{20,28},{24,16},{28,20},{1,9},{5... | collective-permute-start | bytes 405512 | tf_op jit(solution)/shard_map/ppermute | solution.py:204
  19.0 0.4 collective-permute-start.4
  19.4 1.5 %collective-permute-done.2.refs_1_ = f32[264,128]{1,0:T(8,128)S(1)} collective-permute-done((f32[264,128]{1,0:T(8,128)S(1)}, f32[264,128]{1,0:T(8,128)S(1)}, u32[]{:S(2)}, u32[]{:S(2)}) %collective-permute-start.2) | collective-permute-done | bytes 135200 | tf_op jit(solution)/shard_map/ppermute | solution.py:204
  21.0 1.5 %collective-permute-done.3.refs_2_ = f32[264,128]{1,0:T(8,128)S(1)} collective-permute-done((f32[264,128]{1,0:T(8,128)S(1)}, f32[264,128]{1,0:T(8,128)S(1)}, u32[]{:S(2)}, u32[]{:S(2)}) %collective-permute-start.3) | collective-permute-done | bytes 135200 | tf_op jit(solution)/shard_map/ppermute | solution.py:204
  22.4 3.9 %collective-permute-done.4.refs_3_ = f32[264,128]{1,0:T(8,128)S(1)} collective-permute-done((f32[264,128]{1,0:T(8,128)S(1)}, f32[264,128]{1,0:T(8,128)S(1)}, u32[]{:S(2)}, u32[]{:S(2)}) %collective-permute-start.4) | collective-permute-done | bytes 135200 | tf_op jit(solution)/shard_map/ppermute | solution.py:204
  26.4 2.7 %collective-permute-start.5 = (f32[264,128]{1,0:T(8,128)S(1)}, f32[264,128]{1,0:T(8,128)S(1)}, u32[]{:S(2)}, u32[]{:S(2)}) collective-permute-start(f32[264,128]{1,0:T(8,128)S(1)} %shard_map.56.refs_0_), channel_id=1, source_target_pairs={{0,16},{4,20},{8,24},{12,28},{16,0},{20,4},{24,8},{28,12},{1,17},{... | collective-permute-start | bytes 405512 | tf_op jit(solution)/shard_map/ppermute | solution.py:204
  29.1 6.7 %collective-permute-done.5.refs_1_ = f32[264,128]{1,0:T(8,128)S(1)} collective-permute-done((f32[264,128]{1,0:T(8,128)S(1)}, f32[264,128]{1,0:T(8,128)S(1)}, u32[]{:S(2)}, u32[]{:S(2)}) %collective-permute-start.5) | collective-permute-done | bytes 135200 | tf_op jit(solution)/shard_map/ppermute | solution.py:204
  35.8 0.5 %collective-permute-start.8 = (f32[264,128]{1,0:T(8,128)S(1)}, f32[264,128]{1,0:T(8,128)S(1)}, u32[]{:S(2)}, u32[]{:S(2)}) collective-permute-start(f32[264,128]{1,0:T(8,128)S(1)} %shard_map.57.refs_0_), channel_id=1, source_target_pairs={{0,12},{4,8},{8,4},{12,0},{16,28},{20,24},{24,20},{28,16},{1,13},{... | collective-permute-start | bytes 405512 | tf_op jit(solution)/shard_map/ppermute | solution.py:204
  36.3 1.0 %collective-permute-start.7 = (f32[264,128]{1,0:T(8,128)S(1)}, f32[264,128]{1,0:T(8,128)S(1)}, u32[]{:S(2)}, u32[]{:S(2)}) collective-permute-start(f32[264,128]{1,0:T(8,128)S(1)} %shard_map.57.refs_0_), channel_id=1, source_target_pairs={{0,8},{4,12},{8,0},{12,4},{16,24},{20,28},{24,16},{28,20},{1,9},{5... | collective-permute-start | bytes 405512 | tf_op jit(solution)/shard_map/ppermute | solution.py:204
  37.3 2.1 %collective-permute-start.6 = (f32[264,128]{1,0:T(8,128)S(1)}, f32[264,128]{1,0:T(8,128)S(1)}, u32[]{:S(2)}, u32[]{:S(2)}) collective-permute-start(f32[264,128]{1,0:T(8,128)S(1)} %shard_map.57.refs_0_), channel_id=1, source_target_pairs={{0,4},{4,0},{8,12},{12,8},{16,20},{20,16},{24,28},{28,24},{1,5},{5... | collective-permute-start | bytes 405512 | tf_op jit(solution)/shard_map/ppermute | solution.py:204
  39.4 3.9 %collective-permute-done.8.refs_3_ = f32[264,128]{1,0:T(8,128)S(1)} collective-permute-done((f32[264,128]{1,0:T(8,128)S(1)}, f32[264,128]{1,0:T(8,128)S(1)}, u32[]{:S(2)}, u32[]{:S(2)}) %collective-permute-start.8) | collective-permute-done | bytes 135200 | tf_op jit(solution)/shard_map/ppermute | solution.py:204
  43.2 1.1 %collective-permute-done.7.refs_2_ = f32[264,128]{1,0:T(8,128)S(1)} collective-permute-done((f32[264,128]{1,0:T(8,128)S(1)}, f32[264,128]{1,0:T(8,128)S(1)}, u32[]{:S(2)}, u32[]{:S(2)}) %collective-permute-start.7) | collective-permute-done | bytes 135200 | tf_op jit(solution)/shard_map/ppermute | solution.py:204
  44.3 1.0 %collective-permute-done.6.refs_1_ = f32[264,128]{1,0:T(8,128)S(1)} collective-permute-done((f32[264,128]{1,0:T(8,128)S(1)}, f32[264,128]{1,0:T(8,128)S(1)}, u32[]{:S(2)}, u32[]{:S(2)}) %collective-permute-start.6) | collective-permute-done | bytes 135200 | tf_op jit(solution)/shard_map/ppermute | solution.py:204
  45.3 1.0 %shard_map.58 = f32[64,2048]{1,0:T(8,128)} custom-call(s32[1]{0:T(128)} %bitcast.me_ref, s32[1]{0:T(128)S(6)} %copy.6.level_ref, f32[264,128]{1,0:T(8,128)S(1)} %shard_map.57.refs_0_, f32[264,128]{1,0:T(8,128)S(1)} %collective-permute-done.6.refs_1_, f32[264,128]{1,0:T(8,128)S(1)} %collective-permute-done.7.refs_2_, ...), custom_call_target="tpu_custom_call" | custom-call | tf_op jit(solution)/shard_map/pallas_call | solution.py:166
  (4 shorter events, 0.1 us)
Async XLA Ops:
  0.0 9.7 %copy-start = (f32[1,64,2048]{2,1,0:T(8,128)S(1)}, f32[1,64,2048]{2,1,0:T(8,128)}, u32[]{:S(2)}) copy-start(f32[1,64,2048]{2,1,0:T(8,128)} %param.5) | copy-start | bytes 1572868
  0.0 9.7 %copy-start.1 = (f32[1,64,2048]{2,1,0:T(8,128)S(1)}, f32[1,64,2048]{2,1,0:T(8,128)}, u32[]{:S(2)}) copy-start(f32[1,64,2048]{2,1,0:T(8,128)} %param.6) | copy-start | bytes 1572868
  2.0 5.0 %collective-permute-start = (f32[16,2048]{1,0:T(8,128)S(1)}, f32[16,2048]{1,0:T(8,128)S(1)}, u32[]{:S(2)}, u32[]{:S(2)}) collective-permute-start(f32[16,2048]{1,0:T(8,128)S(1)} %pad_maximum_fusion), channel_id=1, source_target_pairs={{0,1},{1,2},{2,3},{4,5},{5,6},{6,7},{8,9},{9,10},{10,11},{12,13},{... | collective-permute-start | bytes 393224 | tf_op jit(solution)/shard_map/ppermute | solution.py:190
  4.4 5.4 %collective-permute-start.1 = (f32[16,2048]{1,0:T(8,128)S(1)}, f32[16,2048]{1,0:T(8,128)S(1)}, u32[]{:S(2)}, u32[]{:S(2)}) collective-permute-start(f32[16,2048]{1,0:T(8,128)S(1)} %pad_maximum_fusion.1), channel_id=1, source_target_pairs={{1,0},{2,1},{3,2},{5,4},{6,5},{7,6},{9,8},{10,9},{11,10},{13,12},{... | collective-permute-start | bytes 393224 | tf_op jit(solution)/shard_map/ppermute | solution.py:191
  9.8 1.0 %copy-start.2 = (f32[1,64,2048]{2,1,0:T(8,128)S(1)}, f32[1,64,2048]{2,1,0:T(8,128)}, u32[]{:S(2)}) copy-start(f32[1,64,2048]{2,1,0:T(8,128)} %param.7) | copy-start | bytes 1572868
  15.9 5.1 %collective-permute-start.2 = (f32[264,128]{1,0:T(8,128)S(1)}, f32[264,128]{1,0:T(8,128)S(1)}, u32[]{:S(2)}, u32[]{:S(2)}) collective-permute-start(f32[264,128]{1,0:T(8,128)S(1)} %get-tuple-element.10), channel_id=1, source_target_pairs={{0,4},{4,0},{8,12},{12,8},{16,20},{20,16},{24,28},{28,24},{1,5},{5... | collective-permute-start | bytes 405512 | tf_op jit(solution)/shard_map/ppermute | solution.py:204
  17.4 5.0 %collective-permute-start.3 = (f32[264,128]{1,0:T(8,128)S(1)}, f32[264,128]{1,0:T(8,128)S(1)}, u32[]{:S(2)}, u32[]{:S(2)}) collective-permute-start(f32[264,128]{1,0:T(8,128)S(1)} %get-tuple-element.11), channel_id=1, source_target_pairs={{0,8},{4,12},{8,0},{12,4},{16,24},{20,28},{24,16},{28,20},{1,9},{5... | collective-permute-start | bytes 405512 | tf_op jit(solution)/shard_map/ppermute | solution.py:204
  19.0 7.4 %collective-permute-start.4 = (f32[264,128]{1,0:T(8,128)S(1)}, f32[264,128]{1,0:T(8,128)S(1)}, u32[]{:S(2)}, u32[]{:S(2)}) collective-permute-start(f32[264,128]{1,0:T(8,128)S(1)} %get-tuple-element.12), channel_id=1, source_target_pairs={{0,12},{4,8},{8,4},{12,0},{16,28},{20,24},{24,20},{28,16},{1,13},{... | collective-permute-start | bytes 405512 | tf_op jit(solution)/shard_map/ppermute | solution.py:204
  26.4 9.4 %collective-permute-start.5 = (f32[264,128]{1,0:T(8,128)S(1)}, f32[264,128]{1,0:T(8,128)S(1)}, u32[]{:S(2)}, u32[]{:S(2)}) collective-permute-start(f32[264,128]{1,0:T(8,128)S(1)} %shard_map.56.refs_0_), channel_id=1, source_target_pairs={{0,16},{4,20},{8,24},{12,28},{16,0},{20,4},{24,8},{28,12},{1,17},{... | collective-permute-start | bytes 405512 | tf_op jit(solution)/shard_map/ppermute | solution.py:204
  35.8 7.4 %collective-permute-start.8 = (f32[264,128]{1,0:T(8,128)S(1)}, f32[264,128]{1,0:T(8,128)S(1)}, u32[]{:S(2)}, u32[]{:S(2)}) collective-permute-start(f32[264,128]{1,0:T(8,128)S(1)} %shard_map.57.refs_0_), channel_id=1, source_target_pairs={{0,12},{4,8},{8,4},{12,0},{16,28},{20,24},{24,20},{28,16},{1,13},{... | collective-permute-start | bytes 405512 | tf_op jit(solution)/shard_map/ppermute | solution.py:204
  36.3 8.0 %collective-permute-start.7 = (f32[264,128]{1,0:T(8,128)S(1)}, f32[264,128]{1,0:T(8,128)S(1)}, u32[]{:S(2)}, u32[]{:S(2)}) collective-permute-start(f32[264,128]{1,0:T(8,128)S(1)} %shard_map.57.refs_0_), channel_id=1, source_target_pairs={{0,8},{4,12},{8,0},{12,4},{16,24},{20,28},{24,16},{28,20},{1,9},{5... | collective-permute-start | bytes 405512 | tf_op jit(solution)/shard_map/ppermute | solution.py:204
  37.3 8.0 %collective-permute-start.6 = (f32[264,128]{1,0:T(8,128)S(1)}, f32[264,128]{1,0:T(8,128)S(1)}, u32[]{:S(2)}, u32[]{:S(2)}) collective-permute-start(f32[264,128]{1,0:T(8,128)S(1)} %shard_map.57.refs_0_), channel_id=1, source_target_pairs={{0,4},{4,0},{8,12},{12,8},{16,20},{20,16},{24,28},{28,24},{1,5},{5... | collective-permute-start | bytes 405512 | tf_op jit(solution)/shard_map/ppermute | solution.py:204

commit v4 on v0

v4 whole, which is shorter than its diff:
```python
import functools

import jax
import jax.numpy as jnp
from jax import lax
from jax.experimental import pallas as pl
from jax.experimental.pallas import tpu as pltpu
from jax.sharding import PartitionSpec as P

STEPS = 4
LANES = 128
TILE = 8
HALF = TILE // 2
SLAB = 4 * TILE
SQUARE = 4
VMEM_LIMIT = 40 * 1024 * 1024


def tiles_of(block):
    rows, cols = block.shape
    return block.reshape(rows // TILE, TILE, cols // LANES, LANES).transpose(0, 2, 1, 3)


def block_of(tiles):
    many, strips = tiles.shape[:2]
    return tiles.transpose(0, 2, 1, 3).reshape(many * TILE, strips * LANES)


def flat(ref):
    return ref.reshape(ref.size // LANES, LANES)


def spaced(first, count, stride):
    return pl.ds(first, count, stride=stride) if count > 1 else pl.ds(first, 1)


def roll_rows(value, shift):
    count = value.shape[0]
    return pltpu.roll(value, shift % count, 0) if count > 1 else value


def per_strip(strips, body, unroll):
    def step(j, carry):
        body(j)
        return carry

    lax.fori_loop(0, strips, step, 0, unroll=unroll)


def advance(strips, classes, source, coefs, emit, unroll):
    shape = source.shape[2:]
    lanes = lax.broadcasted_iota(jnp.int32, shape, 1)
    center, above_c, below_c, side = coefs

    def body(j, carry):
        cur, right_prev, left_cur = carry
        nxt = [source[j + 2, t] for t in range(classes)]
        left_next = [pltpu.roll(x, LANES - 1, 1) for x in nxt]
        right_cur = [pltpu.roll(x, 1, 1) for x in cur]
        above = cur[1:] + [roll_rows(cur[0], -1)]
        below = [roll_rows(cur[-1], 1)] + cur[:-1]
        new = []
        for t in range(classes):
            left = jnp.where(lanes == 0, right_prev[t], right_cur[t])
            right = jnp.where(lanes == LANES - 1, left_next[t], left_cur[t])
            new.append(
                center[j, t] * cur[t]
                + above_c[j, t] * above[t]
                + below_c[j, t] * below[t]
                + side[j, t] * (left + right)
            )
        emit(j, new)
        return nxt, right_cur, left_next

    cur = [source[1, t] for t in range(classes)]
    zeros = [jnp.zeros(shape, jnp.float32)] * classes
    first = (cur, zeros, [pltpu.roll(x, LANES - 1, 1) for x in cur])
    lax.fori_loop(0, strips, body, first, unroll=unroll)


def run_steps(strips, classes, load, buffers, coefs, finish, unroll):
    center, above_c, below_c, side = coefs
    for buf in buffers:
        for edge in (0, strips + 1):
            buf[edge] = jnp.zeros(buf.shape[1:], jnp.float32)

    def begin(j):
        for t in range(classes):
            state, diffuse, drifts = load(j, t)
            half = 0.5 * drifts
            buffers[0][j + 1, t] = state
            center[j, t] = 1.0 - 4.0 * diffuse
            above_c[j, t] = diffuse - half
            below_c[j, t] = diffuse + half
            side[j, t] = diffuse

    per_strip(strips, begin, unroll)
    for step in range(STEPS):
        source, target = buffers[step % 2], buffers[1 - step % 2]

        def keep(j, new, target=target):
            for t in range(classes):
                target[j + 1, t] = new[t]

        emit = keep if step < STEPS - 1 else finish
        advance(strips, classes, source, coefs, emit, unroll)


def pack_kernel(parity_ref, dens_ref, diff_ref, drift_ref, far_ref, near_ref, ends_ref):
    many, strips = dens_ref.shape[:2]
    odd = parity_ref[0] == 1
    upper = lax.broadcasted_iota(jnp.int32, (TILE, LANES), 0) < HALF

    def body(j):
        refs = (dens_ref, diff_ref, drift_ref)
        heads, tails = ([ref[at, j] for ref in refs] for at in (0, many - 1))
        for k in range(3):
            ends_ref[k, 0, j], ends_ref[k, 1, j] = heads[k], tails[k]
        mix_next = jnp.where(upper, pltpu.roll(tails[2], HALF, 0), tails[1])
        mix_prev = jnp.where(upper, heads[1], pltpu.roll(heads[2], HALF, 0))
        to_next, to_prev = (tails[0], mix_next), (heads[0], mix_prev)
        for k in range(2):
            at = pl.ds(k * TILE, TILE)
            far_ref[j, at] = jnp.where(odd, to_next[k], to_prev[k])
            near_ref[j, at] = jnp.where(odd, to_prev[k], to_next[k])

    per_strip(strips, body, 4)


def inner_kernel(dens_ref, diff_ref, drift_ref, out_ref, state_a, state_b, *coefs):
    many, strips = dens_ref.shape[:2]
    refs = [flat(ref) for ref in (dens_ref, diff_ref, drift_ref)]

    def load(j, t):
        at = spaced(j * TILE + t, many, strips * TILE)
        return [ref[at, :] for ref in refs]

    def finish(j, new):
        for t in range(TILE):
            out_ref[j, t] = new[t]

    run_steps(strips, TILE, load, (state_a, state_b), coefs, finish, 2)


def edge_kernel(
    per_chunk, depth, parity_ref, me_ref, level_ref, coef_ref, ends_ref, inner_ref, far_ref,
    near_ref, own_ref, one_ref, two_ref, three_ref, slab, state_a, state_b, *coefs
):
    strips, _, many = inner_ref.shape[:3]
    odd = parity_ref[0] == 1

    def stage(j):
        far, near = far_ref[j], near_ref[j]
        up, dn = jnp.where(odd, near, far), jnp.where(odd, far, near)
        up_mix, dn_mix = up[TILE:], dn[TILE:]
        outer = (
            (up[:TILE], dn[:TILE]),
            (up_mix, dn_mix),
            (pltpu.roll(up_mix, HALF, 0), pltpu.roll(dn_mix, HALF, 0)),
        )
        for k, (before, after) in enumerate(outer):
            for e, tile in enumerate((before, ends_ref[k, 0, j], ends_ref[k, 1, j], after)):
                slab[k, j, e * TILE : (e + 1) * TILE] = tile

    per_strip(strips, stage, 4)
    slabs = flat(slab)

    def load(j, t):
        return [
            slabs[pl.ds((k * strips + j) * SLAB + t, TILE, stride=HALF), :] for k in range(3)
        ]

    coef = coef_ref[0].astype(jnp.float32)
    fine, mid, low = (
        jnp.where(level_ref[0] >= depth - down, coef, 0.0) for down in range(3)
    )
    place = lax.broadcasted_iota(jnp.int32, (many, LANES), 0)
    out_refs = (own_ref, one_ref, two_ref, three_ref)

    def finish(j, new):
        s = [inner_ref[j, t] for t in range(TILE)]
        for t in range(HALF):
            s[t] = jnp.where(place == 0, new[t][2:3], s[t])
        for t in range(HALF):
            s[HALF + t] = jnp.where(place == many - 1, new[t][5:6], s[HALF + t])
        before = new[HALF - 1][1:2]
        prev = jnp.where(place == 0, before, roll_rows(s[7], 1))
        weighted = [
            fine * (s[0] - 0.5 * (prev + s[1])),
            mid * (s[1] - 0.5 * (prev + s[3])),
            fine * (s[2] - 0.5 * (s[1] + s[3])),
            low * (s[3] - 0.5 * (prev + s[7])),
            fine * (s[4] - 0.5 * (s[3] + s[5])),
            mid * (s[5] - 0.5 * (s[3] + s[7])),
            fine * (s[6] - 0.5 * (s[5] + s[7])),
            coef * s[7],
        ]
        away = (j // per_chunk) ^ me_ref[0]
        part = lax.rem(j, per_chunk)
        for k, ref in enumerate(out_refs):

            @pl.when(away == k)
            def _(ref=ref):
                for t in range(TILE):
                    ref[part * TILE + t] = weighted[t]
                ref[per_chunk * TILE + part // many, pl.ds(lax.rem(part, many), 1), :] = (
                    coef * before
                )

    run_steps(strips, HALF, load, (state_a, state_b), coefs, finish, 2)


def sum_kernel(*refs):
    *parts, out_ref = refs
    total = parts[0][...]
    for part in parts[1:]:
        total = total + part[...]
    out_ref[...] = total


def nodal_kernel(per_chunk, depth, me_ref, level_ref, *refs):
    *totals, out_ref = refs
    many, strips = out_ref.shape[:2]
    out = flat(out_ref)
    fine, mid, low = (jnp.where(level_ref[0] >= depth - down, 1.0, 0.0) for down in range(3))
    place = lax.broadcasted_iota(jnp.int32, (many, LANES), 0)
    for away, ref in enumerate(totals):
        first = (me_ref[0] ^ away) * per_chunk

        def body(part, ref=ref, first=first):
            w = [ref[part * TILE + t] for t in range(TILE)]
            before = ref[per_chunk * TILE + part // many, pl.ds(lax.rem(part, many), 1), :]
            prev = jnp.where(place == 0, before, roll_rows(w[7], 1))
            v3 = 0.5 * (prev + w[7]) + low * w[3]
            v1 = 0.5 * (prev + v3) + mid * w[1]
            v5 = 0.5 * (v3 + w[7]) + mid * w[5]
            values = (
                0.5 * (prev + v1) + fine * w[0],
                v1,
                0.5 * (v1 + v3) + fine * w[2],
                v3,
                0.5 * (v3 + v5) + fine * w[4],
                v5,
                0.5 * (v5 + w[7]) + fine * w[6],
                w[7],
            )
            for t in range(TILE):
                out[spaced((first + part) * TILE + t, many, strips * TILE), :] = values[t]

        per_strip(per_chunk, body, 2)


def call(kernel, out_shapes, operands, in_smem=0, scratch=(), flops=0):
    specs = [
        pl.BlockSpec(memory_space=pltpu.SMEM if k < in_smem else pltpu.VMEM)
        for k in range(len(operands))
    ]
    moved = 4 * sum(x.size for x in operands)
    return pl.pallas_call(
        kernel,
        out_shape=[jax.ShapeDtypeStruct(shape, jnp.float32) for shape in out_shapes],
        in_specs=specs,
        out_specs=[pl.BlockSpec(memory_space=pltpu.VMEM) for _ in out_shapes],
        scratch_shapes=list(scratch),
        compiler_params=pltpu.CompilerParams(vmem_limit_bytes=VMEM_LIMIT),
        cost_estimate=pl.CostEstimate(flops=flops, bytes_accessed=moved, transcendentals=0),
    )(*operands)


def on_device(density, diffusion, drift_speed, levels, coefficient):
    rows, cols = density.shape[1:]
    doms, grids = lax.axis_size("dom"), lax.axis_size("grp")
    many, strips = rows // TILE, cols // LANES
    per_chunk = strips // SQUARE
    depth = (rows * doms).bit_length() - 1
    tiles = [tiles_of(x[0]) for x in (density, diffusion, drift_speed)]
    me = (lax.axis_index("grp") % SQUARE).astype(jnp.int32)[None]
    parity = (lax.axis_index("dom") % 2).astype(jnp.int32)[None]

    def vmem(*shape):
        return pltpu.VMEM(shape, jnp.float32)

    far, near, ends = call(
        pack_kernel,
        [(strips, 2 * TILE, LANES)] * 2 + [(3, 2, strips, TILE, LANES)],
        (parity, *tiles),
        1,
    )
    far_pairs = [(d, d + 1) for d in range(1, doms - 1, 2)]
    near_pairs = [(d, d + 1) for d in range(0, doms, 2)]
    far, near = (
        lax.ppermute(array, "dom", pairs + [(b, a) for a, b in pairs])
        for array, pairs in ((far, far_pairs), (near, near_pairs))
    )
    (inner,) = call(
        inner_kernel,
        [(strips, TILE, many, LANES)],
        tiles,
        0,
        [vmem(strips + 2, TILE, many, LANES)] * 2 + [vmem(strips, TILE, many, LANES)] * 4,
        flops=40 * rows * cols,
    )

    chunk = (per_chunk * TILE + -(-per_chunk // many), many, LANES)
    own, *others = call(
        functools.partial(edge_kernel, per_chunk, depth),
        [chunk] * SQUARE,
        (parity, me, levels, coefficient, ends, inner, far, near),
        4,
        [vmem(3, strips, SLAB, LANES)]
        + [vmem(strips + 2, HALF, TILE, LANES)] * 2
        + [vmem(strips, HALF, TILE, LANES)] * 4,
        flops=40 * SLAB * cols,
    )

    def swap(array, apart):
        return lax.ppermute(array, "grp", [(g, g ^ apart) for g in range(grids)])

    theirs = [swap(array, apart) for apart, array in enumerate(others, 1)]
    (total,) = call(sum_kernel, [chunk], (own, *theirs))
    apart = SQUARE
    while apart < grids:
        (total,) = call(sum_kernel, [chunk], (total, swap(total, apart)))
        apart *= 2
    totals = [total] + [swap(total, apart) for apart in range(1, SQUARE)]
    (nodal,) = call(
        functools.partial(nodal_kernel, per_chunk, depth),
        [(many, strips, TILE, LANES)],
        (me, levels, *totals),
        2,
    )
    return block_of(nodal)[None]


def solution(mesh):
    return jax.shard_map(
        on_device,
        mesh=mesh,
        in_specs=(
            P("grp", "dom", None),
            P("grp", "dom", None),
            P("grp", "dom", None),
            P("grp"),
            P("grp"),
        ),
        out_specs=P("grp", "dom", None),
        check_vma=False,
    )
```

time: 152 us -> 47.1 us (0.31)
  waiting for transfers between devices: 82.9 us -> 17.1 us
  starting transfers between devices: 28.5 us -> 14.9 us
  between operations: 14.9 us -> 1.39 us
  blocking collectives: 11.4 us -> 0 us
  Pallas kernels: 0 us -> 10.2 us
  other arithmetic: 5.19 us -> 0 us
  matrix products: 3.47 us -> 0 us
  local copies, waits for them, and re-layouts: 5.22 us -> 3.13 us
    psum x1 -> x0, waiting for transfers between devices: 72.8 us -> none  [on_device(): total = lax.psum(weighted, 'grp')]
    ppermute x8 -> x9, waiting for transfers between devices: 3.21 us -> 17.1 us  [the longest x7 17.1 us: swap(): return lax.ppermute(array, 'grp', [(g, g ^ apart) for g in range(grids)])]
    all_to_all x1 -> x0, blocking collectives: 11.4 us -> none  [on_device(): lax.all_to_all(nodal, 'dom', split_axis=0, concat_axis=1, tiled=True)]
    pallas_call x0 -> x6, Pallas kernels: none -> 10.2 us  [call(): pl.pallas_call(kernel, out_shape=[jax.ShapeDtypeStruct(shape, jnp.float32...]
    ppermute x8 -> x9, starting transfers between devices: 22.8 us -> 14.9 us  [the longest x7 9.76 us: swap(): return lax.ppermute(array, 'grp', [(g, g ^ apart) for g in range(grids)])]
    all_to_all x1 -> x0, waiting for transfers between devices: 6.86 us -> none  [on_device(): lax.all_to_all(state, 'dom', split_axis=1, concat_axis=0, tiled=True)]
    all_to_all x1 -> x0, starting transfers between devices: 5.68 us -> none  [on_device(): lax.all_to_all(state, 'dom', split_axis=1, concat_axis=0, tiled=True)]
    dot_general x2 -> x0, matrix products: 3.47 us -> none  [the longest x1 1.79 us: on_device(): jnp.dot(to_surplus, poles, precision=lax.Precision.HIGHEST, preferred_ele...]
  transfers between devices with their start and end apart: 10 -> 9, of which waited for: 6 -> 7; matrix products, arithmetic and copies ran while one was open for 0% -> 0% of each run, Pallas kernels for 0% -> 10%
where the time goes in v4:
time: 47.1 us; the launch traced here: 46.8 us
  waiting for transfers between devices  17.1 us (36%)
  starting transfers between devices  14.9 us (32%)
  Pallas kernels  10.2 us (22%)
  local copies, waits for them, and re-layouts  3.13 us (7%)
  between operations  1.39 us (3%)
    ppermute x7, waiting for transfers between devices, swap(): return lax.ppermute(array, 'grp', [(g, g ^ apart) for g in range(grids)])  17.1 us
    pallas_call x6, Pallas kernels, call(): pl.pallas_call(kernel, out_shape=[jax.ShapeDtypeStruct(shape, jnp.float32...  10.2 us
    ppermute x7, starting transfers between devices, swap(): return lax.ppermute(array, 'grp', [(g, g ^ apart) for g in range(grids)])  9.76 us
    ppermute x2, starting transfers between devices, on_device(): lax.ppermute(array, 'dom', pairs + [(b, a) for a, b in pairs])  5.19 us
    unnamed x12, local copies, waits for them, and re-layouts  3.13 us
  transfers between devices with their start and end apart: 9, of which 7 were waited for; matrix products, arithmetic and copies ran while one was open for 0% of the time, Pallas kernels for 10%

profile of v4, /device:TPU:0, one launch (start us, length us, event | category | flops | bytes accessed | tf_op | source)
XLA Modules:
  0.0 46.8 jit_solution(14434337938623599531)
XLA Ops:
  0.0 0.0 copy-start
  0.0 1.0 %copy-done = f32[1,64,2048]{2,1,0:T(8,128)S(1)} copy-done((f32[1,64,2048]{2,1,0:T(8,128)S(1)}, f32[1,64,2048]{2,1,0:T(8,128)}, u32[]{:S(2)}) %copy-start) | copy-done | bytes 524312
  1.0 0.0 copy-start.2
  1.0 1.0 %copy-done.2 = f32[1,64,2048]{2,1,0:T(8,128)S(1)} copy-done((f32[1,64,2048]{2,1,0:T(8,128)S(1)}, f32[1,64,2048]{2,1,0:T(8,128)}, u32[]{:S(2)}) %copy-start.2) | copy-done | bytes 524312
  2.1 0.0 copy-start.4
  2.1 1.0 %copy-done.4 = f32[1,64,2048]{2,1,0:T(8,128)S(1)} copy-done((f32[1,64,2048]{2,1,0:T(8,128)S(1)}, f32[1,64,2048]{2,1,0:T(8,128)}, u32[]{:S(2)}) %copy-start.4) | copy-done | bytes 524312
  3.1 0.0 copy-start.1
  3.1 0.0 copy-start.3
  3.1 0.0 copy-start.5
  3.2 0.8 %collective-permute-start = (f32[16,16,128]{2,1,0:T(8,128)S(1)}, f32[16,16,128]{2,1,0:T(8,128)S(1)}, u32[]{:S(2)}, u32[]{:S(2)}) collective-permute-start(f32[16,16,128]{2,1,0:T(8,128)S(1)} %get-tuple-element.13), channel_id=1, source_target_pairs={{1,2},{2,1},{5,6},{6,5},{9,10},{10,9},{13,14},{14,13},{17,18},{18,... | collective-permute-start | bytes 393224 | tf_op jit(solution)/shard_map/ppermute | solution.py:292
  4.0 4.4 %collective-permute-start.1 = (f32[16,16,128]{2,1,0:T(8,128)S(1)}, f32[16,16,128]{2,1,0:T(8,128)S(1)}, u32[]{:S(2)}, u32[]{:S(2)}) collective-permute-start(f32[16,16,128]{2,1,0:T(8,128)S(1)} %get-tuple-element.14), channel_id=1, source_target_pairs={{0,1},{2,3},{1,0},{3,2},{4,5},{6,7},{5,4},{7,6},{8,9},{10,11},{9,8... | collective-permute-start | bytes 393224 | tf_op jit(solution)/shard_map/ppermute | solution.py:292
  9.7 0.0 copy-done.1
  9.7 0.0 copy-done.3
  9.7 0.0 copy-done.5
  9.7 4.7 %shard_map.56.inner_ref = f32[16,8,8,128]{3,2,1,0:T(8,128)S(1)} custom-call(f32[8,16,8,128]{3,2,1,0:T(8,128)S(1)} %bitcast.15, f32[8,16,8,128]{3,2,1,0:T(8,128)S(1)} %bitcast.17, f32[8,16,8,128]{3,2,1,0:T(8,128)S(1)} %bitcast.19), custom_call_target="tpu_custom_call" | custom-call | flops 5242880 | bytes 1572864 | tf_op jit(solution)/shard_map/pallas_call | solution.py:259
  14.4 0.0 collective-permute-done.far_ref
  14.4 0.0 collective-permute-done.1.near_ref
  14.4 4.2 %shard_map.57 = (f32[33,8,128]{2,1,0:T(8,128)S(1)}, f32[33,8,128]{2,1,0:T(8,128)S(1)}, f32[33,8,128]{2,1,0:T(8,128)S(1)}, f32[33,8,128]{2,1,0:T(8,128)S(1)}) custom-call(s32[1]{0:T(128)} %bitcast.1.parity_ref, s32[1]{0:T(128)} %bitcast.me_ref, s32[1]{0:T(128)S(6)} %copy.6.level_ref, s32[1]{0:T(128)S(6)} %copy.7.coef_ref, ...), custom_call_target="tpu_custom_call" | custom-call | flops 2621440 | bytes 1179664 | tf_op jit(solution)/shard_map/pallas_call | solution.py:259
  18.7 1.6 %collective-permute-start.2 = (f32[33,8,128]{2,1,0:T(8,128)S(1)}, f32[33,8,128]{2,1,0:T(8,128)S(1)}, u32[]{:S(2)}, u32[]{:S(2)}) collective-permute-start(f32[33,8,128]{2,1,0:T(8,128)S(1)} %get-tuple-element.16), channel_id=1, source_target_pairs={{0,4},{4,0},{8,12},{12,8},{16,20},{20,16},{24,28},{28,24},{1,5},{5... | collective-permute-start | bytes 405512 | tf_op jit(solution)/shard_map/ppermute | solution.py:317
  20.2 1.6 %collective-permute-start.3 = (f32[33,8,128]{2,1,0:T(8,128)S(1)}, f32[33,8,128]{2,1,0:T(8,128)S(1)}, u32[]{:S(2)}, u32[]{:S(2)}) collective-permute-start(f32[33,8,128]{2,1,0:T(8,128)S(1)} %get-tuple-element.17), channel_id=1, source_target_pairs={{0,8},{4,12},{8,0},{12,4},{16,24},{20,28},{24,16},{28,20},{1,9},{5... | collective-permute-start | bytes 405512 | tf_op jit(solution)/shard_map/ppermute | solution.py:317
  21.8 0.4 collective-permute-start.4
  22.2 2.0 %collective-permute-done.2.refs_1_ = f32[33,8,128]{2,1,0:T(8,128)S(1)} collective-permute-done((f32[33,8,128]{2,1,0:T(8,128)S(1)}, f32[33,8,128]{2,1,0:T(8,128)S(1)}, u32[]{:S(2)}, u32[]{:S(2)}) %collective-permute-start.2) | collective-permute-done | bytes 135200 | tf_op jit(solution)/shard_map/ppermute | solution.py:317
  24.2 2.5 %collective-permute-done.3.refs_2_ = f32[33,8,128]{2,1,0:T(8,128)S(1)} collective-permute-done((f32[33,8,128]{2,1,0:T(8,128)S(1)}, f32[33,8,128]{2,1,0:T(8,128)S(1)}, u32[]{:S(2)}, u32[]{:S(2)}) %collective-permute-start.3) | collective-permute-done | bytes 135200 | tf_op jit(solution)/shard_map/ppermute | solution.py:317
  26.7 1.6 %collective-permute-done.4.refs_3_ = f32[33,8,128]{2,1,0:T(8,128)S(1)} collective-permute-done((f32[33,8,128]{2,1,0:T(8,128)S(1)}, f32[33,8,128]{2,1,0:T(8,128)S(1)}, u32[]{:S(2)}, u32[]{:S(2)}) %collective-permute-start.4) | collective-permute-done | bytes 135200 | tf_op jit(solution)/shard_map/ppermute | solution.py:317
  28.4 2.7 %collective-permute-start.5 = (f32[33,8,128]{2,1,0:T(8,128)S(1)}, f32[33,8,128]{2,1,0:T(8,128)S(1)}, u32[]{:S(2)}, u32[]{:S(2)}) collective-permute-start(f32[33,8,128]{2,1,0:T(8,128)S(1)} %shard_map.58.refs_0_), channel_id=1, source_target_pairs={{0,16},{4,20},{8,24},{12,28},{16,0},{20,4},{24,8},{28,12},{1,17},{... | collective-permute-start | bytes 405512 | tf_op jit(solution)/shard_map/ppermute | solution.py:317
  31.0 5.9 %collective-permute-done.5.refs_1_ = f32[33,8,128]{2,1,0:T(8,128)S(1)} collective-permute-done((f32[33,8,128]{2,1,0:T(8,128)S(1)}, f32[33,8,128]{2,1,0:T(8,128)S(1)}, u32[]{:S(2)}, u32[]{:S(2)}) %collective-permute-start.5) | collective-permute-done | bytes 135200 | tf_op jit(solution)/shard_map/ppermute | solution.py:317
  36.9 1.3 %collective-permute-start.8 = (f32[33,8,128]{2,1,0:T(8,128)S(1)}, f32[33,8,128]{2,1,0:T(8,128)S(1)}, u32[]{:S(2)}, u32[]{:S(2)}) collective-permute-start(f32[33,8,128]{2,1,0:T(8,128)S(1)} %shard_map.59.refs_0_), channel_id=1, source_target_pairs={{0,12},{4,8},{8,4},{12,0},{16,28},{20,24},{24,20},{28,16},{1,13},{... | collective-permute-start | bytes 405512 | tf_op jit(solution)/shard_map/ppermute | solution.py:317
  38.3 1.4 %collective-permute-start.7 = (f32[33,8,128]{2,1,0:T(8,128)S(1)}, f32[33,8,128]{2,1,0:T(8,128)S(1)}, u32[]{:S(2)}, u32[]{:S(2)}) collective-permute-start(f32[33,8,128]{2,1,0:T(8,128)S(1)} %shard_map.59.refs_0_), channel_id=1, source_target_pairs={{0,8},{4,12},{8,0},{12,4},{16,24},{20,28},{24,16},{28,20},{1,9},{5... | collective-permute-start | bytes 405512 | tf_op jit(solution)/shard_map/ppermute | solution.py:317
  39.6 0.9 %collective-permute-start.6 = (f32[33,8,128]{2,1,0:T(8,128)S(1)}, f32[33,8,128]{2,1,0:T(8,128)S(1)}, u32[]{:S(2)}, u32[]{:S(2)}) collective-permute-start(f32[33,8,128]{2,1,0:T(8,128)S(1)} %shard_map.59.refs_0_), channel_id=1, source_target_pairs={{0,4},{4,0},{8,12},{12,8},{16,20},{20,16},{24,28},{28,24},{1,5},{5... | collective-permute-start | bytes 405512 | tf_op jit(solution)/shard_map/ppermute | solution.py:317
  40.5 3.7 %collective-permute-done.8.refs_3_ = f32[33,8,128]{2,1,0:T(8,128)S(1)} collective-permute-done((f32[33,8,128]{2,1,0:T(8,128)S(1)}, f32[33,8,128]{2,1,0:T(8,128)S(1)}, u32[]{:S(2)}, u32[]{:S(2)}) %collective-permute-start.8) | collective-permute-done | bytes 135200 | tf_op jit(solution)/shard_map/ppermute | solution.py:317
  44.2 0.1 collective-permute-done.7.refs_2_
  44.2 1.4 %collective-permute-done.6.refs_1_ = f32[33,8,128]{2,1,0:T(8,128)S(1)} collective-permute-done((f32[33,8,128]{2,1,0:T(8,128)S(1)}, f32[33,8,128]{2,1,0:T(8,128)S(1)}, u32[]{:S(2)}, u32[]{:S(2)}) %collective-permute-start.6) | collective-permute-done | bytes 135200 | tf_op jit(solution)/shard_map/ppermute | solution.py:317
  45.6 1.2 %shard_map.60 = f32[8,16,8,128]{3,2,1,0:T(8,128)} custom-call(s32[1]{0:T(128)} %bitcast.me_ref, s32[1]{0:T(128)S(6)} %copy.6.level_ref, f32[33,8,128]{2,1,0:T(8,128)S(1)} %shard_map.59.refs_0_, f32[33,8,128]{2,1,0:T(8,128)S(1)} %collective-permute-done.6.refs_1_, f32[33,8,128]{2,1,0:T(8,128)S(1)} %collective-permute-done.7.refs_2_, ...), custom_call_target="tpu_custom_call" | custom-call | bytes 540680 | tf_op jit(solution)/shard_map/pallas_call | solution.py:259
  (3 shorter events, 0.1 us)
Async XLA Ops:
  0.0 1.0 %copy-start = (f32[1,64,2048]{2,1,0:T(8,128)S(1)}, f32[1,64,2048]{2,1,0:T(8,128)}, u32[]{:S(2)}) copy-start(f32[1,64,2048]{2,1,0:T(8,128)} %param.5) | copy-start | bytes 1572868
  1.0 1.0 %copy-start.2 = (f32[1,64,2048]{2,1,0:T(8,128)S(1)}, f32[1,64,2048]{2,1,0:T(8,128)}, u32[]{:S(2)}) copy-start(f32[1,64,2048]{2,1,0:T(8,128)} %param.6) | copy-start | bytes 1572868
  2.1 1.0 %copy-start.4 = (f32[1,64,2048]{2,1,0:T(8,128)S(1)}, f32[1,64,2048]{2,1,0:T(8,128)}, u32[]{:S(2)}) copy-start(f32[1,64,2048]{2,1,0:T(8,128)} %param.7) | copy-start | bytes 1572868
  3.1 6.6 %copy-start.1 = (f32[1,64,2048]{2,1,0:T(8,128)S(1)}, f32[1,64,2048]{2,1,0:T(8,128)}, u32[]{:S(2)}) copy-start(f32[1,64,2048]{2,1,0:T(8,128)} %param.5) | copy-start | bytes 1572868
  3.1 6.6 %copy-start.3 = (f32[1,64,2048]{2,1,0:T(8,128)S(1)}, f32[1,64,2048]{2,1,0:T(8,128)}, u32[]{:S(2)}) copy-start(f32[1,64,2048]{2,1,0:T(8,128)} %param.6) | copy-start | bytes 1572868
  3.1 6.6 %copy-start.5 = (f32[1,64,2048]{2,1,0:T(8,128)S(1)}, f32[1,64,2048]{2,1,0:T(8,128)}, u32[]{:S(2)}) copy-start(f32[1,64,2048]{2,1,0:T(8,128)} %param.7) | copy-start | bytes 1572868
  3.2 11.2 %collective-permute-start = (f32[16,16,128]{2,1,0:T(8,128)S(1)}, f32[16,16,128]{2,1,0:T(8,128)S(1)}, u32[]{:S(2)}, u32[]{:S(2)}) collective-permute-start(f32[16,16,128]{2,1,0:T(8,128)S(1)} %get-tuple-element.13), channel_id=1, source_target_pairs={{1,2},{2,1},{5,6},{6,5},{9,10},{10,9},{13,14},{14,13},{17,18},{18,... | collective-permute-start | bytes 393224 | tf_op jit(solution)/shard_map/ppermute | solution.py:292
  4.0 10.4 %collective-permute-start.1 = (f32[16,16,128]{2,1,0:T(8,128)S(1)}, f32[16,16,128]{2,1,0:T(8,128)S(1)}, u32[]{:S(2)}, u32[]{:S(2)}) collective-permute-start(f32[16,16,128]{2,1,0:T(8,128)S(1)} %get-tuple-element.14), channel_id=1, source_target_pairs={{0,1},{2,3},{1,0},{3,2},{4,5},{6,7},{5,4},{7,6},{8,9},{10,11},{9,8... | collective-permute-start | bytes 393224 | tf_op jit(solution)/shard_map/ppermute | solution.py:292
  18.7 5.6 %collective-permute-start.2 = (f32[33,8,128]{2,1,0:T(8,128)S(1)}, f32[33,8,128]{2,1,0:T(8,128)S(1)}, u32[]{:S(2)}, u32[]{:S(2)}) collective-permute-start(f32[33,8,128]{2,1,0:T(8,128)S(1)} %get-tuple-element.16), channel_id=1, source_target_pairs={{0,4},{4,0},{8,12},{12,8},{16,20},{20,16},{24,28},{28,24},{1,5},{5... | collective-permute-start | bytes 405512 | tf_op jit(solution)/shard_map/ppermute | solution.py:317
  20.2 6.5 %collective-permute-start.3 = (f32[33,8,128]{2,1,0:T(8,128)S(1)}, f32[33,8,128]{2,1,0:T(8,128)S(1)}, u32[]{:S(2)}, u32[]{:S(2)}) collective-permute-start(f32[33,8,128]{2,1,0:T(8,128)S(1)} %get-tuple-element.17), channel_id=1, source_target_pairs={{0,8},{4,12},{8,0},{12,4},{16,24},{20,28},{24,16},{28,20},{1,9},{5... | collective-permute-start | bytes 405512 | tf_op jit(solution)/shard_map/ppermute | solution.py:317
  21.8 6.5 %collective-permute-start.4 = (f32[33,8,128]{2,1,0:T(8,128)S(1)}, f32[33,8,128]{2,1,0:T(8,128)S(1)}, u32[]{:S(2)}, u32[]{:S(2)}) collective-permute-start(f32[33,8,128]{2,1,0:T(8,128)S(1)} %get-tuple-element.18), channel_id=1, source_target_pairs={{0,12},{4,8},{8,4},{12,0},{16,28},{20,24},{24,20},{28,16},{1,13},{... | collective-permute-start | bytes 405512 | tf_op jit(solution)/shard_map/ppermute | solution.py:317
  28.4 8.6 %collective-permute-start.5 = (f32[33,8,128]{2,1,0:T(8,128)S(1)}, f32[33,8,128]{2,1,0:T(8,128)S(1)}, u32[]{:S(2)}, u32[]{:S(2)}) collective-permute-start(f32[33,8,128]{2,1,0:T(8,128)S(1)} %shard_map.58.refs_0_), channel_id=1, source_target_pairs={{0,16},{4,20},{8,24},{12,28},{16,0},{20,4},{24,8},{28,12},{1,17},{... | collective-permute-start | bytes 405512 | tf_op jit(solution)/shard_map/ppermute | solution.py:317
  36.9 7.2 %collective-permute-start.8 = (f32[33,8,128]{2,1,0:T(8,128)S(1)}, f32[33,8,128]{2,1,0:T(8,128)S(1)}, u32[]{:S(2)}, u32[]{:S(2)}) collective-permute-start(f32[33,8,128]{2,1,0:T(8,128)S(1)} %shard_map.59.refs_0_), channel_id=1, source_target_pairs={{0,12},{4,8},{8,4},{12,0},{16,28},{20,24},{24,20},{28,16},{1,13},{... | collective-permute-start | bytes 405512 | tf_op jit(solution)/shard_map/ppermute | solution.py:317
  38.3 6.0 %collective-permute-start.7 = (f32[33,8,128]{2,1,0:T(8,128)S(1)}, f32[33,8,128]{2,1,0:T(8,128)S(1)}, u32[]{:S(2)}, u32[]{:S(2)}) collective-permute-start(f32[33,8,128]{2,1,0:T(8,128)S(1)} %shard_map.59.refs_0_), channel_id=1, source_target_pairs={{0,8},{4,12},{8,0},{12,4},{16,24},{20,28},{24,16},{28,20},{1,9},{5... | collective-permute-start | bytes 405512 | tf_op jit(solution)/shard_map/ppermute | solution.py:317
  39.6 6.0 %collective-permute-start.6 = (f32[33,8,128]{2,1,0:T(8,128)S(1)}, f32[33,8,128]{2,1,0:T(8,128)S(1)}, u32[]{:S(2)}, u32[]{:S(2)}) collective-permute-start(f32[33,8,128]{2,1,0:T(8,128)S(1)} %shard_map.59.refs_0_), channel_id=1, source_target_pairs={{0,4},{4,0},{8,12},{12,8},{16,20},{20,16},{24,28},{28,24},{1,5},{5... | collective-permute-start | bytes 405512 | tf_op jit(solution)/shard_map/ppermute | solution.py:317

commit v5 on v4

--- a/solution.py
+++ b/solution.py
@@ -13,6 +13,7 @@
 HALF = TILE // 2
 SLAB = 4 * TILE
 SQUARE = 4
+UNROLL = 16
 VMEM_LIMIT = 40 * 1024 * 1024
 
 
@@ -106,16 +107,14 @@
         advance(strips, classes, source, coefs, emit, unroll)
 
 
-def pack_kernel(parity_ref, dens_ref, diff_ref, drift_ref, far_ref, near_ref, ends_ref):
-    many, strips = dens_ref.shape[:2]
+def pack_kernel(parity_ref, *refs):
+    *ends, far_ref, near_ref = refs
+    strips = far_ref.shape[0]
     odd = parity_ref[0] == 1
     upper = lax.broadcasted_iota(jnp.int32, (TILE, LANES), 0) < HALF
 
     def body(j):
-        refs = (dens_ref, diff_ref, drift_ref)
-        heads, tails = ([ref[at, j] for ref in refs] for at in (0, many - 1))
-        for k in range(3):
-            ends_ref[k, 0, j], ends_ref[k, 1, j] = heads[k], tails[k]
+        heads, tails = ([ref[j] for ref in ends[e::2]] for e in range(2))
         mix_next = jnp.where(upper, pltpu.roll(tails[2], HALF, 0), tails[1])
         mix_prev = jnp.where(upper, heads[1], pltpu.roll(heads[2], HALF, 0))
         to_next, to_prev = (tails[0], mix_next), (heads[0], mix_prev)
@@ -127,7 +126,10 @@
     per_strip(strips, body, 4)
 
 
-def inner_kernel(dens_ref, diff_ref, drift_ref, out_ref, state_a, state_b, *coefs):
+def inner_kernel(
+    depth, level_ref, coef_ref, dens_ref, diff_ref, drift_ref, out_ref, keep_ref, weight_ref,
+    state_a, state_b, *coefs
+):
     many, strips = dens_ref.shape[:2]
     refs = [flat(ref) for ref in (dens_ref, diff_ref, drift_ref)]
 
@@ -139,13 +141,20 @@
         for t in range(TILE):
             out_ref[j, t] = new[t]
 
-    run_steps(strips, TILE, load, (state_a, state_b), coefs, finish, 2)
+    run_steps(strips, TILE, load, (state_a, state_b), coefs, finish, min(strips, UNROLL))
+    coef = coef_ref[0].astype(jnp.float32)
+    for down in range(3):
+        keep = jnp.where(level_ref[0] >= depth - down, 1.0, 0.0)
+        keep_ref[down] = jnp.full((many, LANES), keep)
+        weight_ref[down] = jnp.full((many, LANES), keep * coef)
+    weight_ref[3] = jnp.full((many, LANES), coef)
 
 
 def edge_kernel(
-    per_chunk, depth, parity_ref, me_ref, level_ref, coef_ref, ends_ref, inner_ref, far_ref,
-    near_ref, own_ref, one_ref, two_ref, three_ref, slab, state_a, state_b, *coefs
+    per_chunk, parity_ref, me_ref, weight_ref, *refs
 ):
+    ends, (inner_ref, far_ref, near_ref), out_refs = refs[:6], refs[6:9], refs[9:13]
+    slab, state_a, state_b, *coefs = refs[13:]
     strips, _, many = inner_ref.shape[:3]
     odd = parity_ref[0] == 1
 
@@ -159,7 +168,7 @@
             (pltpu.roll(up_mix, HALF, 0), pltpu.roll(dn_mix, HALF, 0)),
         )
         for k, (before, after) in enumerate(outer):
-            for e, tile in enumerate((before, ends_ref[k, 0, j], ends_ref[k, 1, j], after)):
+            for e, tile in enumerate((before, ends[2 * k][j], ends[2 * k + 1][j], after)):
                 slab[k, j, e * TILE : (e + 1) * TILE] = tile
 
     per_strip(strips, stage, 4)
@@ -170,12 +179,8 @@
             slabs[pl.ds((k * strips + j) * SLAB + t, TILE, stride=HALF), :] for k in range(3)
         ]
 
-    coef = coef_ref[0].astype(jnp.float32)
-    fine, mid, low = (
-        jnp.where(level_ref[0] >= depth - down, coef, 0.0) for down in range(3)
-    )
+    fine, mid, low, coef = (weight_ref[k] for k in range(4))
     place = lax.broadcasted_iota(jnp.int32, (many, LANES), 0)
-    out_refs = (own_ref, one_ref, two_ref, three_ref)
 
     def finish(j, new):
         s = [inner_ref[j, t] for t in range(TILE)]
@@ -204,10 +209,10 @@
                 for t in range(TILE):
                     ref[part * TILE + t] = weighted[t]
                 ref[per_chunk * TILE + part // many, pl.ds(lax.rem(part, many), 1), :] = (
-                    coef * before
+                    coef[0:1] * before
                 )
 
-    run_steps(strips, HALF, load, (state_a, state_b), coefs, finish, 2)
+    run_steps(strips, HALF, load, (state_a, state_b), coefs, finish, min(strips, UNROLL))
 
 
 def sum_kernel(*refs):
@@ -218,11 +223,11 @@
     out_ref[...] = total
 
 
-def nodal_kernel(per_chunk, depth, me_ref, level_ref, *refs):
+def nodal_kernel(per_chunk, me_ref, keep_ref, *refs):
     *totals, out_ref = refs
     many, strips = out_ref.shape[:2]
     out = flat(out_ref)
-    fine, mid, low = (jnp.where(level_ref[0] >= depth - down, 1.0, 0.0) for down in range(3))
+    fine, mid, low = (keep_ref[k] for k in range(3))
     place = lax.broadcasted_iota(jnp.int32, (many, LANES), 0)
     for away, ref in enumerate(totals):
         first = (me_ref[0] ^ away) * per_chunk
@@ -247,14 +252,12 @@
             for t in range(TILE):
                 out[spaced((first + part) * TILE + t, many, strips * TILE), :] = values[t]
 
-        per_strip(per_chunk, body, 2)
+        per_strip(per_chunk, body, min(per_chunk, 4))
 
 
 def call(kernel, out_shapes, operands, in_smem=0, scratch=(), flops=0):
-    specs = [
-        pl.BlockSpec(memory_space=pltpu.SMEM if k < in_smem else pltpu.VMEM)
-        for k in range(len(operands))
-    ]
+    spaces = [pltpu.SMEM] * in_smem + [pltpu.VMEM] * (len(operands) - in_smem)
+    specs = [pl.BlockSpec(memory_space=space) for space in spaces]
     moved = 4 * sum(x.size for x in operands)
     return pl.pallas_call(
         kernel,
@@ -280,10 +283,11 @@
     def vmem(*shape):
         return pltpu.VMEM(shape, jnp.float32)
 
-    far, near, ends = call(
+    ends = [x[at] for x in tiles for at in (0, many - 1)]
+    far, near = call(
         pack_kernel,
-        [(strips, 2 * TILE, LANES)] * 2 + [(3, 2, strips, TILE, LANES)],
-        (parity, *tiles),
+        [(strips, 2 * TILE, LANES)] * 2,
+        (parity, *ends),
         1,
     )
     far_pairs = [(d, d + 1) for d in range(1, doms - 1, 2)]
@@ -292,21 +296,21 @@
         lax.ppermute(array, "dom", pairs + [(b, a) for a, b in pairs])
         for array, pairs in ((far, far_pairs), (near, near_pairs))
     )
-    (inner,) = call(
-        inner_kernel,
-        [(strips, TILE, many, LANES)],
-        tiles,
-        0,
+    inner, keep, weight = call(
+        functools.partial(inner_kernel, depth),
+        [(strips, TILE, many, LANES), (3, many, LANES), (4, many, LANES)],
+        (levels, coefficient, *tiles),
+        2,
         [vmem(strips + 2, TILE, many, LANES)] * 2 + [vmem(strips, TILE, many, LANES)] * 4,
         flops=40 * rows * cols,
     )
 
     chunk = (per_chunk * TILE + -(-per_chunk // many), many, LANES)
     own, *others = call(
-        functools.partial(edge_kernel, per_chunk, depth),
+        functools.partial(edge_kernel, per_chunk),
         [chunk] * SQUARE,
-        (parity, me, levels, coefficient, ends, inner, far, near),
-        4,
+        (parity, me, weight, *ends, inner, far, near),
+        2,
         [vmem(3, strips, SLAB, LANES)]
         + [vmem(strips + 2, HALF, TILE, LANES)] * 2
         + [vmem(strips, HALF, TILE, LANES)] * 4,
@@ -324,10 +328,10 @@
         apart *= 2
     totals = [total] + [swap(total, apart) for apart in range(1, SQUARE)]
     (nodal,) = call(
-        functools.partial(nodal_kernel, per_chunk, depth),
+        functools.partial(nodal_kernel, per_chunk),
         [(many, strips, TILE, LANES)],
-        (me, levels, *totals),
-        2,
+        (me, keep, *totals),
+        1,
     )
     return block_of(nodal)[None]
 

time: 47.1 us -> 41.9 us (0.89)
  Pallas kernels: 10.2 us -> 5.14 us
    pallas_call x6, Pallas kernels: 10.2 us -> 5.14 us  [call(): pl.pallas_call(kernel, out_shape=[jax.ShapeDtypeStruct(shape, jnp.float32...]
    unnamed x12 -> x6, local copies, waits for them, and re-layouts: 3.13 us -> 1.05 us
    squeeze x0 -> x2, local copies, waits for them, and re-layouts: none -> 1.95 us  [on_device(): ends = [x[at] for x in tiles for at in (0, many - 1)]]
  transfers between devices with their start and end apart: 9 -> 9, of which waited for: 7 -> 7; matrix products, arithmetic and copies ran while one was open for 0% -> 0% of each run, Pallas kernels for 10% -> 4%
where the time goes in v5:
time: 41.9 us; the launch traced here: 41.7 us
  waiting for transfers between devices  17.4 us (42%)
  starting transfers between devices  14.8 us (35%)
  Pallas kernels  5.14 us (12%)
  local copies, waits for them, and re-layouts  3 us (7%)
  between operations  1.41 us (3%)
    ppermute x7, waiting for transfers between devices, swap(): return lax.ppermute(array, 'grp', [(g, g ^ apart) for g in range(grids)])  17.4 us
    ppermute x7, starting transfers between devices, swap(): return lax.ppermute(array, 'grp', [(g, g ^ apart) for g in range(grids)])  9.75 us
    pallas_call x6, Pallas kernels, call(): pl.pallas_call(kernel, out_shape=[jax.ShapeDtypeStruct(shape, jnp.float32...  5.14 us
    ppermute x2, starting transfers between devices, on_device(): lax.ppermute(array, 'dom', pairs + [(b, a) for a, b in pairs])  5.06 us
    squeeze x2, local copies, waits for them, and re-layouts, on_device(): ends = [x[at] for x in tiles for at in (0, many - 1)]  1.95 us
    unnamed x6, local copies, waits for them, and re-layouts  1.05 us
  transfers between devices with their start and end apart: 9, of which 7 were waited for; matrix products, arithmetic and copies ran while one was open for 0% of the time, Pallas kernels for 4%

profile of v5, /device:TPU:0, one launch (start us, length us, event | category | flops | bytes accessed | tf_op | source)
XLA Modules:
  0.0 41.7 jit_solution(4820727810190118899)
XLA Ops:
  0.0 0.0 copy-start.1
  0.0 0.9 %slice_bitcast_fusion.4 = (f32[16,8,128]{2,1,0:T(8,128)S(1)}, f32[16,8,128]{2,1,0:T(8,128)S(1)}) fusion(f32[8,16,8,128]{3,2,1,0:T(8,128)} %bitcast.26), kind=kLoop, calls=%fused_computation.4 | loop fusion | bytes 262144 | tf_op jit(solution)/shard_map/squeeze | solution.py:286
  0.9 0.0 copy-start
  1.0 1.0 %slice_bitcast_fusion = (f32[16,8,128]{2,1,0:T(8,128)S(1)}, f32[16,8,128]{2,1,0:T(8,128)S(1)}, f32[16,8,128]{2,1,0:T(8,128)S(1)}, f32[16,8,128]{2,1,0:T(8,128)S(1)}) fusion(f32[8,16,8,128]{3,2,1,0:T(8,128)} %bitcast.30, f32[8,16,8,128]{3,2,1,0:T(8,128)} %bitcast.28), kind=kLoop, calls=%fused_computation | loop fusion | bytes 524288 | tf_op jit(solution)/shard_map/squeeze | solution.py:286
  2.0 0.7 %collective-permute-start = (f32[16,16,128]{2,1,0:T(8,128)S(1)}, f32[16,16,128]{2,1,0:T(8,128)S(1)}, u32[]{:S(2)}, u32[]{:S(2)}) collective-permute-start(f32[16,16,128]{2,1,0:T(8,128)S(1)} %get-tuple-element.17), channel_id=1, source_target_pairs={{1,2},{2,1},{5,6},{6,5},{9,10},{10,9},{13,14},{14,13},{17,18},{18,... | collective-permute-start | bytes 393224 | tf_op jit(solution)/shard_map/ppermute | solution.py:296
  2.7 4.4 %collective-permute-start.1 = (f32[16,16,128]{2,1,0:T(8,128)S(1)}, f32[16,16,128]{2,1,0:T(8,128)S(1)}, u32[]{:S(2)}, u32[]{:S(2)}) collective-permute-start(f32[16,16,128]{2,1,0:T(8,128)S(1)} %get-tuple-element.18), channel_id=1, source_target_pairs={{0,1},{2,3},{1,0},{3,2},{4,5},{6,7},{5,4},{7,6},{8,9},{10,11},{9,8... | collective-permute-start | bytes 393224 | tf_op jit(solution)/shard_map/ppermute | solution.py:296
  8.4 0.0 copy-done.1
  8.4 0.0 copy-done
  8.4 0.0 copy-start.2
  8.4 1.0 %copy-done.2 = f32[1,64,2048]{2,1,0:T(8,128)S(1)} copy-done((f32[1,64,2048]{2,1,0:T(8,128)S(1)}, f32[1,64,2048]{2,1,0:T(8,128)}, u32[]{:S(2)}) %copy-start.2) | copy-done | bytes 524312
  9.5 1.9 %shard_map.55 = (f32[16,8,8,128]{3,2,1,0:T(8,128)S(1)}, f32[3,8,128]{2,1,0:T(8,128)S(1)}, f32[4,8,128]{2,1,0:T(8,128)S(1)}) custom-call(s32[1]{0:T(128)S(6)} %copy.6.level_ref, s32[1]{0:T(128)S(6)} %copy.7.coef_ref, f32[8,16,8,128]{3,2,1,0:T(8,128)S(1)} %bitcast.27, f32[8,16,8,128]{3,2,1,0:T(8,128)S(1)} %bitcast.29, f32[8,16,8,128]{3,2,1,0:T(8,128)S(1)} %bitcast.31), custom_call_target="tpu_custom_call" | custom-call | flops 5242880 | bytes 1572872 | tf_op jit(solution)/shard_map/pallas_call | solution.py:262
  11.3 0.0 collective-permute-done.refs_7_
  11.3 0.0 collective-permute-done.1.refs_8_
  11.4 2.0 %shard_map.57 = (f32[33,8,128]{2,1,0:T(8,128)S(1)}, f32[33,8,128]{2,1,0:T(8,128)S(1)}, f32[33,8,128]{2,1,0:T(8,128)S(1)}, f32[33,8,128]{2,1,0:T(8,128)S(1)}) custom-call(s32[1]{0:T(128)} %bitcast.7.parity_ref, s32[1]{0:T(128)} %bitcast.me_ref, f32[4,8,128]{2,1,0:T(8,128)S(1)} %get-tuple-element.15.weight_ref, f32[16,8,128]{2,1,0:T(8,128)S(1)} %get-tuple-element.28.refs_0_, ...), custom_call_target="tpu_custom_call" | custom-call | flops 2621440 | bytes 1196040 | tf_op jit(solution)/shard_map/pallas_call | solution.py:262
  13.4 1.6 %collective-permute-start.2 = (f32[33,8,128]{2,1,0:T(8,128)S(1)}, f32[33,8,128]{2,1,0:T(8,128)S(1)}, u32[]{:S(2)}, u32[]{:S(2)}) collective-permute-start(f32[33,8,128]{2,1,0:T(8,128)S(1)} %get-tuple-element.20), channel_id=1, source_target_pairs={{0,4},{4,0},{8,12},{12,8},{16,20},{20,16},{24,28},{28,24},{1,5},{5... | collective-permute-start | bytes 405512 | tf_op jit(solution)/shard_map/ppermute | solution.py:321
  14.9 1.6 %collective-permute-start.3 = (f32[33,8,128]{2,1,0:T(8,128)S(1)}, f32[33,8,128]{2,1,0:T(8,128)S(1)}, u32[]{:S(2)}, u32[]{:S(2)}) collective-permute-start(f32[33,8,128]{2,1,0:T(8,128)S(1)} %get-tuple-element.21), channel_id=1, source_target_pairs={{0,8},{4,12},{8,0},{12,4},{16,24},{20,28},{24,16},{28,20},{1,9},{5... | collective-permute-start | bytes 405512 | tf_op jit(solution)/shard_map/ppermute | solution.py:321
  16.5 0.4 %collective-permute-start.4 = (f32[33,8,128]{2,1,0:T(8,128)S(1)}, f32[33,8,128]{2,1,0:T(8,128)S(1)}, u32[]{:S(2)}, u32[]{:S(2)}) collective-permute-start(f32[33,8,128]{2,1,0:T(8,128)S(1)} %get-tuple-element.22), channel_id=1, source_target_pairs={{0,12},{4,8},{8,4},{12,0},{16,28},{20,24},{24,20},{28,16},{1,13},{... | collective-permute-start | bytes 405512 | tf_op jit(solution)/shard_map/ppermute | solution.py:321
  16.9 2.0 %collective-permute-done.2.refs_1_ = f32[33,8,128]{2,1,0:T(8,128)S(1)} collective-permute-done((f32[33,8,128]{2,1,0:T(8,128)S(1)}, f32[33,8,128]{2,1,0:T(8,128)S(1)}, u32[]{:S(2)}, u32[]{:S(2)}) %collective-permute-start.2) | collective-permute-done | bytes 135200 | tf_op jit(solution)/shard_map/ppermute | solution.py:321
  19.0 2.5 %collective-permute-done.3.refs_2_ = f32[33,8,128]{2,1,0:T(8,128)S(1)} collective-permute-done((f32[33,8,128]{2,1,0:T(8,128)S(1)}, f32[33,8,128]{2,1,0:T(8,128)S(1)}, u32[]{:S(2)}, u32[]{:S(2)}) %collective-permute-start.3) | collective-permute-done | bytes 135200 | tf_op jit(solution)/shard_map/ppermute | solution.py:321
  21.4 1.6 %collective-permute-done.4.refs_3_ = f32[33,8,128]{2,1,0:T(8,128)S(1)} collective-permute-done((f32[33,8,128]{2,1,0:T(8,128)S(1)}, f32[33,8,128]{2,1,0:T(8,128)S(1)}, u32[]{:S(2)}, u32[]{:S(2)}) %collective-permute-start.4) | collective-permute-done | bytes 135200 | tf_op jit(solution)/shard_map/ppermute | solution.py:321
  23.0 0.1 shard_map.58.refs_0_
  23.1 2.6 %collective-permute-start.5 = (f32[33,8,128]{2,1,0:T(8,128)S(1)}, f32[33,8,128]{2,1,0:T(8,128)S(1)}, u32[]{:S(2)}, u32[]{:S(2)}) collective-permute-start(f32[33,8,128]{2,1,0:T(8,128)S(1)} %shard_map.58.refs_0_), channel_id=1, source_target_pairs={{0,16},{4,20},{8,24},{12,28},{16,0},{20,4},{24,8},{28,12},{1,17},{... | collective-permute-start | bytes 405512 | tf_op jit(solution)/shard_map/ppermute | solution.py:321
  25.7 5.9 %collective-permute-done.5.refs_1_ = f32[33,8,128]{2,1,0:T(8,128)S(1)} collective-permute-done((f32[33,8,128]{2,1,0:T(8,128)S(1)}, f32[33,8,128]{2,1,0:T(8,128)S(1)}, u32[]{:S(2)}, u32[]{:S(2)}) %collective-permute-start.5) | collective-permute-done | bytes 135200 | tf_op jit(solution)/shard_map/ppermute | solution.py:321
  31.7 1.2 %collective-permute-start.6 = (f32[33,8,128]{2,1,0:T(8,128)S(1)}, f32[33,8,128]{2,1,0:T(8,128)S(1)}, u32[]{:S(2)}, u32[]{:S(2)}) collective-permute-start(f32[33,8,128]{2,1,0:T(8,128)S(1)} %shard_map.59.refs_0_), channel_id=1, source_target_pairs={{0,4},{4,0},{8,12},{12,8},{16,20},{20,16},{24,28},{28,24},{1,5},{5... | collective-permute-start | bytes 405512 | tf_op jit(solution)/shard_map/ppermute | solution.py:321
  32.9 0.7 %collective-permute-start.7 = (f32[33,8,128]{2,1,0:T(8,128)S(1)}, f32[33,8,128]{2,1,0:T(8,128)S(1)}, u32[]{:S(2)}, u32[]{:S(2)}) collective-permute-start(f32[33,8,128]{2,1,0:T(8,128)S(1)} %shard_map.59.refs_0_), channel_id=1, source_target_pairs={{0,8},{4,12},{8,0},{12,4},{16,24},{20,28},{24,16},{28,20},{1,9},{5... | collective-permute-start | bytes 405512 | tf_op jit(solution)/shard_map/ppermute | solution.py:321
  33.5 1.7 %collective-permute-start.8 = (f32[33,8,128]{2,1,0:T(8,128)S(1)}, f32[33,8,128]{2,1,0:T(8,128)S(1)}, u32[]{:S(2)}, u32[]{:S(2)}) collective-permute-start(f32[33,8,128]{2,1,0:T(8,128)S(1)} %shard_map.59.refs_0_), channel_id=1, source_target_pairs={{0,12},{4,8},{8,4},{12,0},{16,28},{20,24},{24,20},{28,16},{1,13},{... | collective-permute-start | bytes 405512 | tf_op jit(solution)/shard_map/ppermute | solution.py:321
  35.2 2.6 %collective-permute-done.6.refs_1_ = f32[33,8,128]{2,1,0:T(8,128)S(1)} collective-permute-done((f32[33,8,128]{2,1,0:T(8,128)S(1)}, f32[33,8,128]{2,1,0:T(8,128)S(1)}, u32[]{:S(2)}, u32[]{:S(2)}) %collective-permute-start.6) | collective-permute-done | bytes 135200 | tf_op jit(solution)/shard_map/ppermute | solution.py:321
  37.8 0.3 collective-permute-done.7.refs_2_
  38.1 2.5 %collective-permute-done.8.refs_3_ = f32[33,8,128]{2,1,0:T(8,128)S(1)} collective-permute-done((f32[33,8,128]{2,1,0:T(8,128)S(1)}, f32[33,8,128]{2,1,0:T(8,128)S(1)}, u32[]{:S(2)}, u32[]{:S(2)}) %collective-permute-start.8) | collective-permute-done | bytes 135200 | tf_op jit(solution)/shard_map/ppermute | solution.py:321
  40.6 1.1 %shard_map.60 = f32[8,16,8,128]{3,2,1,0:T(8,128)} custom-call(s32[1]{0:T(128)} %bitcast.me_ref, f32[3,8,128]{2,1,0:T(8,128)S(1)} %get-tuple-element.14.keep_ref, f32[33,8,128]{2,1,0:T(8,128)S(1)} %shard_map.59.refs_0_, f32[33,8,128]{2,1,0:T(8,128)S(1)} %collective-permute-done.6.refs_1_, f32[33,8,128]{2,1,0:T(8,128)S(1)} %collective-permute-done.7.refs_2_, ...), custom_call_target="tpu_custom_call" | custom-call | bytes 552964 | tf_op jit(solution)/shard_map/pallas_call | solution.py:262
  (2 shorter events, 0.1 us)
Async XLA Ops:
  0.0 8.4 %copy-start.1 = (f32[1,64,2048]{2,1,0:T(8,128)S(1)}, f32[1,64,2048]{2,1,0:T(8,128)}, u32[]{:S(2)}) copy-start(f32[1,64,2048]{2,1,0:T(8,128)} %param.6) | copy-start | bytes 1572868
  0.9 7.5 %copy-start = (f32[1,64,2048]{2,1,0:T(8,128)S(1)}, f32[1,64,2048]{2,1,0:T(8,128)}, u32[]{:S(2)}) copy-start(f32[1,64,2048]{2,1,0:T(8,128)} %param.5) | copy-start | bytes 1572868
  2.0 9.3 %collective-permute-start = (f32[16,16,128]{2,1,0:T(8,128)S(1)}, f32[16,16,128]{2,1,0:T(8,128)S(1)}, u32[]{:S(2)}, u32[]{:S(2)}) collective-permute-start(f32[16,16,128]{2,1,0:T(8,128)S(1)} %get-tuple-element.17), channel_id=1, source_target_pairs={{1,2},{2,1},{5,6},{6,5},{9,10},{10,9},{13,14},{14,13},{17,18},{18,... | collective-permute-start | bytes 393224 | tf_op jit(solution)/shard_map/ppermute | solution.py:296
  2.7 8.6 %collective-permute-start.1 = (f32[16,16,128]{2,1,0:T(8,128)S(1)}, f32[16,16,128]{2,1,0:T(8,128)S(1)}, u32[]{:S(2)}, u32[]{:S(2)}) collective-permute-start(f32[16,16,128]{2,1,0:T(8,128)S(1)} %get-tuple-element.18), channel_id=1, source_target_pairs={{0,1},{2,3},{1,0},{3,2},{4,5},{6,7},{5,4},{7,6},{8,9},{10,11},{9,8... | collective-permute-start | bytes 393224 | tf_op jit(solution)/shard_map/ppermute | solution.py:296
  8.4 1.0 %copy-start.2 = (f32[1,64,2048]{2,1,0:T(8,128)S(1)}, f32[1,64,2048]{2,1,0:T(8,128)}, u32[]{:S(2)}) copy-start(f32[1,64,2048]{2,1,0:T(8,128)} %param.7) | copy-start | bytes 1572868
  13.4 5.6 %collective-permute-start.2 = (f32[33,8,128]{2,1,0:T(8,128)S(1)}, f32[33,8,128]{2,1,0:T(8,128)S(1)}, u32[]{:S(2)}, u32[]{:S(2)}) collective-permute-start(f32[33,8,128]{2,1,0:T(8,128)S(1)} %get-tuple-element.20), channel_id=1, source_target_pairs={{0,4},{4,0},{8,12},{12,8},{16,20},{20,16},{24,28},{28,24},{1,5},{5... | collective-permute-start | bytes 405512 | tf_op jit(solution)/shard_map/ppermute | solution.py:321
  14.9 6.5 %collective-permute-start.3 = (f32[33,8,128]{2,1,0:T(8,128)S(1)}, f32[33,8,128]{2,1,0:T(8,128)S(1)}, u32[]{:S(2)}, u32[]{:S(2)}) collective-permute-start(f32[33,8,128]{2,1,0:T(8,128)S(1)} %get-tuple-element.21), channel_id=1, source_target_pairs={{0,8},{4,12},{8,0},{12,4},{16,24},{20,28},{24,16},{28,20},{1,9},{5... | collective-permute-start | bytes 405512 | tf_op jit(solution)/shard_map/ppermute | solution.py:321
  16.5 6.5 %collective-permute-start.4 = (f32[33,8,128]{2,1,0:T(8,128)S(1)}, f32[33,8,128]{2,1,0:T(8,128)S(1)}, u32[]{:S(2)}, u32[]{:S(2)}) collective-permute-start(f32[33,8,128]{2,1,0:T(8,128)S(1)} %get-tuple-element.22), channel_id=1, source_target_pairs={{0,12},{4,8},{8,4},{12,0},{16,28},{20,24},{24,20},{28,16},{1,13},{... | collective-permute-start | bytes 405512 | tf_op jit(solution)/shard_map/ppermute | solution.py:321
  23.1 8.5 %collective-permute-start.5 = (f32[33,8,128]{2,1,0:T(8,128)S(1)}, f32[33,8,128]{2,1,0:T(8,128)S(1)}, u32[]{:S(2)}, u32[]{:S(2)}) collective-permute-start(f32[33,8,128]{2,1,0:T(8,128)S(1)} %shard_map.58.refs_0_), channel_id=1, source_target_pairs={{0,16},{4,20},{8,24},{12,28},{16,0},{20,4},{24,8},{28,12},{1,17},{... | collective-permute-start | bytes 405512 | tf_op jit(solution)/shard_map/ppermute | solution.py:321
  31.7 6.1 %collective-permute-start.6 = (f32[33,8,128]{2,1,0:T(8,128)S(1)}, f32[33,8,128]{2,1,0:T(8,128)S(1)}, u32[]{:S(2)}, u32[]{:S(2)}) collective-permute-start(f32[33,8,128]{2,1,0:T(8,128)S(1)} %shard_map.59.refs_0_), channel_id=1, source_target_pairs={{0,4},{4,0},{8,12},{12,8},{16,20},{20,16},{24,28},{28,24},{1,5},{5... | collective-permute-start | bytes 405512 | tf_op jit(solution)/shard_map/ppermute | solution.py:321
  32.9 5.2 %collective-permute-start.7 = (f32[33,8,128]{2,1,0:T(8,128)S(1)}, f32[33,8,128]{2,1,0:T(8,128)S(1)}, u32[]{:S(2)}, u32[]{:S(2)}) collective-permute-start(f32[33,8,128]{2,1,0:T(8,128)S(1)} %shard_map.59.refs_0_), channel_id=1, source_target_pairs={{0,8},{4,12},{8,0},{12,4},{16,24},{20,28},{24,16},{28,20},{1,9},{5... | collective-permute-start | bytes 405512 | tf_op jit(solution)/shard_map/ppermute | solution.py:321
  33.5 7.1 %collective-permute-start.8 = (f32[33,8,128]{2,1,0:T(8,128)S(1)}, f32[33,8,128]{2,1,0:T(8,128)S(1)}, u32[]{:S(2)}, u32[]{:S(2)}) collective-permute-start(f32[33,8,128]{2,1,0:T(8,128)S(1)} %shard_map.59.refs_0_), channel_id=1, source_target_pairs={{0,12},{4,8},{8,4},{12,0},{16,28},{20,24},{24,20},{28,16},{1,13},{... | collective-permute-start | bytes 405512 | tf_op jit(solution)/shard_map/ppermute | solution.py:321

commit v6 on v5

v6 whole, which is shorter than its diff:
```python
import functools

import jax
import jax.numpy as jnp
from jax import lax
from jax.experimental import pallas as pl
from jax.experimental.pallas import tpu as pltpu
from jax.sharding import PartitionSpec as P

STEPS = 4
LANES = 128
TILE = 8
HALF = TILE // 2
SLAB = 4 * TILE
SQUARE = 4
UNROLL = 16
VMEM_LIMIT = 40 * 1024 * 1024


def tiles_of(block):
    rows, cols = block.shape
    return block.reshape(rows // TILE, TILE, cols // LANES, LANES).transpose(0, 2, 1, 3)


def block_of(tiles):
    many, strips = tiles.shape[:2]
    return tiles.transpose(0, 2, 1, 3).reshape(many * TILE, strips * LANES)


def flat(ref):
    return ref.reshape(ref.size // LANES, LANES)


def spaced(first, count, stride):
    return pl.ds(first, count, stride=stride) if count > 1 else pl.ds(first, 1)


def roll_rows(value, shift):
    count = value.shape[0]
    return pltpu.roll(value, shift % count, 0) if count > 1 else value


def per_strip(strips, body, unroll):
    def step(j, carry):
        body(j)
        return carry

    lax.fori_loop(0, strips, step, 0, unroll=unroll)


def advance(first, count, classes, source, coefs, emit):
    shape = source.shape[2:]
    lanes = lax.broadcasted_iota(jnp.int32, shape, 1)
    center, above_c, below_c, side = coefs

    def body(k, carry):
        j = first + k
        cur, right_prev, left_cur = carry
        nxt = [source[j + 2, t] for t in range(classes)]
        left_next = [pltpu.roll(x, LANES - 1, 1) for x in nxt]
        right_cur = [pltpu.roll(x, 1, 1) for x in cur]
        above = cur[1:] + [roll_rows(cur[0], -1)]
        below = [roll_rows(cur[-1], 1)] + cur[:-1]
        new = []
        for t in range(classes):
            left = jnp.where(lanes == 0, right_prev[t], right_cur[t])
            right = jnp.where(lanes == LANES - 1, left_next[t], left_cur[t])
            new.append(
                center[j, t] * cur[t]
                + above_c[j, t] * above[t]
                + below_c[j, t] * below[t]
                + side[j, t] * (left + right)
            )
        emit(j, k, new)
        return nxt, right_cur, left_next

    prev, cur = ([source[first + at, t] for t in range(classes)] for at in range(2))
    ends = [pltpu.roll(x, 1, 1) for x in prev], [pltpu.roll(x, LANES - 1, 1) for x in cur]
    lax.fori_loop(0, count, body, (cur, *ends), unroll=min(count, UNROLL))


def run_steps(strips, per_chunk, me, classes, load, buffers, coefs, finish):
    center, above_c, below_c, side = coefs
    for buf in buffers:
        for edge in (0, strips + 1):
            buf[edge] = jnp.zeros(buf.shape[1:], jnp.float32)

    def begin(j):
        for t in range(classes):
            state, diffuse, drifts = load(j, t)
            half = 0.5 * drifts
            buffers[0][j + 1, t] = state
            center[j, t] = 1.0 - 4.0 * diffuse
            above_c[j, t] = diffuse - half
            below_c[j, t] = diffuse + half
            side[j, t] = diffuse

    per_strip(strips, begin, min(strips, UNROLL))
    for step in range(STEPS - 1):
        source, target = buffers[step % 2], buffers[1 - step % 2]

        def keep(j, _, new, target=target):
            for t in range(classes):
                target[j + 1, t] = new[t]

        advance(0, strips, classes, source, coefs, keep)
    source = buffers[(STEPS - 1) % 2]
    for away in range(SQUARE):
        emit = functools.partial(finish, away)
        advance((me ^ away) * per_chunk, per_chunk, classes, source, coefs, emit)


def surpluses(s, prev, weight_ref):
    fine, mid, low, coef = (weight_ref[k] for k in range(4))
    return (
        fine * (s[0] - 0.5 * (prev + s[1])),
        mid * (s[1] - 0.5 * (prev + s[3])),
        fine * (s[2] - 0.5 * (s[1] + s[3])),
        low * (s[3] - 0.5 * (prev + s[7])),
        fine * (s[4] - 0.5 * (s[3] + s[5])),
        mid * (s[5] - 0.5 * (s[3] + s[7])),
        fine * (s[6] - 0.5 * (s[5] + s[7])),
        coef * s[7],
    )


def pack(odd, refs, far_ref, near_ref):
    many, strips = refs[0].shape[:2]
    upper = lax.broadcasted_iota(jnp.int32, (TILE, LANES), 0) < HALF

    def body(j):
        heads, tails = ([ref[at, j] for ref in refs] for at in (0, many - 1))
        mix_next = jnp.where(upper, pltpu.roll(tails[2], HALF, 0), tails[1])
        mix_prev = jnp.where(upper, heads[1], pltpu.roll(heads[2], HALF, 0))
        to_next, to_prev = (tails[0], mix_next), (heads[0], mix_prev)
        for k in range(2):
            at = pl.ds(k * TILE, TILE)
            far_ref[j, at] = jnp.where(odd, to_next[k], to_prev[k])
            near_ref[j, at] = jnp.where(odd, to_prev[k], to_next[k])

    per_strip(strips, body, 4)


def inner_kernel(
    per_chunk, depth, parity_ref, me_ref, level_ref, coef_ref, dens_ref, diff_ref, drift_ref,
    far_ref, near_ref, state_ref, keep_ref, weight_ref, *refs
):
    many, strips = dens_ref.shape[:2]
    *out_refs, scratch, state_a, state_b = refs[:-4]
    fields = (dens_ref, diff_ref, drift_ref)
    pack(parity_ref[0] == 1, fields, far_ref, near_ref)
    coef = coef_ref[0].astype(jnp.float32)
    for down in range(3):
        keep = jnp.where(level_ref[0] >= depth - down, 1.0, 0.0)
        keep_ref[down] = jnp.full((many, LANES), keep)
        weight_ref[down] = jnp.full((many, LANES), keep * coef)
    weight_ref[3] = jnp.full((many, LANES), coef)
    rows = [flat(ref) for ref in fields]
    by_row = flat(scratch)
    inside = many - 2

    def load(j, t):
        at = spaced(j * TILE + t, many, strips * TILE)
        return [ref[at, :] for ref in rows]

    def finish(away, j, part, new):
        for t in range(TILE):
            state_ref[j, t] = new[t]
        if inside <= 0:
            return
        weighted = surpluses(new, roll_rows(new[7], 1), weight_ref)
        for t in range(TILE):
            by_row[spaced(j * many * TILE + t, many, TILE), :] = weighted[t]
        for m in range(inside):
            out_refs[away][part * inside + m] = scratch[j, 1 + m]

    run_steps(strips, per_chunk, me_ref[0], TILE, load, (state_a, state_b), refs[-4:], finish)


def edge_kernel(
    per_chunk, parity_ref, me_ref, dens_ref, diff_ref, drift_ref, state_ref, weight_ref, far_ref,
    near_ref, *refs
):
    many, strips = dens_ref.shape[:2]
    odd = parity_ref[0] == 1
    *out_refs, scratch, slab, state_a, state_b = refs[:-4]

    def stage(j):
        far, near = far_ref[j], near_ref[j]
        up, dn = jnp.where(odd, near, far), jnp.where(odd, far, near)
        up_mix, dn_mix = up[TILE:], dn[TILE:]
        tiles = (
            (up[:TILE], dens_ref, dn[:TILE]),
            (up_mix, diff_ref, dn_mix),
            (pltpu.roll(up_mix, HALF, 0), drift_ref, pltpu.roll(dn_mix, HALF, 0)),
        )
        for k, (before, ref, after) in enumerate(tiles):
            for e, tile in enumerate((before, ref[0, j], ref[many - 1, j], after)):
                slab[k, j, e * TILE : (e + 1) * TILE] = tile

    per_strip(strips, stage, 4)
    slabs = flat(slab)

    def load(j, t):
        return [
            slabs[pl.ds((k * strips + j) * SLAB + t, TILE, stride=HALF), :] for k in range(3)
        ]

    place = lax.broadcasted_iota(jnp.int32, (many, LANES), 0)
    by_row = flat(scratch)
    edges = sorted({0, many - 1})

    def finish(away, j, part, new):
        s = [state_ref[j, t] for t in range(TILE)]
        for t in range(HALF):
            s[t] = jnp.where(place == 0, new[t][2:3], s[t])
            s[HALF + t] = jnp.where(place == many - 1, new[t][5:6], s[HALF + t])
        before = new[HALF - 1][1:2]
        weighted = surpluses(s, jnp.where(place == 0, before, roll_rows(s[7], 1)), weight_ref)
        for t in range(TILE):
            by_row[spaced(j * many * TILE + t, many, TILE), :] = weighted[t]
        for e, m in enumerate(edges):
            out_refs[away][part * len(edges) + e] = scratch[j, m]
        last = per_chunk * len(edges) + part // TILE
        out_refs[away][last, pl.ds(lax.rem(part, TILE), 1), :] = weight_ref[3][0:1] * before

    run_steps(strips, per_chunk, me_ref[0], HALF, load, (state_a, state_b), refs[-4:], finish)


def sum_kernel(*refs):
    *parts, out_ref = refs
    total = parts[0][...]
    for part in parts[1:]:
        total = total + part[...]
    out_ref[...] = total


def nodal_kernel(per_chunk, me_ref, keep_ref, *refs):
    *totals, out_ref, scratch = refs
    many, strips = out_ref.shape[:2]
    out, by_row = flat(out_ref), flat(scratch)
    fine, mid, low = (keep_ref[k] for k in range(3))
    place = lax.broadcasted_iota(jnp.int32, (many, LANES), 0)
    edges, inside = sorted({0, many - 1}), many - 2
    for away in range(SQUARE):
        first = (me_ref[0] ^ away) * per_chunk
        outer_ref = totals[away]
        inner_ref = totals[SQUARE + away] if inside > 0 else None

        def body(part, outer_ref=outer_ref, inner_ref=inner_ref, first=first):
            j = first + part
            for e, m in enumerate(edges):
                scratch[j, m] = outer_ref[part * len(edges) + e]
            for m in range(inside):
                scratch[j, 1 + m] = inner_ref[part * inside + m]
            w = [by_row[spaced(j * many * TILE + t, many, TILE), :] for t in range(TILE)]
            last = per_chunk * len(edges) + part // TILE
            before = outer_ref[last, pl.ds(lax.rem(part, TILE), 1), :]
            prev = jnp.where(place == 0, before, roll_rows(w[7], 1))
            v3 = 0.5 * (prev + w[7]) + low * w[3]
            v1 = 0.5 * (prev + v3) + mid * w[1]
            v5 = 0.5 * (v3 + w[7]) + mid * w[5]
            values = (
                0.5 * (prev + v1) + fine * w[0],
                v1,
                0.5 * (v1 + v3) + fine * w[2],
                v3,
                0.5 * (v3 + v5) + fine * w[4],
                v5,
                0.5 * (v5 + w[7]) + fine * w[6],
                w[7],
            )
            for t in range(TILE):
                out[spaced(j * TILE + t, many, strips * TILE), :] = values[t]

        per_strip(per_chunk, body, min(per_chunk, 4))


def call(kernel, out_shapes, operands, in_smem=0, scratch=(), flops=0):
    spaces = [pltpu.SMEM] * in_smem + [pltpu.VMEM] * (len(operands) - in_smem)
    specs = [pl.BlockSpec(memory_space=space) for space in spaces]
    moved = 4 * sum(x.size for x in operands)
    return pl.pallas_call(
        kernel,
        out_shape=[jax.ShapeDtypeStruct(shape, jnp.float32) for shape in out_shapes],
        in_specs=specs,
        out_specs=[pl.BlockSpec(memory_space=pltpu.VMEM) for _ in out_shapes],
        scratch_shapes=list(scratch),
        compiler_params=pltpu.CompilerParams(vmem_limit_bytes=VMEM_LIMIT),
        cost_estimate=pl.CostEstimate(flops=flops, bytes_accessed=moved, transcendentals=0),
    )(*operands)


def on_device(density, diffusion, drift_speed, levels, coefficient):
    rows, cols = density.shape[1:]
    doms, grids = lax.axis_size("dom"), lax.axis_size("grp")
    many, strips = rows // TILE, cols // LANES
    per_chunk = strips // SQUARE
    depth = (rows * doms).bit_length() - 1
    tiles = [tiles_of(x[0]) for x in (density, diffusion, drift_speed)]
    me = (lax.axis_index("grp") % SQUARE).astype(jnp.int32)[None]
    parity = (lax.axis_index("dom") % 2).astype(jnp.int32)[None]

    def vmem(*shape):
        return pltpu.VMEM(shape, jnp.float32)

    place = (strips, TILE, many, LANES)
    pieces = (strips, many, TILE, LANES)
    far, near, state, keep, weight, *inside = call(
        functools.partial(inner_kernel, per_chunk, depth),
        [(strips, 2 * TILE, LANES)] * 2
        + [place, (3, many, LANES), (4, many, LANES)]
        + [(per_chunk * (many - 2), TILE, LANES)] * (SQUARE if many > 2 else 0),
        (parity, me, levels, coefficient, *tiles),
        4,
        [vmem(*pieces)] + [vmem(strips + 2, *place[1:])] * 2 + [vmem(*place)] * 4,
        flops=40 * rows * cols,
    )
    far_pairs = [(d, d + 1) for d in range(1, doms - 1, 2)]
    near_pairs = [(d, d + 1) for d in range(0, doms, 2)]
    far, near = (
        lax.ppermute(array, "dom", pairs + [(b, a) for a, b in pairs])
        for array, pairs in ((far, far_pairs), (near, near_pairs))
    )
    outside = call(
        functools.partial(edge_kernel, per_chunk),
        [(per_chunk * min(many, 2) + -(-per_chunk // TILE), TILE, LANES)] * SQUARE,
        (parity, me, *tiles, state, weight, far, near),
        2,
        [vmem(*pieces), vmem(3, strips, SLAB, LANES)]
        + [vmem(strips + 2, HALF, TILE, LANES)] * 2
        + [vmem(strips, HALF, TILE, LANES)] * 4,
        flops=40 * SLAB * cols,
    )

    def swap(array, apart):
        return lax.ppermute(array, "grp", [(g, g ^ apart) for g in range(grids)])

    def over_grids(own, *others):
        theirs = [swap(array, apart) for apart, array in enumerate(others, 1)]
        (total,) = call(sum_kernel, [own.shape], (own, *theirs))
        apart = SQUARE
        while apart < grids:
            (total,) = call(sum_kernel, [own.shape], (total, swap(total, apart)))
            apart *= 2
        return [total] + [swap(total, apart) for apart in range(1, SQUARE)]

    totals = over_grids(*outside) + (over_grids(*inside) if inside else [])
    (nodal,) = call(
        functools.partial(nodal_kernel, per_chunk),
        [(many, strips, TILE, LANES)],
        (me, keep, *totals),
        1,
        [vmem(*pieces)],
    )
    return block_of(nodal)[None]


def solution(mesh):
    return jax.shard_map(
        on_device,
        mesh=mesh,
        in_specs=(
            P("grp", "dom", None),
            P("grp", "dom", None),
            P("grp", "dom", None),
            P("grp"),
            P("grp"),
        ),
        out_specs=P("grp", "dom", None),
        check_vma=False,
    )
```

time: 41.9 us -> 43.1 us (1.029)
  starting transfers between devices: 14.8 us -> 21.1 us
  waiting for transfers between devices: 17.4 us -> 12.9 us
  Pallas kernels: 5.14 us -> 4.32 us
    ppermute x7 -> x14, starting transfers between devices: 9.75 us -> 17.1 us  [swap(): return lax.ppermute(array, 'grp', [(g, g ^ apart) for g in range(grids)])]
    ppermute x7 -> x14, waiting for transfers between devices: 17.4 us -> 12.9 us  [swap(): return lax.ppermute(array, 'grp', [(g, g ^ apart) for g in range(grids)])]
    unnamed x6 -> x8, local copies, waits for them, and re-layouts: 1.05 us -> 3.12 us
    squeeze x2 -> x0, local copies, waits for them, and re-layouts: 1.95 us -> none  [on_device(): ends = [x[at] for x in tiles for at in (0, many - 1)]]
    ppermute x2, starting transfers between devices: 5.06 us -> 4.01 us  [on_device(): lax.ppermute(array, 'dom', pairs + [(b, a) for a, b in pairs])]
    pallas_call x6 -> x7, Pallas kernels: 5.14 us -> 4.32 us  [call(): pl.pallas_call(kernel, out_shape=[jax.ShapeDtypeStruct(shape, jnp.float32...]
  transfers between devices with their start and end apart: 9 -> 16, of which waited for: 7 -> 7; matrix products, arithmetic and copies ran while one was open for 0% -> 0% of each run, Pallas kernels for 4% -> 2%
where the time goes in v6:
time: 43.1 us; the launch traced here: 42.9 us
  starting transfers between devices  21.1 us (49%)
  waiting for transfers between devices  12.9 us (30%)
  Pallas kernels  4.32 us (10%)
  local copies, waits for them, and re-layouts  3.12 us (7%)
  between operations  1.36 us (3%)
    ppermute x14, starting transfers between devices, swap(): return lax.ppermute(array, 'grp', [(g, g ^ apart) for g in range(grids)])  17.1 us
    ppermute x14, waiting for transfers between devices, swap(): return lax.ppermute(array, 'grp', [(g, g ^ apart) for g in range(grids)])  12.9 us
    pallas_call x7, Pallas kernels, call(): pl.pallas_call(kernel, out_shape=[jax.ShapeDtypeStruct(shape, jnp.float32...  4.32 us
    ppermute x2, starting transfers between devices, on_device(): lax.ppermute(array, 'dom', pairs + [(b, a) for a, b in pairs])  4.01 us
    unnamed x8, local copies, waits for them, and re-layouts  3.12 us
  transfers between devices with their start and end apart: 16, of which 7 were waited for; matrix products, arithmetic and copies ran while one was open for 0% of the time, Pallas kernels for 2%

profile of v6, /device:TPU:0, one launch (start us, length us, event | category | flops | bytes accessed | tf_op | source)
XLA Modules:
  0.0 42.9 jit_solution(8412958357876819547)
XLA Ops:
  1.3 0.0 copy-start
  1.3 1.0 %copy-done = f32[1,64,2048]{2,1,0:T(8,128)S(1)} copy-done((f32[1,64,2048]{2,1,0:T(8,128)S(1)}, f32[1,64,2048]{2,1,0:T(8,128)}, u32[]{:S(2)}) %copy-start) | copy-done | bytes 524312
  2.3 0.0 copy-start.2
  2.4 1.0 %copy-done.2 = f32[1,64,2048]{2,1,0:T(8,128)S(1)} copy-done((f32[1,64,2048]{2,1,0:T(8,128)S(1)}, f32[1,64,2048]{2,1,0:T(8,128)}, u32[]{:S(2)}) %copy-start.2) | copy-done | bytes 524312
  3.4 0.0 copy-start.3
  3.4 1.0 %copy-done.3 = f32[1,64,2048]{2,1,0:T(8,128)S(1)} copy-done((f32[1,64,2048]{2,1,0:T(8,128)S(1)}, f32[1,64,2048]{2,1,0:T(8,128)}, u32[]{:S(2)}) %copy-start.3) | copy-done | bytes 524312
  4.4 0.0 copy-start.1
  4.4 2.1 %shard_map.55 = (f32[16,16,128]{2,1,0:T(8,128)S(1)}, f32[16,16,128]{2,1,0:T(8,128)S(1)}, f32[16,8,8,128]{3,2,1,0:T(8,128)S(1)}, f32[3,8,128]{2,1,0:T(8,128)S(1)}...) custom-call(s32[1]{0:T(128)} %bitcast.1.parity_ref, ...), custom_call_target="tpu_custom_call" | custom-call | flops 5242880 | bytes 1572880 | tf_op jit(solution)/shard_map/pallas_call | solution.py:283
  6.6 3.0 %collective-permute-start.9 = (f32[24,8,128]{2,1,0:T(8,128)S(1)}, f32[24,8,128]{2,1,0:T(8,128)S(1)}, u32[]{:S(2)}, u32[]{:S(2)}) collective-permute-start(f32[24,8,128]{2,1,0:T(8,128)S(1)} %get-tuple-element.28), channel_id=1, source_target_pairs={{0,4},{4,0},{8,12},{12,8},{16,20},{20,16},{24,28},{28,24},{1,5},{5... | collective-permute-start | bytes 294920 | tf_op jit(solution)/shard_map/ppermute | solution.py:337
  9.6 1.6 %collective-permute-start.10 = (f32[24,8,128]{2,1,0:T(8,128)S(1)}, f32[24,8,128]{2,1,0:T(8,128)S(1)}, u32[]{:S(2)}, u32[]{:S(2)}) collective-permute-start(f32[24,8,128]{2,1,0:T(8,128)S(1)} %get-tuple-element.29), channel_id=1, source_target_pairs={{0,8},{4,12},{8,0},{12,4},{16,24},{20,28},{24,16},{28,20},{1,9},{5... | collective-permute-start | bytes 294920 | tf_op jit(solution)/shard_map/ppermute | solution.py:337
  11.1 0.0 collective-permute-start.11
  11.1 0.7 %collective-permute-start = (f32[16,16,128]{2,1,0:T(8,128)S(1)}, f32[16,16,128]{2,1,0:T(8,128)S(1)}, u32[]{:S(2)}, u32[]{:S(2)}) collective-permute-start(f32[16,16,128]{2,1,0:T(8,128)S(1)} %get-tuple-element.21), channel_id=1, source_target_pairs={{1,2},{2,1},{5,6},{6,5},{9,10},{10,9},{13,14},{14,13},{17,18},{18,... | collective-permute-start | bytes 393224 | tf_op jit(solution)/shard_map/ppermute | solution.py:322
  11.8 3.4 %collective-permute-start.1 = (f32[16,16,128]{2,1,0:T(8,128)S(1)}, f32[16,16,128]{2,1,0:T(8,128)S(1)}, u32[]{:S(2)}, u32[]{:S(2)}) collective-permute-start(f32[16,16,128]{2,1,0:T(8,128)S(1)} %get-tuple-element.22), channel_id=1, source_target_pairs={{0,1},{2,3},{1,0},{3,2},{4,5},{6,7},{5,4},{7,6},{8,9},{10,11},{9,8... | collective-permute-start | bytes 393224 | tf_op jit(solution)/shard_map/ppermute | solution.py:322
  15.2 0.0 collective-permute-done.9.refs_1_
  15.2 0.0 collective-permute-done.10.refs_2_
  15.2 1.5 %collective-permute-done.11.refs_3_ = f32[24,8,128]{2,1,0:T(8,128)S(1)} collective-permute-done((f32[24,8,128]{2,1,0:T(8,128)S(1)}, f32[24,8,128]{2,1,0:T(8,128)S(1)}, u32[]{:S(2)}, u32[]{:S(2)}) %collective-permute-start.11) | collective-permute-done | bytes 98336 | tf_op jit(solution)/shard_map/ppermute | solution.py:337
  16.7 2.7 %collective-permute-start.12 = (f32[24,8,128]{2,1,0:T(8,128)S(1)}, f32[24,8,128]{2,1,0:T(8,128)S(1)}, u32[]{:S(2)}, u32[]{:S(2)}) collective-permute-start(f32[24,8,128]{2,1,0:T(8,128)S(1)} %shard_map.59.refs_0_), channel_id=1, source_target_pairs={{0,16},{4,20},{8,24},{12,28},{16,0},{20,4},{24,8},{28,12},{1,17},{... | collective-permute-start | bytes 294920 | tf_op jit(solution)/shard_map/ppermute | solution.py:337
  19.3 0.0 collective-permute-done.far_ref
  19.3 0.0 collective-permute-done.1.near_ref
  19.3 0.0 copy-done.1
  19.4 0.9 %shard_map.56 = (f32[9,8,128]{2,1,0:T(8,128)S(1)}, f32[9,8,128]{2,1,0:T(8,128)S(1)}, f32[9,8,128]{2,1,0:T(8,128)S(1)}, f32[9,8,128]{2,1,0:T(8,128)S(1)}) custom-call(s32[1]{0:T(128)} %bitcast.1.parity_ref, s32[1]{0:T(128)} %bitcast.me_ref, f32[8,16,8,128]{3,2,1,0:T(8,128)S(1)} %bitcast.15, f32[8,16,8,128]{3,2,1,0:T(8,128)S(1)} %bitcast.17, ...), custom_call_target="tpu_custom_call" | custom-call | flops 2621440 | bytes 2375688 | tf_op jit(solution)/shard_map/pallas_call | solution.py:283
  20.3 1.0 %collective-permute-start.2 = (f32[9,8,128]{2,1,0:T(8,128)S(1)}, f32[9,8,128]{2,1,0:T(8,128)S(1)}, u32[]{:S(2)}, u32[]{:S(2)}) collective-permute-start(f32[9,8,128]{2,1,0:T(8,128)S(1)} %get-tuple-element.24), channel_id=1, source_target_pairs={{0,4},{4,0},{8,12},{12,8},{16,20},{20,16},{24,28},{28,24},{1,5},{5... | collective-permute-start | bytes 110600 | tf_op jit(solution)/shard_map/ppermute | solution.py:337
  21.3 1.4 %collective-permute-start.3 = (f32[9,8,128]{2,1,0:T(8,128)S(1)}, f32[9,8,128]{2,1,0:T(8,128)S(1)}, u32[]{:S(2)}, u32[]{:S(2)}) collective-permute-start(f32[9,8,128]{2,1,0:T(8,128)S(1)} %get-tuple-element.25), channel_id=1, source_target_pairs={{0,8},{4,12},{8,0},{12,4},{16,24},{20,28},{24,16},{28,20},{1,9},{5... | collective-permute-start | bytes 110600 | tf_op jit(solution)/shard_map/ppermute | solution.py:337
  22.7 1.2 %collective-permute-start.4 = (f32[9,8,128]{2,1,0:T(8,128)S(1)}, f32[9,8,128]{2,1,0:T(8,128)S(1)}, u32[]{:S(2)}, u32[]{:S(2)}) collective-permute-start(f32[9,8,128]{2,1,0:T(8,128)S(1)} %get-tuple-element.26), channel_id=1, source_target_pairs={{0,12},{4,8},{8,4},{12,0},{16,28},{20,24},{24,20},{28,16},{1,13},{... | collective-permute-start | bytes 110600 | tf_op jit(solution)/shard_map/ppermute | solution.py:337
  23.8 0.5 %collective-permute-done.2.refs_1_ = f32[9,8,128]{2,1,0:T(8,128)S(1)} collective-permute-done((f32[9,8,128]{2,1,0:T(8,128)S(1)}, f32[9,8,128]{2,1,0:T(8,128)S(1)}, u32[]{:S(2)}, u32[]{:S(2)}) %collective-permute-start.2) | collective-permute-done | bytes 36896 | tf_op jit(solution)/shard_map/ppermute | solution.py:337
  24.3 0.9 %collective-permute-done.3.refs_2_ = f32[9,8,128]{2,1,0:T(8,128)S(1)} collective-permute-done((f32[9,8,128]{2,1,0:T(8,128)S(1)}, f32[9,8,128]{2,1,0:T(8,128)S(1)}, u32[]{:S(2)}, u32[]{:S(2)}) %collective-permute-start.3) | collective-permute-done | bytes 36896 | tf_op jit(solution)/shard_map/ppermute | solution.py:337
  25.3 2.3 %collective-permute-done.4.refs_3_ = f32[9,8,128]{2,1,0:T(8,128)S(1)} collective-permute-done((f32[9,8,128]{2,1,0:T(8,128)S(1)}, f32[9,8,128]{2,1,0:T(8,128)S(1)}, u32[]{:S(2)}, u32[]{:S(2)}) %collective-permute-start.4) | collective-permute-done | bytes 36896 | tf_op jit(solution)/shard_map/ppermute | solution.py:337
  27.5 0.7 %collective-permute-start.5 = (f32[9,8,128]{2,1,0:T(8,128)S(1)}, f32[9,8,128]{2,1,0:T(8,128)S(1)}, u32[]{:S(2)}, u32[]{:S(2)}) collective-permute-start(f32[9,8,128]{2,1,0:T(8,128)S(1)} %shard_map.57.refs_0_), channel_id=1, source_target_pairs={{0,16},{4,20},{8,24},{12,28},{16,0},{20,4},{24,8},{28,12},{1,17},{... | collective-permute-start | bytes 110600 | tf_op jit(solution)/shard_map/ppermute | solution.py:337
  28.2 0.0 collective-permute-done.12.refs_1_
  28.2 1.5 %collective-permute-start.15 = (f32[24,8,128]{2,1,0:T(8,128)S(1)}, f32[24,8,128]{2,1,0:T(8,128)S(1)}, u32[]{:S(2)}, u32[]{:S(2)}) collective-permute-start(f32[24,8,128]{2,1,0:T(8,128)S(1)} %shard_map.60.refs_4_), channel_id=1, source_target_pairs={{0,12},{4,8},{8,4},{12,0},{16,28},{20,24},{24,20},{28,16},{1,13},{... | collective-permute-start | bytes 294920 | tf_op jit(solution)/shard_map/ppermute | solution.py:337
  29.7 0.6 %collective-permute-start.14 = (f32[24,8,128]{2,1,0:T(8,128)S(1)}, f32[24,8,128]{2,1,0:T(8,128)S(1)}, u32[]{:S(2)}, u32[]{:S(2)}) collective-permute-start(f32[24,8,128]{2,1,0:T(8,128)S(1)} %shard_map.60.refs_4_), channel_id=1, source_target_pairs={{0,8},{4,12},{8,0},{12,4},{16,24},{20,28},{24,16},{28,20},{1,9},{5... | collective-permute-start | bytes 294920 | tf_op jit(solution)/shard_map/ppermute | solution.py:337
  30.3 1.5 %collective-permute-start.13 = (f32[24,8,128]{2,1,0:T(8,128)S(1)}, f32[24,8,128]{2,1,0:T(8,128)S(1)}, u32[]{:S(2)}, u32[]{:S(2)}) collective-permute-start(f32[24,8,128]{2,1,0:T(8,128)S(1)} %shard_map.60.refs_4_), channel_id=1, source_target_pairs={{0,4},{4,0},{8,12},{12,8},{16,20},{20,16},{24,28},{28,24},{1,5},{5... | collective-permute-start | bytes 294920 | tf_op jit(solution)/shard_map/ppermute | solution.py:337
  31.8 1.0 %collective-permute-done.5.refs_1_ = f32[9,8,128]{2,1,0:T(8,128)S(1)} collective-permute-done((f32[9,8,128]{2,1,0:T(8,128)S(1)}, f32[9,8,128]{2,1,0:T(8,128)S(1)}, u32[]{:S(2)}, u32[]{:S(2)}) %collective-permute-start.5) | collective-permute-done | bytes 36896 | tf_op jit(solution)/shard_map/ppermute | solution.py:337
  32.8 1.3 %collective-permute-start.8 = (f32[9,8,128]{2,1,0:T(8,128)S(1)}, f32[9,8,128]{2,1,0:T(8,128)S(1)}, u32[]{:S(2)}, u32[]{:S(2)}) collective-permute-start(f32[9,8,128]{2,1,0:T(8,128)S(1)} %shard_map.58.refs_0_), channel_id=1, source_target_pairs={{0,12},{4,8},{8,4},{12,0},{16,28},{20,24},{24,20},{28,16},{1,13},{... | collective-permute-start | bytes 110600 | tf_op jit(solution)/shard_map/ppermute | solution.py:337
  34.1 0.5 %collective-permute-start.7 = (f32[9,8,128]{2,1,0:T(8,128)S(1)}, f32[9,8,128]{2,1,0:T(8,128)S(1)}, u32[]{:S(2)}, u32[]{:S(2)}) collective-permute-start(f32[9,8,128]{2,1,0:T(8,128)S(1)} %shard_map.58.refs_0_), channel_id=1, source_target_pairs={{0,8},{4,12},{8,0},{12,4},{16,24},{20,28},{24,16},{28,20},{1,9},{5... | collective-permute-start | bytes 110600 | tf_op jit(solution)/shard_map/ppermute | solution.py:337
  34.6 3.1 %collective-permute-done.8.refs_3_ = f32[9,8,128]{2,1,0:T(8,128)S(1)} collective-permute-done((f32[9,8,128]{2,1,0:T(8,128)S(1)}, f32[9,8,128]{2,1,0:T(8,128)S(1)}, u32[]{:S(2)}, u32[]{:S(2)}) %collective-permute-start.8) | collective-permute-done | bytes 36896 | tf_op jit(solution)/shard_map/ppermute | solution.py:337
  37.7 0.3 collective-permute-start.6
  38.0 0.0 collective-permute-done.7.refs_2_
  38.0 3.6 %collective-permute-done.6.refs_1_ = f32[9,8,128]{2,1,0:T(8,128)S(1)} collective-permute-done((f32[9,8,128]{2,1,0:T(8,128)S(1)}, f32[9,8,128]{2,1,0:T(8,128)S(1)}, u32[]{:S(2)}, u32[]{:S(2)}) %collective-permute-start.6) | collective-permute-done | bytes 36896 | tf_op jit(solution)/shard_map/ppermute | solution.py:337
  41.6 0.0 collective-permute-done.15.refs_7_
  41.6 0.0 collective-permute-done.14.refs_6_
  41.6 0.0 collective-permute-done.13.refs_5_
  41.6 1.2 %shard_map.61 = f32[8,16,8,128]{3,2,1,0:T(8,128)} custom-call(s32[1]{0:T(128)} %bitcast.me_ref, f32[3,8,128]{2,1,0:T(8,128)S(1)} %get-tuple-element.18.keep_ref, f32[9,8,128]{2,1,0:T(8,128)S(1)} %shard_map.58.refs_0_, f32[9,8,128]{2,1,0:T(8,128)S(1)} %collective-permute-done.6.refs_1_, f32[9,8,128]{2,1,0:T(8,128)S(1)} %collective-permute-done.7.refs_2_, ...), custom_call_target="tpu_custom_call" | custom-call | bytes 552964 | tf_op jit(solution)/shard_map/pallas_call | solution.py:283
  (4 shorter events, 0.1 us)
Async XLA Ops:
  1.3 1.0 %copy-start = (f32[1,64,2048]{2,1,0:T(8,128)S(1)}, f32[1,64,2048]{2,1,0:T(8,128)}, u32[]{:S(2)}) copy-start(f32[1,64,2048]{2,1,0:T(8,128)} %param.5) | copy-start | bytes 1572868
  2.3 1.0 %copy-start.2 = (f32[1,64,2048]{2,1,0:T(8,128)S(1)}, f32[1,64,2048]{2,1,0:T(8,128)}, u32[]{:S(2)}) copy-start(f32[1,64,2048]{2,1,0:T(8,128)} %param.6) | copy-start | bytes 1572868
  3.4 1.0 %copy-start.3 = (f32[1,64,2048]{2,1,0:T(8,128)S(1)}, f32[1,64,2048]{2,1,0:T(8,128)}, u32[]{:S(2)}) copy-start(f32[1,64,2048]{2,1,0:T(8,128)} %param.7) | copy-start | bytes 1572868
  4.4 14.9 %copy-start.1 = (f32[1,64,2048]{2,1,0:T(8,128)S(1)}, f32[1,64,2048]{2,1,0:T(8,128)}, u32[]{:S(2)}) copy-start(f32[1,64,2048]{2,1,0:T(8,128)} %param.5) | copy-start | bytes 1572868
  6.6 8.6 %collective-permute-start.9 = (f32[24,8,128]{2,1,0:T(8,128)S(1)}, f32[24,8,128]{2,1,0:T(8,128)S(1)}, u32[]{:S(2)}, u32[]{:S(2)}) collective-permute-start(f32[24,8,128]{2,1,0:T(8,128)S(1)} %get-tuple-element.28), channel_id=1, source_target_pairs={{0,4},{4,0},{8,12},{12,8},{16,20},{20,16},{24,28},{28,24},{1,5},{5... | collective-permute-start | bytes 294920 | tf_op jit(solution)/shard_map/ppermute | solution.py:337
  9.6 5.6 %collective-permute-start.10 = (f32[24,8,128]{2,1,0:T(8,128)S(1)}, f32[24,8,128]{2,1,0:T(8,128)S(1)}, u32[]{:S(2)}, u32[]{:S(2)}) collective-permute-start(f32[24,8,128]{2,1,0:T(8,128)S(1)} %get-tuple-element.29), channel_id=1, source_target_pairs={{0,8},{4,12},{8,0},{12,4},{16,24},{20,28},{24,16},{28,20},{1,9},{5... | collective-permute-start | bytes 294920 | tf_op jit(solution)/shard_map/ppermute | solution.py:337
  11.1 5.5 %collective-permute-start.11 = (f32[24,8,128]{2,1,0:T(8,128)S(1)}, f32[24,8,128]{2,1,0:T(8,128)S(1)}, u32[]{:S(2)}, u32[]{:S(2)}) collective-permute-start(f32[24,8,128]{2,1,0:T(8,128)S(1)} %get-tuple-element.30), channel_id=1, source_target_pairs={{0,12},{4,8},{8,4},{12,0},{16,28},{20,24},{24,20},{28,16},{1,13},{... | collective-permute-start | bytes 294920 | tf_op jit(solution)/shard_map/ppermute | solution.py:337
  11.1 8.2 %collective-permute-start = (f32[16,16,128]{2,1,0:T(8,128)S(1)}, f32[16,16,128]{2,1,0:T(8,128)S(1)}, u32[]{:S(2)}, u32[]{:S(2)}) collective-permute-start(f32[16,16,128]{2,1,0:T(8,128)S(1)} %get-tuple-element.21), channel_id=1, source_target_pairs={{1,2},{2,1},{5,6},{6,5},{9,10},{10,9},{13,14},{14,13},{17,18},{18,... | collective-permute-start | bytes 393224 | tf_op jit(solution)/shard_map/ppermute | solution.py:322
  11.8 7.5 %collective-permute-start.1 = (f32[16,16,128]{2,1,0:T(8,128)S(1)}, f32[16,16,128]{2,1,0:T(8,128)S(1)}, u32[]{:S(2)}, u32[]{:S(2)}) collective-permute-start(f32[16,16,128]{2,1,0:T(8,128)S(1)} %get-tuple-element.22), channel_id=1, source_target_pairs={{0,1},{2,3},{1,0},{3,2},{4,5},{6,7},{5,4},{7,6},{8,9},{10,11},{9,8... | collective-permute-start | bytes 393224 | tf_op jit(solution)/shard_map/ppermute | solution.py:322
  16.7 11.5 %collective-permute-start.12 = (f32[24,8,128]{2,1,0:T(8,128)S(1)}, f32[24,8,128]{2,1,0:T(8,128)S(1)}, u32[]{:S(2)}, u32[]{:S(2)}) collective-permute-start(f32[24,8,128]{2,1,0:T(8,128)S(1)} %shard_map.59.refs_0_), channel_id=1, source_target_pairs={{0,16},{4,20},{8,24},{12,28},{16,0},{20,4},{24,8},{28,12},{1,17},{... | collective-permute-start | bytes 294920 | tf_op jit(solution)/shard_map/ppermute | solution.py:337
  20.3 4.0 %collective-permute-start.2 = (f32[9,8,128]{2,1,0:T(8,128)S(1)}, f32[9,8,128]{2,1,0:T(8,128)S(1)}, u32[]{:S(2)}, u32[]{:S(2)}) collective-permute-start(f32[9,8,128]{2,1,0:T(8,128)S(1)} %get-tuple-element.24), channel_id=1, source_target_pairs={{0,4},{4,0},{8,12},{12,8},{16,20},{20,16},{24,28},{28,24},{1,5},{5... | collective-permute-start | bytes 110600 | tf_op jit(solution)/shard_map/ppermute | solution.py:337
  21.3 4.0 %collective-permute-start.3 = (f32[9,8,128]{2,1,0:T(8,128)S(1)}, f32[9,8,128]{2,1,0:T(8,128)S(1)}, u32[]{:S(2)}, u32[]{:S(2)}) collective-permute-start(f32[9,8,128]{2,1,0:T(8,128)S(1)} %get-tuple-element.25), channel_id=1, source_target_pairs={{0,8},{4,12},{8,0},{12,4},{16,24},{20,28},{24,16},{28,20},{1,9},{5... | collective-permute-start | bytes 110600 | tf_op jit(solution)/shard_map/ppermute | solution.py:337
  22.7 4.9 %collective-permute-start.4 = (f32[9,8,128]{2,1,0:T(8,128)S(1)}, f32[9,8,128]{2,1,0:T(8,128)S(1)}, u32[]{:S(2)}, u32[]{:S(2)}) collective-permute-start(f32[9,8,128]{2,1,0:T(8,128)S(1)} %get-tuple-element.26), channel_id=1, source_target_pairs={{0,12},{4,8},{8,4},{12,0},{16,28},{20,24},{24,20},{28,16},{1,13},{... | collective-permute-start | bytes 110600 | tf_op jit(solution)/shard_map/ppermute | solution.py:337
  27.5 5.3 %collective-permute-start.5 = (f32[9,8,128]{2,1,0:T(8,128)S(1)}, f32[9,8,128]{2,1,0:T(8,128)S(1)}, u32[]{:S(2)}, u32[]{:S(2)}) collective-permute-start(f32[9,8,128]{2,1,0:T(8,128)S(1)} %shard_map.57.refs_0_), channel_id=1, source_target_pairs={{0,16},{4,20},{8,24},{12,28},{16,0},{20,4},{24,8},{28,12},{1,17},{... | collective-permute-start | bytes 110600 | tf_op jit(solution)/shard_map/ppermute | solution.py:337
  28.2 13.4 %collective-permute-start.15 = (f32[24,8,128]{2,1,0:T(8,128)S(1)}, f32[24,8,128]{2,1,0:T(8,128)S(1)}, u32[]{:S(2)}, u32[]{:S(2)}) collective-permute-start(f32[24,8,128]{2,1,0:T(8,128)S(1)} %shard_map.60.refs_4_), channel_id=1, source_target_pairs={{0,12},{4,8},{8,4},{12,0},{16,28},{20,24},{24,20},{28,16},{1,13},{... | collective-permute-start | bytes 294920 | tf_op jit(solution)/shard_map/ppermute | solution.py:337
  29.7 11.9 %collective-permute-start.14 = (f32[24,8,128]{2,1,0:T(8,128)S(1)}, f32[24,8,128]{2,1,0:T(8,128)S(1)}, u32[]{:S(2)}, u32[]{:S(2)}) collective-permute-start(f32[24,8,128]{2,1,0:T(8,128)S(1)} %shard_map.60.refs_4_), channel_id=1, source_target_pairs={{0,8},{4,12},{8,0},{12,4},{16,24},{20,28},{24,16},{28,20},{1,9},{5... | collective-permute-start | bytes 294920 | tf_op jit(solution)/shard_map/ppermute | solution.py:337
  30.3 11.4 %collective-permute-start.13 = (f32[24,8,128]{2,1,0:T(8,128)S(1)}, f32[24,8,128]{2,1,0:T(8,128)S(1)}, u32[]{:S(2)}, u32[]{:S(2)}) collective-permute-start(f32[24,8,128]{2,1,0:T(8,128)S(1)} %shard_map.60.refs_4_), channel_id=1, source_target_pairs={{0,4},{4,0},{8,12},{12,8},{16,20},{20,16},{24,28},{28,24},{1,5},{5... | collective-permute-start | bytes 294920 | tf_op jit(solution)/shard_map/ppermute | solution.py:337
  32.8 4.9 %collective-permute-start.8 = (f32[9,8,128]{2,1,0:T(8,128)S(1)}, f32[9,8,128]{2,1,0:T(8,128)S(1)}, u32[]{:S(2)}, u32[]{:S(2)}) collective-permute-start(f32[9,8,128]{2,1,0:T(8,128)S(1)} %shard_map.58.refs_0_), channel_id=1, source_target_pairs={{0,12},{4,8},{8,4},{12,0},{16,28},{20,24},{24,20},{28,16},{1,13},{... | collective-permute-start | bytes 110600 | tf_op jit(solution)/shard_map/ppermute | solution.py:337
  34.1 4.0 %collective-permute-start.7 = (f32[9,8,128]{2,1,0:T(8,128)S(1)}, f32[9,8,128]{2,1,0:T(8,128)S(1)}, u32[]{:S(2)}, u32[]{:S(2)}) collective-permute-start(f32[9,8,128]{2,1,0:T(8,128)S(1)} %shard_map.58.refs_0_), channel_id=1, source_target_pairs={{0,8},{4,12},{8,0},{12,4},{16,24},{20,28},{24,16},{28,20},{1,9},{5... | collective-permute-start | bytes 110600 | tf_op jit(solution)/shard_map/ppermute | solution.py:337
  37.7 4.0 %collective-permute-start.6 = (f32[9,8,128]{2,1,0:T(8,128)S(1)}, f32[9,8,128]{2,1,0:T(8,128)S(1)}, u32[]{:S(2)}, u32[]{:S(2)}) collective-permute-start(f32[9,8,128]{2,1,0:T(8,128)S(1)} %shard_map.58.refs_0_), channel_id=1, source_target_pairs={{0,4},{4,0},{8,12},{12,8},{16,20},{20,16},{24,28},{28,24},{1,5},{5... | collective-permute-start | bytes 110600 | tf_op jit(solution)/shard_map/ppermute | solution.py:337

commit v7 on v6

--- a/solution.py
+++ b/solution.py
@@ -79,7 +79,7 @@
     lax.fori_loop(0, count, body, (cur, *ends), unroll=min(count, UNROLL))
 
 
-def run_steps(strips, per_chunk, me, classes, load, buffers, coefs, finish):
+def run_steps(strips, per_chunk, classes, load, buffers, coefs, finish):
     center, above_c, below_c, side = coefs
     for buf in buffers:
         for edge in (0, strips + 1):
@@ -105,9 +105,9 @@
 
         advance(0, strips, classes, source, coefs, keep)
     source = buffers[(STEPS - 1) % 2]
-    for away in range(SQUARE):
-        emit = functools.partial(finish, away)
-        advance((me ^ away) * per_chunk, per_chunk, classes, source, coefs, emit)
+    for chunk in range(SQUARE):
+        emit = functools.partial(finish, chunk)
+        advance(chunk * per_chunk, per_chunk, classes, source, coefs, emit)
 
 
 def surpluses(s, prev, weight_ref):
@@ -142,11 +142,11 @@
 
 
 def inner_kernel(
-    per_chunk, depth, parity_ref, me_ref, level_ref, coef_ref, dens_ref, diff_ref, drift_ref,
+    per_chunk, depth, parity_ref, level_ref, coef_ref, dens_ref, diff_ref, drift_ref,
     far_ref, near_ref, state_ref, keep_ref, weight_ref, *refs
 ):
     many, strips = dens_ref.shape[:2]
-    *out_refs, scratch, state_a, state_b = refs[:-4]
+    *outs, scratch, state_a, state_b = refs[:-4]
     fields = (dens_ref, diff_ref, drift_ref)
     pack(parity_ref[0] == 1, fields, far_ref, near_ref)
     coef = coef_ref[0].astype(jnp.float32)
@@ -163,7 +163,7 @@
         at = spaced(j * TILE + t, many, strips * TILE)
         return [ref[at, :] for ref in rows]
 
-    def finish(away, j, part, new):
+    def finish(chunk, j, part, new):
         for t in range(TILE):
             state_ref[j, t] = new[t]
         if inside <= 0:
@@ -172,18 +172,18 @@
         for t in range(TILE):
             by_row[spaced(j * many * TILE + t, many, TILE), :] = weighted[t]
         for m in range(inside):
-            out_refs[away][part * inside + m] = scratch[j, 1 + m]
-
-    run_steps(strips, per_chunk, me_ref[0], TILE, load, (state_a, state_b), refs[-4:], finish)
+            outs[0][chunk, part * inside + m] = scratch[j, 1 + m]
+
+    run_steps(strips, per_chunk, TILE, load, (state_a, state_b), refs[-4:], finish)
 
 
 def edge_kernel(
-    per_chunk, parity_ref, me_ref, dens_ref, diff_ref, drift_ref, state_ref, weight_ref, far_ref,
+    per_chunk, parity_ref, dens_ref, diff_ref, drift_ref, state_ref, weight_ref, far_ref,
     near_ref, *refs
 ):
     many, strips = dens_ref.shape[:2]
     odd = parity_ref[0] == 1
-    *out_refs, scratch, slab, state_a, state_b = refs[:-4]
+    out_ref, scratch, slab, state_a, state_b = refs[:-4]
 
     def stage(j):
         far, near = far_ref[j], near_ref[j]
@@ -210,7 +210,7 @@
     by_row = flat(scratch)
     edges = sorted({0, many - 1})
 
-    def finish(away, j, part, new):
+    def finish(chunk, j, part, new):
         s = [state_ref[j, t] for t in range(TILE)]
         for t in range(HALF):
             s[t] = jnp.where(place == 0, new[t][2:3], s[t])
@@ -220,42 +220,44 @@
         for t in range(TILE):
             by_row[spaced(j * many * TILE + t, many, TILE), :] = weighted[t]
         for e, m in enumerate(edges):
-            out_refs[away][part * len(edges) + e] = scratch[j, m]
+            out_ref[chunk, part * len(edges) + e] = scratch[j, m]
         last = per_chunk * len(edges) + part // TILE
-        out_refs[away][last, pl.ds(lax.rem(part, TILE), 1), :] = weight_ref[3][0:1] * before
-
-    run_steps(strips, per_chunk, me_ref[0], HALF, load, (state_a, state_b), refs[-4:], finish)
-
-
-def sum_kernel(*refs):
-    *parts, out_ref = refs
-    total = parts[0][...]
-    for part in parts[1:]:
-        total = total + part[...]
+        out_ref[chunk, last, pl.ds(lax.rem(part, TILE), 1), :] = weight_ref[3][0:1] * before
+
+    run_steps(strips, per_chunk, HALF, load, (state_a, state_b), refs[-4:], finish)
+
+
+def sum_kernel(parts_ref, out_ref):
+    total = parts_ref[0]
+    for g in range(1, parts_ref.shape[0]):
+        total = total + parts_ref[g]
     out_ref[...] = total
 
 
-def nodal_kernel(per_chunk, me_ref, keep_ref, *refs):
+def spread_kernel(mine_ref, theirs_ref, out_ref):
+    total = mine_ref[...] + theirs_ref[...]
+    for g in range(out_ref.shape[0]):
+        out_ref[g] = total
+
+
+def nodal_kernel(per_chunk, keep_ref, *refs):
     *totals, out_ref, scratch = refs
     many, strips = out_ref.shape[:2]
     out, by_row = flat(out_ref), flat(scratch)
     fine, mid, low = (keep_ref[k] for k in range(3))
     place = lax.broadcasted_iota(jnp.int32, (many, LANES), 0)
     edges, inside = sorted({0, many - 1}), many - 2
-    for away in range(SQUARE):
-        first = (me_ref[0] ^ away) * per_chunk
-        outer_ref = totals[away]
-        inner_ref = totals[SQUARE + away] if inside > 0 else None
-
-        def body(part, outer_ref=outer_ref, inner_ref=inner_ref, first=first):
-            j = first + part
+    for chunk in range(SQUARE):
+
+        def body(part, chunk=chunk):
+            j = chunk * per_chunk + part
             for e, m in enumerate(edges):
-                scratch[j, m] = outer_ref[part * len(edges) + e]
+                scratch[j, m] = totals[0][chunk, part * len(edges) + e]
             for m in range(inside):
-                scratch[j, 1 + m] = inner_ref[part * inside + m]
+                scratch[j, 1 + m] = totals[1][chunk, part * inside + m]
             w = [by_row[spaced(j * many * TILE + t, many, TILE), :] for t in range(TILE)]
             last = per_chunk * len(edges) + part // TILE
-            before = outer_ref[last, pl.ds(lax.rem(part, TILE), 1), :]
+            before = totals[0][chunk, last, pl.ds(lax.rem(part, TILE), 1), :]
             prev = jnp.where(place == 0, before, roll_rows(w[7], 1))
             v3 = 0.5 * (prev + w[7]) + low * w[3]
             v1 = 0.5 * (prev + v3) + mid * w[1]
@@ -298,7 +300,7 @@
     per_chunk = strips // SQUARE
     depth = (rows * doms).bit_length() - 1
     tiles = [tiles_of(x[0]) for x in (density, diffusion, drift_speed)]
-    me = (lax.axis_index("grp") % SQUARE).astype(jnp.int32)[None]
+    squares = [list(range(g, g + SQUARE)) for g in range(0, grids, SQUARE)]
     parity = (lax.axis_index("dom") % 2).astype(jnp.int32)[None]
 
     def vmem(*shape):
@@ -310,9 +312,9 @@
         functools.partial(inner_kernel, per_chunk, depth),
         [(strips, 2 * TILE, LANES)] * 2
         + [place, (3, many, LANES), (4, many, LANES)]
-        + [(per_chunk * (many - 2), TILE, LANES)] * (SQUARE if many > 2 else 0),
-        (parity, me, levels, coefficient, *tiles),
-        4,
+        + [(SQUARE, per_chunk * (many - 2), TILE, LANES)] * (many > 2),
+        (parity, levels, coefficient, *tiles),
+        3,
         [vmem(*pieces)] + [vmem(strips + 2, *place[1:])] * 2 + [vmem(*place)] * 4,
         flops=40 * rows * cols,
     )
@@ -322,35 +324,37 @@
         lax.ppermute(array, "dom", pairs + [(b, a) for a, b in pairs])
         for array, pairs in ((far, far_pairs), (near, near_pairs))
     )
-    outside = call(
+    (outside,) = call(
         functools.partial(edge_kernel, per_chunk),
-        [(per_chunk * min(many, 2) + -(-per_chunk // TILE), TILE, LANES)] * SQUARE,
-        (parity, me, *tiles, state, weight, far, near),
-        2,
+        [(SQUARE, per_chunk * min(many, 2) + -(-per_chunk // TILE), TILE, LANES)],
+        (parity, *tiles, state, weight, far, near),
+        1,
         [vmem(*pieces), vmem(3, strips, SLAB, LANES)]
         + [vmem(strips + 2, HALF, TILE, LANES)] * 2
         + [vmem(strips, HALF, TILE, LANES)] * 4,
         flops=40 * SLAB * cols,
     )
 
-    def swap(array, apart):
-        return lax.ppermute(array, "grp", [(g, g ^ apart) for g in range(grids)])
-
-    def over_grids(own, *others):
-        theirs = [swap(array, apart) for apart, array in enumerate(others, 1)]
-        (total,) = call(sum_kernel, [own.shape], (own, *theirs))
+    def exchange(array):
+        return lax.all_to_all(array, "grp", 0, 0, axis_index_groups=squares, tiled=True)
+
+    def over_grids(weighted):
+        (total,) = call(sum_kernel, [weighted.shape[1:]], (exchange(weighted),))
         apart = SQUARE
         while apart < grids:
-            (total,) = call(sum_kernel, [own.shape], (total, swap(total, apart)))
+            other = lax.ppermute(total, "grp", [(g, g ^ apart) for g in range(grids)])
             apart *= 2
-        return [total] + [swap(total, apart) for apart in range(1, SQUARE)]
-
-    totals = over_grids(*outside) + (over_grids(*inside) if inside else [])
+            if apart < grids:
+                total = total + other
+        (spread,) = call(spread_kernel, [weighted.shape], (total, other))
+        return exchange(spread)
+
+    totals = [over_grids(weighted) for weighted in (outside, *inside)]
     (nodal,) = call(
         functools.partial(nodal_kernel, per_chunk),
         [(many, strips, TILE, LANES)],
-        (me, keep, *totals),
-        1,
+        (keep, *totals),
+        0,
         [vmem(*pieces)],
     )
     return block_of(nodal)[None]

time: 43.1 us -> 58.4 us (1.35)
  blocking collectives: 0 us -> 18.4 us
  starting transfers between devices: 21.1 us -> 16.8 us
  Pallas kernels: 4.32 us -> 5.63 us
    all_to_all x0 -> x2, blocking collectives: none -> 18.4 us  [exchange(): lax.all_to_all(array, 'grp', 0, 0, axis_index_groups=squares, tiled=True)]
    ppermute x14 -> x2, starting transfers between devices: 17.1 us -> 2.83 us  [over_grids(): other = lax.ppermute(total, 'grp', [(g, g ^ apart) for g in range(grids)])]
    all_to_all x0 -> x2, starting transfers between devices: none -> 8.93 us  [exchange(): lax.all_to_all(array, 'grp', 0, 0, axis_index_groups=squares, tiled=True)]
    ppermute x14 -> x2, waiting for transfers between devices: 12.9 us -> 10.1 us  [over_grids(): other = lax.ppermute(total, 'grp', [(g, g ^ apart) for g in range(grids)])]
    all_to_all x0 -> x2, waiting for transfers between devices: none -> 1.52 us  [exchange(): lax.all_to_all(array, 'grp', 0, 0, axis_index_groups=squares, tiled=True)]
    pallas_call x7, Pallas kernels: 4.32 us -> 5.63 us  [call(): pl.pallas_call(kernel, out_shape=[jax.ShapeDtypeStruct(shape, jnp.float32...]
    ppermute x2, starting transfers between devices: 4.01 us -> 5.04 us  [on_device(): lax.ppermute(array, 'dom', pairs + [(b, a) for a, b in pairs])]
    ppermute x2, waiting for transfers between devices: 0.01 us -> 0.99 us  [on_device(): lax.ppermute(array, 'dom', pairs + [(b, a) for a, b in pairs])]
  transfers between devices with their start and end apart: 16 -> 6, of which waited for: 7 -> 4; matrix products, arithmetic and copies ran while one was open for 0% -> 0% of each run, Pallas kernels for 2% -> 1%
where the time goes in v7:
time: 58.4 us; the launch traced here: 57.9 us
  blocking collectives  18.4 us (32%)
  starting transfers between devices  16.8 us (29%)
  waiting for transfers between devices  12.6 us (22%)
  Pallas kernels  5.63 us (10%)
  local copies, waits for them, and re-layouts  3.12 us (5%)
  between operations  1.36 us (2%)
    all_to_all x2, blocking collectives, exchange(): lax.all_to_all(array, 'grp', 0, 0, axis_index_groups=squares, tiled=True)  18.4 us
    ppermute x2, waiting for transfers between devices, over_grids(): other = lax.ppermute(total, 'grp', [(g, g ^ apart) for g in range(grids)])  10.1 us
    all_to_all x2, starting transfers between devices, exchange(): lax.all_to_all(array, 'grp', 0, 0, axis_index_groups=squares, tiled=True)  8.93 us
    pallas_call x7, Pallas kernels, call(): pl.pallas_call(kernel, out_shape=[jax.ShapeDtypeStruct(shape, jnp.float32...  5.63 us
    ppermute x2, starting transfers between devices, on_device(): lax.ppermute(array, 'dom', pairs + [(b, a) for a, b in pairs])  5.04 us
    unnamed x6, local copies, waits for them, and re-layouts  3.12 us
    ppermute x2, starting transfers between devices, over_grids(): other = lax.ppermute(total, 'grp', [(g, g ^ apart) for g in range(grids)])  2.83 us
    all_to_all x2, waiting for transfers between devices, exchange(): lax.all_to_all(array, 'grp', 0, 0, axis_index_groups=squares, tiled=True)  1.52 us
  transfers between devices with their start and end apart: 6, of which 4 were waited for; matrix products, arithmetic and copies ran while one was open for 0% of the time, Pallas kernels for 1%

profile of v7, /device:TPU:0, one launch (start us, length us, event | category | flops | bytes accessed | tf_op | source)
XLA Modules:
  0.0 57.9 jit_solution(4615874030087030783)
XLA Ops:
  1.3 0.0 copy-start
  1.3 1.0 %copy-done = f32[1,64,2048]{2,1,0:T(8,128)S(1)} copy-done((f32[1,64,2048]{2,1,0:T(8,128)S(1)}, f32[1,64,2048]{2,1,0:T(8,128)}, u32[]{:S(2)}) %copy-start) | copy-done | bytes 524312
  2.3 0.0 copy-start.1
  2.3 1.0 %copy-done.1 = f32[1,64,2048]{2,1,0:T(8,128)S(1)} copy-done((f32[1,64,2048]{2,1,0:T(8,128)S(1)}, f32[1,64,2048]{2,1,0:T(8,128)}, u32[]{:S(2)}) %copy-start.1) | copy-done | bytes 524312
  3.4 0.0 copy-start.2
  3.4 1.0 %copy-done.2 = f32[1,64,2048]{2,1,0:T(8,128)S(1)} copy-done((f32[1,64,2048]{2,1,0:T(8,128)S(1)}, f32[1,64,2048]{2,1,0:T(8,128)}, u32[]{:S(2)}) %copy-start.2) | copy-done | bytes 524312
  4.4 2.9 %shard_map.55 = (f32[16,16,128]{2,1,0:T(8,128)S(1)}, f32[16,16,128]{2,1,0:T(8,128)S(1)}, f32[16,8,8,128]{3,2,1,0:T(8,128)S(1)}, f32[3,8,128]{2,1,0:T(8,128)S(1)}...) custom-call(s32[1]{0:T(128)} %bitcast.parity_ref, s32[1]{0:T(128)S(6)} %copy.6.level_ref, s32[1]{0:T(128)S(6)} %copy.7.coef_ref, ...), custom_call_target="tpu_custom_call" | custom-call | flops 5242880 | bytes 1572876 | tf_op jit(solution)/shard_map/pallas_call | solution.py:285
  7.3 0.7 %collective-permute-start = (f32[16,16,128]{2,1,0:T(8,128)S(1)}, f32[16,16,128]{2,1,0:T(8,128)S(1)}, u32[]{:S(2)}, u32[]{:S(2)}) collective-permute-start(f32[16,16,128]{2,1,0:T(8,128)S(1)} %get-tuple-element.14), channel_id=1, source_target_pairs={{1,2},{2,1},{5,6},{6,5},{9,10},{10,9},{13,14},{14,13},{17,18},{18,... | collective-permute-start | bytes 393224 | tf_op jit(solution)/shard_map/ppermute | solution.py:324
  8.0 4.4 %collective-permute-start.1 = (f32[16,16,128]{2,1,0:T(8,128)S(1)}, f32[16,16,128]{2,1,0:T(8,128)S(1)}, u32[]{:S(2)}, u32[]{:S(2)}) collective-permute-start(f32[16,16,128]{2,1,0:T(8,128)S(1)} %get-tuple-element.15), channel_id=1, source_target_pairs={{0,1},{2,3},{1,0},{3,2},{4,5},{6,7},{5,4},{7,6},{8,9},{10,11},{9,8... | collective-permute-start | bytes 393224 | tf_op jit(solution)/shard_map/ppermute | solution.py:324
  12.4 0.0 collective-permute-done.far_ref
  12.4 1.0 %collective-permute-done.1.near_ref = f32[16,16,128]{2,1,0:T(8,128)S(1)} collective-permute-done((f32[16,16,128]{2,1,0:T(8,128)S(1)}, f32[16,16,128]{2,1,0:T(8,128)S(1)}, u32[]{:S(2)}, u32[]{:S(2)}) %collective-permute-start.1) | collective-permute-done | bytes 131104 | tf_op jit(solution)/shard_map/ppermute | solution.py:324
  13.3 0.8 %shard_map.56 = f32[4,9,8,128]{3,2,1,0:T(8,128)S(1)} custom-call(s32[1]{0:T(128)} %bitcast.parity_ref, f32[8,16,8,128]{3,2,1,0:T(8,128)S(1)} %bitcast.14, f32[8,16,8,128]{3,2,1,0:T(8,128)S(1)} %bitcast.16, f32[8,16,8,128]{3,2,1,0:T(8,128)S(1)} %bitcast.18, f32[16,8,8,128]{3,2,1,0:T(8,128)S(1)} %get-tuple-element.12.state_ref, ...), custom_call_target="tpu_custom_call" | custom-call | flops 2621440 | bytes 2375684 | tf_op jit(solution)/shard_map/pallas_call | solution.py:285
  14.2 9.4 %all_to_all.20.parts_ref = f32[4,9,8,128]{3,2,1,0:T(8,128)S(1)} all-to-all(f32[4,9,8,128]{3,2,1,0:T(8,128)S(1)} %shard_map.56), channel_id=1, replica_groups={{0,4,8,12},{16,20,24,28},{1,5,9,13},{17,21,25,29},{2,6,10,14},{18,22,26..., dimensions={0} | all-to-all | bytes 294912 | tf_op jit(solution)/shard_map/all_to_all | solution.py:339
  23.5 3.5 %all-to-all-start.2 = ((f32[4,24,8,128]{3,2,1,0:T(8,128)}), f32[4,24,8,128]{3,2,1,0:T(8,128)S(1)}, u32[]{:S(2)}, u32[]{:S(2)}) async-start(f32[4,24,8,128]{3,2,1,0:T(8,128)} %get-tuple-element.16), calls=%async_computation.2 | async-start | bytes 786432 | tf_op jit(solution)/shard_map/all_to_all | solution.py:339
  27.0 2.7 %collective-permute-start.2 = (f32[9,8,128]{2,1,0:T(8,128)S(1)}, f32[9,8,128]{2,1,0:T(8,128)S(1)}, u32[]{:S(2)}, u32[]{:S(2)}) collective-permute-start(f32[9,8,128]{2,1,0:T(8,128)S(1)} %shard_map.57.mine_ref), channel_id=1, source_target_pairs={{0,16},{4,20},{8,24},{12,28},{16,0},{20,4},{24,8},{28,12},{1,17},{... | collective-permute-start | bytes 110600 | tf_op jit(solution)/shard_map/ppermute | solution.py:345
  29.7 3.1 %collective-permute-done.2.theirs_ref = f32[9,8,128]{2,1,0:T(8,128)S(1)} collective-permute-done((f32[9,8,128]{2,1,0:T(8,128)S(1)}, f32[9,8,128]{2,1,0:T(8,128)S(1)}, u32[]{:S(2)}, u32[]{:S(2)}) %collective-permute-start.2) | collective-permute-done | bytes 36896 | tf_op jit(solution)/shard_map/ppermute | solution.py:345
  32.8 0.7 %shard_map.58 = f32[4,9,8,128]{3,2,1,0:T(8,128)} custom-call(f32[9,8,128]{2,1,0:T(8,128)S(1)} %shard_map.57.mine_ref, f32[9,8,128]{2,1,0:T(8,128)S(1)} %collective-permute-done.2.theirs_ref), custom_call_target="tpu_custom_call" | custom-call | bytes 73728 | tf_op jit(solution)/shard_map/pallas_call | solution.py:285
  33.5 1.5 %all-to-all-done.2.parts_ref = f32[4,24,8,128]{3,2,1,0:T(8,128)S(1)} async-done(((f32[4,24,8,128]{3,2,1,0:T(8,128)}), f32[4,24,8,128]{3,2,1,0:T(8,128)S(1)}, u32[]{:S(2)}, u32[]{:S(2)}) %all-to-all-start.2) | async-done | bytes 393248 | tf_op jit(solution)/shard_map/all_to_all | solution.py:339
  35.0 5.5 %all-to-all-start.1 = ((f32[4,9,8,128]{3,2,1,0:T(8,128)}), f32[4,9,8,128]{3,2,1,0:T(8,128)S(1)}, u32[]{:S(2)}, u32[]{:S(2)}) async-start(f32[4,9,8,128]{3,2,1,0:T(8,128)} %shard_map.58), calls=%async_computation.1 | async-start | bytes 294912 | tf_op jit(solution)/shard_map/all_to_all | solution.py:339
  40.5 0.2 collective-permute-start.3
  40.7 7.0 %collective-permute-done.3.theirs_ref = f32[24,8,128]{2,1,0:T(8,128)S(1)} collective-permute-done((f32[24,8,128]{2,1,0:T(8,128)S(1)}, f32[24,8,128]{2,1,0:T(8,128)S(1)}, u32[]{:S(2)}, u32[]{:S(2)}) %collective-permute-start.3) | collective-permute-done | bytes 98336 | tf_op jit(solution)/shard_map/ppermute | solution.py:345
  47.7 0.0 all-to-all-done.1.refs_0_
  47.7 9.0 %all_to_all.21.refs_1_ = f32[4,24,8,128]{3,2,1,0:T(8,128)S(1)} all-to-all(f32[4,24,8,128]{3,2,1,0:T(8,128)S(1)} %shard_map.60), channel_id=1, replica_groups={{0,4,8,12},{16,20,24,28},{1,5,9,13},{17,21,25,29},{2,6,10,14},{18,22,26..., dimensions={0} | all-to-all | bytes 786432 | tf_op jit(solution)/shard_map/all_to_all | solution.py:339
  56.7 1.2 %shard_map.61 = f32[8,16,8,128]{3,2,1,0:T(8,128)} custom-call(f32[3,8,128]{2,1,0:T(8,128)S(1)} %get-tuple-element.11.keep_ref, f32[4,9,8,128]{3,2,1,0:T(8,128)S(1)} %all-to-all-done.1.refs_0_, f32[4,24,8,128]{3,2,1,0:T(8,128)S(1)} %all_to_all.21.refs_1_), custom_call_target="tpu_custom_call" | custom-call | bytes 552960 | tf_op jit(solution)/shard_map/pallas_call | solution.py:285
  (3 shorter events, 0.1 us)
Async XLA Ops:
  1.3 1.0 %copy-start = (f32[1,64,2048]{2,1,0:T(8,128)S(1)}, f32[1,64,2048]{2,1,0:T(8,128)}, u32[]{:S(2)}) copy-start(f32[1,64,2048]{2,1,0:T(8,128)} %param.5) | copy-start | bytes 1572868
  2.3 1.0 %copy-start.1 = (f32[1,64,2048]{2,1,0:T(8,128)S(1)}, f32[1,64,2048]{2,1,0:T(8,128)}, u32[]{:S(2)}) copy-start(f32[1,64,2048]{2,1,0:T(8,128)} %param.6) | copy-start | bytes 1572868
  3.4 1.0 %copy-start.2 = (f32[1,64,2048]{2,1,0:T(8,128)S(1)}, f32[1,64,2048]{2,1,0:T(8,128)}, u32[]{:S(2)}) copy-start(f32[1,64,2048]{2,1,0:T(8,128)} %param.7) | copy-start | bytes 1572868
  7.3 5.1 %collective-permute-start = (f32[16,16,128]{2,1,0:T(8,128)S(1)}, f32[16,16,128]{2,1,0:T(8,128)S(1)}, u32[]{:S(2)}, u32[]{:S(2)}) collective-permute-start(f32[16,16,128]{2,1,0:T(8,128)S(1)} %get-tuple-element.14), channel_id=1, source_target_pairs={{1,2},{2,1},{5,6},{6,5},{9,10},{10,9},{13,14},{14,13},{17,18},{18,... | collective-permute-start | bytes 393224 | tf_op jit(solution)/shard_map/ppermute | solution.py:324
  8.0 5.4 %collective-permute-start.1 = (f32[16,16,128]{2,1,0:T(8,128)S(1)}, f32[16,16,128]{2,1,0:T(8,128)S(1)}, u32[]{:S(2)}, u32[]{:S(2)}) collective-permute-start(f32[16,16,128]{2,1,0:T(8,128)S(1)} %get-tuple-element.15), channel_id=1, source_target_pairs={{0,1},{2,3},{1,0},{3,2},{4,5},{6,7},{5,4},{7,6},{8,9},{10,11},{9,8... | collective-permute-start | bytes 393224 | tf_op jit(solution)/shard_map/ppermute | solution.py:324
  23.5 11.4 %all-to-all-start.2 = ((f32[4,24,8,128]{3,2,1,0:T(8,128)}), f32[4,24,8,128]{3,2,1,0:T(8,128)S(1)}, u32[]{:S(2)}, u32[]{:S(2)}) async-start(f32[4,24,8,128]{3,2,1,0:T(8,128)} %get-tuple-element.16), calls=%async_computation.2 | async-start | bytes 786432 | tf_op jit(solution)/shard_map/all_to_all | solution.py:339
  27.0 5.8 %collective-permute-start.2 = (f32[9,8,128]{2,1,0:T(8,128)S(1)}, f32[9,8,128]{2,1,0:T(8,128)S(1)}, u32[]{:S(2)}, u32[]{:S(2)}) collective-permute-start(f32[9,8,128]{2,1,0:T(8,128)S(1)} %shard_map.57.mine_ref), channel_id=1, source_target_pairs={{0,16},{4,20},{8,24},{12,28},{16,0},{20,4},{24,8},{28,12},{1,17},{... | collective-permute-start | bytes 110600 | tf_op jit(solution)/shard_map/ppermute | solution.py:345
  35.0 12.7 %all-to-all-start.1 = ((f32[4,9,8,128]{3,2,1,0:T(8,128)}), f32[4,9,8,128]{3,2,1,0:T(8,128)S(1)}, u32[]{:S(2)}, u32[]{:S(2)}) async-start(f32[4,9,8,128]{3,2,1,0:T(8,128)} %shard_map.58), calls=%async_computation.1 | async-start | bytes 294912 | tf_op jit(solution)/shard_map/all_to_all | solution.py:339
  40.5 7.2 %collective-permute-start.3 = (f32[24,8,128]{2,1,0:T(8,128)S(1)}, f32[24,8,128]{2,1,0:T(8,128)S(1)}, u32[]{:S(2)}, u32[]{:S(2)}) collective-permute-start(f32[24,8,128]{2,1,0:T(8,128)S(1)} %shard_map.59.mine_ref), channel_id=1, source_target_pairs={{0,16},{4,20},{8,24},{12,28},{16,0},{20,4},{24,8},{28,12},{1,17},{... | collective-permute-start | bytes 294920 | tf_op jit(solution)/shard_map/ppermute | solution.py:345

commit v8 on v5

--- a/solution.py
+++ b/solution.py
@@ -48,12 +48,13 @@
     lax.fori_loop(0, strips, step, 0, unroll=unroll)
 
 
-def advance(strips, classes, source, coefs, emit, unroll):
+def advance(first, count, classes, source, coefs, emit):
     shape = source.shape[2:]
     lanes = lax.broadcasted_iota(jnp.int32, shape, 1)
     center, above_c, below_c, side = coefs
 
-    def body(j, carry):
+    def body(k, carry):
+        j = first + k
         cur, right_prev, left_cur = carry
         nxt = [source[j + 2, t] for t in range(classes)]
         left_next = [pltpu.roll(x, LANES - 1, 1) for x in nxt]
@@ -70,16 +71,15 @@
                 + below_c[j, t] * below[t]
                 + side[j, t] * (left + right)
             )
-        emit(j, new)
+        emit(j, k, new)
         return nxt, right_cur, left_next
 
-    cur = [source[1, t] for t in range(classes)]
-    zeros = [jnp.zeros(shape, jnp.float32)] * classes
-    first = (cur, zeros, [pltpu.roll(x, LANES - 1, 1) for x in cur])
-    lax.fori_loop(0, strips, body, first, unroll=unroll)
-
-
-def run_steps(strips, classes, load, buffers, coefs, finish, unroll):
+    prev, cur = ([source[first + at, t] for t in range(classes)] for at in range(2))
+    ends = [pltpu.roll(x, 1, 1) for x in prev], [pltpu.roll(x, LANES - 1, 1) for x in cur]
+    lax.fori_loop(0, count, body, (cur, *ends), unroll=min(count, UNROLL))
+
+
+def run_steps(strips, classes, load, buffers, coefs, last):
     center, above_c, below_c, side = coefs
     for buf in buffers:
         for edge in (0, strips + 1):
@@ -95,29 +95,43 @@
             below_c[j, t] = diffuse + half
             side[j, t] = diffuse
 
-    per_strip(strips, begin, unroll)
-    for step in range(STEPS):
+    per_strip(strips, begin, min(strips, UNROLL))
+    for step in range(STEPS - 1):
         source, target = buffers[step % 2], buffers[1 - step % 2]
 
-        def keep(j, new, target=target):
+        def keep(j, _, new, target=target):
             for t in range(classes):
                 target[j + 1, t] = new[t]
 
-        emit = keep if step < STEPS - 1 else finish
-        advance(strips, classes, source, coefs, emit, unroll)
-
-
-def pack_kernel(parity_ref, *refs):
+        advance(0, strips, classes, source, coefs, keep)
+    last(buffers[(STEPS - 1) % 2])
+
+
+def surpluses(s, prev, weight_ref):
+    fine, mid, low, coef = (weight_ref[k] for k in range(4))
+    return (
+        fine * (s[0] - 0.5 * (prev + s[1])),
+        mid * (s[1] - 0.5 * (prev + s[3])),
+        fine * (s[2] - 0.5 * (s[1] + s[3])),
+        low * (s[3] - 0.5 * (prev + s[7])),
+        fine * (s[4] - 0.5 * (s[3] + s[5])),
+        mid * (s[5] - 0.5 * (s[3] + s[7])),
+        fine * (s[6] - 0.5 * (s[5] + s[7])),
+        coef * s[7],
+    )
+
+
+def pack_kernel(parity_ref, dens_ref, *refs):
     *ends, far_ref, near_ref = refs
-    strips = far_ref.shape[0]
+    many, strips = dens_ref.shape[:2]
     odd = parity_ref[0] == 1
     upper = lax.broadcasted_iota(jnp.int32, (TILE, LANES), 0) < HALF
 
     def body(j):
         heads, tails = ([ref[j] for ref in ends[e::2]] for e in range(2))
-        mix_next = jnp.where(upper, pltpu.roll(tails[2], HALF, 0), tails[1])
-        mix_prev = jnp.where(upper, heads[1], pltpu.roll(heads[2], HALF, 0))
-        to_next, to_prev = (tails[0], mix_next), (heads[0], mix_prev)
+        mix_next = jnp.where(upper, pltpu.roll(tails[1], HALF, 0), tails[0])
+        mix_prev = jnp.where(upper, heads[0], pltpu.roll(heads[1], HALF, 0))
+        to_next, to_prev = (dens_ref[many - 1, j], mix_next), (dens_ref[0, j], mix_prev)
         for k in range(2):
             at = pl.ds(k * TILE, TILE)
             far_ref[j, at] = jnp.where(odd, to_next[k], to_prev[k])
@@ -137,11 +151,14 @@
         at = spaced(j * TILE + t, many, strips * TILE)
         return [ref[at, :] for ref in refs]
 
-    def finish(j, new):
+    def emit(j, _, new):
         for t in range(TILE):
             out_ref[j, t] = new[t]
 
-    run_steps(strips, TILE, load, (state_a, state_b), coefs, finish, min(strips, UNROLL))
+    def last(source):
+        advance(0, strips, TILE, source, coefs, emit)
+
+    run_steps(strips, TILE, load, (state_a, state_b), coefs, last)
     coef = coef_ref[0].astype(jnp.float32)
     for down in range(3):
         keep = jnp.where(level_ref[0] >= depth - down, 1.0, 0.0)
@@ -150,25 +167,27 @@
     weight_ref[3] = jnp.full((many, LANES), coef)
 
 
-def edge_kernel(
-    per_chunk, parity_ref, me_ref, weight_ref, *refs
-):
-    ends, (inner_ref, far_ref, near_ref), out_refs = refs[:6], refs[6:9], refs[9:13]
-    slab, state_a, state_b, *coefs = refs[13:]
-    strips, _, many = inner_ref.shape[:3]
+def partners(parity):
+    return 0, 1 + parity, 2 - parity, 3
+
+
+def edge_kernel(per_chunk, parity_ref, me_ref, weight_ref, dens_ref, *refs):
+    many, strips = dens_ref.shape[:2]
     odd = parity_ref[0] == 1
+    ends, (state_ref, far_ref, near_ref), out_refs = refs[:4], refs[4:7], refs[7:11]
+    slab, state_a, state_b, *coefs = refs[11:]
 
     def stage(j):
         far, near = far_ref[j], near_ref[j]
         up, dn = jnp.where(odd, near, far), jnp.where(odd, far, near)
         up_mix, dn_mix = up[TILE:], dn[TILE:]
-        outer = (
-            (up[:TILE], dn[:TILE]),
-            (up_mix, dn_mix),
-            (pltpu.roll(up_mix, HALF, 0), pltpu.roll(dn_mix, HALF, 0)),
+        tiles = (
+            (up[:TILE], dens_ref[0, j], dens_ref[many - 1, j], dn[:TILE]),
+            (up_mix, ends[0][j], ends[1][j], dn_mix),
+            (pltpu.roll(up_mix, HALF, 0), ends[2][j], ends[3][j], pltpu.roll(dn_mix, HALF, 0)),
         )
-        for k, (before, after) in enumerate(outer):
-            for e, tile in enumerate((before, ends[2 * k][j], ends[2 * k + 1][j], after)):
+        for k, column in enumerate(tiles):
+            for e, tile in enumerate(column):
                 slab[k, j, e * TILE : (e + 1) * TILE] = tile
 
     per_strip(strips, stage, 4)
@@ -179,40 +198,28 @@
             slabs[pl.ds((k * strips + j) * SLAB + t, TILE, stride=HALF), :] for k in range(3)
         ]
 
-    fine, mid, low, coef = (weight_ref[k] for k in range(4))
     place = lax.broadcasted_iota(jnp.int32, (many, LANES), 0)
 
-    def finish(j, new):
-        s = [inner_ref[j, t] for t in range(TILE)]
+    def finish(out_ref, j, part, new):
+        s = [state_ref[j, t] for t in range(TILE)]
         for t in range(HALF):
             s[t] = jnp.where(place == 0, new[t][2:3], s[t])
-        for t in range(HALF):
             s[HALF + t] = jnp.where(place == many - 1, new[t][5:6], s[HALF + t])
         before = new[HALF - 1][1:2]
-        prev = jnp.where(place == 0, before, roll_rows(s[7], 1))
-        weighted = [
-            fine * (s[0] - 0.5 * (prev + s[1])),
-            mid * (s[1] - 0.5 * (prev + s[3])),
-            fine * (s[2] - 0.5 * (s[1] + s[3])),
-            low * (s[3] - 0.5 * (prev + s[7])),
-            fine * (s[4] - 0.5 * (s[3] + s[5])),
-            mid * (s[5] - 0.5 * (s[3] + s[7])),
-            fine * (s[6] - 0.5 * (s[5] + s[7])),
-            coef * s[7],
-        ]
-        away = (j // per_chunk) ^ me_ref[0]
-        part = lax.rem(j, per_chunk)
-        for k, ref in enumerate(out_refs):
-
-            @pl.when(away == k)
-            def _(ref=ref):
-                for t in range(TILE):
-                    ref[part * TILE + t] = weighted[t]
-                ref[per_chunk * TILE + part // many, pl.ds(lax.rem(part, many), 1), :] = (
-                    coef[0:1] * before
-                )
-
-    run_steps(strips, HALF, load, (state_a, state_b), coefs, finish, min(strips, UNROLL))
+        weighted = surpluses(s, jnp.where(place == 0, before, roll_rows(s[7], 1)), weight_ref)
+        for t in range(TILE):
+            out_ref[part * TILE + t] = weighted[t]
+        out_ref[per_chunk * TILE + part // many, pl.ds(lax.rem(part, many), 1), :] = (
+            weight_ref[3][0:1] * before
+        )
+
+    def last(source):
+        for out_ref, away in zip(out_refs, partners(parity_ref[0])):
+            first = (me_ref[0] ^ away) * per_chunk
+            emit = functools.partial(finish, out_ref)
+            advance(first, per_chunk, HALF, source, coefs, emit)
+
+    run_steps(strips, HALF, load, (state_a, state_b), coefs, last)
 
 
 def sum_kernel(*refs):
@@ -223,13 +230,13 @@
     out_ref[...] = total
 
 
-def nodal_kernel(per_chunk, me_ref, keep_ref, *refs):
+def nodal_kernel(per_chunk, parity_ref, me_ref, keep_ref, *refs):
     *totals, out_ref = refs
     many, strips = out_ref.shape[:2]
     out = flat(out_ref)
     fine, mid, low = (keep_ref[k] for k in range(3))
     place = lax.broadcasted_iota(jnp.int32, (many, LANES), 0)
-    for away, ref in enumerate(totals):
+    for ref, away in zip(totals, partners(parity_ref[0])):
         first = (me_ref[0] ^ away) * per_chunk
 
         def body(part, ref=ref, first=first):
@@ -283,11 +290,11 @@
     def vmem(*shape):
         return pltpu.VMEM(shape, jnp.float32)
 
-    ends = [x[at] for x in tiles for at in (0, many - 1)]
+    ends = [x[at] for x in tiles[1:] for at in (0, many - 1)]
     far, near = call(
         pack_kernel,
         [(strips, 2 * TILE, LANES)] * 2,
-        (parity, *ends),
+        (parity, tiles[0], *ends),
         1,
     )
     far_pairs = [(d, d + 1) for d in range(1, doms - 1, 2)]
@@ -296,20 +303,20 @@
         lax.ppermute(array, "dom", pairs + [(b, a) for a, b in pairs])
         for array, pairs in ((far, far_pairs), (near, near_pairs))
     )
-    inner, keep, weight = call(
+    place = (strips, TILE, many, LANES)
+    state, keep, weight = call(
         functools.partial(inner_kernel, depth),
-        [(strips, TILE, many, LANES), (3, many, LANES), (4, many, LANES)],
+        [place, (3, many, LANES), (4, many, LANES)],
         (levels, coefficient, *tiles),
         2,
-        [vmem(strips + 2, TILE, many, LANES)] * 2 + [vmem(strips, TILE, many, LANES)] * 4,
+        [vmem(strips + 2, *place[1:])] * 2 + [vmem(*place)] * 4,
         flops=40 * rows * cols,
     )
-
     chunk = (per_chunk * TILE + -(-per_chunk // many), many, LANES)
     own, *others = call(
         functools.partial(edge_kernel, per_chunk),
         [chunk] * SQUARE,
-        (parity, me, weight, *ends, inner, far, near),
+        (parity, me, weight, tiles[0], *ends, state, far, near),
         2,
         [vmem(3, strips, SLAB, LANES)]
         + [vmem(strips + 2, HALF, TILE, LANES)] * 2
@@ -317,21 +324,24 @@
         flops=40 * SLAB * cols,
     )
 
-    def swap(array, apart):
-        return lax.ppermute(array, "grp", [(g, g ^ apart) for g in range(grids)])
-
-    theirs = [swap(array, apart) for apart, array in enumerate(others, 1)]
+    def swap(array, meet):
+        devices = [(g, d) for g in range(grids) for d in range(doms)]
+        pairs = [(g * doms + d, (g ^ partners(d % 2)[meet]) * doms + d) for g, d in devices]
+        return lax.ppermute(array, ("grp", "dom"), pairs)
+
+    theirs = [swap(array, meet) for meet, array in enumerate(others, 1)]
     (total,) = call(sum_kernel, [chunk], (own, *theirs))
     apart = SQUARE
     while apart < grids:
-        (total,) = call(sum_kernel, [chunk], (total, swap(total, apart)))
+        other = lax.ppermute(total, "grp", [(g, g ^ apart) for g in range(grids)])
+        (total,) = call(sum_kernel, [chunk], (total, other))
         apart *= 2
-    totals = [total] + [swap(total, apart) for apart in range(1, SQUARE)]
+    totals = [total] + [swap(total, meet) for meet in range(1, SQUARE)]
     (nodal,) = call(
         functools.partial(nodal_kernel, per_chunk),
         [(many, strips, TILE, LANES)],
-        (me, keep, *totals),
-        1,
+        (parity, me, keep, *totals),
+        2,
     )
     return block_of(nodal)[None]
 

time: 41.9 us -> 38.7 us (0.924)
  waiting for transfers between devices: 17.4 us -> 16.1 us
  Pallas kernels: 5.14 us -> 3.97 us
  local copies, waits for them, and re-layouts: 3 us -> 2.19 us
    ppermute x7, waiting for transfers between devices: 17.4 us -> 16.1 us  [the longest x6 10.4 us: swap(): return lax.ppermute(array, ('grp', 'dom'), pairs)]
    pallas_call x6, Pallas kernels: 5.14 us -> 3.97 us  [call(): pl.pallas_call(kernel, out_shape=[jax.ShapeDtypeStruct(shape, jnp.float32...]
    squeeze x2 -> x1, local copies, waits for them, and re-layouts: 1.95 us -> 1.01 us  [on_device(): ends = [x[at] for x in tiles[1:] for at in (0, many - 1)]]
  transfers between devices with their start and end apart: 9 -> 9, of which waited for: 7 -> 7; matrix products, arithmetic and copies ran while one was open for 0% -> 0% of each run, Pallas kernels for 4% -> 5%
where the time goes in v8:
time: 38.7 us; the launch traced here: 38.5 us
  waiting for transfers between devices  16.1 us (42%)
  starting transfers between devices  14.8 us (38%)
  Pallas kernels  3.97 us (10%)
  local copies, waits for them, and re-layouts  2.19 us (6%)
  between operations  1.4 us (4%)
    ppermute x6, waiting for transfers between devices, swap(): return lax.ppermute(array, ('grp', 'dom'), pairs)  10.4 us
    ppermute x6, starting transfers between devices, swap(): return lax.ppermute(array, ('grp', 'dom'), pairs)  7.1 us
    ppermute x1, waiting for transfers between devices, on_device(): other = lax.ppermute(total, 'grp', [(g, g ^ apart) for g in range(grids)])  5.72 us
    ppermute x2, starting transfers between devices, on_device(): lax.ppermute(array, 'dom', pairs + [(b, a) for a, b in pairs])  5.06 us
    pallas_call x6, Pallas kernels, call(): pl.pallas_call(kernel, out_shape=[jax.ShapeDtypeStruct(shape, jnp.float32...  3.97 us
    ppermute x1, starting transfers between devices, on_device(): other = lax.ppermute(total, 'grp', [(g, g ^ apart) for g in range(grids)])  2.65 us
    unnamed x6, local copies, waits for them, and re-layouts  1.18 us
    squeeze x1, local copies, waits for them, and re-layouts, on_device(): ends = [x[at] for x in tiles[1:] for at in (0, many - 1)]  1.01 us
  transfers between devices with their start and end apart: 9, of which 7 were waited for; matrix products, arithmetic and copies ran while one was open for 0% of the time, Pallas kernels for 5%

profile of v8, /device:TPU:0, one launch (start us, length us, event | category | flops | bytes accessed | tf_op | source)
XLA Modules:
  0.0 38.5 jit_solution(18086400919033140483)
XLA Ops:
  0.0 0.0 copy-start
  0.0 1.0 %slice_bitcast_fusion = (f32[16,8,128]{2,1,0:T(8,128)S(1)}, f32[16,8,128]{2,1,0:T(8,128)S(1)}, f32[16,8,128]{2,1,0:T(8,128)S(1)}, f32[16,8,128]{2,1,0:T(8,128)S(1)}) fusion(f32[8,16,8,128]{3,2,1,0:T(8,128)} %bitcast.27, f32[8,16,8,128]{3,2,1,0:T(8,128)} %bitcast.25), kind=kLoop, calls=%fused_computation | loop fusion | bytes 524288 | tf_op jit(solution)/shard_map/squeeze | solution.py:293
  1.0 0.0 copy-start.1
  1.0 0.1 copy-done
  1.2 0.7 %collective-permute-start = (f32[16,16,128]{2,1,0:T(8,128)S(1)}, f32[16,16,128]{2,1,0:T(8,128)S(1)}, u32[]{:S(2)}, u32[]{:S(2)}) collective-permute-start(f32[16,16,128]{2,1,0:T(8,128)S(1)} %get-tuple-element.17), channel_id=1, source_target_pairs={{1,2},{2,1},{5,6},{6,5},{9,10},{10,9},{13,14},{14,13},{17,18},{18,... | collective-permute-start | bytes 393224 | tf_op jit(solution)/shard_map/ppermute | solution.py:303
  1.9 4.4 %collective-permute-start.1 = (f32[16,16,128]{2,1,0:T(8,128)S(1)}, f32[16,16,128]{2,1,0:T(8,128)S(1)}, u32[]{:S(2)}, u32[]{:S(2)}) collective-permute-start(f32[16,16,128]{2,1,0:T(8,128)S(1)} %get-tuple-element.18), channel_id=1, source_target_pairs={{0,1},{2,3},{1,0},{3,2},{4,5},{6,7},{5,4},{7,6},{8,9},{10,11},{9,8... | collective-permute-start | bytes 393224 | tf_op jit(solution)/shard_map/ppermute | solution.py:303
  7.6 0.0 copy-done.1
  7.6 0.0 copy-start.2
  7.6 1.0 %copy-done.2 = f32[1,64,2048]{2,1,0:T(8,128)S(1)} copy-done((f32[1,64,2048]{2,1,0:T(8,128)S(1)}, f32[1,64,2048]{2,1,0:T(8,128)}, u32[]{:S(2)}) %copy-start.2) | copy-done | bytes 524312
  8.6 1.9 %shard_map.55 = (f32[16,8,8,128]{3,2,1,0:T(8,128)S(1)}, f32[3,8,128]{2,1,0:T(8,128)S(1)}, f32[4,8,128]{2,1,0:T(8,128)S(1)}) custom-call(s32[1]{0:T(128)S(6)} %copy.6.level_ref, s32[1]{0:T(128)S(6)} %copy.7.coef_ref, f32[8,16,8,128]{3,2,1,0:T(8,128)S(1)} %bitcast.23, f32[8,16,8,128]{3,2,1,0:T(8,128)S(1)} %bitcast.26, f32[8,16,8,128]{3,2,1,0:T(8,128)S(1)} %bitcast.28), custom_call_target="tpu_custom_call" | custom-call | flops 5242880 | bytes 1572872 | tf_op jit(solution)/shard_map/pallas_call | solution.py:269
  10.5 0.0 collective-permute-done.refs_5_
  10.5 0.0 collective-permute-done.1.refs_6_
  10.5 0.9 %shard_map.57 = (f32[33,8,128]{2,1,0:T(8,128)S(1)}, f32[33,8,128]{2,1,0:T(8,128)S(1)}, f32[33,8,128]{2,1,0:T(8,128)S(1)}, f32[33,8,128]{2,1,0:T(8,128)S(1)}) custom-call(s32[1]{0:T(128)} %bitcast.parity_ref, s32[1]{0:T(128)} %bitcast.1.me_ref, f32[4,8,128]{2,1,0:T(8,128)S(1)} %get-tuple-element.15.weight_ref, f32[8,16,8,128]{3,2,1,0:T(8,128)S(1)} %bitcast.24, ...), custom_call_target="tpu_custom_call" | custom-call | flops 2621440 | bytes 1589256 | tf_op jit(solution)/shard_map/pallas_call | solution.py:269
  11.4 1.6 %collective-permute-start.2 = (f32[33,8,128]{2,1,0:T(8,128)S(1)}, f32[33,8,128]{2,1,0:T(8,128)S(1)}, u32[]{:S(2)}, u32[]{:S(2)}) collective-permute-start(f32[33,8,128]{2,1,0:T(8,128)S(1)} %get-tuple-element.20), channel_id=1, source_target_pairs={{0,4},{1,9},{2,6},{3,11},{4,0},{5,13},{6,2},{7,15},{8,12},{9,1},{1... | collective-permute-start | bytes 405512 | tf_op jit(solution)/shard_map/ppermute | solution.py:330
  12.9 1.6 %collective-permute-start.3 = (f32[33,8,128]{2,1,0:T(8,128)S(1)}, f32[33,8,128]{2,1,0:T(8,128)S(1)}, u32[]{:S(2)}, u32[]{:S(2)}) collective-permute-start(f32[33,8,128]{2,1,0:T(8,128)S(1)} %get-tuple-element.21), channel_id=1, source_target_pairs={{0,8},{1,5},{2,10},{3,7},{4,12},{5,1},{6,14},{7,3},{8,0},{9,13},{1... | collective-permute-start | bytes 405512 | tf_op jit(solution)/shard_map/ppermute | solution.py:330
  14.5 0.4 %collective-permute-start.4 = (f32[33,8,128]{2,1,0:T(8,128)S(1)}, f32[33,8,128]{2,1,0:T(8,128)S(1)}, u32[]{:S(2)}, u32[]{:S(2)}) collective-permute-start(f32[33,8,128]{2,1,0:T(8,128)S(1)} %get-tuple-element.22), channel_id=1, source_target_pairs={{0,12},{1,13},{2,14},{3,15},{4,8},{5,9},{6,10},{7,11},{8,4},{9,5},... | collective-permute-start | bytes 405512 | tf_op jit(solution)/shard_map/ppermute | solution.py:330
  14.9 2.6 %collective-permute-done.2.refs_1_ = f32[33,8,128]{2,1,0:T(8,128)S(1)} collective-permute-done((f32[33,8,128]{2,1,0:T(8,128)S(1)}, f32[33,8,128]{2,1,0:T(8,128)S(1)}, u32[]{:S(2)}, u32[]{:S(2)}) %collective-permute-start.2) | collective-permute-done | bytes 135200 | tf_op jit(solution)/shard_map/ppermute | solution.py:330
  17.6 1.8 %collective-permute-done.3.refs_2_ = f32[33,8,128]{2,1,0:T(8,128)S(1)} collective-permute-done((f32[33,8,128]{2,1,0:T(8,128)S(1)}, f32[33,8,128]{2,1,0:T(8,128)S(1)}, u32[]{:S(2)}, u32[]{:S(2)}) %collective-permute-start.3) | collective-permute-done | bytes 135200 | tf_op jit(solution)/shard_map/ppermute | solution.py:330
  19.4 1.5 %collective-permute-done.4.refs_3_ = f32[33,8,128]{2,1,0:T(8,128)S(1)} collective-permute-done((f32[33,8,128]{2,1,0:T(8,128)S(1)}, f32[33,8,128]{2,1,0:T(8,128)S(1)}, u32[]{:S(2)}, u32[]{:S(2)}) %collective-permute-start.4) | collective-permute-done | bytes 135200 | tf_op jit(solution)/shard_map/ppermute | solution.py:330
  20.8 0.1 shard_map.58.refs_0_
  20.9 2.6 %collective-permute-start.5 = (f32[33,8,128]{2,1,0:T(8,128)S(1)}, f32[33,8,128]{2,1,0:T(8,128)S(1)}, u32[]{:S(2)}, u32[]{:S(2)}) collective-permute-start(f32[33,8,128]{2,1,0:T(8,128)S(1)} %shard_map.58.refs_0_), channel_id=1, source_target_pairs={{0,16},{4,20},{8,24},{12,28},{16,0},{20,4},{24,8},{28,12},{1,17},{... | collective-permute-start | bytes 405512 | tf_op jit(solution)/shard_map/ppermute | solution.py:336
  23.5 5.7 %collective-permute-done.5.refs_1_ = f32[33,8,128]{2,1,0:T(8,128)S(1)} collective-permute-done((f32[33,8,128]{2,1,0:T(8,128)S(1)}, f32[33,8,128]{2,1,0:T(8,128)S(1)}, u32[]{:S(2)}, u32[]{:S(2)}) %collective-permute-start.5) | collective-permute-done | bytes 135200 | tf_op jit(solution)/shard_map/ppermute | solution.py:336
  29.3 0.1 collective-permute-start.8
  29.4 2.1 %collective-permute-start.7 = (f32[33,8,128]{2,1,0:T(8,128)S(1)}, f32[33,8,128]{2,1,0:T(8,128)S(1)}, u32[]{:S(2)}, u32[]{:S(2)}) collective-permute-start(f32[33,8,128]{2,1,0:T(8,128)S(1)} %shard_map.59.refs_0_), channel_id=1, source_target_pairs={{0,8},{1,5},{2,10},{3,7},{4,12},{5,1},{6,14},{7,3},{8,0},{9,13},{1... | collective-permute-start | bytes 405512 | tf_op jit(solution)/shard_map/ppermute | solution.py:330
  31.4 1.4 %collective-permute-start.6 = (f32[33,8,128]{2,1,0:T(8,128)S(1)}, f32[33,8,128]{2,1,0:T(8,128)S(1)}, u32[]{:S(2)}, u32[]{:S(2)}) collective-permute-start(f32[33,8,128]{2,1,0:T(8,128)S(1)} %shard_map.59.refs_0_), channel_id=1, source_target_pairs={{0,4},{1,9},{2,6},{3,11},{4,0},{5,13},{6,2},{7,15},{8,12},{9,1},{1... | collective-permute-start | bytes 405512 | tf_op jit(solution)/shard_map/ppermute | solution.py:330
  32.8 3.9 %collective-permute-done.8.refs_3_ = f32[33,8,128]{2,1,0:T(8,128)S(1)} collective-permute-done((f32[33,8,128]{2,1,0:T(8,128)S(1)}, f32[33,8,128]{2,1,0:T(8,128)S(1)}, u32[]{:S(2)}, u32[]{:S(2)}) %collective-permute-start.8) | collective-permute-done | bytes 135200 | tf_op jit(solution)/shard_map/ppermute | solution.py:330
  36.7 0.2 collective-permute-done.7.refs_2_
  37.0 0.4 collective-permute-done.6.refs_1_
  37.3 1.1 %shard_map.60 = f32[8,16,8,128]{3,2,1,0:T(8,128)} custom-call(s32[1]{0:T(128)} %bitcast.parity_ref, s32[1]{0:T(128)} %bitcast.1.me_ref, f32[3,8,128]{2,1,0:T(8,128)S(1)} %get-tuple-element.14.keep_ref, f32[33,8,128]{2,1,0:T(8,128)S(1)} %shard_map.59.refs_0_, f32[33,8,128]{2,1,0:T(8,128)S(1)} %collective-permute-done.6.refs_1_, ...), custom_call_target="tpu_custom_call" | custom-call | bytes 552968 | tf_op jit(solution)/shard_map/pallas_call | solution.py:269
  (2 shorter events, 0.1 us)
Async XLA Ops:
  0.0 1.2 %copy-start = (f32[1,64,2048]{2,1,0:T(8,128)S(1)}, f32[1,64,2048]{2,1,0:T(8,128)}, u32[]{:S(2)}) copy-start(f32[1,64,2048]{2,1,0:T(8,128)} %param.5) | copy-start | bytes 1572868
  1.0 6.6 %copy-start.1 = (f32[1,64,2048]{2,1,0:T(8,128)S(1)}, f32[1,64,2048]{2,1,0:T(8,128)}, u32[]{:S(2)}) copy-start(f32[1,64,2048]{2,1,0:T(8,128)} %param.6) | copy-start | bytes 1572868
  1.2 9.3 %collective-permute-start = (f32[16,16,128]{2,1,0:T(8,128)S(1)}, f32[16,16,128]{2,1,0:T(8,128)S(1)}, u32[]{:S(2)}, u32[]{:S(2)}) collective-permute-start(f32[16,16,128]{2,1,0:T(8,128)S(1)} %get-tuple-element.17), channel_id=1, source_target_pairs={{1,2},{2,1},{5,6},{6,5},{9,10},{10,9},{13,14},{14,13},{17,18},{18,... | collective-permute-start | bytes 393224 | tf_op jit(solution)/shard_map/ppermute | solution.py:303
  1.9 8.6 %collective-permute-start.1 = (f32[16,16,128]{2,1,0:T(8,128)S(1)}, f32[16,16,128]{2,1,0:T(8,128)S(1)}, u32[]{:S(2)}, u32[]{:S(2)}) collective-permute-start(f32[16,16,128]{2,1,0:T(8,128)S(1)} %get-tuple-element.18), channel_id=1, source_target_pairs={{0,1},{2,3},{1,0},{3,2},{4,5},{6,7},{5,4},{7,6},{8,9},{10,11},{9,8... | collective-permute-start | bytes 393224 | tf_op jit(solution)/shard_map/ppermute | solution.py:303
  7.6 1.0 %copy-start.2 = (f32[1,64,2048]{2,1,0:T(8,128)S(1)}, f32[1,64,2048]{2,1,0:T(8,128)}, u32[]{:S(2)}) copy-start(f32[1,64,2048]{2,1,0:T(8,128)} %param.7) | copy-start | bytes 1572868
  11.4 6.2 %collective-permute-start.2 = (f32[33,8,128]{2,1,0:T(8,128)S(1)}, f32[33,8,128]{2,1,0:T(8,128)S(1)}, u32[]{:S(2)}, u32[]{:S(2)}) collective-permute-start(f32[33,8,128]{2,1,0:T(8,128)S(1)} %get-tuple-element.20), channel_id=1, source_target_pairs={{0,4},{1,9},{2,6},{3,11},{4,0},{5,13},{6,2},{7,15},{8,12},{9,1},{1... | collective-permute-start | bytes 405512 | tf_op jit(solution)/shard_map/ppermute | solution.py:330
  12.9 6.4 %collective-permute-start.3 = (f32[33,8,128]{2,1,0:T(8,128)S(1)}, f32[33,8,128]{2,1,0:T(8,128)S(1)}, u32[]{:S(2)}, u32[]{:S(2)}) collective-permute-start(f32[33,8,128]{2,1,0:T(8,128)S(1)} %get-tuple-element.21), channel_id=1, source_target_pairs={{0,8},{1,5},{2,10},{3,7},{4,12},{5,1},{6,14},{7,3},{8,0},{9,13},{1... | collective-permute-start | bytes 405512 | tf_op jit(solution)/shard_map/ppermute | solution.py:330
  14.5 6.3 %collective-permute-start.4 = (f32[33,8,128]{2,1,0:T(8,128)S(1)}, f32[33,8,128]{2,1,0:T(8,128)S(1)}, u32[]{:S(2)}, u32[]{:S(2)}) collective-permute-start(f32[33,8,128]{2,1,0:T(8,128)S(1)} %get-tuple-element.22), channel_id=1, source_target_pairs={{0,12},{1,13},{2,14},{3,15},{4,8},{5,9},{6,10},{7,11},{8,4},{9,5},... | collective-permute-start | bytes 405512 | tf_op jit(solution)/shard_map/ppermute | solution.py:330
  20.9 8.4 %collective-permute-start.5 = (f32[33,8,128]{2,1,0:T(8,128)S(1)}, f32[33,8,128]{2,1,0:T(8,128)S(1)}, u32[]{:S(2)}, u32[]{:S(2)}) collective-permute-start(f32[33,8,128]{2,1,0:T(8,128)S(1)} %shard_map.58.refs_0_), channel_id=1, source_target_pairs={{0,16},{4,20},{8,24},{12,28},{16,0},{20,4},{24,8},{28,12},{1,17},{... | collective-permute-start | bytes 405512 | tf_op jit(solution)/shard_map/ppermute | solution.py:336
  29.3 7.4 %collective-permute-start.8 = (f32[33,8,128]{2,1,0:T(8,128)S(1)}, f32[33,8,128]{2,1,0:T(8,128)S(1)}, u32[]{:S(2)}, u32[]{:S(2)}) collective-permute-start(f32[33,8,128]{2,1,0:T(8,128)S(1)} %shard_map.59.refs_0_), channel_id=1, source_target_pairs={{0,12},{1,13},{2,14},{3,15},{4,8},{5,9},{6,10},{7,11},{8,4},{9,5},... | collective-permute-start | bytes 405512 | tf_op jit(solution)/shard_map/ppermute | solution.py:330
  29.4 7.6 %collective-permute-start.7 = (f32[33,8,128]{2,1,0:T(8,128)S(1)}, f32[33,8,128]{2,1,0:T(8,128)S(1)}, u32[]{:S(2)}, u32[]{:S(2)}) collective-permute-start(f32[33,8,128]{2,1,0:T(8,128)S(1)} %shard_map.59.refs_0_), channel_id=1, source_target_pairs={{0,8},{1,5},{2,10},{3,7},{4,12},{5,1},{6,14},{7,3},{8,0},{9,13},{1... | collective-permute-start | bytes 405512 | tf_op jit(solution)/shard_map/ppermute | solution.py:330
  31.4 5.9 %collective-permute-start.6 = (f32[33,8,128]{2,1,0:T(8,128)S(1)}, f32[33,8,128]{2,1,0:T(8,128)S(1)}, u32[]{:S(2)}, u32[]{:S(2)}) collective-permute-start(f32[33,8,128]{2,1,0:T(8,128)S(1)} %shard_map.59.refs_0_), channel_id=1, source_target_pairs={{0,4},{1,9},{2,6},{3,11},{4,0},{5,13},{6,2},{7,15},{8,12},{9,1},{1... | collective-permute-start | bytes 405512 | tf_op jit(solution)/shard_map/ppermute | solution.py:330

commit v9 on v8

--- a/solution.py
+++ b/solution.py
@@ -15,6 +15,7 @@
 SQUARE = 4
 UNROLL = 16
 VMEM_LIMIT = 40 * 1024 * 1024
+HALO_FLOPS = 4000
 
 
 def tiles_of(block):
@@ -107,8 +108,8 @@
     last(buffers[(STEPS - 1) % 2])
 
 
-def surpluses(s, prev, weight_ref):
-    fine, mid, low, coef = (weight_ref[k] for k in range(4))
+def surpluses(s, prev, weights):
+    fine, mid, low, coef = weights
     return (
         fine * (s[0] - 0.5 * (prev + s[1])),
         mid * (s[1] - 0.5 * (prev + s[3])),
@@ -140,10 +141,7 @@
     per_strip(strips, body, 4)
 
 
-def inner_kernel(
-    depth, level_ref, coef_ref, dens_ref, diff_ref, drift_ref, out_ref, keep_ref, weight_ref,
-    state_a, state_b, *coefs
-):
+def inner_kernel(dens_ref, diff_ref, drift_ref, out_ref, state_a, state_b, *coefs):
     many, strips = dens_ref.shape[:2]
     refs = [flat(ref) for ref in (dens_ref, diff_ref, drift_ref)]
 
@@ -159,19 +157,15 @@
         advance(0, strips, TILE, source, coefs, emit)
 
     run_steps(strips, TILE, load, (state_a, state_b), coefs, last)
-    coef = coef_ref[0].astype(jnp.float32)
-    for down in range(3):
-        keep = jnp.where(level_ref[0] >= depth - down, 1.0, 0.0)
-        keep_ref[down] = jnp.full((many, LANES), keep)
-        weight_ref[down] = jnp.full((many, LANES), keep * coef)
-    weight_ref[3] = jnp.full((many, LANES), coef)
 
 
 def partners(parity):
     return 0, 1 + parity, 2 - parity, 3
 
 
-def edge_kernel(per_chunk, parity_ref, me_ref, weight_ref, dens_ref, *refs):
+def edge_kernel(
+    per_chunk, depth, parity_ref, me_ref, level_ref, coef_ref, dens_ref, *refs
+):
     many, strips = dens_ref.shape[:2]
     odd = parity_ref[0] == 1
     ends, (state_ref, far_ref, near_ref), out_refs = refs[:4], refs[4:7], refs[7:11]
@@ -199,6 +193,8 @@
         ]
 
     place = lax.broadcasted_iota(jnp.int32, (many, LANES), 0)
+    coef = coef_ref[0].astype(jnp.float32)
+    weights = [jnp.where(level_ref[0] >= depth - down, coef, 0.0) for down in range(3)] + [coef]
 
     def finish(out_ref, j, part, new):
         s = [state_ref[j, t] for t in range(TILE)]
@@ -206,11 +202,11 @@
             s[t] = jnp.where(place == 0, new[t][2:3], s[t])
             s[HALF + t] = jnp.where(place == many - 1, new[t][5:6], s[HALF + t])
         before = new[HALF - 1][1:2]
-        weighted = surpluses(s, jnp.where(place == 0, before, roll_rows(s[7], 1)), weight_ref)
+        weighted = surpluses(s, jnp.where(place == 0, before, roll_rows(s[7], 1)), weights)
         for t in range(TILE):
             out_ref[part * TILE + t] = weighted[t]
         out_ref[per_chunk * TILE + part // many, pl.ds(lax.rem(part, many), 1), :] = (
-            weight_ref[3][0:1] * before
+            coef * before
         )
 
     def last(source):
@@ -230,23 +226,25 @@
     out_ref[...] = total
 
 
-def nodal_kernel(per_chunk, parity_ref, me_ref, keep_ref, *refs):
-    *totals, out_ref = refs
-    many, strips = out_ref.shape[:2]
-    out = flat(out_ref)
-    fine, mid, low = (keep_ref[k] for k in range(3))
+def nodal_kernel(per_chunk, depth, meets, parity_ref, me_ref, level_ref, *refs):
+    totals, (out_ref, values, sems) = refs[: len(meets)], refs[-3:]
+    many = values.shape[1]
+    level = level_ref[0]
+    fine, mid, low = (jnp.where(level >= depth - down, 1.0, 0.0) for down in range(3))
     place = lax.broadcasted_iota(jnp.int32, (many, LANES), 0)
-    for ref, away in zip(totals, partners(parity_ref[0])):
-        first = (me_ref[0] ^ away) * per_chunk
-
-        def body(part, ref=ref, first=first):
+    copies = []
+    for k, (ref, meet) in enumerate(zip(totals, meets)):
+        first = (me_ref[0] ^ partners(parity_ref[0])[meet]) * per_chunk
+        by_row = flat(values.at[k])
+
+        def body(part, ref=ref, by_row=by_row):
             w = [ref[part * TILE + t] for t in range(TILE)]
             before = ref[per_chunk * TILE + part // many, pl.ds(lax.rem(part, many), 1), :]
             prev = jnp.where(place == 0, before, roll_rows(w[7], 1))
             v3 = 0.5 * (prev + w[7]) + low * w[3]
             v1 = 0.5 * (prev + v3) + mid * w[1]
             v5 = 0.5 * (v3 + w[7]) + mid * w[5]
-            values = (
+            rows = (
                 0.5 * (prev + v1) + fine * w[0],
                 v1,
                 0.5 * (v1 + v3) + fine * w[2],
@@ -257,20 +255,35 @@
                 w[7],
             )
             for t in range(TILE):
-                out[spaced((first + part) * TILE + t, many, strips * TILE), :] = values[t]
+                by_row[spaced(part * TILE + t, many, per_chunk * TILE), :] = rows[t]
 
         per_strip(per_chunk, body, min(per_chunk, 4))
-
-
-def call(kernel, out_shapes, operands, in_smem=0, scratch=(), flops=0):
+        for m in range(many):
+            copy = pltpu.make_async_copy(
+                values.at[k, m], out_ref.at[m, pl.ds(first, per_chunk)], sems.at[k, m]
+            )
+            copy.start()
+            copies.append(copy)
+    for copy in copies:
+        copy.wait()
+
+
+def call(
+    kernel, out_shapes, operands, in_smem=0, scratch=(), flops=0, out_space=pltpu.VMEM, onto=None
+):
     spaces = [pltpu.SMEM] * in_smem + [pltpu.VMEM] * (len(operands) - in_smem)
+    alias = {}
+    if onto is not None:
+        alias = {len(operands): 0}
+        spaces, operands = spaces + [out_space], (*operands, onto)
     specs = [pl.BlockSpec(memory_space=space) for space in spaces]
     moved = 4 * sum(x.size for x in operands)
     return pl.pallas_call(
         kernel,
         out_shape=[jax.ShapeDtypeStruct(shape, jnp.float32) for shape in out_shapes],
         in_specs=specs,
-        out_specs=[pl.BlockSpec(memory_space=pltpu.VMEM) for _ in out_shapes],
+        out_specs=[pl.BlockSpec(memory_space=out_space) for _ in out_shapes],
+        input_output_aliases=alias,
         scratch_shapes=list(scratch),
         compiler_params=pltpu.CompilerParams(vmem_limit_bytes=VMEM_LIMIT),
         cost_estimate=pl.CostEstimate(flops=flops, bytes_accessed=moved, transcendentals=0),
@@ -296,6 +309,7 @@
         [(strips, 2 * TILE, LANES)] * 2,
         (parity, tiles[0], *ends),
         1,
+        flops=HALO_FLOPS * rows * cols,
     )
     far_pairs = [(d, d + 1) for d in range(1, doms - 1, 2)]
     near_pairs = [(d, d + 1) for d in range(0, doms, 2)]
@@ -304,20 +318,20 @@
         for array, pairs in ((far, far_pairs), (near, near_pairs))
     )
     place = (strips, TILE, many, LANES)
-    state, keep, weight = call(
-        functools.partial(inner_kernel, depth),
-        [place, (3, many, LANES), (4, many, LANES)],
-        (levels, coefficient, *tiles),
-        2,
+    (state,) = call(
+        inner_kernel,
+        [place],
+        tiles,
+        0,
         [vmem(strips + 2, *place[1:])] * 2 + [vmem(*place)] * 4,
         flops=40 * rows * cols,
     )
     chunk = (per_chunk * TILE + -(-per_chunk // many), many, LANES)
     own, *others = call(
-        functools.partial(edge_kernel, per_chunk),
+        functools.partial(edge_kernel, per_chunk, depth),
         [chunk] * SQUARE,
-        (parity, me, weight, tiles[0], *ends, state, far, near),
-        2,
+        (parity, me, levels, coefficient, tiles[0], *ends, state, far, near),
+        4,
         [vmem(3, strips, SLAB, LANES)]
         + [vmem(strips + 2, HALF, TILE, LANES)] * 2
         + [vmem(strips, HALF, TILE, LANES)] * 4,
@@ -337,12 +351,20 @@
         (total,) = call(sum_kernel, [chunk], (total, other))
         apart *= 2
     totals = [total] + [swap(total, meet) for meet in range(1, SQUARE)]
-    (nodal,) = call(
-        functools.partial(nodal_kernel, per_chunk),
-        [(many, strips, TILE, LANES)],
-        (parity, me, keep, *totals),
-        2,
-    )
+    nodal = None
+    for meets in ((0, 1, 2), (3,)):
+        (nodal,) = call(
+            functools.partial(nodal_kernel, per_chunk, depth, meets),
+            [(many, strips, TILE, LANES)],
+            (parity, me, levels, *(totals[meet] for meet in meets)),
+            3,
+            [
+                vmem(len(meets), many, per_chunk, TILE, LANES),
+                pltpu.SemaphoreType.DMA((len(meets), many)),
+            ],
+            out_space=pl.ANY,
+            onto=nodal,
+        )
     return block_of(nodal)[None]
 
 

time: 38.7 us -> 38.5 us (level)
  local copies, waits for them, and re-layouts: 2.19 us -> 1.17 us
  Pallas kernels: 3.97 us -> 4.73 us
    unnamed x6, local copies, waits for them, and re-layouts: 1.18 us -> 0.16 us
    pallas_call x6 -> x7, Pallas kernels: 3.97 us -> 4.73 us  [call(): pl.pallas_call(kernel, out_shape=[jax.ShapeDtypeStruct(shape, jnp.float32...]
  transfers between devices with their start and end apart: 9 -> 9, of which waited for: 7 -> 6; matrix products, arithmetic and copies ran while one was open for 0% -> 0% of each run, Pallas kernels for 5% -> 8%
where the time goes in v9:
time: 38.5 us; the launch traced here: 38.3 us
  waiting for transfers between devices  16.1 us (42%)
  starting transfers between devices  14.9 us (39%)
  Pallas kernels  4.73 us (12%)
  between operations  1.39 us (4%)
  local copies, waits for them, and re-layouts  1.17 us (3%)
    ppermute x6, waiting for transfers between devices, swap(): return lax.ppermute(array, ('grp', 'dom'), pairs)  10.4 us
    ppermute x6, starting transfers between devices, swap(): return lax.ppermute(array, ('grp', 'dom'), pairs)  7.11 us
    ppermute x1, waiting for transfers between devices, on_device(): other = lax.ppermute(total, 'grp', [(g, g ^ apart) for g in range(grids)])  5.69 us
    ppermute x2, starting transfers between devices, on_device(): lax.ppermute(array, 'dom', pairs + [(b, a) for a, b in pairs])  5.19 us
    pallas_call x7, Pallas kernels, call(): pl.pallas_call(kernel, out_shape=[jax.ShapeDtypeStruct(shape, jnp.float32...  4.73 us
    ppermute x1, starting transfers between devices, on_device(): other = lax.ppermute(total, 'grp', [(g, g ^ apart) for g in range(grids)])  2.65 us
    squeeze x1, local copies, waits for them, and re-layouts, on_device(): ends = [x[at] for x in tiles[1:] for at in (0, many - 1)]  1.01 us
  transfers between devices with their start and end apart: 9, of which 6 were waited for; matrix products, arithmetic and copies ran while one was open for 0% of the time, Pallas kernels for 8%

profile of v9, /device:TPU:0, one launch (start us, length us, event | category | flops | bytes accessed | tf_op | source)
XLA Modules:
  0.0 38.3 jit_solution(2781221391663498005)
XLA Ops:
  0.0 0.0 copy-start
  0.0 1.0 %slice_bitcast_fusion = (f32[16,8,128]{2,1,0:T(8,128)S(1)}, f32[16,8,128]{2,1,0:T(8,128)S(1)}, f32[16,8,128]{2,1,0:T(8,128)S(1)}, f32[16,8,128]{2,1,0:T(8,128)S(1)}) fusion(f32[8,16,8,128]{3,2,1,0:T(8,128)} %bitcast.25, f32[8,16,8,128]{3,2,1,0:T(8,128)} %bitcast.27), kind=kLoop, calls=%fused_computation | loop fusion | bytes 524288 | tf_op jit(solution)/shard_map/squeeze | solution.py:306
  1.0 0.1 copy-done
  1.2 0.0 copy-start.1
  1.2 0.0 copy-start.2
  1.2 0.8 %collective-permute-start = (f32[16,16,128]{2,1,0:T(8,128)S(1)}, f32[16,16,128]{2,1,0:T(8,128)S(1)}, u32[]{:S(2)}, u32[]{:S(2)}) collective-permute-start(f32[16,16,128]{2,1,0:T(8,128)S(1)} %get-tuple-element.11), channel_id=1, source_target_pairs={{1,2},{2,1},{5,6},{6,5},{9,10},{10,9},{13,14},{14,13},{17,18},{18,... | collective-permute-start | bytes 393224 | tf_op jit(solution)/shard_map/ppermute | solution.py:317
  2.0 4.4 %collective-permute-start.1 = (f32[16,16,128]{2,1,0:T(8,128)S(1)}, f32[16,16,128]{2,1,0:T(8,128)S(1)}, u32[]{:S(2)}, u32[]{:S(2)}) collective-permute-start(f32[16,16,128]{2,1,0:T(8,128)S(1)} %get-tuple-element.12), channel_id=1, source_target_pairs={{0,1},{2,3},{1,0},{3,2},{4,5},{6,7},{5,4},{7,6},{8,9},{10,11},{9,8... | collective-permute-start | bytes 393224 | tf_op jit(solution)/shard_map/ppermute | solution.py:317
  7.7 0.0 copy-done.1
  7.7 0.0 copy-done.2
  7.7 1.9 %shard_map.55.refs_4_ = f32[16,8,8,128]{3,2,1,0:T(8,128)S(1)} custom-call(f32[8,16,8,128]{3,2,1,0:T(8,128)S(1)} %bitcast.23, f32[8,16,8,128]{3,2,1,0:T(8,128)S(1)} %bitcast.28, f32[8,16,8,128]{3,2,1,0:T(8,128)S(1)} %bitcast.26), custom_call_target="tpu_custom_call" | custom-call | flops 5242880 | bytes 1572864 | tf_op jit(solution)/shard_map/pallas_call | solution.py:281
  9.6 0.0 collective-permute-done.refs_5_
  9.6 0.0 collective-permute-done.1.refs_6_
  9.6 0.9 %shard_map.57 = (f32[33,8,128]{2,1,0:T(8,128)S(1)}, f32[33,8,128]{2,1,0:T(8,128)S(1)}, f32[33,8,128]{2,1,0:T(8,128)S(1)}, f32[33,8,128]{2,1,0:T(8,128)S(1)}) custom-call(s32[1]{0:T(128)} %bitcast.parity_ref, s32[1]{0:T(128)} %bitcast.1.me_ref, s32[1]{0:T(128)S(6)} %copy.8.level_ref, s32[1]{0:T(128)S(6)} %copy.9.coef_ref, f32[8,16,8,128]{3,2,1,0:T(8,128)S(1)} %bitcast.24, ...), custom_call_target="tpu_custom_call" | custom-call | flops 2621440 | bytes 1572880 | tf_op jit(solution)/shard_map/pallas_call | solution.py:281
  10.5 1.6 %collective-permute-start.2 = (f32[33,8,128]{2,1,0:T(8,128)S(1)}, f32[33,8,128]{2,1,0:T(8,128)S(1)}, u32[]{:S(2)}, u32[]{:S(2)}) collective-permute-start(f32[33,8,128]{2,1,0:T(8,128)S(1)} %get-tuple-element.14), channel_id=1, source_target_pairs={{0,4},{1,9},{2,6},{3,11},{4,0},{5,13},{6,2},{7,15},{8,12},{9,1},{1... | collective-permute-start | bytes 405512 | tf_op jit(solution)/shard_map/ppermute | solution.py:344
  12.0 1.6 %collective-permute-start.3 = (f32[33,8,128]{2,1,0:T(8,128)S(1)}, f32[33,8,128]{2,1,0:T(8,128)S(1)}, u32[]{:S(2)}, u32[]{:S(2)}) collective-permute-start(f32[33,8,128]{2,1,0:T(8,128)S(1)} %get-tuple-element.15), channel_id=1, source_target_pairs={{0,8},{1,5},{2,10},{3,7},{4,12},{5,1},{6,14},{7,3},{8,0},{9,13},{1... | collective-permute-start | bytes 405512 | tf_op jit(solution)/shard_map/ppermute | solution.py:344
  13.6 0.4 %collective-permute-start.4 = (f32[33,8,128]{2,1,0:T(8,128)S(1)}, f32[33,8,128]{2,1,0:T(8,128)S(1)}, u32[]{:S(2)}, u32[]{:S(2)}) collective-permute-start(f32[33,8,128]{2,1,0:T(8,128)S(1)} %get-tuple-element.16), channel_id=1, source_target_pairs={{0,12},{1,13},{2,14},{3,15},{4,8},{5,9},{6,10},{7,11},{8,4},{9,5},... | collective-permute-start | bytes 405512 | tf_op jit(solution)/shard_map/ppermute | solution.py:344
  14.0 2.6 %collective-permute-done.2.refs_1_ = f32[33,8,128]{2,1,0:T(8,128)S(1)} collective-permute-done((f32[33,8,128]{2,1,0:T(8,128)S(1)}, f32[33,8,128]{2,1,0:T(8,128)S(1)}, u32[]{:S(2)}, u32[]{:S(2)}) %collective-permute-start.2) | collective-permute-done | bytes 135200 | tf_op jit(solution)/shard_map/ppermute | solution.py:344
  16.7 1.8 %collective-permute-done.3.refs_2_ = f32[33,8,128]{2,1,0:T(8,128)S(1)} collective-permute-done((f32[33,8,128]{2,1,0:T(8,128)S(1)}, f32[33,8,128]{2,1,0:T(8,128)S(1)}, u32[]{:S(2)}, u32[]{:S(2)}) %collective-permute-start.3) | collective-permute-done | bytes 135200 | tf_op jit(solution)/shard_map/ppermute | solution.py:344
  18.5 1.5 %collective-permute-done.4.refs_3_ = f32[33,8,128]{2,1,0:T(8,128)S(1)} collective-permute-done((f32[33,8,128]{2,1,0:T(8,128)S(1)}, f32[33,8,128]{2,1,0:T(8,128)S(1)}, u32[]{:S(2)}, u32[]{:S(2)}) %collective-permute-start.4) | collective-permute-done | bytes 135200 | tf_op jit(solution)/shard_map/ppermute | solution.py:344
  20.0 2.7 %collective-permute-start.5 = (f32[33,8,128]{2,1,0:T(8,128)S(1)}, f32[33,8,128]{2,1,0:T(8,128)S(1)}, u32[]{:S(2)}, u32[]{:S(2)}) collective-permute-start(f32[33,8,128]{2,1,0:T(8,128)S(1)} %shard_map.58.refs_0_), channel_id=1, source_target_pairs={{0,16},{4,20},{8,24},{12,28},{16,0},{20,4},{24,8},{28,12},{1,17},{... | collective-permute-start | bytes 405512 | tf_op jit(solution)/shard_map/ppermute | solution.py:350
  22.6 5.7 %collective-permute-done.5.refs_1_ = f32[33,8,128]{2,1,0:T(8,128)S(1)} collective-permute-done((f32[33,8,128]{2,1,0:T(8,128)S(1)}, f32[33,8,128]{2,1,0:T(8,128)S(1)}, u32[]{:S(2)}, u32[]{:S(2)}) %collective-permute-start.5) | collective-permute-done | bytes 135200 | tf_op jit(solution)/shard_map/ppermute | solution.py:350
  28.3 0.1 collective-permute-start.8
  28.4 0.7 %collective-permute-start.7 = (f32[33,8,128]{2,1,0:T(8,128)S(1)}, f32[33,8,128]{2,1,0:T(8,128)S(1)}, u32[]{:S(2)}, u32[]{:S(2)}) collective-permute-start(f32[33,8,128]{2,1,0:T(8,128)S(1)} %shard_map.59.refs_0_), channel_id=1, source_target_pairs={{0,4},{1,9},{2,6},{3,11},{4,0},{5,13},{6,2},{7,15},{8,12},{9,1},{1... | collective-permute-start | bytes 405512 | tf_op jit(solution)/shard_map/ppermute | solution.py:344
  29.1 2.8 %collective-permute-start.6 = (f32[33,8,128]{2,1,0:T(8,128)S(1)}, f32[33,8,128]{2,1,0:T(8,128)S(1)}, u32[]{:S(2)}, u32[]{:S(2)}) collective-permute-start(f32[33,8,128]{2,1,0:T(8,128)S(1)} %shard_map.59.refs_0_), channel_id=1, source_target_pairs={{0,12},{1,13},{2,14},{3,15},{4,8},{5,9},{6,10},{7,11},{8,4},{9,5},... | collective-permute-start | bytes 405512 | tf_op jit(solution)/shard_map/ppermute | solution.py:344
  31.9 3.0 %collective-permute-done.8.refs_2_ = f32[33,8,128]{2,1,0:T(8,128)S(1)} collective-permute-done((f32[33,8,128]{2,1,0:T(8,128)S(1)}, f32[33,8,128]{2,1,0:T(8,128)S(1)}, u32[]{:S(2)}, u32[]{:S(2)}) %collective-permute-start.8) | collective-permute-done | bytes 135200 | tf_op jit(solution)/shard_map/ppermute | solution.py:344
  34.9 0.0 collective-permute-done.7.refs_1_
  34.9 1.1 %shard_map.60.refs_1_ = f32[8,16,8,128]{3,2,1,0:T(8,128)} custom-call(s32[1]{0:T(128)} %bitcast.parity_ref, s32[1]{0:T(128)} %bitcast.1.me_ref, s32[1]{0:T(128)S(6)} %copy.8.level_ref, f32[33,8,128]{2,1,0:T(8,128)S(1)} %shard_map.59.refs_0_, f32[33,8,128]{2,1,0:T(8,128)S(1)} %collective-permute-done.7.refs_1_, f32[33,8,128]{2,1,0:T(8,128)S(1)} %collective-permute-done.8.refs_2_), custom_call_target="tpu_custom_call" | custom-call | bytes 405516 | tf_op jit(solution)/shard_map/pallas_call | solution.py:281
  36.0 1.5 %collective-permute-done.6.refs_0_ = f32[33,8,128]{2,1,0:T(8,128)S(1)} collective-permute-done((f32[33,8,128]{2,1,0:T(8,128)S(1)}, f32[33,8,128]{2,1,0:T(8,128)S(1)}, u32[]{:S(2)}, u32[]{:S(2)}) %collective-permute-start.6) | collective-permute-done | bytes 135200 | tf_op jit(solution)/shard_map/ppermute | solution.py:344
  37.5 0.8 %shard_map.61 = f32[8,16,8,128]{3,2,1,0:T(8,128)} custom-call(s32[1]{0:T(128)} %bitcast.parity_ref, s32[1]{0:T(128)} %bitcast.1.me_ref, s32[1]{0:T(128)S(6)} %copy.8.level_ref, f32[33,8,128]{2,1,0:T(8,128)S(1)} %collective-permute-done.6.refs_0_, f32[8,16,8,128]{3,2,1,0:T(8,128)} %shard_map.60.refs_1_), custom_call_target="tpu_custom_call", output_to_operand_aliasing={{}: (4, {})} | custom-call | bytes 659468 | tf_op jit(solution)/shard_map/pallas_call | solution.py:281
  (3 shorter events, 0.1 us)
Async XLA Ops:
  0.0 1.2 %copy-start = (f32[1,64,2048]{2,1,0:T(8,128)S(1)}, f32[1,64,2048]{2,1,0:T(8,128)}, u32[]{:S(2)}) copy-start(f32[1,64,2048]{2,1,0:T(8,128)} %param.5) | copy-start | bytes 1572868
  1.2 6.5 %copy-start.1 = (f32[1,64,2048]{2,1,0:T(8,128)S(1)}, f32[1,64,2048]{2,1,0:T(8,128)}, u32[]{:S(2)}) copy-start(f32[1,64,2048]{2,1,0:T(8,128)} %param.7) | copy-start | bytes 1572868
  1.2 6.6 %copy-start.2 = (f32[1,64,2048]{2,1,0:T(8,128)S(1)}, f32[1,64,2048]{2,1,0:T(8,128)}, u32[]{:S(2)}) copy-start(f32[1,64,2048]{2,1,0:T(8,128)} %param.6) | copy-start | bytes 1572868
  1.2 8.4 %collective-permute-start = (f32[16,16,128]{2,1,0:T(8,128)S(1)}, f32[16,16,128]{2,1,0:T(8,128)S(1)}, u32[]{:S(2)}, u32[]{:S(2)}) collective-permute-start(f32[16,16,128]{2,1,0:T(8,128)S(1)} %get-tuple-element.11), channel_id=1, source_target_pairs={{1,2},{2,1},{5,6},{6,5},{9,10},{10,9},{13,14},{14,13},{17,18},{18,... | collective-permute-start | bytes 393224 | tf_op jit(solution)/shard_map/ppermute | solution.py:317
  2.0 7.6 %collective-permute-start.1 = (f32[16,16,128]{2,1,0:T(8,128)S(1)}, f32[16,16,128]{2,1,0:T(8,128)S(1)}, u32[]{:S(2)}, u32[]{:S(2)}) collective-permute-start(f32[16,16,128]{2,1,0:T(8,128)S(1)} %get-tuple-element.12), channel_id=1, source_target_pairs={{0,1},{2,3},{1,0},{3,2},{4,5},{6,7},{5,4},{7,6},{8,9},{10,11},{9,8... | collective-permute-start | bytes 393224 | tf_op jit(solution)/shard_map/ppermute | solution.py:317
  10.5 6.2 %collective-permute-start.2 = (f32[33,8,128]{2,1,0:T(8,128)S(1)}, f32[33,8,128]{2,1,0:T(8,128)S(1)}, u32[]{:S(2)}, u32[]{:S(2)}) collective-permute-start(f32[33,8,128]{2,1,0:T(8,128)S(1)} %get-tuple-element.14), channel_id=1, source_target_pairs={{0,4},{1,9},{2,6},{3,11},{4,0},{5,13},{6,2},{7,15},{8,12},{9,1},{1... | collective-permute-start | bytes 405512 | tf_op jit(solution)/shard_map/ppermute | solution.py:344
  12.0 6.4 %collective-permute-start.3 = (f32[33,8,128]{2,1,0:T(8,128)S(1)}, f32[33,8,128]{2,1,0:T(8,128)S(1)}, u32[]{:S(2)}, u32[]{:S(2)}) collective-permute-start(f32[33,8,128]{2,1,0:T(8,128)S(1)} %get-tuple-element.15), channel_id=1, source_target_pairs={{0,8},{1,5},{2,10},{3,7},{4,12},{5,1},{6,14},{7,3},{8,0},{9,13},{1... | collective-permute-start | bytes 405512 | tf_op jit(solution)/shard_map/ppermute | solution.py:344
  13.6 6.3 %collective-permute-start.4 = (f32[33,8,128]{2,1,0:T(8,128)S(1)}, f32[33,8,128]{2,1,0:T(8,128)S(1)}, u32[]{:S(2)}, u32[]{:S(2)}) collective-permute-start(f32[33,8,128]{2,1,0:T(8,128)S(1)} %get-tuple-element.16), channel_id=1, source_target_pairs={{0,12},{1,13},{2,14},{3,15},{4,8},{5,9},{6,10},{7,11},{8,4},{9,5},... | collective-permute-start | bytes 405512 | tf_op jit(solution)/shard_map/ppermute | solution.py:344
  20.0 8.3 %collective-permute-start.5 = (f32[33,8,128]{2,1,0:T(8,128)S(1)}, f32[33,8,128]{2,1,0:T(8,128)S(1)}, u32[]{:S(2)}, u32[]{:S(2)}) collective-permute-start(f32[33,8,128]{2,1,0:T(8,128)S(1)} %shard_map.58.refs_0_), channel_id=1, source_target_pairs={{0,16},{4,20},{8,24},{12,28},{16,0},{20,4},{24,8},{28,12},{1,17},{... | collective-permute-start | bytes 405512 | tf_op jit(solution)/shard_map/ppermute | solution.py:350
  28.3 6.6 %collective-permute-start.8 = (f32[33,8,128]{2,1,0:T(8,128)S(1)}, f32[33,8,128]{2,1,0:T(8,128)S(1)}, u32[]{:S(2)}, u32[]{:S(2)}) collective-permute-start(f32[33,8,128]{2,1,0:T(8,128)S(1)} %shard_map.59.refs_0_), channel_id=1, source_target_pairs={{0,8},{1,5},{2,10},{3,7},{4,12},{5,1},{6,14},{7,3},{8,0},{9,13},{1... | collective-permute-start | bytes 405512 | tf_op jit(solution)/shard_map/ppermute | solution.py:344
  28.4 6.5 %collective-permute-start.7 = (f32[33,8,128]{2,1,0:T(8,128)S(1)}, f32[33,8,128]{2,1,0:T(8,128)S(1)}, u32[]{:S(2)}, u32[]{:S(2)}) collective-permute-start(f32[33,8,128]{2,1,0:T(8,128)S(1)} %shard_map.59.refs_0_), channel_id=1, source_target_pairs={{0,4},{1,9},{2,6},{3,11},{4,0},{5,13},{6,2},{7,15},{8,12},{9,1},{1... | collective-permute-start | bytes 405512 | tf_op jit(solution)/shard_map/ppermute | solution.py:344
  29.1 8.4 %collective-permute-start.6 = (f32[33,8,128]{2,1,0:T(8,128)S(1)}, f32[33,8,128]{2,1,0:T(8,128)S(1)}, u32[]{:S(2)}, u32[]{:S(2)}) collective-permute-start(f32[33,8,128]{2,1,0:T(8,128)S(1)} %shard_map.59.refs_0_), channel_id=1, source_target_pairs={{0,12},{1,13},{2,14},{3,15},{4,8},{5,9},{6,10},{7,11},{8,4},{9,5},... | collective-permute-start | bytes 405512 | tf_op jit(solution)/shard_map/ppermute | solution.py:344

commit v10 on v9

--- a/solution.py
+++ b/solution.py
@@ -122,10 +122,10 @@
     )
 
 
-def pack_kernel(parity_ref, dens_ref, *refs):
+def pack_kernel(dom_ref, dens_ref, *refs):
     *ends, far_ref, near_ref = refs
     many, strips = dens_ref.shape[:2]
-    odd = parity_ref[0] == 1
+    odd = dom_ref[0] % 2 == 1
     upper = lax.broadcasted_iota(jnp.int32, (TILE, LANES), 0) < HALF
 
     def body(j):
@@ -159,21 +159,23 @@
     run_steps(strips, TILE, load, (state_a, state_b), coefs, last)
 
 
-def partners(parity):
-    return 0, 1 + parity, 2 - parity, 3
+def partners(dom):
+    return 0, 1 + dom % 2, 2 - dom % 2, 3
 
 
 def edge_kernel(
-    per_chunk, depth, parity_ref, me_ref, level_ref, coef_ref, dens_ref, *refs
+    per_chunk, depth, doms, dom_ref, me_ref, level_ref, coef_ref, dens_ref, *refs
 ):
     many, strips = dens_ref.shape[:2]
-    odd = parity_ref[0] == 1
+    dom = dom_ref[0]
+    odd = dom % 2 == 1
     ends, (state_ref, far_ref, near_ref), out_refs = refs[:4], refs[4:7], refs[7:11]
     slab, state_a, state_b, *coefs = refs[11:]
 
     def stage(j):
         far, near = far_ref[j], near_ref[j]
-        up, dn = jnp.where(odd, near, far), jnp.where(odd, far, near)
+        up = jnp.where(dom == 0, 0.0, jnp.where(odd, near, far))
+        dn = jnp.where(dom == doms - 1, 0.0, jnp.where(odd, far, near))
         up_mix, dn_mix = up[TILE:], dn[TILE:]
         tiles = (
             (up[:TILE], dens_ref[0, j], dens_ref[many - 1, j], dn[:TILE]),
@@ -210,7 +212,7 @@
         )
 
     def last(source):
-        for out_ref, away in zip(out_refs, partners(parity_ref[0])):
+        for out_ref, away in zip(out_refs, partners(dom_ref[0])):
             first = (me_ref[0] ^ away) * per_chunk
             emit = functools.partial(finish, out_ref)
             advance(first, per_chunk, HALF, source, coefs, emit)
@@ -226,15 +228,15 @@
     out_ref[...] = total
 
 
-def nodal_kernel(per_chunk, depth, meets, parity_ref, me_ref, level_ref, *refs):
-    totals, (out_ref, values, sems) = refs[: len(meets)], refs[-3:]
+def nodal_kernel(per_chunk, depth, dom_ref, me_ref, level_ref, *refs):
+    *totals, out_ref, values, sems = refs
     many = values.shape[1]
     level = level_ref[0]
     fine, mid, low = (jnp.where(level >= depth - down, 1.0, 0.0) for down in range(3))
     place = lax.broadcasted_iota(jnp.int32, (many, LANES), 0)
     copies = []
-    for k, (ref, meet) in enumerate(zip(totals, meets)):
-        first = (me_ref[0] ^ partners(parity_ref[0])[meet]) * per_chunk
+    for k, (ref, away) in enumerate(zip(totals, partners(dom_ref[0]))):
+        first = (me_ref[0] ^ away) * per_chunk
         by_row = flat(values.at[k])
 
         def body(part, ref=ref, by_row=by_row):
@@ -269,13 +271,9 @@
 
 
 def call(
-    kernel, out_shapes, operands, in_smem=0, scratch=(), flops=0, out_space=pltpu.VMEM, onto=None
+    kernel, out_shapes, operands, in_smem=0, scratch=(), flops=0, out_space=pltpu.VMEM
 ):
     spaces = [pltpu.SMEM] * in_smem + [pltpu.VMEM] * (len(operands) - in_smem)
-    alias = {}
-    if onto is not None:
-        alias = {len(operands): 0}
-        spaces, operands = spaces + [out_space], (*operands, onto)
     specs = [pl.BlockSpec(memory_space=space) for space in spaces]
     moved = 4 * sum(x.size for x in operands)
     return pl.pallas_call(
@@ -283,7 +281,6 @@
         out_shape=[jax.ShapeDtypeStruct(shape, jnp.float32) for shape in out_shapes],
         in_specs=specs,
         out_specs=[pl.BlockSpec(memory_space=out_space) for _ in out_shapes],
-        input_output_aliases=alias,
         scratch_shapes=list(scratch),
         compiler_params=pltpu.CompilerParams(vmem_limit_bytes=VMEM_LIMIT),
         cost_estimate=pl.CostEstimate(flops=flops, bytes_accessed=moved, transcendentals=0),
@@ -298,7 +295,7 @@
     depth = (rows * doms).bit_length() - 1
     tiles = [tiles_of(x[0]) for x in (density, diffusion, drift_speed)]
     me = (lax.axis_index("grp") % SQUARE).astype(jnp.int32)[None]
-    parity = (lax.axis_index("dom") % 2).astype(jnp.int32)[None]
+    dom = lax.axis_index("dom").astype(jnp.int32)[None]
 
     def vmem(*shape):
         return pltpu.VMEM(shape, jnp.float32)
@@ -307,15 +304,14 @@
     far, near = call(
         pack_kernel,
         [(strips, 2 * TILE, LANES)] * 2,
-        (parity, tiles[0], *ends),
+        (dom, tiles[0], *ends),
         1,
         flops=HALO_FLOPS * rows * cols,
     )
-    far_pairs = [(d, d + 1) for d in range(1, doms - 1, 2)]
-    near_pairs = [(d, d + 1) for d in range(0, doms, 2)]
+    near_pairs = [(d, d ^ 1) for d in range(doms)]
+    far_pairs = [(d, min(max((d - 1 ^ 1) + 1, 0), doms - 1)) for d in range(doms)]
     far, near = (
-        lax.ppermute(array, "dom", pairs + [(b, a) for a, b in pairs])
-        for array, pairs in ((far, far_pairs), (near, near_pairs))
+        lax.ppermute(array, "dom", pairs) for array, pairs in ((far, far_pairs), (near, near_pairs))
     )
     place = (strips, TILE, many, LANES)
     (state,) = call(
@@ -328,9 +324,9 @@
     )
     chunk = (per_chunk * TILE + -(-per_chunk // many), many, LANES)
     own, *others = call(
-        functools.partial(edge_kernel, per_chunk, depth),
+        functools.partial(edge_kernel, per_chunk, depth, doms),
         [chunk] * SQUARE,
-        (parity, me, levels, coefficient, tiles[0], *ends, state, far, near),
+        (dom, me, levels, coefficient, tiles[0], *ends, state, far, near),
         4,
         [vmem(3, strips, SLAB, LANES)]
         + [vmem(strips + 2, HALF, TILE, LANES)] * 2
@@ -351,20 +347,14 @@
         (total,) = call(sum_kernel, [chunk], (total, other))
         apart *= 2
     totals = [total] + [swap(total, meet) for meet in range(1, SQUARE)]
-    nodal = None
-    for meets in ((0, 1, 2), (3,)):
-        (nodal,) = call(
-            functools.partial(nodal_kernel, per_chunk, depth, meets),
-            [(many, strips, TILE, LANES)],
-            (parity, me, levels, *(totals[meet] for meet in meets)),
-            3,
-            [
-                vmem(len(meets), many, per_chunk, TILE, LANES),
-                pltpu.SemaphoreType.DMA((len(meets), many)),
-            ],
-            out_space=pl.ANY,
-            onto=nodal,
-        )
+    (nodal,) = call(
+        functools.partial(nodal_kernel, per_chunk, depth),
+        [(many, strips, TILE, LANES)],
+        (dom, me, levels, *totals),
+        3,
+        [vmem(SQUARE, many, per_chunk, TILE, LANES), pltpu.SemaphoreType.DMA((SQUARE, many))],
+        out_space=pl.ANY,
+    )
     return block_of(nodal)[None]
 
 

time: 38.5 us -> 37.9 us (0.984)
  Pallas kernels: 4.73 us -> 4.1 us
    pallas_call x7 -> x6, Pallas kernels: 4.73 us -> 4.1 us  [call(): pl.pallas_call(kernel, out_shape=[jax.ShapeDtypeStruct(shape, jnp.float32...]
  transfers between devices with their start and end apart: 9 -> 9, of which waited for: 6 -> 7; matrix products, arithmetic and copies ran while one was open for 0% -> 0% of each run, Pallas kernels for 8% -> 5%
where the time goes in v10:
time: 37.9 us; the launch traced here: 37.7 us
  waiting for transfers between devices  16.1 us (42%)
  starting transfers between devices  14.9 us (39%)
  Pallas kernels  4.1 us (11%)
  between operations  1.39 us (4%)
  local copies, waits for them, and re-layouts  1.17 us (3%)
    ppermute x6, waiting for transfers between devices, swap(): return lax.ppermute(array, ('grp', 'dom'), pairs)  10.4 us
    ppermute x6, starting transfers between devices, swap(): return lax.ppermute(array, ('grp', 'dom'), pairs)  7.1 us
    ppermute x1, waiting for transfers between devices, on_device(): other = lax.ppermute(total, 'grp', [(g, g ^ apart) for g in range(grids)])  5.72 us
    ppermute x2, starting transfers between devices, on_device(): lax.ppermute(array, 'dom', pairs)  5.19 us
    pallas_call x6, Pallas kernels, call(): pl.pallas_call(kernel, out_shape=[jax.ShapeDtypeStruct(shape, jnp.float32...  4.1 us
    ppermute x1, starting transfers between devices, on_device(): other = lax.ppermute(total, 'grp', [(g, g ^ apart) for g in range(grids)])  2.65 us
    squeeze x1, local copies, waits for them, and re-layouts, on_device(): ends = [x[at] for x in tiles[1:] for at in (0, many - 1)]  1.01 us
  transfers between devices with their start and end apart: 9, of which 7 were waited for; matrix products, arithmetic and copies ran while one was open for 0% of the time, Pallas kernels for 5%

profile of v10, /device:TPU:0, one launch (start us, length us, event | category | flops | bytes accessed | tf_op | source)
XLA Modules:
  0.0 37.7 jit_solution(2508012199505272859)
XLA Ops:
  0.0 0.0 copy-start
  0.0 1.0 %slice_bitcast_fusion = (f32[16,8,128]{2,1,0:T(8,128)S(1)}, f32[16,8,128]{2,1,0:T(8,128)S(1)}, f32[16,8,128]{2,1,0:T(8,128)S(1)}, f32[16,8,128]{2,1,0:T(8,128)S(1)}) fusion(f32[8,16,8,128]{3,2,1,0:T(8,128)} %bitcast.25, f32[8,16,8,128]{3,2,1,0:T(8,128)} %bitcast.27), kind=kLoop, calls=%fused_computation | loop fusion | bytes 524288 | tf_op jit(solution)/shard_map/squeeze | solution.py:303
  1.0 0.1 copy-done
  1.2 0.0 copy-start.1
  1.2 0.0 copy-start.2
  1.2 0.8 %collective-permute-start = (f32[16,16,128]{2,1,0:T(8,128)S(1)}, f32[16,16,128]{2,1,0:T(8,128)S(1)}, u32[]{:S(2)}, u32[]{:S(2)}) collective-permute-start(f32[16,16,128]{2,1,0:T(8,128)S(1)} %get-tuple-element.11), channel_id=1, source_target_pairs={{0,0},{1,2},{2,1},{3,3},{4,4},{5,6},{6,5},{7,7},{8,8},{9,10},{10,9... | collective-permute-start | bytes 393224 | tf_op jit(solution)/shard_map/ppermute | solution.py:314
  2.0 4.4 %collective-permute-start.1 = (f32[16,16,128]{2,1,0:T(8,128)S(1)}, f32[16,16,128]{2,1,0:T(8,128)S(1)}, u32[]{:S(2)}, u32[]{:S(2)}) collective-permute-start(f32[16,16,128]{2,1,0:T(8,128)S(1)} %get-tuple-element.12), channel_id=1, source_target_pairs={{0,1},{1,0},{2,3},{3,2},{4,5},{5,4},{6,7},{7,6},{8,9},{9,8},{10,11... | collective-permute-start | bytes 393224 | tf_op jit(solution)/shard_map/ppermute | solution.py:314
  7.7 0.0 copy-done.1
  7.7 0.0 copy-done.2
  7.7 1.9 %shard_map.55.refs_4_ = f32[16,8,8,128]{3,2,1,0:T(8,128)S(1)} custom-call(f32[8,16,8,128]{3,2,1,0:T(8,128)S(1)} %bitcast.23, f32[8,16,8,128]{3,2,1,0:T(8,128)S(1)} %bitcast.28, f32[8,16,8,128]{3,2,1,0:T(8,128)S(1)} %bitcast.26), custom_call_target="tpu_custom_call" | custom-call | flops 5242880 | bytes 1572864 | tf_op jit(solution)/shard_map/pallas_call | solution.py:279
  9.6 0.0 collective-permute-done.refs_5_
  9.6 0.0 collective-permute-done.1.refs_6_
  9.6 0.9 %shard_map.57 = (f32[33,8,128]{2,1,0:T(8,128)S(1)}, f32[33,8,128]{2,1,0:T(8,128)S(1)}, f32[33,8,128]{2,1,0:T(8,128)S(1)}, f32[33,8,128]{2,1,0:T(8,128)S(1)}) custom-call(s32[1]{0:T(128)} %bitcast.dom_ref, s32[1]{0:T(128)} %bitcast.1.me_ref, s32[1]{0:T(128)S(6)} %copy.6.level_ref, s32[1]{0:T(128)S(6)} %copy.7.coef_ref, f32[8,16,8,128]{3,2,1,0:T(8,128)S(1)} %bitcast.24, ...), custom_call_target="tpu_custom_call" | custom-call | flops 2621440 | bytes 1572880 | tf_op jit(solution)/shard_map/pallas_call | solution.py:279
  10.5 1.6 %collective-permute-start.2 = (f32[33,8,128]{2,1,0:T(8,128)S(1)}, f32[33,8,128]{2,1,0:T(8,128)S(1)}, u32[]{:S(2)}, u32[]{:S(2)}) collective-permute-start(f32[33,8,128]{2,1,0:T(8,128)S(1)} %get-tuple-element.14), channel_id=1, source_target_pairs={{0,4},{1,9},{2,6},{3,11},{4,0},{5,13},{6,2},{7,15},{8,12},{9,1},{1... | collective-permute-start | bytes 405512 | tf_op jit(solution)/shard_map/ppermute | solution.py:340
  12.1 1.6 %collective-permute-start.3 = (f32[33,8,128]{2,1,0:T(8,128)S(1)}, f32[33,8,128]{2,1,0:T(8,128)S(1)}, u32[]{:S(2)}, u32[]{:S(2)}) collective-permute-start(f32[33,8,128]{2,1,0:T(8,128)S(1)} %get-tuple-element.15), channel_id=1, source_target_pairs={{0,8},{1,5},{2,10},{3,7},{4,12},{5,1},{6,14},{7,3},{8,0},{9,13},{1... | collective-permute-start | bytes 405512 | tf_op jit(solution)/shard_map/ppermute | solution.py:340
  13.6 0.4 %collective-permute-start.4 = (f32[33,8,128]{2,1,0:T(8,128)S(1)}, f32[33,8,128]{2,1,0:T(8,128)S(1)}, u32[]{:S(2)}, u32[]{:S(2)}) collective-permute-start(f32[33,8,128]{2,1,0:T(8,128)S(1)} %get-tuple-element.16), channel_id=1, source_target_pairs={{0,12},{1,13},{2,14},{3,15},{4,8},{5,9},{6,10},{7,11},{8,4},{9,5},... | collective-permute-start | bytes 405512 | tf_op jit(solution)/shard_map/ppermute | solution.py:340
  14.1 2.6 %collective-permute-done.2.refs_1_ = f32[33,8,128]{2,1,0:T(8,128)S(1)} collective-permute-done((f32[33,8,128]{2,1,0:T(8,128)S(1)}, f32[33,8,128]{2,1,0:T(8,128)S(1)}, u32[]{:S(2)}, u32[]{:S(2)}) %collective-permute-start.2) | collective-permute-done | bytes 135200 | tf_op jit(solution)/shard_map/ppermute | solution.py:340
  16.7 1.8 %collective-permute-done.3.refs_2_ = f32[33,8,128]{2,1,0:T(8,128)S(1)} collective-permute-done((f32[33,8,128]{2,1,0:T(8,128)S(1)}, f32[33,8,128]{2,1,0:T(8,128)S(1)}, u32[]{:S(2)}, u32[]{:S(2)}) %collective-permute-start.3) | collective-permute-done | bytes 135200 | tf_op jit(solution)/shard_map/ppermute | solution.py:340
  18.5 1.5 %collective-permute-done.4.refs_3_ = f32[33,8,128]{2,1,0:T(8,128)S(1)} collective-permute-done((f32[33,8,128]{2,1,0:T(8,128)S(1)}, f32[33,8,128]{2,1,0:T(8,128)S(1)}, u32[]{:S(2)}, u32[]{:S(2)}) %collective-permute-start.4) | collective-permute-done | bytes 135200 | tf_op jit(solution)/shard_map/ppermute | solution.py:340
  20.0 2.7 %collective-permute-start.5 = (f32[33,8,128]{2,1,0:T(8,128)S(1)}, f32[33,8,128]{2,1,0:T(8,128)S(1)}, u32[]{:S(2)}, u32[]{:S(2)}) collective-permute-start(f32[33,8,128]{2,1,0:T(8,128)S(1)} %shard_map.58.refs_0_), channel_id=1, source_target_pairs={{0,16},{4,20},{8,24},{12,28},{16,0},{20,4},{24,8},{28,12},{1,17},{... | collective-permute-start | bytes 405512 | tf_op jit(solution)/shard_map/ppermute | solution.py:346
  22.6 5.7 %collective-permute-done.5.refs_1_ = f32[33,8,128]{2,1,0:T(8,128)S(1)} collective-permute-done((f32[33,8,128]{2,1,0:T(8,128)S(1)}, f32[33,8,128]{2,1,0:T(8,128)S(1)}, u32[]{:S(2)}, u32[]{:S(2)}) %collective-permute-start.5) | collective-permute-done | bytes 135200 | tf_op jit(solution)/shard_map/ppermute | solution.py:346
  28.4 0.1 collective-permute-start.8
  28.5 2.1 %collective-permute-start.7 = (f32[33,8,128]{2,1,0:T(8,128)S(1)}, f32[33,8,128]{2,1,0:T(8,128)S(1)}, u32[]{:S(2)}, u32[]{:S(2)}) collective-permute-start(f32[33,8,128]{2,1,0:T(8,128)S(1)} %shard_map.59.refs_0_), channel_id=1, source_target_pairs={{0,8},{1,5},{2,10},{3,7},{4,12},{5,1},{6,14},{7,3},{8,0},{9,13},{1... | collective-permute-start | bytes 405512 | tf_op jit(solution)/shard_map/ppermute | solution.py:340
  30.5 1.4 %collective-permute-start.6 = (f32[33,8,128]{2,1,0:T(8,128)S(1)}, f32[33,8,128]{2,1,0:T(8,128)S(1)}, u32[]{:S(2)}, u32[]{:S(2)}) collective-permute-start(f32[33,8,128]{2,1,0:T(8,128)S(1)} %shard_map.59.refs_0_), channel_id=1, source_target_pairs={{0,4},{1,9},{2,6},{3,11},{4,0},{5,13},{6,2},{7,15},{8,12},{9,1},{1... | collective-permute-start | bytes 405512 | tf_op jit(solution)/shard_map/ppermute | solution.py:340
  31.9 3.9 %collective-permute-done.8.refs_3_ = f32[33,8,128]{2,1,0:T(8,128)S(1)} collective-permute-done((f32[33,8,128]{2,1,0:T(8,128)S(1)}, f32[33,8,128]{2,1,0:T(8,128)S(1)}, u32[]{:S(2)}, u32[]{:S(2)}) %collective-permute-start.8) | collective-permute-done | bytes 135200 | tf_op jit(solution)/shard_map/ppermute | solution.py:340
  35.8 0.2 collective-permute-done.7.refs_2_
  36.0 0.4 collective-permute-done.6.refs_1_
  36.4 1.3 %shard_map.60 = f32[8,16,8,128]{3,2,1,0:T(8,128)} custom-call(s32[1]{0:T(128)} %bitcast.dom_ref, s32[1]{0:T(128)} %bitcast.1.me_ref, s32[1]{0:T(128)S(6)} %copy.6.level_ref, f32[33,8,128]{2,1,0:T(8,128)S(1)} %shard_map.59.refs_0_, f32[33,8,128]{2,1,0:T(8,128)S(1)} %collective-permute-done.6.refs_1_, f32[33,8,128]{2,1,0:T(8,128)S(1)} %collective-permute-done.7.refs_2_, ...), custom_call_target="tpu_custom_call" | custom-call | bytes 540684 | tf_op jit(solution)/shard_map/pallas_call | solution.py:279
  (3 shorter events, 0.1 us)
Async XLA Ops:
  0.0 1.2 %copy-start = (f32[1,64,2048]{2,1,0:T(8,128)S(1)}, f32[1,64,2048]{2,1,0:T(8,128)}, u32[]{:S(2)}) copy-start(f32[1,64,2048]{2,1,0:T(8,128)} %param.5) | copy-start | bytes 1572868
  1.2 6.5 %copy-start.1 = (f32[1,64,2048]{2,1,0:T(8,128)S(1)}, f32[1,64,2048]{2,1,0:T(8,128)}, u32[]{:S(2)}) copy-start(f32[1,64,2048]{2,1,0:T(8,128)} %param.7) | copy-start | bytes 1572868
  1.2 6.6 %copy-start.2 = (f32[1,64,2048]{2,1,0:T(8,128)S(1)}, f32[1,64,2048]{2,1,0:T(8,128)}, u32[]{:S(2)}) copy-start(f32[1,64,2048]{2,1,0:T(8,128)} %param.6) | copy-start | bytes 1572868
  1.2 8.4 %collective-permute-start = (f32[16,16,128]{2,1,0:T(8,128)S(1)}, f32[16,16,128]{2,1,0:T(8,128)S(1)}, u32[]{:S(2)}, u32[]{:S(2)}) collective-permute-start(f32[16,16,128]{2,1,0:T(8,128)S(1)} %get-tuple-element.11), channel_id=1, source_target_pairs={{0,0},{1,2},{2,1},{3,3},{4,4},{5,6},{6,5},{7,7},{8,8},{9,10},{10,9... | collective-permute-start | bytes 393224 | tf_op jit(solution)/shard_map/ppermute | solution.py:314
  2.0 7.6 %collective-permute-start.1 = (f32[16,16,128]{2,1,0:T(8,128)S(1)}, f32[16,16,128]{2,1,0:T(8,128)S(1)}, u32[]{:S(2)}, u32[]{:S(2)}) collective-permute-start(f32[16,16,128]{2,1,0:T(8,128)S(1)} %get-tuple-element.12), channel_id=1, source_target_pairs={{0,1},{1,0},{2,3},{3,2},{4,5},{5,4},{6,7},{7,6},{8,9},{9,8},{10,11... | collective-permute-start | bytes 393224 | tf_op jit(solution)/shard_map/ppermute | solution.py:314
  10.5 6.2 %collective-permute-start.2 = (f32[33,8,128]{2,1,0:T(8,128)S(1)}, f32[33,8,128]{2,1,0:T(8,128)S(1)}, u32[]{:S(2)}, u32[]{:S(2)}) collective-permute-start(f32[33,8,128]{2,1,0:T(8,128)S(1)} %get-tuple-element.14), channel_id=1, source_target_pairs={{0,4},{1,9},{2,6},{3,11},{4,0},{5,13},{6,2},{7,15},{8,12},{9,1},{1... | collective-permute-start | bytes 405512 | tf_op jit(solution)/shard_map/ppermute | solution.py:340
  12.1 6.4 %collective-permute-start.3 = (f32[33,8,128]{2,1,0:T(8,128)S(1)}, f32[33,8,128]{2,1,0:T(8,128)S(1)}, u32[]{:S(2)}, u32[]{:S(2)}) collective-permute-start(f32[33,8,128]{2,1,0:T(8,128)S(1)} %get-tuple-element.15), channel_id=1, source_target_pairs={{0,8},{1,5},{2,10},{3,7},{4,12},{5,1},{6,14},{7,3},{8,0},{9,13},{1... | collective-permute-start | bytes 405512 | tf_op jit(solution)/shard_map/ppermute | solution.py:340
  13.6 6.3 %collective-permute-start.4 = (f32[33,8,128]{2,1,0:T(8,128)S(1)}, f32[33,8,128]{2,1,0:T(8,128)S(1)}, u32[]{:S(2)}, u32[]{:S(2)}) collective-permute-start(f32[33,8,128]{2,1,0:T(8,128)S(1)} %get-tuple-element.16), channel_id=1, source_target_pairs={{0,12},{1,13},{2,14},{3,15},{4,8},{5,9},{6,10},{7,11},{8,4},{9,5},... | collective-permute-start | bytes 405512 | tf_op jit(solution)/shard_map/ppermute | solution.py:340
  20.0 8.4 %collective-permute-start.5 = (f32[33,8,128]{2,1,0:T(8,128)S(1)}, f32[33,8,128]{2,1,0:T(8,128)S(1)}, u32[]{:S(2)}, u32[]{:S(2)}) collective-permute-start(f32[33,8,128]{2,1,0:T(8,128)S(1)} %shard_map.58.refs_0_), channel_id=1, source_target_pairs={{0,16},{4,20},{8,24},{12,28},{16,0},{20,4},{24,8},{28,12},{1,17},{... | collective-permute-start | bytes 405512 | tf_op jit(solution)/shard_map/ppermute | solution.py:346
  28.4 7.4 %collective-permute-start.8 = (f32[33,8,128]{2,1,0:T(8,128)S(1)}, f32[33,8,128]{2,1,0:T(8,128)S(1)}, u32[]{:S(2)}, u32[]{:S(2)}) collective-permute-start(f32[33,8,128]{2,1,0:T(8,128)S(1)} %shard_map.59.refs_0_), channel_id=1, source_target_pairs={{0,12},{1,13},{2,14},{3,15},{4,8},{5,9},{6,10},{7,11},{8,4},{9,5},... | collective-permute-start | bytes 405512 | tf_op jit(solution)/shard_map/ppermute | solution.py:340
  28.5 7.6 %collective-permute-start.7 = (f32[33,8,128]{2,1,0:T(8,128)S(1)}, f32[33,8,128]{2,1,0:T(8,128)S(1)}, u32[]{:S(2)}, u32[]{:S(2)}) collective-permute-start(f32[33,8,128]{2,1,0:T(8,128)S(1)} %shard_map.59.refs_0_), channel_id=1, source_target_pairs={{0,8},{1,5},{2,10},{3,7},{4,12},{5,1},{6,14},{7,3},{8,0},{9,13},{1... | collective-permute-start | bytes 405512 | tf_op jit(solution)/shard_map/ppermute | solution.py:340
  30.5 5.9 %collective-permute-start.6 = (f32[33,8,128]{2,1,0:T(8,128)S(1)}, f32[33,8,128]{2,1,0:T(8,128)S(1)}, u32[]{:S(2)}, u32[]{:S(2)}) collective-permute-start(f32[33,8,128]{2,1,0:T(8,128)S(1)} %shard_map.59.refs_0_), channel_id=1, source_target_pairs={{0,4},{1,9},{2,6},{3,11},{4,0},{5,13},{6,2},{7,15},{8,12},{9,1},{1... | collective-permute-start | bytes 405512 | tf_op jit(solution)/shard_map/ppermute | solution.py:340

commit v11 on v10

--- a/solution.py
+++ b/solution.py
@@ -122,16 +122,20 @@
     )
 
 
-def pack_kernel(dom_ref, dens_ref, *refs):
-    *ends, far_ref, near_ref = refs
+def first_kernel(out_ref):
+    out_ref[...] = jnp.zeros(out_ref.shape, jnp.float32)
+
+
+def pack_kernel(dom_ref, ready_ref, dens_ref, *refs):
+    del ready_ref
+    diff_ref, drift_ref, far_ref, near_ref = refs
     many, strips = dens_ref.shape[:2]
     odd = dom_ref[0] % 2 == 1
     upper = lax.broadcasted_iota(jnp.int32, (TILE, LANES), 0) < HALF
 
     def body(j):
-        heads, tails = ([ref[j] for ref in ends[e::2]] for e in range(2))
-        mix_next = jnp.where(upper, pltpu.roll(tails[1], HALF, 0), tails[0])
-        mix_prev = jnp.where(upper, heads[0], pltpu.roll(heads[1], HALF, 0))
+        mix_next = jnp.where(upper, pltpu.roll(drift_ref[many - 1, j], HALF, 0), diff_ref[many - 1, j])
+        mix_prev = jnp.where(upper, diff_ref[0, j], pltpu.roll(drift_ref[0, j], HALF, 0))
         to_next, to_prev = (dens_ref[many - 1, j], mix_next), (dens_ref[0, j], mix_prev)
         for k in range(2):
             at = pl.ds(k * TILE, TILE)
@@ -169,8 +173,8 @@
     many, strips = dens_ref.shape[:2]
     dom = dom_ref[0]
     odd = dom % 2 == 1
-    ends, (state_ref, far_ref, near_ref), out_refs = refs[:4], refs[4:7], refs[7:11]
-    slab, state_a, state_b, *coefs = refs[11:]
+    diff_ref, drift_ref, state_ref, far_ref, near_ref, *rest = refs
+    out_refs, (slab, state_a, state_b, *coefs) = rest[:SQUARE], rest[SQUARE:]
 
     def stage(j):
         far, near = far_ref[j], near_ref[j]
@@ -179,8 +183,13 @@
         up_mix, dn_mix = up[TILE:], dn[TILE:]
         tiles = (
             (up[:TILE], dens_ref[0, j], dens_ref[many - 1, j], dn[:TILE]),
-            (up_mix, ends[0][j], ends[1][j], dn_mix),
-            (pltpu.roll(up_mix, HALF, 0), ends[2][j], ends[3][j], pltpu.roll(dn_mix, HALF, 0)),
+            (up_mix, diff_ref[0, j], diff_ref[many - 1, j], dn_mix),
+            (
+                pltpu.roll(up_mix, HALF, 0),
+                drift_ref[0, j],
+                drift_ref[many - 1, j],
+                pltpu.roll(dn_mix, HALF, 0),
+            ),
         )
         for k, column in enumerate(tiles):
             for e, tile in enumerate(column):
@@ -300,16 +309,16 @@
     def vmem(*shape):
         return pltpu.VMEM(shape, jnp.float32)
 
-    ends = [x[at] for x in tiles[1:] for at in (0, many - 1)]
+    near_pairs = [(d, d ^ 1) for d in range(doms)]
+    far_pairs = [(d, min(max((d - 1 ^ 1) + 1, 0), doms - 1)) for d in range(doms)]
+    (first,) = call(first_kernel, [(TILE, LANES)], (), flops=HALO_FLOPS * rows * cols)
+    ready = lax.ppermute(first, "dom", near_pairs)
     far, near = call(
         pack_kernel,
         [(strips, 2 * TILE, LANES)] * 2,
-        (dom, tiles[0], *ends),
+        (dom, ready, *tiles),
         1,
-        flops=HALO_FLOPS * rows * cols,
-    )
-    near_pairs = [(d, d ^ 1) for d in range(doms)]
-    far_pairs = [(d, min(max((d - 1 ^ 1) + 1, 0), doms - 1)) for d in range(doms)]
+    )
     far, near = (
         lax.ppermute(array, "dom", pairs) for array, pairs in ((far, far_pairs), (near, near_pairs))
     )
@@ -326,7 +335,7 @@
     own, *others = call(
         functools.partial(edge_kernel, per_chunk, depth, doms),
         [chunk] * SQUARE,
-        (dom, me, levels, coefficient, tiles[0], *ends, state, far, near),
+        (dom, me, levels, coefficient, *tiles, state, far, near),
         4,
         [vmem(3, strips, SLAB, LANES)]
         + [vmem(strips + 2, HALF, TILE, LANES)] * 2

time: 37.9 us -> 37.9 us (level)
  local copies, waits for them, and re-layouts: 1.17 us -> 0.01 us
  waiting for transfers between devices: 16.1 us -> 16.9 us
  starting transfers between devices: 14.9 us -> 15.3 us
    squeeze x1 -> x0, local copies, waits for them, and re-layouts: 1.01 us -> none  [on_device(): ends = [x[at] for x in tiles[1:] for at in (0, many - 1)]]
    ppermute x0 -> x1, waiting for transfers between devices: none -> 0.82 us  [on_device(): ready = lax.ppermute(first, 'dom', near_pairs)]
    ppermute x0 -> x1, starting transfers between devices: none -> 0.53 us  [on_device(): ready = lax.ppermute(first, 'dom', near_pairs)]
    pallas_call x6 -> x7, Pallas kernels: 4.1 us -> 4.11 us  [call(): pl.pallas_call(kernel, out_shape=[jax.ShapeDtypeStruct(shape, jnp.float32...]
  transfers between devices with their start and end apart: 9 -> 10, of which waited for: 7 -> 8; matrix products, arithmetic and copies ran while one was open for 0% -> 0% of each run, Pallas kernels for 5% -> 5%
where the time goes in v11:
time: 37.9 us; the launch traced here: 37.7 us
  waiting for transfers between devices  16.9 us (45%)
  starting transfers between devices  15.3 us (40%)
  Pallas kernels  4.11 us (11%)
  between operations  1.37 us (4%)
    ppermute x6, waiting for transfers between devices, swap(): return lax.ppermute(array, ('grp', 'dom'), pairs)  10.4 us
    ppermute x6, starting transfers between devices, swap(): return lax.ppermute(array, ('grp', 'dom'), pairs)  7.1 us
    ppermute x1, waiting for transfers between devices, on_device(): other = lax.ppermute(total, 'grp', [(g, g ^ apart) for g in range(grids)])  5.72 us
    ppermute x2, starting transfers between devices, on_device(): lax.ppermute(array, 'dom', pairs)  5.04 us
    pallas_call x7, Pallas kernels, call(): pl.pallas_call(kernel, out_shape=[jax.ShapeDtypeStruct(shape, jnp.float32...  4.11 us
    ppermute x1, starting transfers between devices, on_device(): other = lax.ppermute(total, 'grp', [(g, g ^ apart) for g in range(grids)])  2.65 us
    ppermute x1, waiting for transfers between devices, on_device(): ready = lax.ppermute(first, 'dom', near_pairs)  0.82 us
  transfers between devices with their start and end apart: 10, of which 8 were waited for; matrix products, arithmetic and copies ran while one was open for 0% of the time, Pallas kernels for 5%

profile of v11, /device:TPU:0, one launch (start us, length us, event | category | flops | bytes accessed | tf_op | source)
XLA Modules:
  0.0 37.7 jit_solution(496245045587709035)
XLA Ops:
  0.0 0.0 copy-start.2
  0.0 0.0 copy-start.1
  0.0 0.0 copy-start
  0.0 0.5 %collective-permute-start = (f32[8,128]{1,0:T(8,128)S(1)}, f32[8,128]{1,0:T(8,128)S(1)}, u32[]{:S(2)}, u32[]{:S(2)}) collective-permute-start(f32[8,128]{1,0:T(8,128)S(1)} %shard_map.56), channel_id=1, source_target_pairs={{0,1},{1,0},{2,3},{3,2},{4,5},{5,4},{6,7},{7,6},{8,9},{9,8},{10,11... | collective-permute-start | bytes 12296 | tf_op jit(solution)/shard_map/ppermute | solution.py:315
  0.5 0.8 %collective-permute-done.ready_ref = f32[8,128]{1,0:T(8,128)S(1)} collective-permute-done((f32[8,128]{1,0:T(8,128)S(1)}, f32[8,128]{1,0:T(8,128)S(1)}, u32[]{:S(2)}, u32[]{:S(2)}) %collective-permute-start) | collective-permute-done | bytes 4128 | tf_op jit(solution)/shard_map/ppermute | solution.py:315
  1.4 0.0 copy-done.2
  1.4 0.0 copy-done.1
  1.4 0.0 copy-done
  1.4 0.7 %collective-permute-start.1 = (f32[16,16,128]{2,1,0:T(8,128)S(1)}, f32[16,16,128]{2,1,0:T(8,128)S(1)}, u32[]{:S(2)}, u32[]{:S(2)}) collective-permute-start(f32[16,16,128]{2,1,0:T(8,128)S(1)} %get-tuple-element.11), channel_id=1, source_target_pairs={{0,0},{1,2},{2,1},{3,3},{4,4},{5,6},{6,5},{7,7},{8,8},{9,10},{10,9... | collective-permute-start | bytes 393224 | tf_op jit(solution)/shard_map/ppermute | solution.py:323
  2.1 4.4 %collective-permute-start.2 = (f32[16,16,128]{2,1,0:T(8,128)S(1)}, f32[16,16,128]{2,1,0:T(8,128)S(1)}, u32[]{:S(2)}, u32[]{:S(2)}) collective-permute-start(f32[16,16,128]{2,1,0:T(8,128)S(1)} %get-tuple-element.12), channel_id=1, source_target_pairs={{0,1},{1,0},{2,3},{3,2},{4,5},{5,4},{6,7},{7,6},{8,9},{9,8},{10,11... | collective-permute-start | bytes 393224 | tf_op jit(solution)/shard_map/ppermute | solution.py:323
  7.8 1.9 %shard_map.55.refs_2_ = f32[16,8,8,128]{3,2,1,0:T(8,128)S(1)} custom-call(f32[8,16,8,128]{3,2,1,0:T(8,128)S(1)} %bitcast.15, f32[8,16,8,128]{3,2,1,0:T(8,128)S(1)} %bitcast.18, f32[8,16,8,128]{3,2,1,0:T(8,128)S(1)} %bitcast.21), custom_call_target="tpu_custom_call" | custom-call | flops 5242880 | bytes 1572864 | tf_op jit(solution)/shard_map/pallas_call | solution.py:288
  9.6 0.0 collective-permute-done.1.refs_3_
  9.6 0.0 collective-permute-done.2.refs_4_
  9.7 0.9 %shard_map.58 = (f32[33,8,128]{2,1,0:T(8,128)S(1)}, f32[33,8,128]{2,1,0:T(8,128)S(1)}, f32[33,8,128]{2,1,0:T(8,128)S(1)}, f32[33,8,128]{2,1,0:T(8,128)S(1)}) custom-call(s32[1]{0:T(128)} %bitcast.dom_ref, s32[1]{0:T(128)} %bitcast.1.me_ref, s32[1]{0:T(128)S(6)} %copy.6.level_ref, s32[1]{0:T(128)S(6)} %copy.7.coef_ref, f32[8,16,8,128]{3,2,1,0:T(8,128)S(1)} %bitcast.16, ...), custom_call_target="tpu_custom_call" | custom-call | flops 2621440 | bytes 2359312 | tf_op jit(solution)/shard_map/pallas_call | solution.py:288
  10.5 1.6 %collective-permute-start.3 = (f32[33,8,128]{2,1,0:T(8,128)S(1)}, f32[33,8,128]{2,1,0:T(8,128)S(1)}, u32[]{:S(2)}, u32[]{:S(2)}) collective-permute-start(f32[33,8,128]{2,1,0:T(8,128)S(1)} %get-tuple-element.14), channel_id=1, source_target_pairs={{0,4},{1,9},{2,6},{3,11},{4,0},{5,13},{6,2},{7,15},{8,12},{9,1},{1... | collective-permute-start | bytes 405512 | tf_op jit(solution)/shard_map/ppermute | solution.py:349
  12.1 1.6 %collective-permute-start.4 = (f32[33,8,128]{2,1,0:T(8,128)S(1)}, f32[33,8,128]{2,1,0:T(8,128)S(1)}, u32[]{:S(2)}, u32[]{:S(2)}) collective-permute-start(f32[33,8,128]{2,1,0:T(8,128)S(1)} %get-tuple-element.15), channel_id=1, source_target_pairs={{0,8},{1,5},{2,10},{3,7},{4,12},{5,1},{6,14},{7,3},{8,0},{9,13},{1... | collective-permute-start | bytes 405512 | tf_op jit(solution)/shard_map/ppermute | solution.py:349
  13.7 0.4 %collective-permute-start.5 = (f32[33,8,128]{2,1,0:T(8,128)S(1)}, f32[33,8,128]{2,1,0:T(8,128)S(1)}, u32[]{:S(2)}, u32[]{:S(2)}) collective-permute-start(f32[33,8,128]{2,1,0:T(8,128)S(1)} %get-tuple-element.16), channel_id=1, source_target_pairs={{0,12},{1,13},{2,14},{3,15},{4,8},{5,9},{6,10},{7,11},{8,4},{9,5},... | collective-permute-start | bytes 405512 | tf_op jit(solution)/shard_map/ppermute | solution.py:349
  14.1 2.6 %collective-permute-done.3.refs_1_ = f32[33,8,128]{2,1,0:T(8,128)S(1)} collective-permute-done((f32[33,8,128]{2,1,0:T(8,128)S(1)}, f32[33,8,128]{2,1,0:T(8,128)S(1)}, u32[]{:S(2)}, u32[]{:S(2)}) %collective-permute-start.3) | collective-permute-done | bytes 135200 | tf_op jit(solution)/shard_map/ppermute | solution.py:349
  16.7 1.8 %collective-permute-done.4.refs_2_ = f32[33,8,128]{2,1,0:T(8,128)S(1)} collective-permute-done((f32[33,8,128]{2,1,0:T(8,128)S(1)}, f32[33,8,128]{2,1,0:T(8,128)S(1)}, u32[]{:S(2)}, u32[]{:S(2)}) %collective-permute-start.4) | collective-permute-done | bytes 135200 | tf_op jit(solution)/shard_map/ppermute | solution.py:349
  18.5 1.5 %collective-permute-done.5.refs_3_ = f32[33,8,128]{2,1,0:T(8,128)S(1)} collective-permute-done((f32[33,8,128]{2,1,0:T(8,128)S(1)}, f32[33,8,128]{2,1,0:T(8,128)S(1)}, u32[]{:S(2)}, u32[]{:S(2)}) %collective-permute-start.5) | collective-permute-done | bytes 135200 | tf_op jit(solution)/shard_map/ppermute | solution.py:349
  20.0 2.7 %collective-permute-start.6 = (f32[33,8,128]{2,1,0:T(8,128)S(1)}, f32[33,8,128]{2,1,0:T(8,128)S(1)}, u32[]{:S(2)}, u32[]{:S(2)}) collective-permute-start(f32[33,8,128]{2,1,0:T(8,128)S(1)} %shard_map.59.refs_0_), channel_id=1, source_target_pairs={{0,16},{4,20},{8,24},{12,28},{16,0},{20,4},{24,8},{28,12},{1,17},{... | collective-permute-start | bytes 405512 | tf_op jit(solution)/shard_map/ppermute | solution.py:355
  22.7 5.7 %collective-permute-done.6.refs_1_ = f32[33,8,128]{2,1,0:T(8,128)S(1)} collective-permute-done((f32[33,8,128]{2,1,0:T(8,128)S(1)}, f32[33,8,128]{2,1,0:T(8,128)S(1)}, u32[]{:S(2)}, u32[]{:S(2)}) %collective-permute-start.6) | collective-permute-done | bytes 135200 | tf_op jit(solution)/shard_map/ppermute | solution.py:355
  28.4 0.1 collective-permute-start.9
  28.5 2.1 %collective-permute-start.8 = (f32[33,8,128]{2,1,0:T(8,128)S(1)}, f32[33,8,128]{2,1,0:T(8,128)S(1)}, u32[]{:S(2)}, u32[]{:S(2)}) collective-permute-start(f32[33,8,128]{2,1,0:T(8,128)S(1)} %shard_map.60.refs_0_), channel_id=1, source_target_pairs={{0,8},{1,5},{2,10},{3,7},{4,12},{5,1},{6,14},{7,3},{8,0},{9,13},{1... | collective-permute-start | bytes 405512 | tf_op jit(solution)/shard_map/ppermute | solution.py:349
  30.5 1.4 %collective-permute-start.7 = (f32[33,8,128]{2,1,0:T(8,128)S(1)}, f32[33,8,128]{2,1,0:T(8,128)S(1)}, u32[]{:S(2)}, u32[]{:S(2)}) collective-permute-start(f32[33,8,128]{2,1,0:T(8,128)S(1)} %shard_map.60.refs_0_), channel_id=1, source_target_pairs={{0,4},{1,9},{2,6},{3,11},{4,0},{5,13},{6,2},{7,15},{8,12},{9,1},{1... | collective-permute-start | bytes 405512 | tf_op jit(solution)/shard_map/ppermute | solution.py:349
  32.0 3.9 %collective-permute-done.9.refs_3_ = f32[33,8,128]{2,1,0:T(8,128)S(1)} collective-permute-done((f32[33,8,128]{2,1,0:T(8,128)S(1)}, f32[33,8,128]{2,1,0:T(8,128)S(1)}, u32[]{:S(2)}, u32[]{:S(2)}) %collective-permute-start.9) | collective-permute-done | bytes 135200 | tf_op jit(solution)/shard_map/ppermute | solution.py:349
  35.8 0.2 collective-permute-done.8.refs_2_
  36.1 0.4 collective-permute-done.7.refs_1_
  36.5 1.3 %shard_map.61 = f32[8,16,8,128]{3,2,1,0:T(8,128)} custom-call(s32[1]{0:T(128)} %bitcast.dom_ref, s32[1]{0:T(128)} %bitcast.1.me_ref, s32[1]{0:T(128)S(6)} %copy.6.level_ref, f32[33,8,128]{2,1,0:T(8,128)S(1)} %shard_map.60.refs_0_, f32[33,8,128]{2,1,0:T(8,128)S(1)} %collective-permute-done.7.refs_1_, f32[33,8,128]{2,1,0:T(8,128)S(1)} %collective-permute-done.8.refs_2_, ...), custom_call_target="tpu_custom_call" | custom-call | bytes 540684 | tf_op jit(solution)/shard_map/pallas_call | solution.py:288
  (4 shorter events, 0.1 us)
Async XLA Ops:
  0.0 1.4 %copy-start.2 = (f32[1,64,2048]{2,1,0:T(8,128)S(1)}, f32[1,64,2048]{2,1,0:T(8,128)}, u32[]{:S(2)}) copy-start(f32[1,64,2048]{2,1,0:T(8,128)} %param.7) | copy-start | bytes 1572868
  0.0 1.4 %copy-start.1 = (f32[1,64,2048]{2,1,0:T(8,128)S(1)}, f32[1,64,2048]{2,1,0:T(8,128)}, u32[]{:S(2)}) copy-start(f32[1,64,2048]{2,1,0:T(8,128)} %param.6) | copy-start | bytes 1572868
  0.0 1.4 %copy-start = (f32[1,64,2048]{2,1,0:T(8,128)S(1)}, f32[1,64,2048]{2,1,0:T(8,128)}, u32[]{:S(2)}) copy-start(f32[1,64,2048]{2,1,0:T(8,128)} %param.5) | copy-start | bytes 1572868
  0.0 1.4 %collective-permute-start = (f32[8,128]{1,0:T(8,128)S(1)}, f32[8,128]{1,0:T(8,128)S(1)}, u32[]{:S(2)}, u32[]{:S(2)}) collective-permute-start(f32[8,128]{1,0:T(8,128)S(1)} %shard_map.56), channel_id=1, source_target_pairs={{0,1},{1,0},{2,3},{3,2},{4,5},{5,4},{6,7},{7,6},{8,9},{9,8},{10,11... | collective-permute-start | bytes 12296 | tf_op jit(solution)/shard_map/ppermute | solution.py:315
  1.4 8.2 %collective-permute-start.1 = (f32[16,16,128]{2,1,0:T(8,128)S(1)}, f32[16,16,128]{2,1,0:T(8,128)S(1)}, u32[]{:S(2)}, u32[]{:S(2)}) collective-permute-start(f32[16,16,128]{2,1,0:T(8,128)S(1)} %get-tuple-element.11), channel_id=1, source_target_pairs={{0,0},{1,2},{2,1},{3,3},{4,4},{5,6},{6,5},{7,7},{8,8},{9,10},{10,9... | collective-permute-start | bytes 393224 | tf_op jit(solution)/shard_map/ppermute | solution.py:323
  2.1 7.6 %collective-permute-start.2 = (f32[16,16,128]{2,1,0:T(8,128)S(1)}, f32[16,16,128]{2,1,0:T(8,128)S(1)}, u32[]{:S(2)}, u32[]{:S(2)}) collective-permute-start(f32[16,16,128]{2,1,0:T(8,128)S(1)} %get-tuple-element.12), channel_id=1, source_target_pairs={{0,1},{1,0},{2,3},{3,2},{4,5},{5,4},{6,7},{7,6},{8,9},{9,8},{10,11... | collective-permute-start | bytes 393224 | tf_op jit(solution)/shard_map/ppermute | solution.py:323
  10.5 6.2 %collective-permute-start.3 = (f32[33,8,128]{2,1,0:T(8,128)S(1)}, f32[33,8,128]{2,1,0:T(8,128)S(1)}, u32[]{:S(2)}, u32[]{:S(2)}) collective-permute-start(f32[33,8,128]{2,1,0:T(8,128)S(1)} %get-tuple-element.14), channel_id=1, source_target_pairs={{0,4},{1,9},{2,6},{3,11},{4,0},{5,13},{6,2},{7,15},{8,12},{9,1},{1... | collective-permute-start | bytes 405512 | tf_op jit(solution)/shard_map/ppermute | solution.py:349
  12.1 6.4 %collective-permute-start.4 = (f32[33,8,128]{2,1,0:T(8,128)S(1)}, f32[33,8,128]{2,1,0:T(8,128)S(1)}, u32[]{:S(2)}, u32[]{:S(2)}) collective-permute-start(f32[33,8,128]{2,1,0:T(8,128)S(1)} %get-tuple-element.15), channel_id=1, source_target_pairs={{0,8},{1,5},{2,10},{3,7},{4,12},{5,1},{6,14},{7,3},{8,0},{9,13},{1... | collective-permute-start | bytes 405512 | tf_op jit(solution)/shard_map/ppermute | solution.py:349
  13.7 6.3 %collective-permute-start.5 = (f32[33,8,128]{2,1,0:T(8,128)S(1)}, f32[33,8,128]{2,1,0:T(8,128)S(1)}, u32[]{:S(2)}, u32[]{:S(2)}) collective-permute-start(f32[33,8,128]{2,1,0:T(8,128)S(1)} %get-tuple-element.16), channel_id=1, source_target_pairs={{0,12},{1,13},{2,14},{3,15},{4,8},{5,9},{6,10},{7,11},{8,4},{9,5},... | collective-permute-start | bytes 405512 | tf_op jit(solution)/shard_map/ppermute | solution.py:349
  20.0 8.4 %collective-permute-start.6 = (f32[33,8,128]{2,1,0:T(8,128)S(1)}, f32[33,8,128]{2,1,0:T(8,128)S(1)}, u32[]{:S(2)}, u32[]{:S(2)}) collective-permute-start(f32[33,8,128]{2,1,0:T(8,128)S(1)} %shard_map.59.refs_0_), channel_id=1, source_target_pairs={{0,16},{4,20},{8,24},{12,28},{16,0},{20,4},{24,8},{28,12},{1,17},{... | collective-permute-start | bytes 405512 | tf_op jit(solution)/shard_map/ppermute | solution.py:355
  28.4 7.4 %collective-permute-start.9 = (f32[33,8,128]{2,1,0:T(8,128)S(1)}, f32[33,8,128]{2,1,0:T(8,128)S(1)}, u32[]{:S(2)}, u32[]{:S(2)}) collective-permute-start(f32[33,8,128]{2,1,0:T(8,128)S(1)} %shard_map.60.refs_0_), channel_id=1, source_target_pairs={{0,12},{1,13},{2,14},{3,15},{4,8},{5,9},{6,10},{7,11},{8,4},{9,5},... | collective-permute-start | bytes 405512 | tf_op jit(solution)/shard_map/ppermute | solution.py:349
  28.5 7.6 %collective-permute-start.8 = (f32[33,8,128]{2,1,0:T(8,128)S(1)}, f32[33,8,128]{2,1,0:T(8,128)S(1)}, u32[]{:S(2)}, u32[]{:S(2)}) collective-permute-start(f32[33,8,128]{2,1,0:T(8,128)S(1)} %shard_map.60.refs_0_), channel_id=1, source_target_pairs={{0,8},{1,5},{2,10},{3,7},{4,12},{5,1},{6,14},{7,3},{8,0},{9,13},{1... | collective-permute-start | bytes 405512 | tf_op jit(solution)/shard_map/ppermute | solution.py:349
  30.5 5.9 %collective-permute-start.7 = (f32[33,8,128]{2,1,0:T(8,128)S(1)}, f32[33,8,128]{2,1,0:T(8,128)S(1)}, u32[]{:S(2)}, u32[]{:S(2)}) collective-permute-start(f32[33,8,128]{2,1,0:T(8,128)S(1)} %shard_map.60.refs_0_), channel_id=1, source_target_pairs={{0,4},{1,9},{2,6},{3,11},{4,0},{5,13},{6,2},{7,15},{8,12},{9,1},{1... | collective-permute-start | bytes 405512 | tf_op jit(solution)/shard_map/ppermute | solution.py:349

commit v12 on v10

--- a/solution.py
+++ b/solution.py
@@ -14,6 +14,7 @@
 SLAB = 4 * TILE
 SQUARE = 4
 UNROLL = 16
+STREAMS = 2
 VMEM_LIMIT = 40 * 1024 * 1024
 HALO_FLOPS = 4000
 
@@ -169,8 +170,8 @@
     many, strips = dens_ref.shape[:2]
     dom = dom_ref[0]
     odd = dom % 2 == 1
-    ends, (state_ref, far_ref, near_ref), out_refs = refs[:4], refs[4:7], refs[7:11]
-    slab, state_a, state_b, *coefs = refs[11:]
+    ends, (state_ref, far_ref, near_ref), refs = refs[:4], refs[4:7], refs[7:]
+    out_refs, (slab, state_a, state_b, *coefs) = refs[:-7], refs[-7:]
 
     def stage(j):
         far, near = far_ref[j], near_ref[j]
@@ -212,10 +213,11 @@
         )
 
     def last(source):
-        for out_ref, away in zip(out_refs, partners(dom_ref[0])):
-            first = (me_ref[0] ^ away) * per_chunk
+        for k, out_ref in enumerate(out_refs):
+            stream, meet = divmod(k, SQUARE)
+            chunk = stream * SQUARE + (me_ref[0] ^ partners(dom_ref[0])[meet])
             emit = functools.partial(finish, out_ref)
-            advance(first, per_chunk, HALF, source, coefs, emit)
+            advance(chunk * per_chunk, per_chunk, HALF, source, coefs, emit)
 
     run_steps(strips, HALF, load, (state_a, state_b), coefs, last)
 
@@ -228,15 +230,15 @@
     out_ref[...] = total
 
 
-def nodal_kernel(per_chunk, depth, dom_ref, me_ref, level_ref, *refs):
-    *totals, out_ref, values, sems = refs
+def nodal_kernel(per_chunk, depth, stream, dom_ref, me_ref, level_ref, *refs):
+    totals, (out_ref, values, sems) = refs[:SQUARE], refs[-3:]
     many = values.shape[1]
     level = level_ref[0]
     fine, mid, low = (jnp.where(level >= depth - down, 1.0, 0.0) for down in range(3))
     place = lax.broadcasted_iota(jnp.int32, (many, LANES), 0)
     copies = []
     for k, (ref, away) in enumerate(zip(totals, partners(dom_ref[0]))):
-        first = (me_ref[0] ^ away) * per_chunk
+        first = (stream * SQUARE + (me_ref[0] ^ away)) * per_chunk
         by_row = flat(values.at[k])
 
         def body(part, ref=ref, by_row=by_row):
@@ -271,9 +273,13 @@
 
 
 def call(
-    kernel, out_shapes, operands, in_smem=0, scratch=(), flops=0, out_space=pltpu.VMEM
+    kernel, out_shapes, operands, in_smem=0, scratch=(), flops=0, out_space=pltpu.VMEM, onto=None
 ):
     spaces = [pltpu.SMEM] * in_smem + [pltpu.VMEM] * (len(operands) - in_smem)
+    alias = {}
+    if onto is not None:
+        alias = {len(operands): 0}
+        spaces, operands = spaces + [out_space], (*operands, onto)
     specs = [pl.BlockSpec(memory_space=space) for space in spaces]
     moved = 4 * sum(x.size for x in operands)
     return pl.pallas_call(
@@ -281,6 +287,7 @@
         out_shape=[jax.ShapeDtypeStruct(shape, jnp.float32) for shape in out_shapes],
         in_specs=specs,
         out_specs=[pl.BlockSpec(memory_space=out_space) for _ in out_shapes],
+        input_output_aliases=alias,
         scratch_shapes=list(scratch),
         compiler_params=pltpu.CompilerParams(vmem_limit_bytes=VMEM_LIMIT),
         cost_estimate=pl.CostEstimate(flops=flops, bytes_accessed=moved, transcendentals=0),
@@ -291,7 +298,7 @@
     rows, cols = density.shape[1:]
     doms, grids = lax.axis_size("dom"), lax.axis_size("grp")
     many, strips = rows // TILE, cols // LANES
-    per_chunk = strips // SQUARE
+    per_chunk = strips // (SQUARE * STREAMS)
     depth = (rows * doms).bit_length() - 1
     tiles = [tiles_of(x[0]) for x in (density, diffusion, drift_speed)]
     me = (lax.axis_index("grp") % SQUARE).astype(jnp.int32)[None]
@@ -323,9 +330,9 @@
         flops=40 * rows * cols,
     )
     chunk = (per_chunk * TILE + -(-per_chunk // many), many, LANES)
-    own, *others = call(
+    weighted = call(
         functools.partial(edge_kernel, per_chunk, depth, doms),
-        [chunk] * SQUARE,
+        [chunk] * (SQUARE * STREAMS),
         (dom, me, levels, coefficient, tiles[0], *ends, state, far, near),
         4,
         [vmem(3, strips, SLAB, LANES)]
@@ -339,22 +346,28 @@
         pairs = [(g * doms + d, (g ^ partners(d % 2)[meet]) * doms + d) for g, d in devices]
         return lax.ppermute(array, ("grp", "dom"), pairs)
 
-    theirs = [swap(array, meet) for meet, array in enumerate(others, 1)]
-    (total,) = call(sum_kernel, [chunk], (own, *theirs))
-    apart = SQUARE
-    while apart < grids:
-        other = lax.ppermute(total, "grp", [(g, g ^ apart) for g in range(grids)])
-        (total,) = call(sum_kernel, [chunk], (total, other))
-        apart *= 2
-    totals = [total] + [swap(total, meet) for meet in range(1, SQUARE)]
-    (nodal,) = call(
-        functools.partial(nodal_kernel, per_chunk, depth),
-        [(many, strips, TILE, LANES)],
-        (dom, me, levels, *totals),
-        3,
-        [vmem(SQUARE, many, per_chunk, TILE, LANES), pltpu.SemaphoreType.DMA((SQUARE, many))],
-        out_space=pl.ANY,
-    )
+    def over_grids(own, *others):
+        theirs = [swap(array, meet) for meet, array in enumerate(others, 1)]
+        (total,) = call(sum_kernel, [chunk], (own, *theirs))
+        apart = SQUARE
+        while apart < grids:
+            other = lax.ppermute(total, "grp", [(g, g ^ apart) for g in range(grids)])
+            (total,) = call(sum_kernel, [chunk], (total, other))
+            apart *= 2
+        return [total] + [swap(total, meet) for meet in range(1, SQUARE)]
+
+    nodal = None
+    for stream in range(STREAMS):
+        totals = over_grids(*weighted[stream * SQUARE : (stream + 1) * SQUARE])
+        (nodal,) = call(
+            functools.partial(nodal_kernel, per_chunk, depth, stream),
+            [(many, strips, TILE, LANES)],
+            (dom, me, levels, *totals),
+            3,
+            [vmem(SQUARE, many, per_chunk, TILE, LANES), pltpu.SemaphoreType.DMA((SQUARE, many))],
+            out_space=pl.ANY,
+            onto=nodal,
+        )
     return block_of(nodal)[None]
 
 

time: 37.9 us -> 38.3 us (1.011)
  waiting for transfers between devices: 16.1 us -> 5.13 us
  starting transfers between devices: 14.9 us -> 25.5 us
  Pallas kernels: 4.1 us -> 4.95 us
    ppermute x6 -> x12, starting transfers between devices: 7.1 us -> 15.1 us  [swap(): return lax.ppermute(array, ('grp', 'dom'), pairs)]
    ppermute x6 -> x12, waiting for transfers between devices: 10.4 us -> 4.36 us  [swap(): return lax.ppermute(array, ('grp', 'dom'), pairs)]
    ppermute x1 -> x2, waiting for transfers between devices: 5.72 us -> 0.76 us  [over_grids(): other = lax.ppermute(total, 'grp', [(g, g ^ apart) for g in range(grids)])]
    ppermute x1 -> x2, starting transfers between devices: 2.65 us -> 5.16 us  [over_grids(): other = lax.ppermute(total, 'grp', [(g, g ^ apart) for g in range(grids)])]
    pallas_call x6 -> x9, Pallas kernels: 4.1 us -> 4.95 us  [call(): pl.pallas_call(kernel, out_shape=[jax.ShapeDtypeStruct(shape, jnp.float32...]
  transfers between devices with their start and end apart: 9 -> 16, of which waited for: 7 -> 6; matrix products, arithmetic and copies ran while one was open for 0% -> 0% of each run, Pallas kernels for 5% -> 8%
where the time goes in v12:
time: 38.3 us; the launch traced here: 38.1 us
  starting transfers between devices  25.5 us (67%)
  waiting for transfers between devices  5.13 us (13%)
  Pallas kernels  4.95 us (13%)
  between operations  1.4 us (4%)
  local copies, waits for them, and re-layouts  1.17 us (3%)
    ppermute x12, starting transfers between devices, swap(): return lax.ppermute(array, ('grp', 'dom'), pairs)  15.1 us
    ppermute x2, starting transfers between devices, on_device(): lax.ppermute(array, 'dom', pairs)  5.19 us
    ppermute x2, starting transfers between devices, over_grids(): other = lax.ppermute(total, 'grp', [(g, g ^ apart) for g in range(grids)])  5.16 us
    pallas_call x9, Pallas kernels, call(): pl.pallas_call(kernel, out_shape=[jax.ShapeDtypeStruct(shape, jnp.float32...  4.95 us
    ppermute x12, waiting for transfers between devices, swap(): return lax.ppermute(array, ('grp', 'dom'), pairs)  4.36 us
    squeeze x1, local copies, waits for them, and re-layouts, on_device(): ends = [x[at] for x in tiles[1:] for at in (0, many - 1)]  1.01 us
  transfers between devices with their start and end apart: 16, of which 6 were waited for; matrix products, arithmetic and copies ran while one was open for 0% of the time, Pallas kernels for 8%

profile of v12, /device:TPU:0, one launch (start us, length us, event | category | flops | bytes accessed | tf_op | source)
XLA Modules:
  0.0 38.1 jit_solution(2291898183855058845)
XLA Ops:
  0.0 0.0 copy-start
  0.0 1.0 %slice_bitcast_fusion = (f32[16,8,128]{2,1,0:T(8,128)S(1)}, f32[16,8,128]{2,1,0:T(8,128)S(1)}, f32[16,8,128]{2,1,0:T(8,128)S(1)}, f32[16,8,128]{2,1,0:T(8,128)S(1)}) fusion(f32[8,16,8,128]{3,2,1,0:T(8,128)} %bitcast.25, f32[8,16,8,128]{3,2,1,0:T(8,128)} %bitcast.27), kind=kLoop, calls=%fused_computation | loop fusion | bytes 524288 | tf_op jit(solution)/shard_map/squeeze | solution.py:310
  1.0 0.1 copy-done
  1.2 0.0 copy-start.1
  1.2 0.0 copy-start.2
  1.2 0.8 %collective-permute-start = (f32[16,16,128]{2,1,0:T(8,128)S(1)}, f32[16,16,128]{2,1,0:T(8,128)S(1)}, u32[]{:S(2)}, u32[]{:S(2)}) collective-permute-start(f32[16,16,128]{2,1,0:T(8,128)S(1)} %get-tuple-element.15), channel_id=1, source_target_pairs={{0,0},{1,2},{2,1},{3,3},{4,4},{5,6},{6,5},{7,7},{8,8},{9,10},{10,9... | collective-permute-start | bytes 393224 | tf_op jit(solution)/shard_map/ppermute | solution.py:321
  2.0 4.4 %collective-permute-start.1 = (f32[16,16,128]{2,1,0:T(8,128)S(1)}, f32[16,16,128]{2,1,0:T(8,128)S(1)}, u32[]{:S(2)}, u32[]{:S(2)}) collective-permute-start(f32[16,16,128]{2,1,0:T(8,128)S(1)} %get-tuple-element.16), channel_id=1, source_target_pairs={{0,1},{1,0},{2,3},{3,2},{4,5},{5,4},{6,7},{7,6},{8,9},{9,8},{10,11... | collective-permute-start | bytes 393224 | tf_op jit(solution)/shard_map/ppermute | solution.py:321
  7.7 0.0 copy-done.1
  7.7 0.0 copy-done.2
  7.7 1.9 %shard_map.55.refs_4_ = f32[16,8,8,128]{3,2,1,0:T(8,128)S(1)} custom-call(f32[8,16,8,128]{3,2,1,0:T(8,128)S(1)} %bitcast.23, f32[8,16,8,128]{3,2,1,0:T(8,128)S(1)} %bitcast.28, f32[8,16,8,128]{3,2,1,0:T(8,128)S(1)} %bitcast.26), custom_call_target="tpu_custom_call" | custom-call | flops 5242880 | bytes 1572864 | tf_op jit(solution)/shard_map/pallas_call | solution.py:285
  9.6 0.0 collective-permute-done.refs_5_
  9.6 0.0 collective-permute-done.1.refs_6_
  9.6 0.9 %shard_map.57 = (f32[17,8,128]{2,1,0:T(8,128)S(1)}, f32[17,8,128]{2,1,0:T(8,128)S(1)}, f32[17,8,128]{2,1,0:T(8,128)S(1)}, f32[17,8,128]{2,1,0:T(8,128)S(1)}, f32...) custom-call(s32[1]{0:T(128)} %bitcast.dom_ref, ...), custom_call_target="tpu_custom_call" | custom-call | flops 2621440 | bytes 1572880 | tf_op jit(solution)/shard_map/pallas_call | solution.py:285
  10.5 1.6 %collective-permute-start.9 = (f32[17,8,128]{2,1,0:T(8,128)S(1)}, f32[17,8,128]{2,1,0:T(8,128)S(1)}, u32[]{:S(2)}, u32[]{:S(2)}) collective-permute-start(f32[17,8,128]{2,1,0:T(8,128)S(1)} %get-tuple-element.22), channel_id=1, source_target_pairs={{0,4},{1,9},{2,6},{3,11},{4,0},{5,13},{6,2},{7,15},{8,12},{9,1},{1... | collective-permute-start | bytes 208904 | tf_op jit(solution)/shard_map/ppermute | solution.py:347
  12.1 1.6 %collective-permute-start.10 = (f32[17,8,128]{2,1,0:T(8,128)S(1)}, f32[17,8,128]{2,1,0:T(8,128)S(1)}, u32[]{:S(2)}, u32[]{:S(2)}) collective-permute-start(f32[17,8,128]{2,1,0:T(8,128)S(1)} %get-tuple-element.23), channel_id=1, source_target_pairs={{0,8},{1,5},{2,10},{3,7},{4,12},{5,1},{6,14},{7,3},{8,0},{9,13},{1... | collective-permute-start | bytes 208904 | tf_op jit(solution)/shard_map/ppermute | solution.py:347
  13.7 0.4 %collective-permute-start.11 = (f32[17,8,128]{2,1,0:T(8,128)S(1)}, f32[17,8,128]{2,1,0:T(8,128)S(1)}, u32[]{:S(2)}, u32[]{:S(2)}) collective-permute-start(f32[17,8,128]{2,1,0:T(8,128)S(1)} %get-tuple-element.24), channel_id=1, source_target_pairs={{0,12},{1,13},{2,14},{3,15},{4,8},{5,9},{6,10},{7,11},{8,4},{9,5},... | collective-permute-start | bytes 208904 | tf_op jit(solution)/shard_map/ppermute | solution.py:347
  14.1 1.5 %collective-permute-start.2 = (f32[17,8,128]{2,1,0:T(8,128)S(1)}, f32[17,8,128]{2,1,0:T(8,128)S(1)}, u32[]{:S(2)}, u32[]{:S(2)}) collective-permute-start(f32[17,8,128]{2,1,0:T(8,128)S(1)} %get-tuple-element.18), channel_id=1, source_target_pairs={{0,4},{1,9},{2,6},{3,11},{4,0},{5,13},{6,2},{7,15},{8,12},{9,1},{1... | collective-permute-start | bytes 208904 | tf_op jit(solution)/shard_map/ppermute | solution.py:347
  15.6 1.6 %collective-permute-start.3 = (f32[17,8,128]{2,1,0:T(8,128)S(1)}, f32[17,8,128]{2,1,0:T(8,128)S(1)}, u32[]{:S(2)}, u32[]{:S(2)}) collective-permute-start(f32[17,8,128]{2,1,0:T(8,128)S(1)} %get-tuple-element.19), channel_id=1, source_target_pairs={{0,8},{1,5},{2,10},{3,7},{4,12},{5,1},{6,14},{7,3},{8,0},{9,13},{1... | collective-permute-start | bytes 208904 | tf_op jit(solution)/shard_map/ppermute | solution.py:347
  17.2 0.0 collective-permute-done.9.refs_1_
  17.2 1.0 %collective-permute-start.4 = (f32[17,8,128]{2,1,0:T(8,128)S(1)}, f32[17,8,128]{2,1,0:T(8,128)S(1)}, u32[]{:S(2)}, u32[]{:S(2)}) collective-permute-start(f32[17,8,128]{2,1,0:T(8,128)S(1)} %get-tuple-element.20), channel_id=1, source_target_pairs={{0,12},{1,13},{2,14},{3,15},{4,8},{5,9},{6,10},{7,11},{8,4},{9,5},... | collective-permute-start | bytes 208904 | tf_op jit(solution)/shard_map/ppermute | solution.py:347
  18.2 0.0 collective-permute-done.10.refs_2_
  18.2 0.8 %collective-permute-done.11.refs_3_ = f32[17,8,128]{2,1,0:T(8,128)S(1)} collective-permute-done((f32[17,8,128]{2,1,0:T(8,128)S(1)}, f32[17,8,128]{2,1,0:T(8,128)S(1)}, u32[]{:S(2)}, u32[]{:S(2)}) %collective-permute-start.11) | collective-permute-done | bytes 69664 | tf_op jit(solution)/shard_map/ppermute | solution.py:347
  19.0 2.7 %collective-permute-start.12 = (f32[17,8,128]{2,1,0:T(8,128)S(1)}, f32[17,8,128]{2,1,0:T(8,128)S(1)}, u32[]{:S(2)}, u32[]{:S(2)}) collective-permute-start(f32[17,8,128]{2,1,0:T(8,128)S(1)} %shard_map.60.refs_0_), channel_id=1, source_target_pairs={{0,16},{4,20},{8,24},{12,28},{16,0},{20,4},{24,8},{28,12},{1,17},{... | collective-permute-start | bytes 208904 | tf_op jit(solution)/shard_map/ppermute | solution.py:354
  21.7 0.0 collective-permute-done.2.refs_1_
  21.7 0.0 collective-permute-done.3.refs_2_
  21.7 1.3 %collective-permute-done.4.refs_3_ = f32[17,8,128]{2,1,0:T(8,128)S(1)} collective-permute-done((f32[17,8,128]{2,1,0:T(8,128)S(1)}, f32[17,8,128]{2,1,0:T(8,128)S(1)}, u32[]{:S(2)}, u32[]{:S(2)}) %collective-permute-start.4) | collective-permute-done | bytes 69664 | tf_op jit(solution)/shard_map/ppermute | solution.py:347
  23.0 2.5 %collective-permute-start.5 = (f32[17,8,128]{2,1,0:T(8,128)S(1)}, f32[17,8,128]{2,1,0:T(8,128)S(1)}, u32[]{:S(2)}, u32[]{:S(2)}) collective-permute-start(f32[17,8,128]{2,1,0:T(8,128)S(1)} %shard_map.58.refs_0_), channel_id=1, source_target_pairs={{0,16},{4,20},{8,24},{12,28},{16,0},{20,4},{24,8},{28,12},{1,17},{... | collective-permute-start | bytes 208904 | tf_op jit(solution)/shard_map/ppermute | solution.py:354
  25.5 0.8 %collective-permute-done.12.refs_1_ = f32[17,8,128]{2,1,0:T(8,128)S(1)} collective-permute-done((f32[17,8,128]{2,1,0:T(8,128)S(1)}, f32[17,8,128]{2,1,0:T(8,128)S(1)}, u32[]{:S(2)}, u32[]{:S(2)}) %collective-permute-start.12) | collective-permute-done | bytes 69664 | tf_op jit(solution)/shard_map/ppermute | solution.py:354
  26.2 0.8 %collective-permute-start.15 = (f32[17,8,128]{2,1,0:T(8,128)S(1)}, f32[17,8,128]{2,1,0:T(8,128)S(1)}, u32[]{:S(2)}, u32[]{:S(2)}) collective-permute-start(f32[17,8,128]{2,1,0:T(8,128)S(1)} %shard_map.61.refs_0_), channel_id=1, source_target_pairs={{0,12},{1,13},{2,14},{3,15},{4,8},{5,9},{6,10},{7,11},{8,4},{9,5},... | collective-permute-start | bytes 208904 | tf_op jit(solution)/shard_map/ppermute | solution.py:347
  27.1 2.1 %collective-permute-start.14 = (f32[17,8,128]{2,1,0:T(8,128)S(1)}, f32[17,8,128]{2,1,0:T(8,128)S(1)}, u32[]{:S(2)}, u32[]{:S(2)}) collective-permute-start(f32[17,8,128]{2,1,0:T(8,128)S(1)} %shard_map.61.refs_0_), channel_id=1, source_target_pairs={{0,8},{1,5},{2,10},{3,7},{4,12},{5,1},{6,14},{7,3},{8,0},{9,13},{1... | collective-permute-start | bytes 208904 | tf_op jit(solution)/shard_map/ppermute | solution.py:347
  29.2 0.6 %collective-permute-start.13 = (f32[17,8,128]{2,1,0:T(8,128)S(1)}, f32[17,8,128]{2,1,0:T(8,128)S(1)}, u32[]{:S(2)}, u32[]{:S(2)}) collective-permute-start(f32[17,8,128]{2,1,0:T(8,128)S(1)} %shard_map.61.refs_0_), channel_id=1, source_target_pairs={{0,4},{1,9},{2,6},{3,11},{4,0},{5,13},{6,2},{7,15},{8,12},{9,1},{1... | collective-permute-start | bytes 208904 | tf_op jit(solution)/shard_map/ppermute | solution.py:347
  29.8 0.0 collective-permute-done.5.refs_1_
  29.8 0.9 %collective-permute-start.8 = (f32[17,8,128]{2,1,0:T(8,128)S(1)}, f32[17,8,128]{2,1,0:T(8,128)S(1)}, u32[]{:S(2)}, u32[]{:S(2)}) collective-permute-start(f32[17,8,128]{2,1,0:T(8,128)S(1)} %shard_map.59.refs_0_), channel_id=1, source_target_pairs={{0,12},{1,13},{2,14},{3,15},{4,8},{5,9},{6,10},{7,11},{8,4},{9,5},... | collective-permute-start | bytes 208904 | tf_op jit(solution)/shard_map/ppermute | solution.py:347
  30.8 2.0 %collective-permute-start.7 = (f32[17,8,128]{2,1,0:T(8,128)S(1)}, f32[17,8,128]{2,1,0:T(8,128)S(1)}, u32[]{:S(2)}, u32[]{:S(2)}) collective-permute-start(f32[17,8,128]{2,1,0:T(8,128)S(1)} %shard_map.59.refs_0_), channel_id=1, source_target_pairs={{0,8},{1,5},{2,10},{3,7},{4,12},{5,1},{6,14},{7,3},{8,0},{9,13},{1... | collective-permute-start | bytes 208904 | tf_op jit(solution)/shard_map/ppermute | solution.py:347
  32.8 0.0 collective-permute-done.15.refs_3_
  32.8 1.0 %collective-permute-start.6 = (f32[17,8,128]{2,1,0:T(8,128)S(1)}, f32[17,8,128]{2,1,0:T(8,128)S(1)}, u32[]{:S(2)}, u32[]{:S(2)}) collective-permute-start(f32[17,8,128]{2,1,0:T(8,128)S(1)} %shard_map.59.refs_0_), channel_id=1, source_target_pairs={{0,4},{1,9},{2,6},{3,11},{4,0},{5,13},{6,2},{7,15},{8,12},{9,1},{1... | collective-permute-start | bytes 208904 | tf_op jit(solution)/shard_map/ppermute | solution.py:347
  33.8 0.0 collective-permute-done.14.refs_2_
  33.8 0.0 collective-permute-done.13.refs_1_
  33.8 1.0 %shard_map.62.refs_4_ = f32[8,16,8,128]{3,2,1,0:T(8,128)} custom-call(s32[1]{0:T(128)} %bitcast.dom_ref, s32[1]{0:T(128)} %bitcast.1.me_ref, s32[1]{0:T(128)S(6)} %copy.8.level_ref, f32[17,8,128]{2,1,0:T(8,128)S(1)} %shard_map.61.refs_0_, f32[17,8,128]{2,1,0:T(8,128)S(1)} %collective-permute-done.13.refs_1_, ...), custom_call_target="tpu_custom_call" | custom-call | bytes 278540 | tf_op jit(solution)/shard_map/pallas_call | solution.py:285
  34.8 0.2 collective-permute-done.8.refs_3_
  35.1 0.7 %collective-permute-done.7.refs_2_ = f32[17,8,128]{2,1,0:T(8,128)S(1)} collective-permute-done((f32[17,8,128]{2,1,0:T(8,128)S(1)}, f32[17,8,128]{2,1,0:T(8,128)S(1)}, u32[]{:S(2)}, u32[]{:S(2)}) %collective-permute-start.7) | collective-permute-done | bytes 69664 | tf_op jit(solution)/shard_map/ppermute | solution.py:347
  35.8 1.3 %collective-permute-done.6.refs_1_ = f32[17,8,128]{2,1,0:T(8,128)S(1)} collective-permute-done((f32[17,8,128]{2,1,0:T(8,128)S(1)}, f32[17,8,128]{2,1,0:T(8,128)S(1)}, u32[]{:S(2)}, u32[]{:S(2)}) %collective-permute-start.6) | collective-permute-done | bytes 69664 | tf_op jit(solution)/shard_map/ppermute | solution.py:347
  37.1 1.0 %shard_map.63 = f32[8,16,8,128]{3,2,1,0:T(8,128)} custom-call(s32[1]{0:T(128)} %bitcast.dom_ref, s32[1]{0:T(128)} %bitcast.1.me_ref, s32[1]{0:T(128)S(6)} %copy.8.level_ref, f32[17,8,128]{2,1,0:T(8,128)S(1)} %shard_map.59.refs_0_, f32[17,8,128]{2,1,0:T(8,128)S(1)} %collective-permute-done.6.refs_1_, ...), custom_call_target="tpu_custom_call", output_to_operand_aliasing={{}: (7, {})} | custom-call | bytes 802828 | tf_op jit(solution)/shard_map/pallas_call | solution.py:285
  (5 shorter events, 0.1 us)
Async XLA Ops:
  0.0 1.2 %copy-start = (f32[1,64,2048]{2,1,0:T(8,128)S(1)}, f32[1,64,2048]{2,1,0:T(8,128)}, u32[]{:S(2)}) copy-start(f32[1,64,2048]{2,1,0:T(8,128)} %param.5) | copy-start | bytes 1572868
  1.2 6.5 %copy-start.1 = (f32[1,64,2048]{2,1,0:T(8,128)S(1)}, f32[1,64,2048]{2,1,0:T(8,128)}, u32[]{:S(2)}) copy-start(f32[1,64,2048]{2,1,0:T(8,128)} %param.7) | copy-start | bytes 1572868
  1.2 6.6 %copy-start.2 = (f32[1,64,2048]{2,1,0:T(8,128)S(1)}, f32[1,64,2048]{2,1,0:T(8,128)}, u32[]{:S(2)}) copy-start(f32[1,64,2048]{2,1,0:T(8,128)} %param.6) | copy-start | bytes 1572868
  1.2 8.4 %collective-permute-start = (f32[16,16,128]{2,1,0:T(8,128)S(1)}, f32[16,16,128]{2,1,0:T(8,128)S(1)}, u32[]{:S(2)}, u32[]{:S(2)}) collective-permute-start(f32[16,16,128]{2,1,0:T(8,128)S(1)} %get-tuple-element.15), channel_id=1, source_target_pairs={{0,0},{1,2},{2,1},{3,3},{4,4},{5,6},{6,5},{7,7},{8,8},{9,10},{10,9... | collective-permute-start | bytes 393224 | tf_op jit(solution)/shard_map/ppermute | solution.py:321
  2.0 7.6 %collective-permute-start.1 = (f32[16,16,128]{2,1,0:T(8,128)S(1)}, f32[16,16,128]{2,1,0:T(8,128)S(1)}, u32[]{:S(2)}, u32[]{:S(2)}) collective-permute-start(f32[16,16,128]{2,1,0:T(8,128)S(1)} %get-tuple-element.16), channel_id=1, source_target_pairs={{0,1},{1,0},{2,3},{3,2},{4,5},{5,4},{6,7},{7,6},{8,9},{9,8},{10,11... | collective-permute-start | bytes 393224 | tf_op jit(solution)/shard_map/ppermute | solution.py:321
  10.5 6.6 %collective-permute-start.9 = (f32[17,8,128]{2,1,0:T(8,128)S(1)}, f32[17,8,128]{2,1,0:T(8,128)S(1)}, u32[]{:S(2)}, u32[]{:S(2)}) collective-permute-start(f32[17,8,128]{2,1,0:T(8,128)S(1)} %get-tuple-element.22), channel_id=1, source_target_pairs={{0,4},{1,9},{2,6},{3,11},{4,0},{5,13},{6,2},{7,15},{8,12},{9,1},{1... | collective-permute-start | bytes 208904 | tf_op jit(solution)/shard_map/ppermute | solution.py:347
  12.1 6.1 %collective-permute-start.10 = (f32[17,8,128]{2,1,0:T(8,128)S(1)}, f32[17,8,128]{2,1,0:T(8,128)S(1)}, u32[]{:S(2)}, u32[]{:S(2)}) collective-permute-start(f32[17,8,128]{2,1,0:T(8,128)S(1)} %get-tuple-element.23), channel_id=1, source_target_pairs={{0,8},{1,5},{2,10},{3,7},{4,12},{5,1},{6,14},{7,3},{8,0},{9,13},{1... | collective-permute-start | bytes 208904 | tf_op jit(solution)/shard_map/ppermute | solution.py:347
  13.7 5.3 %collective-permute-start.11 = (f32[17,8,128]{2,1,0:T(8,128)S(1)}, f32[17,8,128]{2,1,0:T(8,128)S(1)}, u32[]{:S(2)}, u32[]{:S(2)}) collective-permute-start(f32[17,8,128]{2,1,0:T(8,128)S(1)} %get-tuple-element.24), channel_id=1, source_target_pairs={{0,12},{1,13},{2,14},{3,15},{4,8},{5,9},{6,10},{7,11},{8,4},{9,5},... | collective-permute-start | bytes 208904 | tf_op jit(solution)/shard_map/ppermute | solution.py:347
  14.1 7.6 %collective-permute-start.2 = (f32[17,8,128]{2,1,0:T(8,128)S(1)}, f32[17,8,128]{2,1,0:T(8,128)S(1)}, u32[]{:S(2)}, u32[]{:S(2)}) collective-permute-start(f32[17,8,128]{2,1,0:T(8,128)S(1)} %get-tuple-element.18), channel_id=1, source_target_pairs={{0,4},{1,9},{2,6},{3,11},{4,0},{5,13},{6,2},{7,15},{8,12},{9,1},{1... | collective-permute-start | bytes 208904 | tf_op jit(solution)/shard_map/ppermute | solution.py:347
  15.6 6.1 %collective-permute-start.3 = (f32[17,8,128]{2,1,0:T(8,128)S(1)}, f32[17,8,128]{2,1,0:T(8,128)S(1)}, u32[]{:S(2)}, u32[]{:S(2)}) collective-permute-start(f32[17,8,128]{2,1,0:T(8,128)S(1)} %get-tuple-element.19), channel_id=1, source_target_pairs={{0,8},{1,5},{2,10},{3,7},{4,12},{5,1},{6,14},{7,3},{8,0},{9,13},{1... | collective-permute-start | bytes 208904 | tf_op jit(solution)/shard_map/ppermute | solution.py:347
  17.2 5.8 %collective-permute-start.4 = (f32[17,8,128]{2,1,0:T(8,128)S(1)}, f32[17,8,128]{2,1,0:T(8,128)S(1)}, u32[]{:S(2)}, u32[]{:S(2)}) collective-permute-start(f32[17,8,128]{2,1,0:T(8,128)S(1)} %get-tuple-element.20), channel_id=1, source_target_pairs={{0,12},{1,13},{2,14},{3,15},{4,8},{5,9},{6,10},{7,11},{8,4},{9,5},... | collective-permute-start | bytes 208904 | tf_op jit(solution)/shard_map/ppermute | solution.py:347
  19.0 7.2 %collective-permute-start.12 = (f32[17,8,128]{2,1,0:T(8,128)S(1)}, f32[17,8,128]{2,1,0:T(8,128)S(1)}, u32[]{:S(2)}, u32[]{:S(2)}) collective-permute-start(f32[17,8,128]{2,1,0:T(8,128)S(1)} %shard_map.60.refs_0_), channel_id=1, source_target_pairs={{0,16},{4,20},{8,24},{12,28},{16,0},{20,4},{24,8},{28,12},{1,17},{... | collective-permute-start | bytes 208904 | tf_op jit(solution)/shard_map/ppermute | solution.py:354
  23.0 6.8 %collective-permute-start.5 = (f32[17,8,128]{2,1,0:T(8,128)S(1)}, f32[17,8,128]{2,1,0:T(8,128)S(1)}, u32[]{:S(2)}, u32[]{:S(2)}) collective-permute-start(f32[17,8,128]{2,1,0:T(8,128)S(1)} %shard_map.58.refs_0_), channel_id=1, source_target_pairs={{0,16},{4,20},{8,24},{12,28},{16,0},{20,4},{24,8},{28,12},{1,17},{... | collective-permute-start | bytes 208904 | tf_op jit(solution)/shard_map/ppermute | solution.py:354
  26.2 6.5 %collective-permute-start.15 = (f32[17,8,128]{2,1,0:T(8,128)S(1)}, f32[17,8,128]{2,1,0:T(8,128)S(1)}, u32[]{:S(2)}, u32[]{:S(2)}) collective-permute-start(f32[17,8,128]{2,1,0:T(8,128)S(1)} %shard_map.61.refs_0_), channel_id=1, source_target_pairs={{0,12},{1,13},{2,14},{3,15},{4,8},{5,9},{6,10},{7,11},{8,4},{9,5},... | collective-permute-start | bytes 208904 | tf_op jit(solution)/shard_map/ppermute | solution.py:347
  27.1 6.7 %collective-permute-start.14 = (f32[17,8,128]{2,1,0:T(8,128)S(1)}, f32[17,8,128]{2,1,0:T(8,128)S(1)}, u32[]{:S(2)}, u32[]{:S(2)}) collective-permute-start(f32[17,8,128]{2,1,0:T(8,128)S(1)} %shard_map.61.refs_0_), channel_id=1, source_target_pairs={{0,8},{1,5},{2,10},{3,7},{4,12},{5,1},{6,14},{7,3},{8,0},{9,13},{1... | collective-permute-start | bytes 208904 | tf_op jit(solution)/shard_map/ppermute | solution.py:347
  29.2 4.6 %collective-permute-start.13 = (f32[17,8,128]{2,1,0:T(8,128)S(1)}, f32[17,8,128]{2,1,0:T(8,128)S(1)}, u32[]{:S(2)}, u32[]{:S(2)}) collective-permute-start(f32[17,8,128]{2,1,0:T(8,128)S(1)} %shard_map.61.refs_0_), channel_id=1, source_target_pairs={{0,4},{1,9},{2,6},{3,11},{4,0},{5,13},{6,2},{7,15},{8,12},{9,1},{1... | collective-permute-start | bytes 208904 | tf_op jit(solution)/shard_map/ppermute | solution.py:347
  29.8 5.3 %collective-permute-start.8 = (f32[17,8,128]{2,1,0:T(8,128)S(1)}, f32[17,8,128]{2,1,0:T(8,128)S(1)}, u32[]{:S(2)}, u32[]{:S(2)}) collective-permute-start(f32[17,8,128]{2,1,0:T(8,128)S(1)} %shard_map.59.refs_0_), channel_id=1, source_target_pairs={{0,12},{1,13},{2,14},{3,15},{4,8},{5,9},{6,10},{7,11},{8,4},{9,5},... | collective-permute-start | bytes 208904 | tf_op jit(solution)/shard_map/ppermute | solution.py:347
  30.8 5.1 %collective-permute-start.7 = (f32[17,8,128]{2,1,0:T(8,128)S(1)}, f32[17,8,128]{2,1,0:T(8,128)S(1)}, u32[]{:S(2)}, u32[]{:S(2)}) collective-permute-start(f32[17,8,128]{2,1,0:T(8,128)S(1)} %shard_map.59.refs_0_), channel_id=1, source_target_pairs={{0,8},{1,5},{2,10},{3,7},{4,12},{5,1},{6,14},{7,3},{8,0},{9,13},{1... | collective-permute-start | bytes 208904 | tf_op jit(solution)/shard_map/ppermute | solution.py:347
  32.8 4.3 %collective-permute-start.6 = (f32[17,8,128]{2,1,0:T(8,128)S(1)}, f32[17,8,128]{2,1,0:T(8,128)S(1)}, u32[]{:S(2)}, u32[]{:S(2)}) collective-permute-start(f32[17,8,128]{2,1,0:T(8,128)S(1)} %shard_map.59.refs_0_), channel_id=1, source_target_pairs={{0,4},{1,9},{2,6},{3,11},{4,0},{5,13},{6,2},{7,15},{8,12},{9,1},{1... | collective-permute-start | bytes 208904 | tf_op jit(solution)/shard_map/ppermute | solution.py:347

commit v13 on v12

--- a/solution.py
+++ b/solution.py
@@ -172,6 +172,9 @@
     odd = dom % 2 == 1
     ends, (state_ref, far_ref, near_ref), refs = refs[:4], refs[4:7], refs[7:]
     out_refs, (slab, state_a, state_b, *coefs) = refs[:-7], refs[-7:]
+    chunk_refs = []
+    for own_ref, second_ref, sent_ref in zip(*(out_refs[k::3] for k in range(3))):
+        chunk_refs += [own_ref, sent_ref.at[0], second_ref, sent_ref.at[1]]
 
     def stage(j):
         far, near = far_ref[j], near_ref[j]
@@ -213,7 +216,7 @@
         )
 
     def last(source):
-        for k, out_ref in enumerate(out_refs):
+        for k, out_ref in enumerate(chunk_refs):
             stream, meet = divmod(k, SQUARE)
             chunk = stream * SQUARE + (me_ref[0] ^ partners(dom_ref[0])[meet])
             emit = functools.partial(finish, out_ref)
@@ -222,16 +225,23 @@
     run_steps(strips, HALF, load, (state_a, state_b), coefs, last)
 
 
-def sum_kernel(*refs):
-    *parts, out_ref = refs
-    total = parts[0][...]
-    for part in parts[1:]:
-        total = total + part[...]
-    out_ref[...] = total
+def first_kernel(own_ref, second_ref, theirs_ref, own_out, second_out):
+    own_out[...] = own_ref[...] + theirs_ref[0]
+    second_out[...] = second_ref[...] + theirs_ref[1]
+
+
+def sum_kernel(mine_ref, theirs_ref, out_ref):
+    out_ref[...] = mine_ref[...] + theirs_ref[...]
+
+
+def pair_kernel(own_ref, second_ref, out_ref):
+    out_ref[0] = own_ref[...]
+    out_ref[1] = second_ref[...]
 
 
 def nodal_kernel(per_chunk, depth, stream, dom_ref, me_ref, level_ref, *refs):
-    totals, (out_ref, values, sems) = refs[:SQUARE], refs[-3:]
+    (own_ref, second_ref, theirs_ref), (out_ref, values, sems) = refs[:3], refs[-3:]
+    totals = own_ref, theirs_ref.at[0], second_ref, theirs_ref.at[1]
     many = values.shape[1]
     level = level_ref[0]
     fine, mid, low = (jnp.where(level >= depth - down, 1.0, 0.0) for down in range(3))
@@ -332,7 +342,7 @@
     chunk = (per_chunk * TILE + -(-per_chunk // many), many, LANES)
     weighted = call(
         functools.partial(edge_kernel, per_chunk, depth, doms),
-        [chunk] * (SQUARE * STREAMS),
+        [chunk, chunk, (2, *chunk)] * STREAMS,
         (dom, me, levels, coefficient, tiles[0], *ends, state, far, near),
         4,
         [vmem(3, strips, SLAB, LANES)]
@@ -346,19 +356,21 @@
         pairs = [(g * doms + d, (g ^ partners(d % 2)[meet]) * doms + d) for g, d in devices]
         return lax.ppermute(array, ("grp", "dom"), pairs)
 
-    def over_grids(own, *others):
-        theirs = [swap(array, meet) for meet, array in enumerate(others, 1)]
-        (total,) = call(sum_kernel, [chunk], (own, *theirs))
+    def over_grids(own, second, sent):
+        own, second = call(first_kernel, [chunk] * 2, (own, second, swap(sent, 1)))
+        (total,) = call(sum_kernel, [chunk], (own, swap(second, 2)))
         apart = SQUARE
         while apart < grids:
             other = lax.ppermute(total, "grp", [(g, g ^ apart) for g in range(grids)])
             (total,) = call(sum_kernel, [chunk], (total, other))
             apart *= 2
-        return [total] + [swap(total, meet) for meet in range(1, SQUARE)]
+        second = swap(total, 2)
+        (pair,) = call(pair_kernel, [(2, *chunk)], (total, second))
+        return total, second, swap(pair, 1)
 
     nodal = None
     for stream in range(STREAMS):
-        totals = over_grids(*weighted[stream * SQUARE : (stream + 1) * SQUARE])
+        totals = over_grids(*weighted[stream * 3 : (stream + 1) * 3])
         (nodal,) = call(
             functools.partial(nodal_kernel, per_chunk, depth, stream),
             [(many, strips, TILE, LANES)],

time: 38.3 us -> 39.7 us (1.037)
  waiting for transfers between devices: 5.13 us -> 12 us
  starting transfers between devices: 25.5 us -> 20 us
    ppermute x12 -> x8, starting transfers between devices: 15.1 us -> 10.1 us  [swap(): return lax.ppermute(array, ('grp', 'dom'), pairs)]
    ppermute x12 -> x8, waiting for transfers between devices: 4.36 us -> 9.03 us  [swap(): return lax.ppermute(array, ('grp', 'dom'), pairs)]
    ppermute x2, waiting for transfers between devices: 0.76 us -> 2.96 us  [over_grids(): other = lax.ppermute(total, 'grp', [(g, g ^ apart) for g in range(grids)])]
    ppermute x2, starting transfers between devices: 5.16 us -> 4.7 us  [over_grids(): other = lax.ppermute(total, 'grp', [(g, g ^ apart) for g in range(grids)])]
    pallas_call x9 -> x13, Pallas kernels: 4.95 us -> 4.96 us  [call(): pl.pallas_call(kernel, out_shape=[jax.ShapeDtypeStruct(shape, jnp.float32...]
  transfers between devices with their start and end apart: 16 -> 12, of which waited for: 6 -> 7; matrix products, arithmetic and copies ran while one was open for 0% -> 0% of each run, Pallas kernels for 8% -> 8%
where the time goes in v13:
time: 39.7 us; the launch traced here: 39.6 us
  starting transfers between devices  20 us (50%)
  waiting for transfers between devices  12 us (30%)
  Pallas kernels  4.96 us (12%)
  between operations  1.41 us (4%)
  local copies, waits for them, and re-layouts  1.17 us (3%)
    ppermute x8, starting transfers between devices, swap(): return lax.ppermute(array, ('grp', 'dom'), pairs)  10.1 us
    ppermute x8, waiting for transfers between devices, swap(): return lax.ppermute(array, ('grp', 'dom'), pairs)  9.03 us
    ppermute x2, starting transfers between devices, on_device(): lax.ppermute(array, 'dom', pairs)  5.19 us
    pallas_call x13, Pallas kernels, call(): pl.pallas_call(kernel, out_shape=[jax.ShapeDtypeStruct(shape, jnp.float32...  4.96 us
    ppermute x2, starting transfers between devices, over_grids(): other = lax.ppermute(total, 'grp', [(g, g ^ apart) for g in range(grids)])  4.7 us
    ppermute x2, waiting for transfers between devices, over_grids(): other = lax.ppermute(total, 'grp', [(g, g ^ apart) for g in range(grids)])  2.96 us
    squeeze x1, local copies, waits for them, and re-layouts, on_device(): ends = [x[at] for x in tiles[1:] for at in (0, many - 1)]  1.01 us
  transfers between devices with their start and end apart: 12, of which 7 were waited for; matrix products, arithmetic and copies ran while one was open for 0% of the time, Pallas kernels for 8%

profile of v13, /device:TPU:0, one launch (start us, length us, event | category | flops | bytes accessed | tf_op | source)
XLA Modules:
  0.0 39.6 jit_solution(7737421278705639635)
XLA Ops:
  0.0 0.0 copy-start
  0.0 1.0 %slice_bitcast_fusion = (f32[16,8,128]{2,1,0:T(8,128)S(1)}, f32[16,8,128]{2,1,0:T(8,128)S(1)}, f32[16,8,128]{2,1,0:T(8,128)S(1)}, f32[16,8,128]{2,1,0:T(8,128)S(1)}) fusion(f32[8,16,8,128]{3,2,1,0:T(8,128)} %bitcast.25, f32[8,16,8,128]{3,2,1,0:T(8,128)} %bitcast.27), kind=kLoop, calls=%fused_computation | loop fusion | bytes 524288 | tf_op jit(solution)/shard_map/squeeze | solution.py:320
  1.0 0.1 copy-done
  1.2 0.0 copy-start.1
  1.2 0.0 copy-start.2
  1.2 0.8 %collective-permute-start = (f32[16,16,128]{2,1,0:T(8,128)S(1)}, f32[16,16,128]{2,1,0:T(8,128)S(1)}, u32[]{:S(2)}, u32[]{:S(2)}) collective-permute-start(f32[16,16,128]{2,1,0:T(8,128)S(1)} %get-tuple-element.17), channel_id=1, source_target_pairs={{0,0},{1,2},{2,1},{3,3},{4,4},{5,6},{6,5},{7,7},{8,8},{9,10},{10,9... | collective-permute-start | bytes 393224 | tf_op jit(solution)/shard_map/ppermute | solution.py:331
  2.0 4.4 %collective-permute-start.1 = (f32[16,16,128]{2,1,0:T(8,128)S(1)}, f32[16,16,128]{2,1,0:T(8,128)S(1)}, u32[]{:S(2)}, u32[]{:S(2)}) collective-permute-start(f32[16,16,128]{2,1,0:T(8,128)S(1)} %get-tuple-element.18), channel_id=1, source_target_pairs={{0,1},{1,0},{2,3},{3,2},{4,5},{5,4},{6,7},{7,6},{8,9},{9,8},{10,11... | collective-permute-start | bytes 393224 | tf_op jit(solution)/shard_map/ppermute | solution.py:331
  7.7 0.0 copy-done.1
  7.7 0.0 copy-done.2
  7.7 1.9 %shard_map.55.refs_4_ = f32[16,8,8,128]{3,2,1,0:T(8,128)S(1)} custom-call(f32[8,16,8,128]{3,2,1,0:T(8,128)S(1)} %bitcast.23, f32[8,16,8,128]{3,2,1,0:T(8,128)S(1)} %bitcast.28, f32[8,16,8,128]{3,2,1,0:T(8,128)S(1)} %bitcast.26), custom_call_target="tpu_custom_call" | custom-call | flops 5242880 | bytes 1572864 | tf_op jit(solution)/shard_map/pallas_call | solution.py:295
  9.6 0.0 collective-permute-done.refs_5_
  9.6 0.0 collective-permute-done.1.refs_6_
  9.6 0.9 %shard_map.57 = (f32[17,8,128]{2,1,0:T(8,128)S(1)}, f32[17,8,128]{2,1,0:T(8,128)S(1)}, f32[2,17,8,128]{3,2,1,0:T(8,128)S(1)}, f32[17,8,128]{2,1,0:T(8,128)S(1)},...) custom-call(s32[1]{0:T(128)} %bitcast.dom_ref, s32[1]{0:T(128)} %bitcast.1.me_ref, s32[1]{0:T(128)S(6)} %copy.8.level_ref, ...), custom_call_target="tpu_custom_call" | custom-call | flops 2621440 | bytes 1572880 | tf_op jit(solution)/shard_map/pallas_call | solution.py:295
  10.5 1.6 %collective-permute-start.7 = (f32[2,17,8,128]{3,2,1,0:T(8,128)S(1)}, f32[2,17,8,128]{3,2,1,0:T(8,128)S(1)}, u32[]{:S(2)}, u32[]{:S(2)}) collective-permute-start(f32[2,17,8,128]{3,2,1,0:T(8,128)S(1)} %get-tuple-element.26), channel_id=1, source_target_pairs={{0,4},{1,9},{2,6},{3,11},{4,0},{5,13},{6,2},{7,15},{8,12},{9,1},{1... | collective-permute-start | bytes 417800 | tf_op jit(solution)/shard_map/ppermute | solution.py:357
  12.1 0.5 %collective-permute-start.2 = (f32[2,17,8,128]{3,2,1,0:T(8,128)S(1)}, f32[2,17,8,128]{3,2,1,0:T(8,128)S(1)}, u32[]{:S(2)}, u32[]{:S(2)}) collective-permute-start(f32[2,17,8,128]{3,2,1,0:T(8,128)S(1)} %get-tuple-element.21), channel_id=1, source_target_pairs={{0,4},{1,9},{2,6},{3,11},{4,0},{5,13},{6,2},{7,15},{8,12},{9,1},{1... | collective-permute-start | bytes 417800 | tf_op jit(solution)/shard_map/ppermute | solution.py:357
  12.6 3.0 %collective-permute-done.7.theirs_ref = f32[2,17,8,128]{3,2,1,0:T(8,128)S(1)} collective-permute-done((f32[2,17,8,128]{3,2,1,0:T(8,128)S(1)}, f32[2,17,8,128]{3,2,1,0:T(8,128)S(1)}, u32[]{:S(2)}, u32[]{:S(2)}) %collective-permute-start.7) | collective-permute-done | bytes 139296 | tf_op jit(solution)/shard_map/ppermute | solution.py:357
  15.7 1.6 %collective-permute-start.8 = (f32[17,8,128]{2,1,0:T(8,128)S(1)}, f32[17,8,128]{2,1,0:T(8,128)S(1)}, u32[]{:S(2)}, u32[]{:S(2)}) collective-permute-start(f32[17,8,128]{2,1,0:T(8,128)S(1)} %get-tuple-element.28), channel_id=1, source_target_pairs={{0,8},{1,5},{2,10},{3,7},{4,12},{5,1},{6,14},{7,3},{8,0},{9,13},{1... | collective-permute-start | bytes 208904 | tf_op jit(solution)/shard_map/ppermute | solution.py:357
  17.3 0.0 collective-permute-done.2.theirs_ref
  17.3 1.5 %collective-permute-start.3 = (f32[17,8,128]{2,1,0:T(8,128)S(1)}, f32[17,8,128]{2,1,0:T(8,128)S(1)}, u32[]{:S(2)}, u32[]{:S(2)}) collective-permute-start(f32[17,8,128]{2,1,0:T(8,128)S(1)} %get-tuple-element.23), channel_id=1, source_target_pairs={{0,8},{1,5},{2,10},{3,7},{4,12},{5,1},{6,14},{7,3},{8,0},{9,13},{1... | collective-permute-start | bytes 208904 | tf_op jit(solution)/shard_map/ppermute | solution.py:357
  18.8 1.2 %collective-permute-done.8.theirs_ref = f32[17,8,128]{2,1,0:T(8,128)S(1)} collective-permute-done((f32[17,8,128]{2,1,0:T(8,128)S(1)}, f32[17,8,128]{2,1,0:T(8,128)S(1)}, u32[]{:S(2)}, u32[]{:S(2)}) %collective-permute-start.8) | collective-permute-done | bytes 69664 | tf_op jit(solution)/shard_map/ppermute | solution.py:357
  20.1 2.7 %collective-permute-start.9 = (f32[17,8,128]{2,1,0:T(8,128)S(1)}, f32[17,8,128]{2,1,0:T(8,128)S(1)}, u32[]{:S(2)}, u32[]{:S(2)}) collective-permute-start(f32[17,8,128]{2,1,0:T(8,128)S(1)} %shard_map.63.mine_ref), channel_id=1, source_target_pairs={{0,16},{4,20},{8,24},{12,28},{16,0},{20,4},{24,8},{28,12},{1,17},{... | collective-permute-start | bytes 208904 | tf_op jit(solution)/shard_map/ppermute | solution.py:364
  22.7 0.0 collective-permute-done.3.theirs_ref
  22.7 2.0 %collective-permute-start.4 = (f32[17,8,128]{2,1,0:T(8,128)S(1)}, f32[17,8,128]{2,1,0:T(8,128)S(1)}, u32[]{:S(2)}, u32[]{:S(2)}) collective-permute-start(f32[17,8,128]{2,1,0:T(8,128)S(1)} %shard_map.59.mine_ref), channel_id=1, source_target_pairs={{0,16},{4,20},{8,24},{12,28},{16,0},{20,4},{24,8},{28,12},{1,17},{... | collective-permute-start | bytes 208904 | tf_op jit(solution)/shard_map/ppermute | solution.py:364
  24.8 2.3 %collective-permute-done.9.theirs_ref = f32[17,8,128]{2,1,0:T(8,128)S(1)} collective-permute-done((f32[17,8,128]{2,1,0:T(8,128)S(1)}, f32[17,8,128]{2,1,0:T(8,128)S(1)}, u32[]{:S(2)}, u32[]{:S(2)}) %collective-permute-start.9) | collective-permute-done | bytes 69664 | tf_op jit(solution)/shard_map/ppermute | solution.py:364
  27.0 0.3 collective-permute-start.10
  27.3 0.7 %collective-permute-done.4.theirs_ref = f32[17,8,128]{2,1,0:T(8,128)S(1)} collective-permute-done((f32[17,8,128]{2,1,0:T(8,128)S(1)}, f32[17,8,128]{2,1,0:T(8,128)S(1)}, u32[]{:S(2)}, u32[]{:S(2)}) %collective-permute-start.4) | collective-permute-done | bytes 69664 | tf_op jit(solution)/shard_map/ppermute | solution.py:364
  28.0 1.6 %collective-permute-start.5 = (f32[17,8,128]{2,1,0:T(8,128)S(1)}, f32[17,8,128]{2,1,0:T(8,128)S(1)}, u32[]{:S(2)}, u32[]{:S(2)}) collective-permute-start(f32[17,8,128]{2,1,0:T(8,128)S(1)} %shard_map.60.own_ref.refs_0_), channel_id=1, source_target_pairs={{0,8},{1,5},{2,10},{3,7},{4,12},{5,1},{6,14},{7,3},{8,0},{9,13},{1... | collective-permute-start | bytes 208904 | tf_op jit(solution)/shard_map/ppermute | solution.py:357
  29.7 2.2 %collective-permute-done.10.second_ref.refs_1_ = f32[17,8,128]{2,1,0:T(8,128)S(1)} collective-permute-done((f32[17,8,128]{2,1,0:T(8,128)S(1)}, f32[17,8,128]{2,1,0:T(8,128)S(1)}, u32[]{:S(2)}, u32[]{:S(2)}) %collective-permute-start.10) | collective-permute-done | bytes 69664 | tf_op jit(solution)/shard_map/ppermute | solution.py:357
  31.8 1.6 %collective-permute-start.11 = (f32[2,17,8,128]{3,2,1,0:T(8,128)S(1)}, f32[2,17,8,128]{3,2,1,0:T(8,128)S(1)}, u32[]{:S(2)}, u32[]{:S(2)}) collective-permute-start(f32[2,17,8,128]{3,2,1,0:T(8,128)S(1)} %shard_map.65), channel_id=1, source_target_pairs={{0,4},{1,9},{2,6},{3,11},{4,0},{5,13},{6,2},{7,15},{8,12},{9,1},{1... | collective-permute-start | bytes 417800 | tf_op jit(solution)/shard_map/ppermute | solution.py:357
  33.4 0.0 collective-permute-done.5.second_ref.refs_1_
  33.4 1.5 %collective-permute-start.6 = (f32[2,17,8,128]{3,2,1,0:T(8,128)S(1)}, f32[2,17,8,128]{3,2,1,0:T(8,128)S(1)}, u32[]{:S(2)}, u32[]{:S(2)}) collective-permute-start(f32[2,17,8,128]{3,2,1,0:T(8,128)S(1)} %shard_map.61), channel_id=1, source_target_pairs={{0,4},{1,9},{2,6},{3,11},{4,0},{5,13},{6,2},{7,15},{8,12},{9,1},{1... | collective-permute-start | bytes 417800 | tf_op jit(solution)/shard_map/ppermute | solution.py:357
  34.9 2.1 %collective-permute-done.11.refs_2_ = f32[2,17,8,128]{3,2,1,0:T(8,128)S(1)} collective-permute-done((f32[2,17,8,128]{3,2,1,0:T(8,128)S(1)}, f32[2,17,8,128]{3,2,1,0:T(8,128)S(1)}, u32[]{:S(2)}, u32[]{:S(2)}) %collective-permute-start.11) | collective-permute-done | bytes 139296 | tf_op jit(solution)/shard_map/ppermute | solution.py:357
  36.9 1.0 %shard_map.66.refs_3_ = f32[8,16,8,128]{3,2,1,0:T(8,128)} custom-call(s32[1]{0:T(128)} %bitcast.dom_ref, s32[1]{0:T(128)} %bitcast.1.me_ref, s32[1]{0:T(128)S(6)} %copy.8.level_ref, f32[17,8,128]{2,1,0:T(8,128)S(1)} %shard_map.64.own_ref.refs_0_, f32[17,8,128]{2,1,0:T(8,128)S(1)} %collective-permute-done.10.second_ref.refs_1_, ...), custom_call_target="tpu_custom_call" | custom-call | bytes 278540 | tf_op jit(solution)/shard_map/pallas_call | solution.py:295
  38.0 0.5 %collective-permute-done.6.refs_2_ = f32[2,17,8,128]{3,2,1,0:T(8,128)S(1)} collective-permute-done((f32[2,17,8,128]{3,2,1,0:T(8,128)S(1)}, f32[2,17,8,128]{3,2,1,0:T(8,128)S(1)}, u32[]{:S(2)}, u32[]{:S(2)}) %collective-permute-start.6) | collective-permute-done | bytes 139296 | tf_op jit(solution)/shard_map/ppermute | solution.py:357
  38.5 1.0 %shard_map.67 = f32[8,16,8,128]{3,2,1,0:T(8,128)} custom-call(s32[1]{0:T(128)} %bitcast.dom_ref, s32[1]{0:T(128)} %bitcast.1.me_ref, s32[1]{0:T(128)S(6)} %copy.8.level_ref, f32[17,8,128]{2,1,0:T(8,128)S(1)} %shard_map.60.own_ref.refs_0_, f32[17,8,128]{2,1,0:T(8,128)S(1)} %collective-permute-done.5.second_ref.refs_1_, ...), custom_call_target="tpu_custom_call", output_to_operand_aliasing={{}: (6, {})} | custom-call | bytes 802828 | tf_op jit(solution)/shard_map/pallas_call | solution.py:295
  (9 shorter events, 0.1 us)
Async XLA Ops:
  0.0 1.2 %copy-start = (f32[1,64,2048]{2,1,0:T(8,128)S(1)}, f32[1,64,2048]{2,1,0:T(8,128)}, u32[]{:S(2)}) copy-start(f32[1,64,2048]{2,1,0:T(8,128)} %param.5) | copy-start | bytes 1572868
  1.2 6.5 %copy-start.1 = (f32[1,64,2048]{2,1,0:T(8,128)S(1)}, f32[1,64,2048]{2,1,0:T(8,128)}, u32[]{:S(2)}) copy-start(f32[1,64,2048]{2,1,0:T(8,128)} %param.7) | copy-start | bytes 1572868
  1.2 6.6 %copy-start.2 = (f32[1,64,2048]{2,1,0:T(8,128)S(1)}, f32[1,64,2048]{2,1,0:T(8,128)}, u32[]{:S(2)}) copy-start(f32[1,64,2048]{2,1,0:T(8,128)} %param.6) | copy-start | bytes 1572868
  1.2 8.4 %collective-permute-start = (f32[16,16,128]{2,1,0:T(8,128)S(1)}, f32[16,16,128]{2,1,0:T(8,128)S(1)}, u32[]{:S(2)}, u32[]{:S(2)}) collective-permute-start(f32[16,16,128]{2,1,0:T(8,128)S(1)} %get-tuple-element.17), channel_id=1, source_target_pairs={{0,0},{1,2},{2,1},{3,3},{4,4},{5,6},{6,5},{7,7},{8,8},{9,10},{10,9... | collective-permute-start | bytes 393224 | tf_op jit(solution)/shard_map/ppermute | solution.py:331
  2.0 7.6 %collective-permute-start.1 = (f32[16,16,128]{2,1,0:T(8,128)S(1)}, f32[16,16,128]{2,1,0:T(8,128)S(1)}, u32[]{:S(2)}, u32[]{:S(2)}) collective-permute-start(f32[16,16,128]{2,1,0:T(8,128)S(1)} %get-tuple-element.18), channel_id=1, source_target_pairs={{0,1},{1,0},{2,3},{3,2},{4,5},{5,4},{6,7},{7,6},{8,9},{9,8},{10,11... | collective-permute-start | bytes 393224 | tf_op jit(solution)/shard_map/ppermute | solution.py:331
  10.5 5.1 %collective-permute-start.7 = (f32[2,17,8,128]{3,2,1,0:T(8,128)S(1)}, f32[2,17,8,128]{3,2,1,0:T(8,128)S(1)}, u32[]{:S(2)}, u32[]{:S(2)}) collective-permute-start(f32[2,17,8,128]{3,2,1,0:T(8,128)S(1)} %get-tuple-element.26), channel_id=1, source_target_pairs={{0,4},{1,9},{2,6},{3,11},{4,0},{5,13},{6,2},{7,15},{8,12},{9,1},{1... | collective-permute-start | bytes 417800 | tf_op jit(solution)/shard_map/ppermute | solution.py:357
  12.1 5.2 %collective-permute-start.2 = (f32[2,17,8,128]{3,2,1,0:T(8,128)S(1)}, f32[2,17,8,128]{3,2,1,0:T(8,128)S(1)}, u32[]{:S(2)}, u32[]{:S(2)}) collective-permute-start(f32[2,17,8,128]{3,2,1,0:T(8,128)S(1)} %get-tuple-element.21), channel_id=1, source_target_pairs={{0,4},{1,9},{2,6},{3,11},{4,0},{5,13},{6,2},{7,15},{8,12},{9,1},{1... | collective-permute-start | bytes 417800 | tf_op jit(solution)/shard_map/ppermute | solution.py:357
  15.7 4.4 %collective-permute-start.8 = (f32[17,8,128]{2,1,0:T(8,128)S(1)}, f32[17,8,128]{2,1,0:T(8,128)S(1)}, u32[]{:S(2)}, u32[]{:S(2)}) collective-permute-start(f32[17,8,128]{2,1,0:T(8,128)S(1)} %get-tuple-element.28), channel_id=1, source_target_pairs={{0,8},{1,5},{2,10},{3,7},{4,12},{5,1},{6,14},{7,3},{8,0},{9,13},{1... | collective-permute-start | bytes 208904 | tf_op jit(solution)/shard_map/ppermute | solution.py:357
  17.3 5.4 %collective-permute-start.3 = (f32[17,8,128]{2,1,0:T(8,128)S(1)}, f32[17,8,128]{2,1,0:T(8,128)S(1)}, u32[]{:S(2)}, u32[]{:S(2)}) collective-permute-start(f32[17,8,128]{2,1,0:T(8,128)S(1)} %get-tuple-element.23), channel_id=1, source_target_pairs={{0,8},{1,5},{2,10},{3,7},{4,12},{5,1},{6,14},{7,3},{8,0},{9,13},{1... | collective-permute-start | bytes 208904 | tf_op jit(solution)/shard_map/ppermute | solution.py:357
  20.1 7.0 %collective-permute-start.9 = (f32[17,8,128]{2,1,0:T(8,128)S(1)}, f32[17,8,128]{2,1,0:T(8,128)S(1)}, u32[]{:S(2)}, u32[]{:S(2)}) collective-permute-start(f32[17,8,128]{2,1,0:T(8,128)S(1)} %shard_map.63.mine_ref), channel_id=1, source_target_pairs={{0,16},{4,20},{8,24},{12,28},{16,0},{20,4},{24,8},{28,12},{1,17},{... | collective-permute-start | bytes 208904 | tf_op jit(solution)/shard_map/ppermute | solution.py:364
  22.7 5.3 %collective-permute-start.4 = (f32[17,8,128]{2,1,0:T(8,128)S(1)}, f32[17,8,128]{2,1,0:T(8,128)S(1)}, u32[]{:S(2)}, u32[]{:S(2)}) collective-permute-start(f32[17,8,128]{2,1,0:T(8,128)S(1)} %shard_map.59.mine_ref), channel_id=1, source_target_pairs={{0,16},{4,20},{8,24},{12,28},{16,0},{20,4},{24,8},{28,12},{1,17},{... | collective-permute-start | bytes 208904 | tf_op jit(solution)/shard_map/ppermute | solution.py:364
  27.0 4.8 %collective-permute-start.10 = (f32[17,8,128]{2,1,0:T(8,128)S(1)}, f32[17,8,128]{2,1,0:T(8,128)S(1)}, u32[]{:S(2)}, u32[]{:S(2)}) collective-permute-start(f32[17,8,128]{2,1,0:T(8,128)S(1)} %shard_map.64.own_ref.refs_0_), channel_id=1, source_target_pairs={{0,8},{1,5},{2,10},{3,7},{4,12},{5,1},{6,14},{7,3},{8,0},{9,13},{1... | collective-permute-start | bytes 208904 | tf_op jit(solution)/shard_map/ppermute | solution.py:357
  28.0 5.4 %collective-permute-start.5 = (f32[17,8,128]{2,1,0:T(8,128)S(1)}, f32[17,8,128]{2,1,0:T(8,128)S(1)}, u32[]{:S(2)}, u32[]{:S(2)}) collective-permute-start(f32[17,8,128]{2,1,0:T(8,128)S(1)} %shard_map.60.own_ref.refs_0_), channel_id=1, source_target_pairs={{0,8},{1,5},{2,10},{3,7},{4,12},{5,1},{6,14},{7,3},{8,0},{9,13},{1... | collective-permute-start | bytes 208904 | tf_op jit(solution)/shard_map/ppermute | solution.py:357
  31.8 5.1 %collective-permute-start.11 = (f32[2,17,8,128]{3,2,1,0:T(8,128)S(1)}, f32[2,17,8,128]{3,2,1,0:T(8,128)S(1)}, u32[]{:S(2)}, u32[]{:S(2)}) collective-permute-start(f32[2,17,8,128]{3,2,1,0:T(8,128)S(1)} %shard_map.65), channel_id=1, source_target_pairs={{0,4},{1,9},{2,6},{3,11},{4,0},{5,13},{6,2},{7,15},{8,12},{9,1},{1... | collective-permute-start | bytes 417800 | tf_op jit(solution)/shard_map/ppermute | solution.py:357
  33.4 5.1 %collective-permute-start.6 = (f32[2,17,8,128]{3,2,1,0:T(8,128)S(1)}, f32[2,17,8,128]{3,2,1,0:T(8,128)S(1)}, u32[]{:S(2)}, u32[]{:S(2)}) collective-permute-start(f32[2,17,8,128]{3,2,1,0:T(8,128)S(1)} %shard_map.61), channel_id=1, source_target_pairs={{0,4},{1,9},{2,6},{3,11},{4,0},{5,13},{6,2},{7,15},{8,12},{9,1},{1... | collective-permute-start | bytes 417800 | tf_op jit(solution)/shard_map/ppermute | solution.py:357

commit v14 on v11

--- a/solution.py
+++ b/solution.py
@@ -15,7 +15,7 @@
 SQUARE = 4
 UNROLL = 16
 VMEM_LIMIT = 40 * 1024 * 1024
-HALO_FLOPS = 4000
+LOAD_FLOPS = 4000
 
 
 def tiles_of(block):
@@ -122,19 +122,27 @@
     )
 
 
-def first_kernel(out_ref):
-    out_ref[...] = jnp.zeros(out_ref.shape, jnp.float32)
-
-
-def pack_kernel(dom_ref, ready_ref, dens_ref, *refs):
-    del ready_ref
-    diff_ref, drift_ref, far_ref, near_ref = refs
+def ones_kernel(out_ref):
+    out_ref[...] = jnp.ones(out_ref.shape, jnp.float32)
+
+
+def weights_kernel(depth, level_ref, coef_ref, ones_ref, keep_ref, weight_ref):
+    coef = coef_ref[0].astype(jnp.float32)
+    for down in range(3):
+        keep_ref[down] = jnp.where(level_ref[0] >= depth - down, ones_ref[...], 0.0)
+        weight_ref[down] = coef * keep_ref[down]
+    weight_ref[3] = coef * ones_ref[...]
+
+
+def pack_kernel(dom_ref, weight_ref, dens_ref, diff_ref, drift_ref, near_ref, far_ref):
+    del weight_ref
     many, strips = dens_ref.shape[:2]
     odd = dom_ref[0] % 2 == 1
     upper = lax.broadcasted_iota(jnp.int32, (TILE, LANES), 0) < HALF
 
     def body(j):
-        mix_next = jnp.where(upper, pltpu.roll(drift_ref[many - 1, j], HALF, 0), diff_ref[many - 1, j])
+        drift_last = pltpu.roll(drift_ref[many - 1, j], HALF, 0)
+        mix_next = jnp.where(upper, drift_last, diff_ref[many - 1, j])
         mix_prev = jnp.where(upper, diff_ref[0, j], pltpu.roll(drift_ref[0, j], HALF, 0))
         to_next, to_prev = (dens_ref[many - 1, j], mix_next), (dens_ref[0, j], mix_prev)
         for k in range(2):
@@ -168,12 +176,12 @@
 
 
 def edge_kernel(
-    per_chunk, depth, doms, dom_ref, me_ref, level_ref, coef_ref, dens_ref, *refs
+    per_chunk, doms, dom_ref, me_ref, weight_ref, dens_ref, *refs
 ):
     many, strips = dens_ref.shape[:2]
     dom = dom_ref[0]
     odd = dom % 2 == 1
-    diff_ref, drift_ref, state_ref, far_ref, near_ref, *rest = refs
+    diff_ref, drift_ref, state_ref, near_ref, far_ref, *rest = refs
     out_refs, (slab, state_a, state_b, *coefs) = rest[:SQUARE], rest[SQUARE:]
 
     def stage(j):
@@ -204,8 +212,7 @@
         ]
 
     place = lax.broadcasted_iota(jnp.int32, (many, LANES), 0)
-    coef = coef_ref[0].astype(jnp.float32)
-    weights = [jnp.where(level_ref[0] >= depth - down, coef, 0.0) for down in range(3)] + [coef]
+    weights = [weight_ref[k] for k in range(4)]
 
     def finish(out_ref, j, part, new):
         s = [state_ref[j, t] for t in range(TILE)]
@@ -217,7 +224,7 @@
         for t in range(TILE):
             out_ref[part * TILE + t] = weighted[t]
         out_ref[per_chunk * TILE + part // many, pl.ds(lax.rem(part, many), 1), :] = (
-            coef * before
+            weights[3][0:1] * before
         )
 
     def last(source):
@@ -237,11 +244,10 @@
     out_ref[...] = total
 
 
-def nodal_kernel(per_chunk, depth, dom_ref, me_ref, level_ref, *refs):
+def nodal_kernel(per_chunk, dom_ref, me_ref, keep_ref, *refs):
     *totals, out_ref, values, sems = refs
     many = values.shape[1]
-    level = level_ref[0]
-    fine, mid, low = (jnp.where(level >= depth - down, 1.0, 0.0) for down in range(3))
+    fine, mid, low = (keep_ref[k] for k in range(3))
     place = lax.broadcasted_iota(jnp.int32, (many, LANES), 0)
     copies = []
     for k, (ref, away) in enumerate(zip(totals, partners(dom_ref[0]))):
@@ -311,17 +317,21 @@
 
     near_pairs = [(d, d ^ 1) for d in range(doms)]
     far_pairs = [(d, min(max((d - 1 ^ 1) + 1, 0), doms - 1)) for d in range(doms)]
-    (first,) = call(first_kernel, [(TILE, LANES)], (), flops=HALO_FLOPS * rows * cols)
-    ready = lax.ppermute(first, "dom", near_pairs)
-    far, near = call(
+    (ones,) = call(ones_kernel, [(many, LANES)], (), flops=LOAD_FLOPS * rows * cols)
+    keep, weight = call(
+        functools.partial(weights_kernel, depth),
+        [(3, many, LANES), (4, many, LANES)],
+        (levels, coefficient, ones),
+        2,
+    )
+    near, far = call(
         pack_kernel,
         [(strips, 2 * TILE, LANES)] * 2,
-        (dom, ready, *tiles),
+        (dom, weight, *tiles),
         1,
     )
-    far, near = (
-        lax.ppermute(array, "dom", pairs) for array, pairs in ((far, far_pairs), (near, near_pairs))
-    )
+    near = lax.ppermute(near, "dom", near_pairs)
+    far = lax.ppermute(far, "dom", far_pairs)
     place = (strips, TILE, many, LANES)
     (state,) = call(
         inner_kernel,
@@ -333,10 +343,10 @@
     )
     chunk = (per_chunk * TILE + -(-per_chunk // many), many, LANES)
     own, *others = call(
-        functools.partial(edge_kernel, per_chunk, depth, doms),
+        functools.partial(edge_kernel, per_chunk, doms),
         [chunk] * SQUARE,
-        (dom, me, levels, coefficient, *tiles, state, far, near),
-        4,
+        (dom, me, weight, *tiles, state, near, far),
+        2,
         [vmem(3, strips, SLAB, LANES)]
         + [vmem(strips + 2, HALF, TILE, LANES)] * 2
         + [vmem(strips, HALF, TILE, LANES)] * 4,
@@ -357,10 +367,10 @@
         apart *= 2
     totals = [total] + [swap(total, meet) for meet in range(1, SQUARE)]
     (nodal,) = call(
-        functools.partial(nodal_kernel, per_chunk, depth),
+        functools.partial(nodal_kernel, per_chunk),
         [(many, strips, TILE, LANES)],
-        (dom, me, levels, *totals),
-        3,
+        (dom, me, keep, *totals),
+        2,
         [vmem(SQUARE, many, per_chunk, TILE, LANES), pltpu.SemaphoreType.DMA((SQUARE, many))],
         out_space=pl.ANY,
     )

time: 37.9 us -> 37.1 us (0.979)
  starting transfers between devices: 15.3 us -> 11.5 us
  waiting for transfers between devices: 16.9 us -> 19.8 us
    ppermute x3 -> x2, starting transfers between devices: 5.57 us -> 1.18 us  [the longest x1 0.66 us: on_device(): far = lax.ppermute(far, 'dom', far_pairs)]
    ppermute x6, waiting for transfers between devices: 10.4 us -> 13.4 us  [swap(): return lax.ppermute(array, ('grp', 'dom'), pairs)]
    ppermute x3 -> x2, waiting for transfers between devices: 0.83 us -> 0.01 us  [the longest x1 0.01 us: on_device(): far = lax.ppermute(far, 'dom', far_pairs)]
    ppermute x1, waiting for transfers between devices: 5.72 us -> 6.35 us  [on_device(): other = lax.ppermute(total, 'grp', [(g, g ^ apart) for g in range(grids)])]
    ppermute x6, starting transfers between devices: 7.1 us -> 7.71 us  [swap(): return lax.ppermute(array, ('grp', 'dom'), pairs)]
    pallas_call x7 -> x8, Pallas kernels: 4.11 us -> 4.14 us  [call(): pl.pallas_call(kernel, out_shape=[jax.ShapeDtypeStruct(shape, jnp.float32...]
  transfers between devices with their start and end apart: 10 -> 9, of which waited for: 8 -> 6; matrix products, arithmetic and copies ran while one was open for 0% -> 0% of each run, Pallas kernels for 5% -> 5%
where the time goes in v14:
time: 37.1 us; the launch traced here: 37 us
  waiting for transfers between devices  19.8 us (53%)
  starting transfers between devices  11.5 us (31%)
  Pallas kernels  4.14 us (11%)
  between operations  1.52 us (4%)
    ppermute x6, waiting for transfers between devices, swap(): return lax.ppermute(array, ('grp', 'dom'), pairs)  13.4 us
    ppermute x6, starting transfers between devices, swap(): return lax.ppermute(array, ('grp', 'dom'), pairs)  7.71 us
    ppermute x1, waiting for transfers between devices, on_device(): other = lax.ppermute(total, 'grp', [(g, g ^ apart) for g in range(grids)])  6.35 us
    pallas_call x8, Pallas kernels, call(): pl.pallas_call(kernel, out_shape=[jax.ShapeDtypeStruct(shape, jnp.float32...  4.14 us
    ppermute x1, starting transfers between devices, on_device(): other = lax.ppermute(total, 'grp', [(g, g ^ apart) for g in range(grids)])  2.65 us
  transfers between devices with their start and end apart: 9, of which 6 were waited for; matrix products, arithmetic and copies ran while one was open for 0% of the time, Pallas kernels for 5%

profile of v14, /device:TPU:0, one launch (start us, length us, event | category | flops | bytes accessed | tf_op | source)
XLA Modules:
  0.0 37.0 jit_solution(4118648927152503554)
XLA Ops:
  0.0 0.0 copy-start
  0.0 0.0 copy-start.1
  0.0 0.0 copy-start.2
  1.4 0.0 copy-done
  1.5 0.0 copy-done.1
  1.5 0.0 copy-done.2
  1.5 0.1 shard_map.58
  1.5 0.5 %collective-permute-start = (f32[16,16,128]{2,1,0:T(8,128)S(1)}, f32[16,16,128]{2,1,0:T(8,128)S(1)}, u32[]{:S(2)}, u32[]{:S(2)}) collective-permute-start(f32[16,16,128]{2,1,0:T(8,128)S(1)} %get-tuple-element.15), channel_id=1, source_target_pairs={{0,1},{1,0},{2,3},{3,2},{4,5},{5,4},{6,7},{7,6},{8,9},{9,8},{10,11... | collective-permute-start | bytes 393224 | tf_op jit(solution)/shard_map/ppermute | solution.py:333
  2.1 0.7 %collective-permute-start.1 = (f32[16,16,128]{2,1,0:T(8,128)S(1)}, f32[16,16,128]{2,1,0:T(8,128)S(1)}, u32[]{:S(2)}, u32[]{:S(2)}) collective-permute-start(f32[16,16,128]{2,1,0:T(8,128)S(1)} %get-tuple-element.16), channel_id=1, source_target_pairs={{0,0},{1,2},{2,1},{3,3},{4,4},{5,6},{6,5},{7,7},{8,8},{9,10},{10,9... | collective-permute-start | bytes 393224 | tf_op jit(solution)/shard_map/ppermute | solution.py:334
  2.7 1.9 %shard_map.57.refs_2_ = f32[16,8,8,128]{3,2,1,0:T(8,128)S(1)} custom-call(f32[8,16,8,128]{3,2,1,0:T(8,128)S(1)} %bitcast.15, f32[8,16,8,128]{3,2,1,0:T(8,128)S(1)} %bitcast.18, f32[8,16,8,128]{3,2,1,0:T(8,128)S(1)} %bitcast.21), custom_call_target="tpu_custom_call" | custom-call | flops 5242880 | bytes 1572864 | tf_op jit(solution)/shard_map/pallas_call | solution.py:294
  4.6 0.0 collective-permute-done.refs_3_
  4.6 0.0 collective-permute-done.1.refs_4_
  4.6 0.9 %shard_map.59 = (f32[33,8,128]{2,1,0:T(8,128)S(1)}, f32[33,8,128]{2,1,0:T(8,128)S(1)}, f32[33,8,128]{2,1,0:T(8,128)S(1)}, f32[33,8,128]{2,1,0:T(8,128)S(1)}) custom-call(s32[1]{0:T(128)} %bitcast.dom_ref, s32[1]{0:T(128)} %bitcast.1.me_ref, f32[4,8,128]{2,1,0:T(8,128)S(1)} %get-tuple-element.14.weight_ref, f32[8,16,8,128]{3,2,1,0:T(8,128)S(1)} %bitcast.16, ...), custom_call_target="tpu_custom_call" | custom-call | flops 2621440 | bytes 2375688 | tf_op jit(solution)/shard_map/pallas_call | solution.py:294
  5.5 2.6 %collective-permute-start.2 = (f32[33,8,128]{2,1,0:T(8,128)S(1)}, f32[33,8,128]{2,1,0:T(8,128)S(1)}, u32[]{:S(2)}, u32[]{:S(2)}) collective-permute-start(f32[33,8,128]{2,1,0:T(8,128)S(1)} %get-tuple-element.18), channel_id=1, source_target_pairs={{0,4},{1,9},{2,6},{3,11},{4,0},{5,13},{6,2},{7,15},{8,12},{9,1},{1... | collective-permute-start | bytes 405512 | tf_op jit(solution)/shard_map/ppermute | solution.py:359
  8.1 1.6 %collective-permute-start.3 = (f32[33,8,128]{2,1,0:T(8,128)S(1)}, f32[33,8,128]{2,1,0:T(8,128)S(1)}, u32[]{:S(2)}, u32[]{:S(2)}) collective-permute-start(f32[33,8,128]{2,1,0:T(8,128)S(1)} %get-tuple-element.19), channel_id=1, source_target_pairs={{0,8},{1,5},{2,10},{3,7},{4,12},{5,1},{6,14},{7,3},{8,0},{9,13},{1... | collective-permute-start | bytes 405512 | tf_op jit(solution)/shard_map/ppermute | solution.py:359
  9.7 0.0 collective-permute-start.4
  9.7 1.4 %collective-permute-done.2.refs_1_ = f32[33,8,128]{2,1,0:T(8,128)S(1)} collective-permute-done((f32[33,8,128]{2,1,0:T(8,128)S(1)}, f32[33,8,128]{2,1,0:T(8,128)S(1)}, u32[]{:S(2)}, u32[]{:S(2)}) %collective-permute-start.2) | collective-permute-done | bytes 135200 | tf_op jit(solution)/shard_map/ppermute | solution.py:359
  11.1 2.0 %collective-permute-done.3.refs_2_ = f32[33,8,128]{2,1,0:T(8,128)S(1)} collective-permute-done((f32[33,8,128]{2,1,0:T(8,128)S(1)}, f32[33,8,128]{2,1,0:T(8,128)S(1)}, u32[]{:S(2)}, u32[]{:S(2)}) %collective-permute-start.3) | collective-permute-done | bytes 135200 | tf_op jit(solution)/shard_map/ppermute | solution.py:359
  13.1 3.8 %collective-permute-done.4.refs_3_ = f32[33,8,128]{2,1,0:T(8,128)S(1)} collective-permute-done((f32[33,8,128]{2,1,0:T(8,128)S(1)}, f32[33,8,128]{2,1,0:T(8,128)S(1)}, u32[]{:S(2)}, u32[]{:S(2)}) %collective-permute-start.4) | collective-permute-done | bytes 135200 | tf_op jit(solution)/shard_map/ppermute | solution.py:359
  16.9 2.7 %collective-permute-start.5 = (f32[33,8,128]{2,1,0:T(8,128)S(1)}, f32[33,8,128]{2,1,0:T(8,128)S(1)}, u32[]{:S(2)}, u32[]{:S(2)}) collective-permute-start(f32[33,8,128]{2,1,0:T(8,128)S(1)} %shard_map.60.refs_0_), channel_id=1, source_target_pairs={{0,16},{4,20},{8,24},{12,28},{16,0},{20,4},{24,8},{28,12},{1,17},{... | collective-permute-start | bytes 405512 | tf_op jit(solution)/shard_map/ppermute | solution.py:365
  19.5 6.3 %collective-permute-done.5.refs_1_ = f32[33,8,128]{2,1,0:T(8,128)S(1)} collective-permute-done((f32[33,8,128]{2,1,0:T(8,128)S(1)}, f32[33,8,128]{2,1,0:T(8,128)S(1)}, u32[]{:S(2)}, u32[]{:S(2)}) %collective-permute-start.5) | collective-permute-done | bytes 135200 | tf_op jit(solution)/shard_map/ppermute | solution.py:365
  25.9 1.6 %collective-permute-start.8 = (f32[33,8,128]{2,1,0:T(8,128)S(1)}, f32[33,8,128]{2,1,0:T(8,128)S(1)}, u32[]{:S(2)}, u32[]{:S(2)}) collective-permute-start(f32[33,8,128]{2,1,0:T(8,128)S(1)} %shard_map.61.refs_0_), channel_id=1, source_target_pairs={{0,12},{1,13},{2,14},{3,15},{4,8},{5,9},{6,10},{7,11},{8,4},{9,5},... | collective-permute-start | bytes 405512 | tf_op jit(solution)/shard_map/ppermute | solution.py:359
  27.6 1.2 %collective-permute-start.7 = (f32[33,8,128]{2,1,0:T(8,128)S(1)}, f32[33,8,128]{2,1,0:T(8,128)S(1)}, u32[]{:S(2)}, u32[]{:S(2)}) collective-permute-start(f32[33,8,128]{2,1,0:T(8,128)S(1)} %shard_map.61.refs_0_), channel_id=1, source_target_pairs={{0,8},{1,5},{2,10},{3,7},{4,12},{5,1},{6,14},{7,3},{8,0},{9,13},{1... | collective-permute-start | bytes 405512 | tf_op jit(solution)/shard_map/ppermute | solution.py:359
  28.8 0.7 %collective-permute-start.6 = (f32[33,8,128]{2,1,0:T(8,128)S(1)}, f32[33,8,128]{2,1,0:T(8,128)S(1)}, u32[]{:S(2)}, u32[]{:S(2)}) collective-permute-start(f32[33,8,128]{2,1,0:T(8,128)S(1)} %shard_map.61.refs_0_), channel_id=1, source_target_pairs={{0,4},{1,9},{2,6},{3,11},{4,0},{5,13},{6,2},{7,15},{8,12},{9,1},{1... | collective-permute-start | bytes 405512 | tf_op jit(solution)/shard_map/ppermute | solution.py:359
  29.5 3.8 %collective-permute-done.8.refs_3_ = f32[33,8,128]{2,1,0:T(8,128)S(1)} collective-permute-done((f32[33,8,128]{2,1,0:T(8,128)S(1)}, f32[33,8,128]{2,1,0:T(8,128)S(1)}, u32[]{:S(2)}, u32[]{:S(2)}) %collective-permute-start.8) | collective-permute-done | bytes 135200 | tf_op jit(solution)/shard_map/ppermute | solution.py:359
  33.3 2.4 %collective-permute-done.7.refs_2_ = f32[33,8,128]{2,1,0:T(8,128)S(1)} collective-permute-done((f32[33,8,128]{2,1,0:T(8,128)S(1)}, f32[33,8,128]{2,1,0:T(8,128)S(1)}, u32[]{:S(2)}, u32[]{:S(2)}) %collective-permute-start.7) | collective-permute-done | bytes 135200 | tf_op jit(solution)/shard_map/ppermute | solution.py:359
  35.7 0.0 collective-permute-done.6.refs_1_
  35.7 1.3 %shard_map.62 = f32[8,16,8,128]{3,2,1,0:T(8,128)} custom-call(s32[1]{0:T(128)} %bitcast.dom_ref, s32[1]{0:T(128)} %bitcast.1.me_ref, f32[3,8,128]{2,1,0:T(8,128)S(1)} %get-tuple-element.13.keep_ref, f32[33,8,128]{2,1,0:T(8,128)S(1)} %shard_map.61.refs_0_, f32[33,8,128]{2,1,0:T(8,128)S(1)} %collective-permute-done.6.refs_1_, ...), custom_call_target="tpu_custom_call" | custom-call | bytes 552968 | tf_op jit(solution)/shard_map/pallas_call | solution.py:294
  (4 shorter events, 0.1 us)
Async XLA Ops:
  0.0 1.4 %copy-start = (f32[1,64,2048]{2,1,0:T(8,128)S(1)}, f32[1,64,2048]{2,1,0:T(8,128)}, u32[]{:S(2)}) copy-start(f32[1,64,2048]{2,1,0:T(8,128)} %param.5) | copy-start | bytes 1572868
  0.0 1.5 %copy-start.1 = (f32[1,64,2048]{2,1,0:T(8,128)S(1)}, f32[1,64,2048]{2,1,0:T(8,128)}, u32[]{:S(2)}) copy-start(f32[1,64,2048]{2,1,0:T(8,128)} %param.6) | copy-start | bytes 1572868
  0.0 1.5 %copy-start.2 = (f32[1,64,2048]{2,1,0:T(8,128)S(1)}, f32[1,64,2048]{2,1,0:T(8,128)}, u32[]{:S(2)}) copy-start(f32[1,64,2048]{2,1,0:T(8,128)} %param.7) | copy-start | bytes 1572868
  1.5 3.1 %collective-permute-start = (f32[16,16,128]{2,1,0:T(8,128)S(1)}, f32[16,16,128]{2,1,0:T(8,128)S(1)}, u32[]{:S(2)}, u32[]{:S(2)}) collective-permute-start(f32[16,16,128]{2,1,0:T(8,128)S(1)} %get-tuple-element.15), channel_id=1, source_target_pairs={{0,1},{1,0},{2,3},{3,2},{4,5},{5,4},{6,7},{7,6},{8,9},{9,8},{10,11... | collective-permute-start | bytes 393224 | tf_op jit(solution)/shard_map/ppermute | solution.py:333
  2.1 2.6 %collective-permute-start.1 = (f32[16,16,128]{2,1,0:T(8,128)S(1)}, f32[16,16,128]{2,1,0:T(8,128)S(1)}, u32[]{:S(2)}, u32[]{:S(2)}) collective-permute-start(f32[16,16,128]{2,1,0:T(8,128)S(1)} %get-tuple-element.16), channel_id=1, source_target_pairs={{0,0},{1,2},{2,1},{3,3},{4,4},{5,6},{6,5},{7,7},{8,8},{9,10},{10,9... | collective-permute-start | bytes 393224 | tf_op jit(solution)/shard_map/ppermute | solution.py:334
  5.5 5.6 %collective-permute-start.2 = (f32[33,8,128]{2,1,0:T(8,128)S(1)}, f32[33,8,128]{2,1,0:T(8,128)S(1)}, u32[]{:S(2)}, u32[]{:S(2)}) collective-permute-start(f32[33,8,128]{2,1,0:T(8,128)S(1)} %get-tuple-element.18), channel_id=1, source_target_pairs={{0,4},{1,9},{2,6},{3,11},{4,0},{5,13},{6,2},{7,15},{8,12},{9,1},{1... | collective-permute-start | bytes 405512 | tf_op jit(solution)/shard_map/ppermute | solution.py:359
  8.1 5.0 %collective-permute-start.3 = (f32[33,8,128]{2,1,0:T(8,128)S(1)}, f32[33,8,128]{2,1,0:T(8,128)S(1)}, u32[]{:S(2)}, u32[]{:S(2)}) collective-permute-start(f32[33,8,128]{2,1,0:T(8,128)S(1)} %get-tuple-element.19), channel_id=1, source_target_pairs={{0,8},{1,5},{2,10},{3,7},{4,12},{5,1},{6,14},{7,3},{8,0},{9,13},{1... | collective-permute-start | bytes 405512 | tf_op jit(solution)/shard_map/ppermute | solution.py:359
  9.7 7.2 %collective-permute-start.4 = (f32[33,8,128]{2,1,0:T(8,128)S(1)}, f32[33,8,128]{2,1,0:T(8,128)S(1)}, u32[]{:S(2)}, u32[]{:S(2)}) collective-permute-start(f32[33,8,128]{2,1,0:T(8,128)S(1)} %get-tuple-element.20), channel_id=1, source_target_pairs={{0,12},{1,13},{2,14},{3,15},{4,8},{5,9},{6,10},{7,11},{8,4},{9,5},... | collective-permute-start | bytes 405512 | tf_op jit(solution)/shard_map/ppermute | solution.py:359
  16.9 9.0 %collective-permute-start.5 = (f32[33,8,128]{2,1,0:T(8,128)S(1)}, f32[33,8,128]{2,1,0:T(8,128)S(1)}, u32[]{:S(2)}, u32[]{:S(2)}) collective-permute-start(f32[33,8,128]{2,1,0:T(8,128)S(1)} %shard_map.60.refs_0_), channel_id=1, source_target_pairs={{0,16},{4,20},{8,24},{12,28},{16,0},{20,4},{24,8},{28,12},{1,17},{... | collective-permute-start | bytes 405512 | tf_op jit(solution)/shard_map/ppermute | solution.py:365
  25.9 7.4 %collective-permute-start.8 = (f32[33,8,128]{2,1,0:T(8,128)S(1)}, f32[33,8,128]{2,1,0:T(8,128)S(1)}, u32[]{:S(2)}, u32[]{:S(2)}) collective-permute-start(f32[33,8,128]{2,1,0:T(8,128)S(1)} %shard_map.61.refs_0_), channel_id=1, source_target_pairs={{0,12},{1,13},{2,14},{3,15},{4,8},{5,9},{6,10},{7,11},{8,4},{9,5},... | collective-permute-start | bytes 405512 | tf_op jit(solution)/shard_map/ppermute | solution.py:359
  27.6 8.1 %collective-permute-start.7 = (f32[33,8,128]{2,1,0:T(8,128)S(1)}, f32[33,8,128]{2,1,0:T(8,128)S(1)}, u32[]{:S(2)}, u32[]{:S(2)}) collective-permute-start(f32[33,8,128]{2,1,0:T(8,128)S(1)} %shard_map.61.refs_0_), channel_id=1, source_target_pairs={{0,8},{1,5},{2,10},{3,7},{4,12},{5,1},{6,14},{7,3},{8,0},{9,13},{1... | collective-permute-start | bytes 405512 | tf_op jit(solution)/shard_map/ppermute | solution.py:359
  28.8 6.9 %collective-permute-start.6 = (f32[33,8,128]{2,1,0:T(8,128)S(1)}, f32[33,8,128]{2,1,0:T(8,128)S(1)}, u32[]{:S(2)}, u32[]{:S(2)}) collective-permute-start(f32[33,8,128]{2,1,0:T(8,128)S(1)} %shard_map.61.refs_0_), channel_id=1, source_target_pairs={{0,4},{1,9},{2,6},{3,11},{4,0},{5,13},{6,2},{7,15},{8,12},{9,1},{1... | collective-permute-start | bytes 405512 | tf_op jit(solution)/shard_map/ppermute | solution.py:359

commit v15 on v14

--- a/solution.py
+++ b/solution.py
@@ -14,6 +14,7 @@
 SLAB = 4 * TILE
 SQUARE = 4
 UNROLL = 16
+STREAMS = 2
 VMEM_LIMIT = 40 * 1024 * 1024
 LOAD_FLOPS = 4000
 
@@ -182,7 +183,7 @@
     dom = dom_ref[0]
     odd = dom % 2 == 1
     diff_ref, drift_ref, state_ref, near_ref, far_ref, *rest = refs
-    out_refs, (slab, state_a, state_b, *coefs) = rest[:SQUARE], rest[SQUARE:]
+    out_refs, (slab, state_a, state_b, *coefs) = rest[:-7], rest[-7:]
 
     def stage(j):
         far, near = far_ref[j], near_ref[j]
@@ -228,10 +229,11 @@
         )
 
     def last(source):
-        for out_ref, away in zip(out_refs, partners(dom_ref[0])):
-            first = (me_ref[0] ^ away) * per_chunk
+        for k, out_ref in enumerate(out_refs):
+            stream, meet = divmod(k, SQUARE)
+            chunk = stream * SQUARE + (me_ref[0] ^ partners(dom_ref[0])[meet])
             emit = functools.partial(finish, out_ref)
-            advance(first, per_chunk, HALF, source, coefs, emit)
+            advance(chunk * per_chunk, per_chunk, HALF, source, coefs, emit)
 
     run_steps(strips, HALF, load, (state_a, state_b), coefs, last)
 
@@ -244,14 +246,14 @@
     out_ref[...] = total
 
 
-def nodal_kernel(per_chunk, dom_ref, me_ref, keep_ref, *refs):
-    *totals, out_ref, values, sems = refs
+def nodal_kernel(per_chunk, stream, dom_ref, me_ref, keep_ref, *refs):
+    totals, (out_ref, values, sems) = refs[:SQUARE], refs[-3:]
     many = values.shape[1]
     fine, mid, low = (keep_ref[k] for k in range(3))
     place = lax.broadcasted_iota(jnp.int32, (many, LANES), 0)
     copies = []
     for k, (ref, away) in enumerate(zip(totals, partners(dom_ref[0]))):
-        first = (me_ref[0] ^ away) * per_chunk
+        first = (stream * SQUARE + (me_ref[0] ^ away)) * per_chunk
         by_row = flat(values.at[k])
 
         def body(part, ref=ref, by_row=by_row):
@@ -286,9 +288,13 @@
 
 
 def call(
-    kernel, out_shapes, operands, in_smem=0, scratch=(), flops=0, out_space=pltpu.VMEM
+    kernel, out_shapes, operands, in_smem=0, scratch=(), flops=0, out_space=pltpu.VMEM, onto=None
 ):
     spaces = [pltpu.SMEM] * in_smem + [pltpu.VMEM] * (len(operands) - in_smem)
+    alias = {}
+    if onto is not None:
+        alias = {len(operands): 0}
+        spaces, operands = spaces + [out_space], (*operands, onto)
     specs = [pl.BlockSpec(memory_space=space) for space in spaces]
     moved = 4 * sum(x.size for x in operands)
     return pl.pallas_call(
@@ -296,6 +302,7 @@
         out_shape=[jax.ShapeDtypeStruct(shape, jnp.float32) for shape in out_shapes],
         in_specs=specs,
         out_specs=[pl.BlockSpec(memory_space=out_space) for _ in out_shapes],
+        input_output_aliases=alias,
         scratch_shapes=list(scratch),
         compiler_params=pltpu.CompilerParams(vmem_limit_bytes=VMEM_LIMIT),
         cost_estimate=pl.CostEstimate(flops=flops, bytes_accessed=moved, transcendentals=0),
@@ -306,7 +313,7 @@
     rows, cols = density.shape[1:]
     doms, grids = lax.axis_size("dom"), lax.axis_size("grp")
     many, strips = rows // TILE, cols // LANES
-    per_chunk = strips // SQUARE
+    per_chunk = strips // (SQUARE * STREAMS)
     depth = (rows * doms).bit_length() - 1
     tiles = [tiles_of(x[0]) for x in (density, diffusion, drift_speed)]
     me = (lax.axis_index("grp") % SQUARE).astype(jnp.int32)[None]
@@ -342,9 +349,9 @@
         flops=40 * rows * cols,
     )
     chunk = (per_chunk * TILE + -(-per_chunk // many), many, LANES)
-    own, *others = call(
+    weighted = call(
         functools.partial(edge_kernel, per_chunk, doms),
-        [chunk] * SQUARE,
+        [chunk] * (SQUARE * STREAMS),
         (dom, me, weight, *tiles, state, near, far),
         2,
         [vmem(3, strips, SLAB, LANES)]
@@ -358,22 +365,28 @@
         pairs = [(g * doms + d, (g ^ partners(d % 2)[meet]) * doms + d) for g, d in devices]
         return lax.ppermute(array, ("grp", "dom"), pairs)
 
-    theirs = [swap(array, meet) for meet, array in enumerate(others, 1)]
-    (total,) = call(sum_kernel, [chunk], (own, *theirs))
-    apart = SQUARE
-    while apart < grids:
-        other = lax.ppermute(total, "grp", [(g, g ^ apart) for g in range(grids)])
-        (total,) = call(sum_kernel, [chunk], (total, other))
-        apart *= 2
-    totals = [total] + [swap(total, meet) for meet in range(1, SQUARE)]
-    (nodal,) = call(
-        functools.partial(nodal_kernel, per_chunk),
-        [(many, strips, TILE, LANES)],
-        (dom, me, keep, *totals),
-        2,
-        [vmem(SQUARE, many, per_chunk, TILE, LANES), pltpu.SemaphoreType.DMA((SQUARE, many))],
-        out_space=pl.ANY,
-    )
+    def over_grids(own, *others):
+        theirs = [swap(array, meet) for meet, array in enumerate(others, 1)]
+        (total,) = call(sum_kernel, [chunk], (own, *theirs))
+        apart = SQUARE
+        while apart < grids:
+            other = lax.ppermute(total, "grp", [(g, g ^ apart) for g in range(grids)])
+            (total,) = call(sum_kernel, [chunk], (total, other))
+            apart *= 2
+        return [total] + [swap(total, meet) for meet in range(1, SQUARE)]
+
+    nodal = None
+    for stream in range(STREAMS):
+        totals = over_grids(*weighted[stream * SQUARE : (stream + 1) * SQUARE])
+        (nodal,) = call(
+            functools.partial(nodal_kernel, per_chunk, stream),
+            [(many, strips, TILE, LANES)],
+            (dom, me, keep, *totals),
+            2,
+            [vmem(SQUARE, many, per_chunk, TILE, LANES), pltpu.SemaphoreType.DMA((SQUARE, many))],
+            out_space=pl.ANY,
+            onto=nodal,
+        )
     return block_of(nodal)[None]
 
 

time: 37.1 us -> 34.9 us (0.941)
  the two profiles are of different devices: /device:TPU:0 before, /device:TPU:4 now
where the time goes in v15:
time: 34.9 us; the launch traced here: 34.8 us
  starting transfers between devices  22.4 us (64%)
  waiting for transfers between devices  5.9 us (17%)
  Pallas kernels  4.94 us (14%)
  between operations  1.55 us (4%)
    ppermute x12, starting transfers between devices, swap(): return lax.ppermute(array, ('grp', 'dom'), pairs)  14.6 us
    ppermute x2, starting transfers between devices, over_grids(): other = lax.ppermute(total, 'grp', [(g, g ^ apart) for g in range(grids)])  5.77 us
    pallas_call x11, Pallas kernels, call(): pl.pallas_call(kernel, out_shape=[jax.ShapeDtypeStruct(shape, jnp.float32...  4.94 us
    ppermute x12, waiting for transfers between devices, swap(): return lax.ppermute(array, ('grp', 'dom'), pairs)  3.42 us
    ppermute x1, waiting for transfers between devices, on_device(): far = lax.ppermute(far, 'dom', far_pairs)  2.47 us
    ppermute x1, starting transfers between devices, on_device(): far = lax.ppermute(far, 'dom', far_pairs)  1.92 us
  transfers between devices with their start and end apart: 16, of which 6 were waited for; matrix products, arithmetic and copies ran while one was open for 0% of the time, Pallas kernels for 9%

profile of v15, /device:TPU:4, one launch (start us, length us, event | category | flops | bytes accessed | tf_op | source)
XLA Modules:
  0.0 34.8 jit_solution(12880747584046917664)
XLA Ops:
  0.0 0.0 copy-start
  0.0 0.0 copy-start.1
  0.0 0.0 copy-start.2
  1.4 0.0 copy-done
  1.5 0.0 copy-done.1
  1.5 0.0 copy-done.2
  1.5 0.1 shard_map.58
  1.5 0.1 collective-permute-start
  1.6 1.9 %collective-permute-start.1 = (f32[16,16,128]{2,1,0:T(8,128)S(1)}, f32[16,16,128]{2,1,0:T(8,128)S(1)}, u32[]{:S(2)}, u32[]{:S(2)}) collective-permute-start(f32[16,16,128]{2,1,0:T(8,128)S(1)} %get-tuple-element.20), channel_id=1, source_target_pairs={{0,0},{1,2},{2,1},{3,3},{4,4},{5,6},{6,5},{7,7},{8,8},{9,10},{10,9... | collective-permute-start | bytes 393224 | tf_op jit(solution)/shard_map/ppermute | solution.py:341
  3.6 1.9 %shard_map.57.refs_2_ = f32[16,8,8,128]{3,2,1,0:T(8,128)S(1)} custom-call(f32[8,16,8,128]{3,2,1,0:T(8,128)S(1)} %bitcast.15, f32[8,16,8,128]{3,2,1,0:T(8,128)S(1)} %bitcast.18, f32[8,16,8,128]{3,2,1,0:T(8,128)S(1)} %bitcast.21), custom_call_target="tpu_custom_call" | custom-call | flops 5242880 | bytes 1572864 | tf_op jit(solution)/shard_map/pallas_call | solution.py:300
  5.4 0.0 collective-permute-done.refs_3_
  5.4 2.5 %collective-permute-done.1.refs_4_ = f32[16,16,128]{2,1,0:T(8,128)S(1)} collective-permute-done((f32[16,16,128]{2,1,0:T(8,128)S(1)}, f32[16,16,128]{2,1,0:T(8,128)S(1)}, u32[]{:S(2)}, u32[]{:S(2)}) %collective-permute-start.1) | collective-permute-done | bytes 131104 | tf_op jit(solution)/shard_map/ppermute | solution.py:341
  7.9 0.9 %shard_map.59 = (f32[17,8,128]{2,1,0:T(8,128)S(1)}, f32[17,8,128]{2,1,0:T(8,128)S(1)}, f32[17,8,128]{2,1,0:T(8,128)S(1)}, f32[17,8,128]{2,1,0:T(8,128)S(1)}, f32...) custom-call(s32[1]{0:T(128)} %bitcast.dom_ref, ...), custom_call_target="tpu_custom_call" | custom-call | flops 2621440 | bytes 2375688 | tf_op jit(solution)/shard_map/pallas_call | solution.py:300
  8.8 1.6 %collective-permute-start.9 = (f32[17,8,128]{2,1,0:T(8,128)S(1)}, f32[17,8,128]{2,1,0:T(8,128)S(1)}, u32[]{:S(2)}, u32[]{:S(2)}) collective-permute-start(f32[17,8,128]{2,1,0:T(8,128)S(1)} %get-tuple-element.26), channel_id=1, source_target_pairs={{0,4},{1,9},{2,6},{3,11},{4,0},{5,13},{6,2},{7,15},{8,12},{9,1},{1... | collective-permute-start | bytes 208904 | tf_op jit(solution)/shard_map/ppermute | solution.py:366
  10.3 1.6 %collective-permute-start.10 = (f32[17,8,128]{2,1,0:T(8,128)S(1)}, f32[17,8,128]{2,1,0:T(8,128)S(1)}, u32[]{:S(2)}, u32[]{:S(2)}) collective-permute-start(f32[17,8,128]{2,1,0:T(8,128)S(1)} %get-tuple-element.27), channel_id=1, source_target_pairs={{0,8},{1,5},{2,10},{3,7},{4,12},{5,1},{6,14},{7,3},{8,0},{9,13},{1... | collective-permute-start | bytes 208904 | tf_op jit(solution)/shard_map/ppermute | solution.py:366
  11.9 0.4 %collective-permute-start.11 = (f32[17,8,128]{2,1,0:T(8,128)S(1)}, f32[17,8,128]{2,1,0:T(8,128)S(1)}, u32[]{:S(2)}, u32[]{:S(2)}) collective-permute-start(f32[17,8,128]{2,1,0:T(8,128)S(1)} %get-tuple-element.28), channel_id=1, source_target_pairs={{0,12},{1,13},{2,14},{3,15},{4,8},{5,9},{6,10},{7,11},{8,4},{9,5},... | collective-permute-start | bytes 208904 | tf_op jit(solution)/shard_map/ppermute | solution.py:366
  12.3 1.5 %collective-permute-start.2 = (f32[17,8,128]{2,1,0:T(8,128)S(1)}, f32[17,8,128]{2,1,0:T(8,128)S(1)}, u32[]{:S(2)}, u32[]{:S(2)}) collective-permute-start(f32[17,8,128]{2,1,0:T(8,128)S(1)} %get-tuple-element.22), channel_id=1, source_target_pairs={{0,4},{1,9},{2,6},{3,11},{4,0},{5,13},{6,2},{7,15},{8,12},{9,1},{1... | collective-permute-start | bytes 208904 | tf_op jit(solution)/shard_map/ppermute | solution.py:366
  13.8 1.6 %collective-permute-start.3 = (f32[17,8,128]{2,1,0:T(8,128)S(1)}, f32[17,8,128]{2,1,0:T(8,128)S(1)}, u32[]{:S(2)}, u32[]{:S(2)}) collective-permute-start(f32[17,8,128]{2,1,0:T(8,128)S(1)} %get-tuple-element.23), channel_id=1, source_target_pairs={{0,8},{1,5},{2,10},{3,7},{4,12},{5,1},{6,14},{7,3},{8,0},{9,13},{1... | collective-permute-start | bytes 208904 | tf_op jit(solution)/shard_map/ppermute | solution.py:366
  15.4 0.0 collective-permute-done.9.refs_1_
  15.4 0.9 %collective-permute-start.4 = (f32[17,8,128]{2,1,0:T(8,128)S(1)}, f32[17,8,128]{2,1,0:T(8,128)S(1)}, u32[]{:S(2)}, u32[]{:S(2)}) collective-permute-start(f32[17,8,128]{2,1,0:T(8,128)S(1)} %get-tuple-element.24), channel_id=1, source_target_pairs={{0,12},{1,13},{2,14},{3,15},{4,8},{5,9},{6,10},{7,11},{8,4},{9,5},... | collective-permute-start | bytes 208904 | tf_op jit(solution)/shard_map/ppermute | solution.py:366
  16.3 0.0 collective-permute-done.10.refs_2_
  16.3 1.1 %collective-permute-done.11.refs_3_ = f32[17,8,128]{2,1,0:T(8,128)S(1)} collective-permute-done((f32[17,8,128]{2,1,0:T(8,128)S(1)}, f32[17,8,128]{2,1,0:T(8,128)S(1)}, u32[]{:S(2)}, u32[]{:S(2)}) %collective-permute-start.11) | collective-permute-done | bytes 69664 | tf_op jit(solution)/shard_map/ppermute | solution.py:366
  17.4 2.8 %collective-permute-start.12 = (f32[17,8,128]{2,1,0:T(8,128)S(1)}, f32[17,8,128]{2,1,0:T(8,128)S(1)}, u32[]{:S(2)}, u32[]{:S(2)}) collective-permute-start(f32[17,8,128]{2,1,0:T(8,128)S(1)} %shard_map.62.refs_0_), channel_id=1, source_target_pairs={{0,16},{4,20},{8,24},{12,28},{16,0},{20,4},{24,8},{28,12},{1,17},{... | collective-permute-start | bytes 208904 | tf_op jit(solution)/shard_map/ppermute | solution.py:373
  20.1 0.0 collective-permute-done.2.refs_1_
  20.1 0.0 collective-permute-done.3.refs_2_
  20.1 0.6 %collective-permute-done.4.refs_3_ = f32[17,8,128]{2,1,0:T(8,128)S(1)} collective-permute-done((f32[17,8,128]{2,1,0:T(8,128)S(1)}, f32[17,8,128]{2,1,0:T(8,128)S(1)}, u32[]{:S(2)}, u32[]{:S(2)}) %collective-permute-start.4) | collective-permute-done | bytes 69664 | tf_op jit(solution)/shard_map/ppermute | solution.py:366
  20.7 3.0 %collective-permute-start.5 = (f32[17,8,128]{2,1,0:T(8,128)S(1)}, f32[17,8,128]{2,1,0:T(8,128)S(1)}, u32[]{:S(2)}, u32[]{:S(2)}) collective-permute-start(f32[17,8,128]{2,1,0:T(8,128)S(1)} %shard_map.60.refs_0_), channel_id=1, source_target_pairs={{0,16},{4,20},{8,24},{12,28},{16,0},{20,4},{24,8},{28,12},{1,17},{... | collective-permute-start | bytes 208904 | tf_op jit(solution)/shard_map/ppermute | solution.py:373
  23.8 0.0 collective-permute-done.12.refs_1_
  23.8 1.1 %collective-permute-start.15 = (f32[17,8,128]{2,1,0:T(8,128)S(1)}, f32[17,8,128]{2,1,0:T(8,128)S(1)}, u32[]{:S(2)}, u32[]{:S(2)}) collective-permute-start(f32[17,8,128]{2,1,0:T(8,128)S(1)} %shard_map.63.refs_0_), channel_id=1, source_target_pairs={{0,12},{1,13},{2,14},{3,15},{4,8},{5,9},{6,10},{7,11},{8,4},{9,5},... | collective-permute-start | bytes 208904 | tf_op jit(solution)/shard_map/ppermute | solution.py:366
  24.9 0.9 %collective-permute-start.14 = (f32[17,8,128]{2,1,0:T(8,128)S(1)}, f32[17,8,128]{2,1,0:T(8,128)S(1)}, u32[]{:S(2)}, u32[]{:S(2)}) collective-permute-start(f32[17,8,128]{2,1,0:T(8,128)S(1)} %shard_map.63.refs_0_), channel_id=1, source_target_pairs={{0,8},{1,5},{2,10},{3,7},{4,12},{5,1},{6,14},{7,3},{8,0},{9,13},{1... | collective-permute-start | bytes 208904 | tf_op jit(solution)/shard_map/ppermute | solution.py:366
  25.7 1.6 %collective-permute-start.13 = (f32[17,8,128]{2,1,0:T(8,128)S(1)}, f32[17,8,128]{2,1,0:T(8,128)S(1)}, u32[]{:S(2)}, u32[]{:S(2)}) collective-permute-start(f32[17,8,128]{2,1,0:T(8,128)S(1)} %shard_map.63.refs_0_), channel_id=1, source_target_pairs={{0,4},{1,9},{2,6},{3,11},{4,0},{5,13},{6,2},{7,15},{8,12},{9,1},{1... | collective-permute-start | bytes 208904 | tf_op jit(solution)/shard_map/ppermute | solution.py:366
  27.3 0.0 collective-permute-done.5.refs_1_
  27.4 1.1 %collective-permute-start.8 = (f32[17,8,128]{2,1,0:T(8,128)S(1)}, f32[17,8,128]{2,1,0:T(8,128)S(1)}, u32[]{:S(2)}, u32[]{:S(2)}) collective-permute-start(f32[17,8,128]{2,1,0:T(8,128)S(1)} %shard_map.61.refs_0_), channel_id=1, source_target_pairs={{0,12},{1,13},{2,14},{3,15},{4,8},{5,9},{6,10},{7,11},{8,4},{9,5},... | collective-permute-start | bytes 208904 | tf_op jit(solution)/shard_map/ppermute | solution.py:366
  28.5 1.0 %collective-permute-start.7 = (f32[17,8,128]{2,1,0:T(8,128)S(1)}, f32[17,8,128]{2,1,0:T(8,128)S(1)}, u32[]{:S(2)}, u32[]{:S(2)}) collective-permute-start(f32[17,8,128]{2,1,0:T(8,128)S(1)} %shard_map.61.refs_0_), channel_id=1, source_target_pairs={{0,8},{1,5},{2,10},{3,7},{4,12},{5,1},{6,14},{7,3},{8,0},{9,13},{1... | collective-permute-start | bytes 208904 | tf_op jit(solution)/shard_map/ppermute | solution.py:366
  29.4 0.0 collective-permute-done.15.refs_3_
  29.4 1.5 %collective-permute-start.6 = (f32[17,8,128]{2,1,0:T(8,128)S(1)}, f32[17,8,128]{2,1,0:T(8,128)S(1)}, u32[]{:S(2)}, u32[]{:S(2)}) collective-permute-start(f32[17,8,128]{2,1,0:T(8,128)S(1)} %shard_map.61.refs_0_), channel_id=1, source_target_pairs={{0,4},{1,9},{2,6},{3,11},{4,0},{5,13},{6,2},{7,15},{8,12},{9,1},{1... | collective-permute-start | bytes 208904 | tf_op jit(solution)/shard_map/ppermute | solution.py:366
  30.9 0.0 collective-permute-done.14.refs_2_
  30.9 0.0 collective-permute-done.13.refs_1_
  30.9 1.0 %shard_map.64.refs_4_ = f32[8,16,8,128]{3,2,1,0:T(8,128)} custom-call(s32[1]{0:T(128)} %bitcast.dom_ref, s32[1]{0:T(128)} %bitcast.1.me_ref, f32[3,8,128]{2,1,0:T(8,128)S(1)} %get-tuple-element.17.keep_ref, f32[17,8,128]{2,1,0:T(8,128)S(1)} %shard_map.63.refs_0_, f32[17,8,128]{2,1,0:T(8,128)S(1)} %collective-permute-done.13.refs_1_, ...), custom_call_target="tpu_custom_call" | custom-call | bytes 290824 | tf_op jit(solution)/shard_map/pallas_call | solution.py:300
  32.0 0.7 %collective-permute-done.8.refs_3_ = f32[17,8,128]{2,1,0:T(8,128)S(1)} collective-permute-done((f32[17,8,128]{2,1,0:T(8,128)S(1)}, f32[17,8,128]{2,1,0:T(8,128)S(1)}, u32[]{:S(2)}, u32[]{:S(2)}) %collective-permute-start.8) | collective-permute-done | bytes 69664 | tf_op jit(solution)/shard_map/ppermute | solution.py:366
  32.6 0.1 collective-permute-done.7.refs_2_
  32.8 1.0 %collective-permute-done.6.refs_1_ = f32[17,8,128]{2,1,0:T(8,128)S(1)} collective-permute-done((f32[17,8,128]{2,1,0:T(8,128)S(1)}, f32[17,8,128]{2,1,0:T(8,128)S(1)}, u32[]{:S(2)}, u32[]{:S(2)}) %collective-permute-start.6) | collective-permute-done | bytes 69664 | tf_op jit(solution)/shard_map/ppermute | solution.py:366
  33.7 1.0 %shard_map.65 = f32[8,16,8,128]{3,2,1,0:T(8,128)} custom-call(s32[1]{0:T(128)} %bitcast.dom_ref, s32[1]{0:T(128)} %bitcast.1.me_ref, f32[3,8,128]{2,1,0:T(8,128)S(1)} %get-tuple-element.17.keep_ref, f32[17,8,128]{2,1,0:T(8,128)S(1)} %shard_map.61.refs_0_, f32[17,8,128]{2,1,0:T(8,128)S(1)} %collective-permute-done.6.refs_1_, ...), custom_call_target="tpu_custom_call", output_to_operand_aliasing={{}: (7, {})} | custom-call | bytes 815112 | tf_op jit(solution)/shard_map/pallas_call | solution.py:300
  (6 shorter events, 0.1 us)
Async XLA Ops:
  0.0 1.5 %copy-start = (f32[1,64,2048]{2,1,0:T(8,128)S(1)}, f32[1,64,2048]{2,1,0:T(8,128)}, u32[]{:S(2)}) copy-start(f32[1,64,2048]{2,1,0:T(8,128)} %param.5) | copy-start | bytes 1572868
  0.0 1.5 %copy-start.1 = (f32[1,64,2048]{2,1,0:T(8,128)S(1)}, f32[1,64,2048]{2,1,0:T(8,128)}, u32[]{:S(2)}) copy-start(f32[1,64,2048]{2,1,0:T(8,128)} %param.6) | copy-start | bytes 1572868
  0.0 1.5 %copy-start.2 = (f32[1,64,2048]{2,1,0:T(8,128)S(1)}, f32[1,64,2048]{2,1,0:T(8,128)}, u32[]{:S(2)}) copy-start(f32[1,64,2048]{2,1,0:T(8,128)} %param.7) | copy-start | bytes 1572868
  1.5 3.9 %collective-permute-start = (f32[16,16,128]{2,1,0:T(8,128)S(1)}, f32[16,16,128]{2,1,0:T(8,128)S(1)}, u32[]{:S(2)}, u32[]{:S(2)}) collective-permute-start(f32[16,16,128]{2,1,0:T(8,128)S(1)} %get-tuple-element.19), channel_id=1, source_target_pairs={{0,1},{1,0},{2,3},{3,2},{4,5},{5,4},{6,7},{7,6},{8,9},{9,8},{10,11... | collective-permute-start | bytes 393224 | tf_op jit(solution)/shard_map/ppermute | solution.py:340
  1.6 6.3 %collective-permute-start.1 = (f32[16,16,128]{2,1,0:T(8,128)S(1)}, f32[16,16,128]{2,1,0:T(8,128)S(1)}, u32[]{:S(2)}, u32[]{:S(2)}) collective-permute-start(f32[16,16,128]{2,1,0:T(8,128)S(1)} %get-tuple-element.20), channel_id=1, source_target_pairs={{0,0},{1,2},{2,1},{3,3},{4,4},{5,6},{6,5},{7,7},{8,8},{9,10},{10,9... | collective-permute-start | bytes 393224 | tf_op jit(solution)/shard_map/ppermute | solution.py:341
  8.8 6.6 %collective-permute-start.9 = (f32[17,8,128]{2,1,0:T(8,128)S(1)}, f32[17,8,128]{2,1,0:T(8,128)S(1)}, u32[]{:S(2)}, u32[]{:S(2)}) collective-permute-start(f32[17,8,128]{2,1,0:T(8,128)S(1)} %get-tuple-element.26), channel_id=1, source_target_pairs={{0,4},{1,9},{2,6},{3,11},{4,0},{5,13},{6,2},{7,15},{8,12},{9,1},{1... | collective-permute-start | bytes 208904 | tf_op jit(solution)/shard_map/ppermute | solution.py:366
  10.3 6.0 %collective-permute-start.10 = (f32[17,8,128]{2,1,0:T(8,128)S(1)}, f32[17,8,128]{2,1,0:T(8,128)S(1)}, u32[]{:S(2)}, u32[]{:S(2)}) collective-permute-start(f32[17,8,128]{2,1,0:T(8,128)S(1)} %get-tuple-element.27), channel_id=1, source_target_pairs={{0,8},{1,5},{2,10},{3,7},{4,12},{5,1},{6,14},{7,3},{8,0},{9,13},{1... | collective-permute-start | bytes 208904 | tf_op jit(solution)/shard_map/ppermute | solution.py:366
  11.9 5.4 %collective-permute-start.11 = (f32[17,8,128]{2,1,0:T(8,128)S(1)}, f32[17,8,128]{2,1,0:T(8,128)S(1)}, u32[]{:S(2)}, u32[]{:S(2)}) collective-permute-start(f32[17,8,128]{2,1,0:T(8,128)S(1)} %get-tuple-element.28), channel_id=1, source_target_pairs={{0,12},{1,13},{2,14},{3,15},{4,8},{5,9},{6,10},{7,11},{8,4},{9,5},... | collective-permute-start | bytes 208904 | tf_op jit(solution)/shard_map/ppermute | solution.py:366
  12.3 7.8 %collective-permute-start.2 = (f32[17,8,128]{2,1,0:T(8,128)S(1)}, f32[17,8,128]{2,1,0:T(8,128)S(1)}, u32[]{:S(2)}, u32[]{:S(2)}) collective-permute-start(f32[17,8,128]{2,1,0:T(8,128)S(1)} %get-tuple-element.22), channel_id=1, source_target_pairs={{0,4},{1,9},{2,6},{3,11},{4,0},{5,13},{6,2},{7,15},{8,12},{9,1},{1... | collective-permute-start | bytes 208904 | tf_op jit(solution)/shard_map/ppermute | solution.py:366
  13.8 6.3 %collective-permute-start.3 = (f32[17,8,128]{2,1,0:T(8,128)S(1)}, f32[17,8,128]{2,1,0:T(8,128)S(1)}, u32[]{:S(2)}, u32[]{:S(2)}) collective-permute-start(f32[17,8,128]{2,1,0:T(8,128)S(1)} %get-tuple-element.23), channel_id=1, source_target_pairs={{0,8},{1,5},{2,10},{3,7},{4,12},{5,1},{6,14},{7,3},{8,0},{9,13},{1... | collective-permute-start | bytes 208904 | tf_op jit(solution)/shard_map/ppermute | solution.py:366
  15.4 5.3 %collective-permute-start.4 = (f32[17,8,128]{2,1,0:T(8,128)S(1)}, f32[17,8,128]{2,1,0:T(8,128)S(1)}, u32[]{:S(2)}, u32[]{:S(2)}) collective-permute-start(f32[17,8,128]{2,1,0:T(8,128)S(1)} %get-tuple-element.24), channel_id=1, source_target_pairs={{0,12},{1,13},{2,14},{3,15},{4,8},{5,9},{6,10},{7,11},{8,4},{9,5},... | collective-permute-start | bytes 208904 | tf_op jit(solution)/shard_map/ppermute | solution.py:366
  17.4 6.4 %collective-permute-start.12 = (f32[17,8,128]{2,1,0:T(8,128)S(1)}, f32[17,8,128]{2,1,0:T(8,128)S(1)}, u32[]{:S(2)}, u32[]{:S(2)}) collective-permute-start(f32[17,8,128]{2,1,0:T(8,128)S(1)} %shard_map.62.refs_0_), channel_id=1, source_target_pairs={{0,16},{4,20},{8,24},{12,28},{16,0},{20,4},{24,8},{28,12},{1,17},{... | collective-permute-start | bytes 208904 | tf_op jit(solution)/shard_map/ppermute | solution.py:373
  20.7 6.6 %collective-permute-start.5 = (f32[17,8,128]{2,1,0:T(8,128)S(1)}, f32[17,8,128]{2,1,0:T(8,128)S(1)}, u32[]{:S(2)}, u32[]{:S(2)}) collective-permute-start(f32[17,8,128]{2,1,0:T(8,128)S(1)} %shard_map.60.refs_0_), channel_id=1, source_target_pairs={{0,16},{4,20},{8,24},{12,28},{16,0},{20,4},{24,8},{28,12},{1,17},{... | collective-permute-start | bytes 208904 | tf_op jit(solution)/shard_map/ppermute | solution.py:373
  23.8 5.6 %collective-permute-start.15 = (f32[17,8,128]{2,1,0:T(8,128)S(1)}, f32[17,8,128]{2,1,0:T(8,128)S(1)}, u32[]{:S(2)}, u32[]{:S(2)}) collective-permute-start(f32[17,8,128]{2,1,0:T(8,128)S(1)} %shard_map.63.refs_0_), channel_id=1, source_target_pairs={{0,12},{1,13},{2,14},{3,15},{4,8},{5,9},{6,10},{7,11},{8,4},{9,5},... | collective-permute-start | bytes 208904 | tf_op jit(solution)/shard_map/ppermute | solution.py:366
  24.9 6.0 %collective-permute-start.14 = (f32[17,8,128]{2,1,0:T(8,128)S(1)}, f32[17,8,128]{2,1,0:T(8,128)S(1)}, u32[]{:S(2)}, u32[]{:S(2)}) collective-permute-start(f32[17,8,128]{2,1,0:T(8,128)S(1)} %shard_map.63.refs_0_), channel_id=1, source_target_pairs={{0,8},{1,5},{2,10},{3,7},{4,12},{5,1},{6,14},{7,3},{8,0},{9,13},{1... | collective-permute-start | bytes 208904 | tf_op jit(solution)/shard_map/ppermute | solution.py:366
  25.7 5.2 %collective-permute-start.13 = (f32[17,8,128]{2,1,0:T(8,128)S(1)}, f32[17,8,128]{2,1,0:T(8,128)S(1)}, u32[]{:S(2)}, u32[]{:S(2)}) collective-permute-start(f32[17,8,128]{2,1,0:T(8,128)S(1)} %shard_map.63.refs_0_), channel_id=1, source_target_pairs={{0,4},{1,9},{2,6},{3,11},{4,0},{5,13},{6,2},{7,15},{8,12},{9,1},{1... | collective-permute-start | bytes 208904 | tf_op jit(solution)/shard_map/ppermute | solution.py:366
  27.4 5.3 %collective-permute-start.8 = (f32[17,8,128]{2,1,0:T(8,128)S(1)}, f32[17,8,128]{2,1,0:T(8,128)S(1)}, u32[]{:S(2)}, u32[]{:S(2)}) collective-permute-start(f32[17,8,128]{2,1,0:T(8,128)S(1)} %shard_map.61.refs_0_), channel_id=1, source_target_pairs={{0,12},{1,13},{2,14},{3,15},{4,8},{5,9},{6,10},{7,11},{8,4},{9,5},... | collective-permute-start | bytes 208904 | tf_op jit(solution)/shard_map/ppermute | solution.py:366
  28.5 4.3 %collective-permute-start.7 = (f32[17,8,128]{2,1,0:T(8,128)S(1)}, f32[17,8,128]{2,1,0:T(8,128)S(1)}, u32[]{:S(2)}, u32[]{:S(2)}) collective-permute-start(f32[17,8,128]{2,1,0:T(8,128)S(1)} %shard_map.61.refs_0_), channel_id=1, source_target_pairs={{0,8},{1,5},{2,10},{3,7},{4,12},{5,1},{6,14},{7,3},{8,0},{9,13},{1... | collective-permute-start | bytes 208904 | tf_op jit(solution)/shard_map/ppermute | solution.py:366
  29.4 4.3 %collective-permute-start.6 = (f32[17,8,128]{2,1,0:T(8,128)S(1)}, f32[17,8,128]{2,1,0:T(8,128)S(1)}, u32[]{:S(2)}, u32[]{:S(2)}) collective-permute-start(f32[17,8,128]{2,1,0:T(8,128)S(1)} %shard_map.61.refs_0_), channel_id=1, source_target_pairs={{0,4},{1,9},{2,6},{3,11},{4,0},{5,13},{6,2},{7,15},{8,12},{9,1},{1... | collective-permute-start | bytes 208904 | tf_op jit(solution)/shard_map/ppermute | solution.py:366

commit v16 on v15

--- a/solution.py
+++ b/solution.py
@@ -229,13 +229,26 @@
         )
 
     def last(source):
-        for k, out_ref in enumerate(out_refs):
-            stream, meet = divmod(k, SQUARE)
-            chunk = stream * SQUARE + (me_ref[0] ^ partners(dom_ref[0])[meet])
+        for out_ref, away in zip(out_refs, partners(dom_ref[0])):
+            first = (me_ref[0] ^ away) * per_chunk
             emit = functools.partial(finish, out_ref)
-            advance(chunk * per_chunk, per_chunk, HALF, source, coefs, emit)
+            advance(first, per_chunk, HALF, source, coefs, emit)
 
     run_steps(strips, HALF, load, (state_a, state_b), coefs, last)
+
+
+def split_kernel(per_chunk, *refs):
+    parts, out_refs = refs[:SQUARE], refs[SQUARE:]
+    size = per_chunk * TILE // STREAMS
+    for stream, out_ref in enumerate(out_refs):
+        for at, to in (
+            (pl.ds(stream * size, size), pl.ds(0, size)),
+            (pl.ds(per_chunk * TILE, out_ref.shape[0] - size), pl.ds(size, out_ref.shape[0] - size)),
+        ):
+            total = parts[0][at]
+            for part in parts[1:]:
+                total = total + part[at]
+            out_ref[to] = total
 
 
 def sum_kernel(*refs):
@@ -248,17 +261,18 @@
 
 def nodal_kernel(per_chunk, stream, dom_ref, me_ref, keep_ref, *refs):
     totals, (out_ref, values, sems) = refs[:SQUARE], refs[-3:]
-    many = values.shape[1]
+    many, half = values.shape[1:3]
     fine, mid, low = (keep_ref[k] for k in range(3))
     place = lax.broadcasted_iota(jnp.int32, (many, LANES), 0)
     copies = []
     for k, (ref, away) in enumerate(zip(totals, partners(dom_ref[0]))):
-        first = (stream * SQUARE + (me_ref[0] ^ away)) * per_chunk
+        first = (me_ref[0] ^ away) * per_chunk + stream * half
         by_row = flat(values.at[k])
 
         def body(part, ref=ref, by_row=by_row):
             w = [ref[part * TILE + t] for t in range(TILE)]
-            before = ref[per_chunk * TILE + part // many, pl.ds(lax.rem(part, many), 1), :]
+            spot = stream * half + part
+            before = ref[half * TILE + spot // many, pl.ds(lax.rem(spot, many), 1), :]
             prev = jnp.where(place == 0, before, roll_rows(w[7], 1))
             v3 = 0.5 * (prev + w[7]) + low * w[3]
             v1 = 0.5 * (prev + v3) + mid * w[1]
@@ -274,12 +288,12 @@
                 w[7],
             )
             for t in range(TILE):
-                by_row[spaced(part * TILE + t, many, per_chunk * TILE), :] = rows[t]
-
-        per_strip(per_chunk, body, min(per_chunk, 4))
+                by_row[spaced(part * TILE + t, many, half * TILE), :] = rows[t]
+
+        per_strip(half, body, min(half, 4))
         for m in range(many):
             copy = pltpu.make_async_copy(
-                values.at[k, m], out_ref.at[m, pl.ds(first, per_chunk)], sems.at[k, m]
+                values.at[k, m], out_ref.at[m, pl.ds(first, half)], sems.at[k, m]
             )
             copy.start()
             copies.append(copy)
@@ -313,7 +327,7 @@
     rows, cols = density.shape[1:]
     doms, grids = lax.axis_size("dom"), lax.axis_size("grp")
     many, strips = rows // TILE, cols // LANES
-    per_chunk = strips // (SQUARE * STREAMS)
+    per_chunk = strips // SQUARE
     depth = (rows * doms).bit_length() - 1
     tiles = [tiles_of(x[0]) for x in (density, diffusion, drift_speed)]
     me = (lax.axis_index("grp") % SQUARE).astype(jnp.int32)[None]
@@ -349,9 +363,9 @@
         flops=40 * rows * cols,
     )
     chunk = (per_chunk * TILE + -(-per_chunk // many), many, LANES)
-    weighted = call(
+    own, *others = call(
         functools.partial(edge_kernel, per_chunk, doms),
-        [chunk] * (SQUARE * STREAMS),
+        [chunk] * SQUARE,
         (dom, me, weight, *tiles, state, near, far),
         2,
         [vmem(3, strips, SLAB, LANES)]
@@ -365,25 +379,28 @@
         pairs = [(g * doms + d, (g ^ partners(d % 2)[meet]) * doms + d) for g, d in devices]
         return lax.ppermute(array, ("grp", "dom"), pairs)
 
-    def over_grids(own, *others):
-        theirs = [swap(array, meet) for meet, array in enumerate(others, 1)]
-        (total,) = call(sum_kernel, [chunk], (own, *theirs))
+    half = (chunk[0] - per_chunk * TILE + per_chunk * TILE // STREAMS, many, LANES)
+    theirs = [swap(array, meet) for meet, array in enumerate(others, 1)]
+    streams = call(
+        functools.partial(split_kernel, per_chunk), [half] * STREAMS, (own, *theirs)
+    )
+    nodal = None
+    for stream, total in enumerate(streams):
         apart = SQUARE
         while apart < grids:
             other = lax.ppermute(total, "grp", [(g, g ^ apart) for g in range(grids)])
-            (total,) = call(sum_kernel, [chunk], (total, other))
+            (total,) = call(sum_kernel, [half], (total, other))
             apart *= 2
-        return [total] + [swap(total, meet) for meet in range(1, SQUARE)]
-
-    nodal = None
-    for stream in range(STREAMS):
-        totals = over_grids(*weighted[stream * SQUARE : (stream + 1) * SQUARE])
+        totals = [total] + [swap(total, meet) for meet in range(1, SQUARE)]
         (nodal,) = call(
             functools.partial(nodal_kernel, per_chunk, stream),
             [(many, strips, TILE, LANES)],
             (dom, me, keep, *totals),
             2,
-            [vmem(SQUARE, many, per_chunk, TILE, LANES), pltpu.SemaphoreType.DMA((SQUARE, many))],
+            [
+                vmem(SQUARE, many, per_chunk // STREAMS, TILE, LANES),
+                pltpu.SemaphoreType.DMA((SQUARE, many)),
+            ],
             out_space=pl.ANY,
             onto=nodal,
         )

time: 34.9 us -> 36.8 us (1.054)
  the two profiles are of different devices: /device:TPU:4 before, /device:TPU:28 now
where the time goes in v16:
time: 36.8 us; the launch traced here: 36.7 us
  starting transfers between devices  17.3 us (47%)
  waiting for transfers between devices  12.8 us (35%)
  Pallas kernels  4.92 us (13%)
  between operations  1.56 us (4%)
    ppermute x9, starting transfers between devices, swap(): return lax.ppermute(array, ('grp', 'dom'), pairs)  11.8 us
    ppermute x9, waiting for transfers between devices, swap(): return lax.ppermute(array, ('grp', 'dom'), pairs)  8.57 us
    pallas_call x10, Pallas kernels, call(): pl.pallas_call(kernel, out_shape=[jax.ShapeDtypeStruct(shape, jnp.float32...  4.92 us
    ppermute x2, starting transfers between devices, on_device(): other = lax.ppermute(total, 'grp', [(g, g ^ apart) for g in range(grids)])  2.98 us
    ppermute x1, starting transfers between devices, on_device(): far = lax.ppermute(far, 'dom', far_pairs)  2.5 us
    ppermute x2, waiting for transfers between devices, on_device(): other = lax.ppermute(total, 'grp', [(g, g ^ apart) for g in range(grids)])  2.39 us
    ppermute x1, waiting for transfers between devices, on_device(): far = lax.ppermute(far, 'dom', far_pairs)  1.88 us
  transfers between devices with their start and end apart: 13, of which 8 were waited for; matrix products, arithmetic and copies ran while one was open for 0% of the time, Pallas kernels for 8%

profile of v16, /device:TPU:28, one launch (start us, length us, event | category | flops | bytes accessed | tf_op | source)
XLA Modules:
  0.0 36.7 jit_solution(10683690051574644920)
XLA Ops:
  0.0 0.0 copy-start
  0.0 0.0 copy-start.1
  0.0 0.0 copy-start.2
  1.4 0.0 copy-done
  1.5 0.0 copy-done.1
  1.5 0.0 copy-done.2
  1.5 0.1 shard_map.58
  1.5 0.1 collective-permute-start
  1.6 2.5 %collective-permute-start.1 = (f32[16,16,128]{2,1,0:T(8,128)S(1)}, f32[16,16,128]{2,1,0:T(8,128)S(1)}, u32[]{:S(2)}, u32[]{:S(2)}) collective-permute-start(f32[16,16,128]{2,1,0:T(8,128)S(1)} %get-tuple-element.18), channel_id=1, source_target_pairs={{0,0},{1,2},{2,1},{3,3},{4,4},{5,6},{6,5},{7,7},{8,8},{9,10},{10,9... | collective-permute-start | bytes 393224 | tf_op jit(solution)/shard_map/ppermute | solution.py:355
  4.1 1.9 %shard_map.57.refs_2_ = f32[16,8,8,128]{3,2,1,0:T(8,128)S(1)} custom-call(f32[8,16,8,128]{3,2,1,0:T(8,128)S(1)} %bitcast.15, f32[8,16,8,128]{3,2,1,0:T(8,128)S(1)} %bitcast.18, f32[8,16,8,128]{3,2,1,0:T(8,128)S(1)} %bitcast.21), custom_call_target="tpu_custom_call" | custom-call | flops 5242880 | bytes 1572864 | tf_op jit(solution)/shard_map/pallas_call | solution.py:314
  6.0 0.0 collective-permute-done.refs_3_
  6.0 1.9 %collective-permute-done.1.refs_4_ = f32[16,16,128]{2,1,0:T(8,128)S(1)} collective-permute-done((f32[16,16,128]{2,1,0:T(8,128)S(1)}, f32[16,16,128]{2,1,0:T(8,128)S(1)}, u32[]{:S(2)}, u32[]{:S(2)}) %collective-permute-start.1) | collective-permute-done | bytes 131104 | tf_op jit(solution)/shard_map/ppermute | solution.py:355
  7.9 0.9 %shard_map.59 = (f32[33,8,128]{2,1,0:T(8,128)S(1)}, f32[33,8,128]{2,1,0:T(8,128)S(1)}, f32[33,8,128]{2,1,0:T(8,128)S(1)}, f32[33,8,128]{2,1,0:T(8,128)S(1)}) custom-call(s32[1]{0:T(128)} %bitcast.dom_ref, s32[1]{0:T(128)} %bitcast.1.me_ref, f32[4,8,128]{2,1,0:T(8,128)S(1)} %get-tuple-element.16.weight_ref, f32[8,16,8,128]{3,2,1,0:T(8,128)S(1)} %bitcast.16, ...), custom_call_target="tpu_custom_call" | custom-call | flops 2621440 | bytes 2375688 | tf_op jit(solution)/shard_map/pallas_call | solution.py:314
  8.8 1.6 %collective-permute-start.2 = (f32[33,8,128]{2,1,0:T(8,128)S(1)}, f32[33,8,128]{2,1,0:T(8,128)S(1)}, u32[]{:S(2)}, u32[]{:S(2)}) collective-permute-start(f32[33,8,128]{2,1,0:T(8,128)S(1)} %get-tuple-element.20), channel_id=1, source_target_pairs={{0,4},{1,9},{2,6},{3,11},{4,0},{5,13},{6,2},{7,15},{8,12},{9,1},{1... | collective-permute-start | bytes 405512 | tf_op jit(solution)/shard_map/ppermute | solution.py:380
  10.3 0.4 %collective-permute-start.3 = (f32[33,8,128]{2,1,0:T(8,128)S(1)}, f32[33,8,128]{2,1,0:T(8,128)S(1)}, u32[]{:S(2)}, u32[]{:S(2)}) collective-permute-start(f32[33,8,128]{2,1,0:T(8,128)S(1)} %get-tuple-element.21), channel_id=1, source_target_pairs={{0,8},{1,5},{2,10},{3,7},{4,12},{5,1},{6,14},{7,3},{8,0},{9,13},{1... | collective-permute-start | bytes 405512 | tf_op jit(solution)/shard_map/ppermute | solution.py:380
  10.8 1.5 %collective-permute-start.4 = (f32[33,8,128]{2,1,0:T(8,128)S(1)}, f32[33,8,128]{2,1,0:T(8,128)S(1)}, u32[]{:S(2)}, u32[]{:S(2)}) collective-permute-start(f32[33,8,128]{2,1,0:T(8,128)S(1)} %get-tuple-element.22), channel_id=1, source_target_pairs={{0,12},{1,13},{2,14},{3,15},{4,8},{5,9},{6,10},{7,11},{8,4},{9,5},... | collective-permute-start | bytes 405512 | tf_op jit(solution)/shard_map/ppermute | solution.py:380
  12.3 1.5 %collective-permute-done.2.refs_1_ = f32[33,8,128]{2,1,0:T(8,128)S(1)} collective-permute-done((f32[33,8,128]{2,1,0:T(8,128)S(1)}, f32[33,8,128]{2,1,0:T(8,128)S(1)}, u32[]{:S(2)}, u32[]{:S(2)}) %collective-permute-start.2) | collective-permute-done | bytes 135200 | tf_op jit(solution)/shard_map/ppermute | solution.py:380
  13.8 1.5 %collective-permute-done.3.refs_2_ = f32[33,8,128]{2,1,0:T(8,128)S(1)} collective-permute-done((f32[33,8,128]{2,1,0:T(8,128)S(1)}, f32[33,8,128]{2,1,0:T(8,128)S(1)}, u32[]{:S(2)}, u32[]{:S(2)}) %collective-permute-start.3) | collective-permute-done | bytes 135200 | tf_op jit(solution)/shard_map/ppermute | solution.py:380
  15.3 2.5 %collective-permute-done.4.refs_3_ = f32[33,8,128]{2,1,0:T(8,128)S(1)} collective-permute-done((f32[33,8,128]{2,1,0:T(8,128)S(1)}, f32[33,8,128]{2,1,0:T(8,128)S(1)}, u32[]{:S(2)}, u32[]{:S(2)}) %collective-permute-start.4) | collective-permute-done | bytes 135200 | tf_op jit(solution)/shard_map/ppermute | solution.py:380
  17.9 0.1 collective-permute-start.9
  17.9 2.9 %collective-permute-start.5 = (f32[17,8,128]{2,1,0:T(8,128)S(1)}, f32[17,8,128]{2,1,0:T(8,128)S(1)}, u32[]{:S(2)}, u32[]{:S(2)}) collective-permute-start(f32[17,8,128]{2,1,0:T(8,128)S(1)} %get-tuple-element.23.refs_0_), channel_id=1, source_target_pairs={{0,16},{4,20},{8,24},{12,28},{16,0},{20,4},{24,8},{28,12},{1,17},{... | collective-permute-start | bytes 208904 | tf_op jit(solution)/shard_map/ppermute | solution.py:391
  20.9 2.4 %collective-permute-done.9.refs_1_ = f32[17,8,128]{2,1,0:T(8,128)S(1)} collective-permute-done((f32[17,8,128]{2,1,0:T(8,128)S(1)}, f32[17,8,128]{2,1,0:T(8,128)S(1)}, u32[]{:S(2)}, u32[]{:S(2)}) %collective-permute-start.9) | collective-permute-done | bytes 69664 | tf_op jit(solution)/shard_map/ppermute | solution.py:391
  23.3 1.8 %collective-permute-start.12 = (f32[17,8,128]{2,1,0:T(8,128)S(1)}, f32[17,8,128]{2,1,0:T(8,128)S(1)}, u32[]{:S(2)}, u32[]{:S(2)}) collective-permute-start(f32[17,8,128]{2,1,0:T(8,128)S(1)} %shard_map.62.refs_0_), channel_id=1, source_target_pairs={{0,12},{1,13},{2,14},{3,15},{4,8},{5,9},{6,10},{7,11},{8,4},{9,5},... | collective-permute-start | bytes 208904 | tf_op jit(solution)/shard_map/ppermute | solution.py:380
  25.1 2.7 %collective-permute-start.11 = (f32[17,8,128]{2,1,0:T(8,128)S(1)}, f32[17,8,128]{2,1,0:T(8,128)S(1)}, u32[]{:S(2)}, u32[]{:S(2)}) collective-permute-start(f32[17,8,128]{2,1,0:T(8,128)S(1)} %shard_map.62.refs_0_), channel_id=1, source_target_pairs={{0,8},{1,5},{2,10},{3,7},{4,12},{5,1},{6,14},{7,3},{8,0},{9,13},{1... | collective-permute-start | bytes 208904 | tf_op jit(solution)/shard_map/ppermute | solution.py:380
  27.7 0.0 collective-permute-start.10
  27.7 0.0 collective-permute-done.5.refs_1_
  27.8 1.5 %collective-permute-start.8 = (f32[17,8,128]{2,1,0:T(8,128)S(1)}, f32[17,8,128]{2,1,0:T(8,128)S(1)}, u32[]{:S(2)}, u32[]{:S(2)}) collective-permute-start(f32[17,8,128]{2,1,0:T(8,128)S(1)} %shard_map.61.refs_0_), channel_id=1, source_target_pairs={{0,12},{1,13},{2,14},{3,15},{4,8},{5,9},{6,10},{7,11},{8,4},{9,5},... | collective-permute-start | bytes 208904 | tf_op jit(solution)/shard_map/ppermute | solution.py:380
  29.3 2.0 %collective-permute-start.7 = (f32[17,8,128]{2,1,0:T(8,128)S(1)}, f32[17,8,128]{2,1,0:T(8,128)S(1)}, u32[]{:S(2)}, u32[]{:S(2)}) collective-permute-start(f32[17,8,128]{2,1,0:T(8,128)S(1)} %shard_map.61.refs_0_), channel_id=1, source_target_pairs={{0,8},{1,5},{2,10},{3,7},{4,12},{5,1},{6,14},{7,3},{8,0},{9,13},{1... | collective-permute-start | bytes 208904 | tf_op jit(solution)/shard_map/ppermute | solution.py:380
  31.3 0.0 collective-permute-done.12.refs_3_
  31.3 0.2 collective-permute-start.6
  31.5 0.0 collective-permute-done.11.refs_2_
  31.5 0.5 %collective-permute-done.10.refs_1_ = f32[17,8,128]{2,1,0:T(8,128)S(1)} collective-permute-done((f32[17,8,128]{2,1,0:T(8,128)S(1)}, f32[17,8,128]{2,1,0:T(8,128)S(1)}, u32[]{:S(2)}, u32[]{:S(2)}) %collective-permute-start.10) | collective-permute-done | bytes 69664 | tf_op jit(solution)/shard_map/ppermute | solution.py:380
  32.1 1.0 %shard_map.63.refs_4_ = f32[8,16,8,128]{3,2,1,0:T(8,128)} custom-call(s32[1]{0:T(128)} %bitcast.dom_ref, s32[1]{0:T(128)} %bitcast.1.me_ref, f32[3,8,128]{2,1,0:T(8,128)S(1)} %get-tuple-element.15.keep_ref, f32[17,8,128]{2,1,0:T(8,128)S(1)} %shard_map.62.refs_0_, f32[17,8,128]{2,1,0:T(8,128)S(1)} %collective-permute-done.10.refs_1_, ...), custom_call_target="tpu_custom_call" | custom-call | bytes 290824 | tf_op jit(solution)/shard_map/pallas_call | solution.py:314
  33.1 0.0 collective-permute-done.8.refs_3_
  33.1 1.2 %collective-permute-done.7.refs_2_ = f32[17,8,128]{2,1,0:T(8,128)S(1)} collective-permute-done((f32[17,8,128]{2,1,0:T(8,128)S(1)}, f32[17,8,128]{2,1,0:T(8,128)S(1)}, u32[]{:S(2)}, u32[]{:S(2)}) %collective-permute-start.7) | collective-permute-done | bytes 69664 | tf_op jit(solution)/shard_map/ppermute | solution.py:380
  34.3 1.3 %collective-permute-done.6.refs_1_ = f32[17,8,128]{2,1,0:T(8,128)S(1)} collective-permute-done((f32[17,8,128]{2,1,0:T(8,128)S(1)}, f32[17,8,128]{2,1,0:T(8,128)S(1)}, u32[]{:S(2)}, u32[]{:S(2)}) %collective-permute-start.6) | collective-permute-done | bytes 69664 | tf_op jit(solution)/shard_map/ppermute | solution.py:380
  35.6 1.0 %shard_map.64 = f32[8,16,8,128]{3,2,1,0:T(8,128)} custom-call(s32[1]{0:T(128)} %bitcast.dom_ref, s32[1]{0:T(128)} %bitcast.1.me_ref, f32[3,8,128]{2,1,0:T(8,128)S(1)} %get-tuple-element.15.keep_ref, f32[17,8,128]{2,1,0:T(8,128)S(1)} %shard_map.61.refs_0_, f32[17,8,128]{2,1,0:T(8,128)S(1)} %collective-permute-done.6.refs_1_, ...), custom_call_target="tpu_custom_call", output_to_operand_aliasing={{}: (7, {})} | custom-call | bytes 815112 | tf_op jit(solution)/shard_map/pallas_call | solution.py:314
  (5 shorter events, 0.1 us)
Async XLA Ops:
  0.0 1.5 %copy-start = (f32[1,64,2048]{2,1,0:T(8,128)S(1)}, f32[1,64,2048]{2,1,0:T(8,128)}, u32[]{:S(2)}) copy-start(f32[1,64,2048]{2,1,0:T(8,128)} %param.5) | copy-start | bytes 1572868
  0.0 1.5 %copy-start.1 = (f32[1,64,2048]{2,1,0:T(8,128)S(1)}, f32[1,64,2048]{2,1,0:T(8,128)}, u32[]{:S(2)}) copy-start(f32[1,64,2048]{2,1,0:T(8,128)} %param.6) | copy-start | bytes 1572868
  0.0 1.5 %copy-start.2 = (f32[1,64,2048]{2,1,0:T(8,128)S(1)}, f32[1,64,2048]{2,1,0:T(8,128)}, u32[]{:S(2)}) copy-start(f32[1,64,2048]{2,1,0:T(8,128)} %param.7) | copy-start | bytes 1572868
  1.5 4.5 %collective-permute-start = (f32[16,16,128]{2,1,0:T(8,128)S(1)}, f32[16,16,128]{2,1,0:T(8,128)S(1)}, u32[]{:S(2)}, u32[]{:S(2)}) collective-permute-start(f32[16,16,128]{2,1,0:T(8,128)S(1)} %get-tuple-element.17), channel_id=1, source_target_pairs={{0,1},{1,0},{2,3},{3,2},{4,5},{5,4},{6,7},{7,6},{8,9},{9,8},{10,11... | collective-permute-start | bytes 393224 | tf_op jit(solution)/shard_map/ppermute | solution.py:354
  1.6 6.3 %collective-permute-start.1 = (f32[16,16,128]{2,1,0:T(8,128)S(1)}, f32[16,16,128]{2,1,0:T(8,128)S(1)}, u32[]{:S(2)}, u32[]{:S(2)}) collective-permute-start(f32[16,16,128]{2,1,0:T(8,128)S(1)} %get-tuple-element.18), channel_id=1, source_target_pairs={{0,0},{1,2},{2,1},{3,3},{4,4},{5,6},{6,5},{7,7},{8,8},{9,10},{10,9... | collective-permute-start | bytes 393224 | tf_op jit(solution)/shard_map/ppermute | solution.py:355
  8.8 5.1 %collective-permute-start.2 = (f32[33,8,128]{2,1,0:T(8,128)S(1)}, f32[33,8,128]{2,1,0:T(8,128)S(1)}, u32[]{:S(2)}, u32[]{:S(2)}) collective-permute-start(f32[33,8,128]{2,1,0:T(8,128)S(1)} %get-tuple-element.20), channel_id=1, source_target_pairs={{0,4},{1,9},{2,6},{3,11},{4,0},{5,13},{6,2},{7,15},{8,12},{9,1},{1... | collective-permute-start | bytes 405512 | tf_op jit(solution)/shard_map/ppermute | solution.py:380
  10.3 5.0 %collective-permute-start.3 = (f32[33,8,128]{2,1,0:T(8,128)S(1)}, f32[33,8,128]{2,1,0:T(8,128)S(1)}, u32[]{:S(2)}, u32[]{:S(2)}) collective-permute-start(f32[33,8,128]{2,1,0:T(8,128)S(1)} %get-tuple-element.21), channel_id=1, source_target_pairs={{0,8},{1,5},{2,10},{3,7},{4,12},{5,1},{6,14},{7,3},{8,0},{9,13},{1... | collective-permute-start | bytes 405512 | tf_op jit(solution)/shard_map/ppermute | solution.py:380
  10.8 7.1 %collective-permute-start.4 = (f32[33,8,128]{2,1,0:T(8,128)S(1)}, f32[33,8,128]{2,1,0:T(8,128)S(1)}, u32[]{:S(2)}, u32[]{:S(2)}) collective-permute-start(f32[33,8,128]{2,1,0:T(8,128)S(1)} %get-tuple-element.22), channel_id=1, source_target_pairs={{0,12},{1,13},{2,14},{3,15},{4,8},{5,9},{6,10},{7,11},{8,4},{9,5},... | collective-permute-start | bytes 405512 | tf_op jit(solution)/shard_map/ppermute | solution.py:380
  17.9 5.4 %collective-permute-start.9 = (f32[17,8,128]{2,1,0:T(8,128)S(1)}, f32[17,8,128]{2,1,0:T(8,128)S(1)}, u32[]{:S(2)}, u32[]{:S(2)}) collective-permute-start(f32[17,8,128]{2,1,0:T(8,128)S(1)} %get-tuple-element.24.refs_0_), channel_id=1, source_target_pairs={{0,16},{4,20},{8,24},{12,28},{16,0},{20,4},{24,8},{28,12},{1,17},{... | collective-permute-start | bytes 208904 | tf_op jit(solution)/shard_map/ppermute | solution.py:391
  17.9 9.8 %collective-permute-start.5 = (f32[17,8,128]{2,1,0:T(8,128)S(1)}, f32[17,8,128]{2,1,0:T(8,128)S(1)}, u32[]{:S(2)}, u32[]{:S(2)}) collective-permute-start(f32[17,8,128]{2,1,0:T(8,128)S(1)} %get-tuple-element.23.refs_0_), channel_id=1, source_target_pairs={{0,16},{4,20},{8,24},{12,28},{16,0},{20,4},{24,8},{28,12},{1,17},{... | collective-permute-start | bytes 208904 | tf_op jit(solution)/shard_map/ppermute | solution.py:391
  23.3 8.1 %collective-permute-start.12 = (f32[17,8,128]{2,1,0:T(8,128)S(1)}, f32[17,8,128]{2,1,0:T(8,128)S(1)}, u32[]{:S(2)}, u32[]{:S(2)}) collective-permute-start(f32[17,8,128]{2,1,0:T(8,128)S(1)} %shard_map.62.refs_0_), channel_id=1, source_target_pairs={{0,12},{1,13},{2,14},{3,15},{4,8},{5,9},{6,10},{7,11},{8,4},{9,5},... | collective-permute-start | bytes 208904 | tf_op jit(solution)/shard_map/ppermute | solution.py:380
  25.1 6.4 %collective-permute-start.11 = (f32[17,8,128]{2,1,0:T(8,128)S(1)}, f32[17,8,128]{2,1,0:T(8,128)S(1)}, u32[]{:S(2)}, u32[]{:S(2)}) collective-permute-start(f32[17,8,128]{2,1,0:T(8,128)S(1)} %shard_map.62.refs_0_), channel_id=1, source_target_pairs={{0,8},{1,5},{2,10},{3,7},{4,12},{5,1},{6,14},{7,3},{8,0},{9,13},{1... | collective-permute-start | bytes 208904 | tf_op jit(solution)/shard_map/ppermute | solution.py:380
  27.7 4.3 %collective-permute-start.10 = (f32[17,8,128]{2,1,0:T(8,128)S(1)}, f32[17,8,128]{2,1,0:T(8,128)S(1)}, u32[]{:S(2)}, u32[]{:S(2)}) collective-permute-start(f32[17,8,128]{2,1,0:T(8,128)S(1)} %shard_map.62.refs_0_), channel_id=1, source_target_pairs={{0,4},{1,9},{2,6},{3,11},{4,0},{5,13},{6,2},{7,15},{8,12},{9,1},{1... | collective-permute-start | bytes 208904 | tf_op jit(solution)/shard_map/ppermute | solution.py:380
  27.8 5.3 %collective-permute-start.8 = (f32[17,8,128]{2,1,0:T(8,128)S(1)}, f32[17,8,128]{2,1,0:T(8,128)S(1)}, u32[]{:S(2)}, u32[]{:S(2)}) collective-permute-start(f32[17,8,128]{2,1,0:T(8,128)S(1)} %shard_map.61.refs_0_), channel_id=1, source_target_pairs={{0,12},{1,13},{2,14},{3,15},{4,8},{5,9},{6,10},{7,11},{8,4},{9,5},... | collective-permute-start | bytes 208904 | tf_op jit(solution)/shard_map/ppermute | solution.py:380
  29.3 5.1 %collective-permute-start.7 = (f32[17,8,128]{2,1,0:T(8,128)S(1)}, f32[17,8,128]{2,1,0:T(8,128)S(1)}, u32[]{:S(2)}, u32[]{:S(2)}) collective-permute-start(f32[17,8,128]{2,1,0:T(8,128)S(1)} %shard_map.61.refs_0_), channel_id=1, source_target_pairs={{0,8},{1,5},{2,10},{3,7},{4,12},{5,1},{6,14},{7,3},{8,0},{9,13},{1... | collective-permute-start | bytes 208904 | tf_op jit(solution)/shard_map/ppermute | solution.py:380
  31.3 4.3 %collective-permute-start.6 = (f32[17,8,128]{2,1,0:T(8,128)S(1)}, f32[17,8,128]{2,1,0:T(8,128)S(1)}, u32[]{:S(2)}, u32[]{:S(2)}) collective-permute-start(f32[17,8,128]{2,1,0:T(8,128)S(1)} %shard_map.61.refs_0_), channel_id=1, source_target_pairs={{0,4},{1,9},{2,6},{3,11},{4,0},{5,13},{6,2},{7,15},{8,12},{9,1},{1... | collective-permute-start | bytes 208904 | tf_op jit(solution)/shard_map/ppermute | solution.py:380

commit v17 on v15

--- a/solution.py
+++ b/solution.py
@@ -14,7 +14,6 @@
 SLAB = 4 * TILE
 SQUARE = 4
 UNROLL = 16
-STREAMS = 2
 VMEM_LIMIT = 40 * 1024 * 1024
 LOAD_FLOPS = 4000
 
@@ -154,20 +153,52 @@
     per_strip(strips, body, 4)
 
 
-def inner_kernel(dens_ref, diff_ref, drift_ref, out_ref, state_a, state_b, *coefs):
+def middle_tiles(many):
+    return list(range(many // 4, many - many // 4)) if many >= 4 else []
+
+
+def outer_tiles(many):
+    return [m for m in range(many) if m not in middle_tiles(many)]
+
+
+def emit_tiles(tiles, per_chunk, scratch, out_ref, j, part, weighted, before):
+    many = scratch.shape[1]
+    by_row = flat(scratch)
+    for t in range(TILE):
+        by_row[spaced(j * many * TILE + t, many, TILE), :] = weighted[t]
+    for k, m in enumerate(tiles):
+        out_ref[part * len(tiles) + k] = scratch[j, m]
+    last = per_chunk * len(tiles) + part // TILE
+    out_ref[last, pl.ds(lax.rem(part, TILE), 1), :] = before
+
+
+def inner_kernel(
+    per_chunk, dom_ref, me_ref, weight_ref, dens_ref, diff_ref, drift_ref, state_ref, *refs
+):
     many, strips = dens_ref.shape[:2]
-    refs = [flat(ref) for ref in (dens_ref, diff_ref, drift_ref)]
+    *out_refs, scratch, state_a, state_b = refs[:-4]
+    coefs = refs[-4:]
+    rows = [flat(ref) for ref in (dens_ref, diff_ref, drift_ref)]
+    weights = [weight_ref[k] for k in range(4)]
+    tiles = middle_tiles(many)
 
     def load(j, t):
         at = spaced(j * TILE + t, many, strips * TILE)
-        return [ref[at, :] for ref in refs]
-
-    def emit(j, _, new):
+        return [ref[at, :] for ref in rows]
+
+    def finish(out_ref, j, part, new):
         for t in range(TILE):
-            out_ref[j, t] = new[t]
+            state_ref[j, t] = new[t]
+        if out_ref is not None:
+            weighted = surpluses(new, roll_rows(new[7], 1), weights)
+            before = weighted[7][tiles[0] - 1 : tiles[0]]
+            emit_tiles(tiles, per_chunk, scratch, out_ref, j, part, weighted, before)
 
     def last(source):
-        advance(0, strips, TILE, source, coefs, emit)
+        for out_ref, away in zip(out_refs or [None] * SQUARE, partners(dom_ref[0])):
+            first = (me_ref[0] ^ away) * per_chunk
+            emit = functools.partial(finish, out_ref)
+            advance(first, per_chunk, TILE, source, coefs, emit)
 
     run_steps(strips, TILE, load, (state_a, state_b), coefs, last)
 
@@ -183,7 +214,7 @@
     dom = dom_ref[0]
     odd = dom % 2 == 1
     diff_ref, drift_ref, state_ref, near_ref, far_ref, *rest = refs
-    out_refs, (slab, state_a, state_b, *coefs) = rest[:-7], rest[-7:]
+    out_refs, (scratch, slab, state_a, state_b, *coefs) = rest[:-8], rest[-8:]
 
     def stage(j):
         far, near = far_ref[j], near_ref[j]
@@ -222,18 +253,15 @@
             s[HALF + t] = jnp.where(place == many - 1, new[t][5:6], s[HALF + t])
         before = new[HALF - 1][1:2]
         weighted = surpluses(s, jnp.where(place == 0, before, roll_rows(s[7], 1)), weights)
-        for t in range(TILE):
-            out_ref[part * TILE + t] = weighted[t]
-        out_ref[per_chunk * TILE + part // many, pl.ds(lax.rem(part, many), 1), :] = (
-            weights[3][0:1] * before
-        )
+        before = weights[3][0:1] * before
+        tiles = outer_tiles(many)
+        emit_tiles(tiles, per_chunk, scratch, out_ref, j, part, weighted, before)
 
     def last(source):
-        for k, out_ref in enumerate(out_refs):
-            stream, meet = divmod(k, SQUARE)
-            chunk = stream * SQUARE + (me_ref[0] ^ partners(dom_ref[0])[meet])
+        for out_ref, away in zip(out_refs, partners(dom_ref[0])):
+            first = (me_ref[0] ^ away) * per_chunk
             emit = functools.partial(finish, out_ref)
-            advance(chunk * per_chunk, per_chunk, HALF, source, coefs, emit)
+            advance(first, per_chunk, HALF, source, coefs, emit)
 
     run_steps(strips, HALF, load, (state_a, state_b), coefs, last)
 
@@ -246,20 +274,27 @@
     out_ref[...] = total
 
 
-def nodal_kernel(per_chunk, stream, dom_ref, me_ref, keep_ref, *refs):
-    totals, (out_ref, values, sems) = refs[:SQUARE], refs[-3:]
-    many = values.shape[1]
-    fine, mid, low = (keep_ref[k] for k in range(3))
-    place = lax.broadcasted_iota(jnp.int32, (many, LANES), 0)
+def nodal_kernel(per_chunk, tiles, dom_ref, me_ref, keep_ref, *refs):
+    totals, middles, (out_ref, values, sems) = refs[:SQUARE], refs[SQUARE:-3], refs[-3:]
+    count = len(tiles)
+    fine, mid, low = (keep_ref[k, 0:count] for k in range(3))
+    place = lax.broadcasted_iota(jnp.int32, (count, LANES), 0)
+    gaps = [k for k in range(1, count) if tiles[k] != tiles[k - 1] + 1]
     copies = []
     for k, (ref, away) in enumerate(zip(totals, partners(dom_ref[0]))):
-        first = (stream * SQUARE + (me_ref[0] ^ away)) * per_chunk
+        first = (me_ref[0] ^ away) * per_chunk
         by_row = flat(values.at[k])
 
-        def body(part, ref=ref, by_row=by_row):
-            w = [ref[part * TILE + t] for t in range(TILE)]
-            before = ref[per_chunk * TILE + part // many, pl.ds(lax.rem(part, many), 1), :]
+        def body(part, k=k, ref=ref, by_row=by_row):
+            w = [
+                flat(ref)[spaced(part * count * TILE + t, count, TILE), :] for t in range(TILE)
+            ]
+            before = ref[per_chunk * count + part // TILE, pl.ds(lax.rem(part, TILE), 1), :]
             prev = jnp.where(place == 0, before, roll_rows(w[7], 1))
+            for gap in gaps:
+                across = tiles[gap] - tiles[gap - 1] - 1
+                before = middles[k][part * across + across - 1, TILE - 1 : TILE, :]
+                prev = jnp.where(place == gap, before, prev)
             v3 = 0.5 * (prev + w[7]) + low * w[3]
             v1 = 0.5 * (prev + v3) + mid * w[1]
             v5 = 0.5 * (v3 + w[7]) + mid * w[5]
@@ -274,12 +309,12 @@
                 w[7],
             )
             for t in range(TILE):
-                by_row[spaced(part * TILE + t, many, per_chunk * TILE), :] = rows[t]
+                by_row[spaced(part * TILE + t, count, per_chunk * TILE), :] = rows[t]
 
         per_strip(per_chunk, body, min(per_chunk, 4))
-        for m in range(many):
+        for e, m in enumerate(tiles):
             copy = pltpu.make_async_copy(
-                values.at[k, m], out_ref.at[m, pl.ds(first, per_chunk)], sems.at[k, m]
+                values.at[k, e], out_ref.at[m, pl.ds(first, per_chunk)], sems.at[k, e]
             )
             copy.start()
             copies.append(copy)
@@ -313,7 +348,7 @@
     rows, cols = density.shape[1:]
     doms, grids = lax.axis_size("dom"), lax.axis_size("grp")
     many, strips = rows // TILE, cols // LANES
-    per_chunk = strips // (SQUARE * STREAMS)
+    per_chunk = strips // SQUARE
     depth = (rows * doms).bit_length() - 1
     tiles = [tiles_of(x[0]) for x in (density, diffusion, drift_speed)]
     me = (lax.axis_index("grp") % SQUARE).astype(jnp.int32)[None]
@@ -340,21 +375,26 @@
     near = lax.ppermute(near, "dom", near_pairs)
     far = lax.ppermute(far, "dom", far_pairs)
     place = (strips, TILE, many, LANES)
-    (state,) = call(
-        inner_kernel,
-        [place],
-        tiles,
-        0,
-        [vmem(strips + 2, *place[1:])] * 2 + [vmem(*place)] * 4,
+    pieces = (strips, many, TILE, LANES)
+
+    def chunk(tiles):
+        return per_chunk * len(tiles) + -(-per_chunk // TILE), TILE, LANES
+
+    middle, outer = middle_tiles(many), outer_tiles(many)
+    state, *inside = call(
+        functools.partial(inner_kernel, per_chunk),
+        [place] + [chunk(middle)] * (SQUARE if middle else 0),
+        (dom, me, weight, *tiles),
+        2,
+        [vmem(*pieces)] + [vmem(strips + 2, *place[1:])] * 2 + [vmem(*place)] * 4,
         flops=40 * rows * cols,
     )
-    chunk = (per_chunk * TILE + -(-per_chunk // many), many, LANES)
-    weighted = call(
+    outside = call(
         functools.partial(edge_kernel, per_chunk, doms),
-        [chunk] * (SQUARE * STREAMS),
+        [chunk(outer)] * SQUARE,
         (dom, me, weight, *tiles, state, near, far),
         2,
-        [vmem(3, strips, SLAB, LANES)]
+        [vmem(*pieces), vmem(3, strips, SLAB, LANES)]
         + [vmem(strips + 2, HALF, TILE, LANES)] * 2
         + [vmem(strips, HALF, TILE, LANES)] * 4,
         flops=40 * SLAB * cols,
@@ -367,23 +407,28 @@
 
     def over_grids(own, *others):
         theirs = [swap(array, meet) for meet, array in enumerate(others, 1)]
-        (total,) = call(sum_kernel, [chunk], (own, *theirs))
+        (total,) = call(sum_kernel, [own.shape], (own, *theirs))
         apart = SQUARE
         while apart < grids:
             other = lax.ppermute(total, "grp", [(g, g ^ apart) for g in range(grids)])
-            (total,) = call(sum_kernel, [chunk], (total, other))
+            (total,) = call(sum_kernel, [own.shape], (total, other))
             apart *= 2
         return [total] + [swap(total, meet) for meet in range(1, SQUARE)]
 
-    nodal = None
-    for stream in range(STREAMS):
-        totals = over_grids(*weighted[stream * SQUARE : (stream + 1) * SQUARE])
+    nodal, totals = None, []
+    for some, weighted in ((middle, inside), (outer, outside)):
+        if not some:
+            continue
+        totals = over_grids(*weighted) + totals
         (nodal,) = call(
-            functools.partial(nodal_kernel, per_chunk, stream),
+            functools.partial(nodal_kernel, per_chunk, some),
             [(many, strips, TILE, LANES)],
             (dom, me, keep, *totals),
             2,
-            [vmem(SQUARE, many, per_chunk, TILE, LANES), pltpu.SemaphoreType.DMA((SQUARE, many))],
+            [
+                vmem(SQUARE, len(some), per_chunk, TILE, LANES),
+                pltpu.SemaphoreType.DMA((SQUARE, len(some))),
+            ],
             out_space=pl.ANY,
             onto=nodal,
         )

time: 34.9 us -> 34.1 us (0.977)
  the two profiles are of different devices: /device:TPU:4 before, /device:TPU:0 now
where the time goes in v17:
time: 34.1 us; the launch traced here: 33.9 us
  starting transfers between devices  21.3 us (62%)
  waiting for transfers between devices  6.06 us (18%)
  Pallas kernels  5.05 us (15%)
  between operations  1.52 us (4%)
    ppermute x12, starting transfers between devices, swap(): return lax.ppermute(array, ('grp', 'dom'), pairs)  14.8 us
    ppermute x12, waiting for transfers between devices, swap(): return lax.ppermute(array, ('grp', 'dom'), pairs)  5.42 us
    ppermute x2, starting transfers between devices, over_grids(): other = lax.ppermute(total, 'grp', [(g, g ^ apart) for g in range(grids)])  5.26 us
    pallas_call x11, Pallas kernels, call(): pl.pallas_call(kernel, out_shape=[jax.ShapeDtypeStruct(shape, jnp.float32...  5.05 us
  transfers between devices with their start and end apart: 16, of which 6 were waited for; matrix products, arithmetic and copies ran while one was open for 0% of the time, Pallas kernels for 12%

profile of v17, /device:TPU:0, one launch (start us, length us, event | category | flops | bytes accessed | tf_op | source)
XLA Modules:
  0.0 33.9 jit_solution(17774536235375960663)
XLA Ops:
  0.0 0.0 copy-start
  0.0 0.0 copy-start.1
  0.0 0.0 copy-start.2
  1.4 0.0 copy-done
  1.5 0.0 copy-done.1
  1.5 0.0 copy-done.2
  1.5 0.1 shard_map.58
  1.5 0.5 %collective-permute-start = (f32[16,16,128]{2,1,0:T(8,128)S(1)}, f32[16,16,128]{2,1,0:T(8,128)S(1)}, u32[]{:S(2)}, u32[]{:S(2)}) collective-permute-start(f32[16,16,128]{2,1,0:T(8,128)S(1)} %get-tuple-element.21), channel_id=1, source_target_pairs={{0,1},{1,0},{2,3},{3,2},{4,5},{5,4},{6,7},{7,6},{8,9},{9,8},{10,11... | collective-permute-start | bytes 393224 | tf_op jit(solution)/shard_map/ppermute | solution.py:375
  2.1 0.7 %collective-permute-start.1 = (f32[16,16,128]{2,1,0:T(8,128)S(1)}, f32[16,16,128]{2,1,0:T(8,128)S(1)}, u32[]{:S(2)}, u32[]{:S(2)}) collective-permute-start(f32[16,16,128]{2,1,0:T(8,128)S(1)} %get-tuple-element.22), channel_id=1, source_target_pairs={{0,0},{1,2},{2,1},{3,3},{4,4},{5,6},{6,5},{7,7},{8,8},{9,10},{10,9... | collective-permute-start | bytes 393224 | tf_op jit(solution)/shard_map/ppermute | solution.py:376
  2.7 2.1 %shard_map.57 = (f32[16,8,8,128]{3,2,1,0:T(8,128)S(1)}, f32[17,8,128]{2,1,0:T(8,128)S(1)}, f32[17,8,128]{2,1,0:T(8,128)S(1)}, f32[17,8,128]{2,1,0:T(8,128)S(1)}, f32[17,8,128]{2,1,0:T(8,128)S(1)}) custom-call(s32[1]{0:T(128)} %bitcast.dom_ref, s32[1]{0:T(128)} %bitcast.1.me_ref, f32[4,8,128]{2,1,0:T(8,128)S(1)} %get-tuple-element.19.weight_ref, ...), custom_call_target="tpu_custom_call" | custom-call | flops 5242880 | bytes 1589256 | tf_op jit(solution)/shard_map/pallas_call | solution.py:335
  4.8 2.6 %collective-permute-start.9 = (f32[17,8,128]{2,1,0:T(8,128)S(1)}, f32[17,8,128]{2,1,0:T(8,128)S(1)}, u32[]{:S(2)}, u32[]{:S(2)}) collective-permute-start(f32[17,8,128]{2,1,0:T(8,128)S(1)} %get-tuple-element.28), channel_id=1, source_target_pairs={{0,4},{1,9},{2,6},{3,11},{4,0},{5,13},{6,2},{7,15},{8,12},{9,1},{1... | collective-permute-start | bytes 208904 | tf_op jit(solution)/shard_map/ppermute | solution.py:406
  7.4 1.6 %collective-permute-start.10 = (f32[17,8,128]{2,1,0:T(8,128)S(1)}, f32[17,8,128]{2,1,0:T(8,128)S(1)}, u32[]{:S(2)}, u32[]{:S(2)}) collective-permute-start(f32[17,8,128]{2,1,0:T(8,128)S(1)} %get-tuple-element.29), channel_id=1, source_target_pairs={{0,8},{1,5},{2,10},{3,7},{4,12},{5,1},{6,14},{7,3},{8,0},{9,13},{1... | collective-permute-start | bytes 208904 | tf_op jit(solution)/shard_map/ppermute | solution.py:406
  8.9 0.0 collective-permute-start.11
  8.9 0.0 collective-permute-done.refs_3_
  9.0 0.0 collective-permute-done.1.refs_4_
  9.0 0.9 %shard_map.59 = (f32[17,8,128]{2,1,0:T(8,128)S(1)}, f32[17,8,128]{2,1,0:T(8,128)S(1)}, f32[17,8,128]{2,1,0:T(8,128)S(1)}, f32[17,8,128]{2,1,0:T(8,128)S(1)}) custom-call(s32[1]{0:T(128)} %bitcast.dom_ref, s32[1]{0:T(128)} %bitcast.1.me_ref, f32[4,8,128]{2,1,0:T(8,128)S(1)} %get-tuple-element.19.weight_ref, f32[8,16,8,128]{3,2,1,0:T(8,128)S(1)} %bitcast.16, ...), custom_call_target="tpu_custom_call" | custom-call | flops 2621440 | bytes 2375688 | tf_op jit(solution)/shard_map/pallas_call | solution.py:335
  9.9 2.0 %collective-permute-start.2 = (f32[17,8,128]{2,1,0:T(8,128)S(1)}, f32[17,8,128]{2,1,0:T(8,128)S(1)}, u32[]{:S(2)}, u32[]{:S(2)}) collective-permute-start(f32[17,8,128]{2,1,0:T(8,128)S(1)} %get-tuple-element.24), channel_id=1, source_target_pairs={{0,4},{1,9},{2,6},{3,11},{4,0},{5,13},{6,2},{7,15},{8,12},{9,1},{1... | collective-permute-start | bytes 208904 | tf_op jit(solution)/shard_map/ppermute | solution.py:406
  11.9 1.6 %collective-permute-start.3 = (f32[17,8,128]{2,1,0:T(8,128)S(1)}, f32[17,8,128]{2,1,0:T(8,128)S(1)}, u32[]{:S(2)}, u32[]{:S(2)}) collective-permute-start(f32[17,8,128]{2,1,0:T(8,128)S(1)} %get-tuple-element.25), channel_id=1, source_target_pairs={{0,8},{1,5},{2,10},{3,7},{4,12},{5,1},{6,14},{7,3},{8,0},{9,13},{1... | collective-permute-start | bytes 208904 | tf_op jit(solution)/shard_map/ppermute | solution.py:406
  13.4 0.0 collective-permute-done.9.refs_1_
  13.4 0.0 collective-permute-start.4
  13.5 0.0 collective-permute-done.10.refs_2_
  13.5 0.8 %collective-permute-done.11.refs_3_ = f32[17,8,128]{2,1,0:T(8,128)S(1)} collective-permute-done((f32[17,8,128]{2,1,0:T(8,128)S(1)}, f32[17,8,128]{2,1,0:T(8,128)S(1)}, u32[]{:S(2)}, u32[]{:S(2)}) %collective-permute-start.11) | collective-permute-done | bytes 69664 | tf_op jit(solution)/shard_map/ppermute | solution.py:406
  14.2 2.6 %collective-permute-start.12 = (f32[17,8,128]{2,1,0:T(8,128)S(1)}, f32[17,8,128]{2,1,0:T(8,128)S(1)}, u32[]{:S(2)}, u32[]{:S(2)}) collective-permute-start(f32[17,8,128]{2,1,0:T(8,128)S(1)} %shard_map.62.refs_0_), channel_id=1, source_target_pairs={{0,16},{4,20},{8,24},{12,28},{16,0},{20,4},{24,8},{28,12},{1,17},{... | collective-permute-start | bytes 208904 | tf_op jit(solution)/shard_map/ppermute | solution.py:413
  16.9 0.0 collective-permute-done.2.refs_1_
  16.9 0.0 collective-permute-done.3.refs_2_
  16.9 2.1 %collective-permute-done.4.refs_3_ = f32[17,8,128]{2,1,0:T(8,128)S(1)} collective-permute-done((f32[17,8,128]{2,1,0:T(8,128)S(1)}, f32[17,8,128]{2,1,0:T(8,128)S(1)}, u32[]{:S(2)}, u32[]{:S(2)}) %collective-permute-start.4) | collective-permute-done | bytes 69664 | tf_op jit(solution)/shard_map/ppermute | solution.py:406
  19.0 2.6 %collective-permute-start.5 = (f32[17,8,128]{2,1,0:T(8,128)S(1)}, f32[17,8,128]{2,1,0:T(8,128)S(1)}, u32[]{:S(2)}, u32[]{:S(2)}) collective-permute-start(f32[17,8,128]{2,1,0:T(8,128)S(1)} %shard_map.60.refs_0_), channel_id=1, source_target_pairs={{0,16},{4,20},{8,24},{12,28},{16,0},{20,4},{24,8},{28,12},{1,17},{... | collective-permute-start | bytes 208904 | tf_op jit(solution)/shard_map/ppermute | solution.py:413
  21.6 0.0 collective-permute-done.12.refs_1_
  21.7 1.6 %collective-permute-start.15 = (f32[17,8,128]{2,1,0:T(8,128)S(1)}, f32[17,8,128]{2,1,0:T(8,128)S(1)}, u32[]{:S(2)}, u32[]{:S(2)}) collective-permute-start(f32[17,8,128]{2,1,0:T(8,128)S(1)} %shard_map.63.refs_0_.refs_4_), channel_id=1, source_target_pairs={{0,12},{1,13},{2,14},{3,15},{4,8},{5,9},{6,10},{7,11},{8,4},{9,5},... | collective-permute-start | bytes 208904 | tf_op jit(solution)/shard_map/ppermute | solution.py:406
  23.2 0.6 %collective-permute-start.14 = (f32[17,8,128]{2,1,0:T(8,128)S(1)}, f32[17,8,128]{2,1,0:T(8,128)S(1)}, u32[]{:S(2)}, u32[]{:S(2)}) collective-permute-start(f32[17,8,128]{2,1,0:T(8,128)S(1)} %shard_map.63.refs_0_.refs_4_), channel_id=1, source_target_pairs={{0,8},{1,5},{2,10},{3,7},{4,12},{5,1},{6,14},{7,3},{8,0},{9,13},{1... | collective-permute-start | bytes 208904 | tf_op jit(solution)/shard_map/ppermute | solution.py:406
  23.8 1.4 %collective-permute-start.13 = (f32[17,8,128]{2,1,0:T(8,128)S(1)}, f32[17,8,128]{2,1,0:T(8,128)S(1)}, u32[]{:S(2)}, u32[]{:S(2)}) collective-permute-start(f32[17,8,128]{2,1,0:T(8,128)S(1)} %shard_map.63.refs_0_.refs_4_), channel_id=1, source_target_pairs={{0,4},{1,9},{2,6},{3,11},{4,0},{5,13},{6,2},{7,15},{8,12},{9,1},{1... | collective-permute-start | bytes 208904 | tf_op jit(solution)/shard_map/ppermute | solution.py:406
  25.2 0.6 %collective-permute-done.5.refs_1_ = f32[17,8,128]{2,1,0:T(8,128)S(1)} collective-permute-done((f32[17,8,128]{2,1,0:T(8,128)S(1)}, f32[17,8,128]{2,1,0:T(8,128)S(1)}, u32[]{:S(2)}, u32[]{:S(2)}) %collective-permute-start.5) | collective-permute-done | bytes 69664 | tf_op jit(solution)/shard_map/ppermute | solution.py:413
  25.9 0.9 %collective-permute-start.8 = (f32[17,8,128]{2,1,0:T(8,128)S(1)}, f32[17,8,128]{2,1,0:T(8,128)S(1)}, u32[]{:S(2)}, u32[]{:S(2)}) collective-permute-start(f32[17,8,128]{2,1,0:T(8,128)S(1)} %shard_map.61.refs_0_), channel_id=1, source_target_pairs={{0,12},{1,13},{2,14},{3,15},{4,8},{5,9},{6,10},{7,11},{8,4},{9,5},... | collective-permute-start | bytes 208904 | tf_op jit(solution)/shard_map/ppermute | solution.py:406
  26.8 1.8 %collective-permute-start.7 = (f32[17,8,128]{2,1,0:T(8,128)S(1)}, f32[17,8,128]{2,1,0:T(8,128)S(1)}, u32[]{:S(2)}, u32[]{:S(2)}) collective-permute-start(f32[17,8,128]{2,1,0:T(8,128)S(1)} %shard_map.61.refs_0_), channel_id=1, source_target_pairs={{0,8},{1,5},{2,10},{3,7},{4,12},{5,1},{6,14},{7,3},{8,0},{9,13},{1... | collective-permute-start | bytes 208904 | tf_op jit(solution)/shard_map/ppermute | solution.py:406
  28.6 0.0 collective-permute-done.15.refs_3_.refs_7_
  28.6 0.8 %collective-permute-start.6 = (f32[17,8,128]{2,1,0:T(8,128)S(1)}, f32[17,8,128]{2,1,0:T(8,128)S(1)}, u32[]{:S(2)}, u32[]{:S(2)}) collective-permute-start(f32[17,8,128]{2,1,0:T(8,128)S(1)} %shard_map.61.refs_0_), channel_id=1, source_target_pairs={{0,4},{1,9},{2,6},{3,11},{4,0},{5,13},{6,2},{7,15},{8,12},{9,1},{1... | collective-permute-start | bytes 208904 | tf_op jit(solution)/shard_map/ppermute | solution.py:406
  29.4 0.0 collective-permute-done.14.refs_2_.refs_6_
  29.4 0.0 collective-permute-done.13.refs_1_.refs_5_
  29.4 1.0 %shard_map.64.refs_8_ = f32[8,16,8,128]{3,2,1,0:T(8,128)} custom-call(s32[1]{0:T(128)} %bitcast.dom_ref, s32[1]{0:T(128)} %bitcast.1.me_ref, f32[3,8,128]{2,1,0:T(8,128)S(1)} %get-tuple-element.18.keep_ref, f32[17,8,128]{2,1,0:T(8,128)S(1)} %shard_map.63.refs_0_.refs_4_, f32[17,8,128]{2,1,0:T(8,128)S(1)} %collective-permute-done.13.refs_1_.refs_5_, ...), custom_call_target="tpu_custom_call" | custom-call | bytes 290824 | tf_op jit(solution)/shard_map/pallas_call | solution.py:335
  30.4 1.1 %collective-permute-done.8.refs_3_ = f32[17,8,128]{2,1,0:T(8,128)S(1)} collective-permute-done((f32[17,8,128]{2,1,0:T(8,128)S(1)}, f32[17,8,128]{2,1,0:T(8,128)S(1)}, u32[]{:S(2)}, u32[]{:S(2)}) %collective-permute-start.8) | collective-permute-done | bytes 69664 | tf_op jit(solution)/shard_map/ppermute | solution.py:406
  31.5 0.9 %collective-permute-done.7.refs_2_ = f32[17,8,128]{2,1,0:T(8,128)S(1)} collective-permute-done((f32[17,8,128]{2,1,0:T(8,128)S(1)}, f32[17,8,128]{2,1,0:T(8,128)S(1)}, u32[]{:S(2)}, u32[]{:S(2)}) %collective-permute-start.7) | collective-permute-done | bytes 69664 | tf_op jit(solution)/shard_map/ppermute | solution.py:406
  32.4 0.5 %collective-permute-done.6.refs_1_ = f32[17,8,128]{2,1,0:T(8,128)S(1)} collective-permute-done((f32[17,8,128]{2,1,0:T(8,128)S(1)}, f32[17,8,128]{2,1,0:T(8,128)S(1)}, u32[]{:S(2)}, u32[]{:S(2)}) %collective-permute-start.6) | collective-permute-done | bytes 69664 | tf_op jit(solution)/shard_map/ppermute | solution.py:406
  32.9 1.0 %shard_map.65 = f32[8,16,8,128]{3,2,1,0:T(8,128)} custom-call(s32[1]{0:T(128)} %bitcast.dom_ref, s32[1]{0:T(128)} %bitcast.1.me_ref, f32[3,8,128]{2,1,0:T(8,128)S(1)} %get-tuple-element.18.keep_ref, f32[17,8,128]{2,1,0:T(8,128)S(1)} %shard_map.61.refs_0_, f32[17,8,128]{2,1,0:T(8,128)S(1)} %collective-permute-done.6.refs_1_, ...), custom_call_target="tpu_custom_call", output_to_operand_aliasing={{}: (11, {})} | custom-call | bytes 1093640 | tf_op jit(solution)/shard_map/pallas_call | solution.py:335
  (6 shorter events, 0.1 us)
Async XLA Ops:
  0.0 1.4 %copy-start = (f32[1,64,2048]{2,1,0:T(8,128)S(1)}, f32[1,64,2048]{2,1,0:T(8,128)}, u32[]{:S(2)}) copy-start(f32[1,64,2048]{2,1,0:T(8,128)} %param.5) | copy-start | bytes 1572868
  0.0 1.5 %copy-start.1 = (f32[1,64,2048]{2,1,0:T(8,128)S(1)}, f32[1,64,2048]{2,1,0:T(8,128)}, u32[]{:S(2)}) copy-start(f32[1,64,2048]{2,1,0:T(8,128)} %param.6) | copy-start | bytes 1572868
  0.0 1.5 %copy-start.2 = (f32[1,64,2048]{2,1,0:T(8,128)S(1)}, f32[1,64,2048]{2,1,0:T(8,128)}, u32[]{:S(2)}) copy-start(f32[1,64,2048]{2,1,0:T(8,128)} %param.7) | copy-start | bytes 1572868
  1.5 7.4 %collective-permute-start = (f32[16,16,128]{2,1,0:T(8,128)S(1)}, f32[16,16,128]{2,1,0:T(8,128)S(1)}, u32[]{:S(2)}, u32[]{:S(2)}) collective-permute-start(f32[16,16,128]{2,1,0:T(8,128)S(1)} %get-tuple-element.21), channel_id=1, source_target_pairs={{0,1},{1,0},{2,3},{3,2},{4,5},{5,4},{6,7},{7,6},{8,9},{9,8},{10,11... | collective-permute-start | bytes 393224 | tf_op jit(solution)/shard_map/ppermute | solution.py:375
  2.1 6.9 %collective-permute-start.1 = (f32[16,16,128]{2,1,0:T(8,128)S(1)}, f32[16,16,128]{2,1,0:T(8,128)S(1)}, u32[]{:S(2)}, u32[]{:S(2)}) collective-permute-start(f32[16,16,128]{2,1,0:T(8,128)S(1)} %get-tuple-element.22), channel_id=1, source_target_pairs={{0,0},{1,2},{2,1},{3,3},{4,4},{5,6},{6,5},{7,7},{8,8},{9,10},{10,9... | collective-permute-start | bytes 393224 | tf_op jit(solution)/shard_map/ppermute | solution.py:376
  4.8 8.6 %collective-permute-start.9 = (f32[17,8,128]{2,1,0:T(8,128)S(1)}, f32[17,8,128]{2,1,0:T(8,128)S(1)}, u32[]{:S(2)}, u32[]{:S(2)}) collective-permute-start(f32[17,8,128]{2,1,0:T(8,128)S(1)} %get-tuple-element.28), channel_id=1, source_target_pairs={{0,4},{1,9},{2,6},{3,11},{4,0},{5,13},{6,2},{7,15},{8,12},{9,1},{1... | collective-permute-start | bytes 208904 | tf_op jit(solution)/shard_map/ppermute | solution.py:406
  7.4 6.1 %collective-permute-start.10 = (f32[17,8,128]{2,1,0:T(8,128)S(1)}, f32[17,8,128]{2,1,0:T(8,128)S(1)}, u32[]{:S(2)}, u32[]{:S(2)}) collective-permute-start(f32[17,8,128]{2,1,0:T(8,128)S(1)} %get-tuple-element.29), channel_id=1, source_target_pairs={{0,8},{1,5},{2,10},{3,7},{4,12},{5,1},{6,14},{7,3},{8,0},{9,13},{1... | collective-permute-start | bytes 208904 | tf_op jit(solution)/shard_map/ppermute | solution.py:406
  8.9 5.3 %collective-permute-start.11 = (f32[17,8,128]{2,1,0:T(8,128)S(1)}, f32[17,8,128]{2,1,0:T(8,128)S(1)}, u32[]{:S(2)}, u32[]{:S(2)}) collective-permute-start(f32[17,8,128]{2,1,0:T(8,128)S(1)} %get-tuple-element.30), channel_id=1, source_target_pairs={{0,12},{1,13},{2,14},{3,15},{4,8},{5,9},{6,10},{7,11},{8,4},{9,5},... | collective-permute-start | bytes 208904 | tf_op jit(solution)/shard_map/ppermute | solution.py:406
  9.9 7.0 %collective-permute-start.2 = (f32[17,8,128]{2,1,0:T(8,128)S(1)}, f32[17,8,128]{2,1,0:T(8,128)S(1)}, u32[]{:S(2)}, u32[]{:S(2)}) collective-permute-start(f32[17,8,128]{2,1,0:T(8,128)S(1)} %get-tuple-element.24), channel_id=1, source_target_pairs={{0,4},{1,9},{2,6},{3,11},{4,0},{5,13},{6,2},{7,15},{8,12},{9,1},{1... | collective-permute-start | bytes 208904 | tf_op jit(solution)/shard_map/ppermute | solution.py:406
  11.9 5.0 %collective-permute-start.3 = (f32[17,8,128]{2,1,0:T(8,128)S(1)}, f32[17,8,128]{2,1,0:T(8,128)S(1)}, u32[]{:S(2)}, u32[]{:S(2)}) collective-permute-start(f32[17,8,128]{2,1,0:T(8,128)S(1)} %get-tuple-element.25), channel_id=1, source_target_pairs={{0,8},{1,5},{2,10},{3,7},{4,12},{5,1},{6,14},{7,3},{8,0},{9,13},{1... | collective-permute-start | bytes 208904 | tf_op jit(solution)/shard_map/ppermute | solution.py:406
  13.4 5.5 %collective-permute-start.4 = (f32[17,8,128]{2,1,0:T(8,128)S(1)}, f32[17,8,128]{2,1,0:T(8,128)S(1)}, u32[]{:S(2)}, u32[]{:S(2)}) collective-permute-start(f32[17,8,128]{2,1,0:T(8,128)S(1)} %get-tuple-element.26), channel_id=1, source_target_pairs={{0,12},{1,13},{2,14},{3,15},{4,8},{5,9},{6,10},{7,11},{8,4},{9,5},... | collective-permute-start | bytes 208904 | tf_op jit(solution)/shard_map/ppermute | solution.py:406
  14.2 7.4 %collective-permute-start.12 = (f32[17,8,128]{2,1,0:T(8,128)S(1)}, f32[17,8,128]{2,1,0:T(8,128)S(1)}, u32[]{:S(2)}, u32[]{:S(2)}) collective-permute-start(f32[17,8,128]{2,1,0:T(8,128)S(1)} %shard_map.62.refs_0_), channel_id=1, source_target_pairs={{0,16},{4,20},{8,24},{12,28},{16,0},{20,4},{24,8},{28,12},{1,17},{... | collective-permute-start | bytes 208904 | tf_op jit(solution)/shard_map/ppermute | solution.py:413
  19.0 6.9 %collective-permute-start.5 = (f32[17,8,128]{2,1,0:T(8,128)S(1)}, f32[17,8,128]{2,1,0:T(8,128)S(1)}, u32[]{:S(2)}, u32[]{:S(2)}) collective-permute-start(f32[17,8,128]{2,1,0:T(8,128)S(1)} %shard_map.60.refs_0_), channel_id=1, source_target_pairs={{0,16},{4,20},{8,24},{12,28},{16,0},{20,4},{24,8},{28,12},{1,17},{... | collective-permute-start | bytes 208904 | tf_op jit(solution)/shard_map/ppermute | solution.py:413
  21.7 7.0 %collective-permute-start.15 = (f32[17,8,128]{2,1,0:T(8,128)S(1)}, f32[17,8,128]{2,1,0:T(8,128)S(1)}, u32[]{:S(2)}, u32[]{:S(2)}) collective-permute-start(f32[17,8,128]{2,1,0:T(8,128)S(1)} %shard_map.63.refs_0_.refs_4_), channel_id=1, source_target_pairs={{0,12},{1,13},{2,14},{3,15},{4,8},{5,9},{6,10},{7,11},{8,4},{9,5},... | collective-permute-start | bytes 208904 | tf_op jit(solution)/shard_map/ppermute | solution.py:406
  23.2 6.2 %collective-permute-start.14 = (f32[17,8,128]{2,1,0:T(8,128)S(1)}, f32[17,8,128]{2,1,0:T(8,128)S(1)}, u32[]{:S(2)}, u32[]{:S(2)}) collective-permute-start(f32[17,8,128]{2,1,0:T(8,128)S(1)} %shard_map.63.refs_0_.refs_4_), channel_id=1, source_target_pairs={{0,8},{1,5},{2,10},{3,7},{4,12},{5,1},{6,14},{7,3},{8,0},{9,13},{1... | collective-permute-start | bytes 208904 | tf_op jit(solution)/shard_map/ppermute | solution.py:406
  23.8 5.6 %collective-permute-start.13 = (f32[17,8,128]{2,1,0:T(8,128)S(1)}, f32[17,8,128]{2,1,0:T(8,128)S(1)}, u32[]{:S(2)}, u32[]{:S(2)}) collective-permute-start(f32[17,8,128]{2,1,0:T(8,128)S(1)} %shard_map.63.refs_0_.refs_4_), channel_id=1, source_target_pairs={{0,4},{1,9},{2,6},{3,11},{4,0},{5,13},{6,2},{7,15},{8,12},{9,1},{1... | collective-permute-start | bytes 208904 | tf_op jit(solution)/shard_map/ppermute | solution.py:406
  25.9 5.6 %collective-permute-start.8 = (f32[17,8,128]{2,1,0:T(8,128)S(1)}, f32[17,8,128]{2,1,0:T(8,128)S(1)}, u32[]{:S(2)}, u32[]{:S(2)}) collective-permute-start(f32[17,8,128]{2,1,0:T(8,128)S(1)} %shard_map.61.refs_0_), channel_id=1, source_target_pairs={{0,12},{1,13},{2,14},{3,15},{4,8},{5,9},{6,10},{7,11},{8,4},{9,5},... | collective-permute-start | bytes 208904 | tf_op jit(solution)/shard_map/ppermute | solution.py:406
  26.8 5.6 %collective-permute-start.7 = (f32[17,8,128]{2,1,0:T(8,128)S(1)}, f32[17,8,128]{2,1,0:T(8,128)S(1)}, u32[]{:S(2)}, u32[]{:S(2)}) collective-permute-start(f32[17,8,128]{2,1,0:T(8,128)S(1)} %shard_map.61.refs_0_), channel_id=1, source_target_pairs={{0,8},{1,5},{2,10},{3,7},{4,12},{5,1},{6,14},{7,3},{8,0},{9,13},{1... | collective-permute-start | bytes 208904 | tf_op jit(solution)/shard_map/ppermute | solution.py:406
  28.6 4.3 %collective-permute-start.6 = (f32[17,8,128]{2,1,0:T(8,128)S(1)}, f32[17,8,128]{2,1,0:T(8,128)S(1)}, u32[]{:S(2)}, u32[]{:S(2)}) collective-permute-start(f32[17,8,128]{2,1,0:T(8,128)S(1)} %shard_map.61.refs_0_), channel_id=1, source_target_pairs={{0,4},{1,9},{2,6},{3,11},{4,0},{5,13},{6,2},{7,15},{8,12},{9,1},{1... | collective-permute-start | bytes 208904 | tf_op jit(solution)/shard_map/ppermute | solution.py:406

commit v18 on v17

--- a/solution.py
+++ b/solution.py
@@ -16,6 +16,7 @@
 UNROLL = 16
 VMEM_LIMIT = 40 * 1024 * 1024
 LOAD_FLOPS = 4000
+MIDDLE_FLOPS = 2000
 
 
 def tiles_of(block):
@@ -154,7 +155,7 @@
 
 
 def middle_tiles(many):
-    return list(range(many // 4, many - many // 4)) if many >= 4 else []
+    return list(range(1, many - 1)) if many >= 4 else []
 
 
 def outer_tiles(many):
@@ -214,7 +215,8 @@
     dom = dom_ref[0]
     odd = dom % 2 == 1
     diff_ref, drift_ref, state_ref, near_ref, far_ref, *rest = refs
-    out_refs, (scratch, slab, state_a, state_b, *coefs) = rest[:-8], rest[-8:]
+    kept_ref, sent_ref, scratch, slab, state_a, state_b, *coefs = rest
+    out_refs = kept_ref.at[0], sent_ref.at[0], kept_ref.at[1], sent_ref.at[1]
 
     def stage(j):
         far, near = far_ref[j], near_ref[j]
@@ -274,8 +276,17 @@
     out_ref[...] = total
 
 
+def swapped_kernel(mine_ref, theirs_ref, out_ref):
+    for k in range(2):
+        out_ref[k] = mine_ref[k] + theirs_ref[1 - k]
+
+
 def nodal_kernel(per_chunk, tiles, dom_ref, me_ref, keep_ref, *refs):
-    totals, middles, (out_ref, values, sems) = refs[:SQUARE], refs[SQUARE:-3], refs[-3:]
+    out_ref, values, sems = refs[-3:]
+    if refs[0].ndim == 4:
+        totals, middles = [refs[k % 2].at[k // 2] for k in range(SQUARE)], refs[2:]
+    else:
+        totals, middles = refs[:SQUARE], ()
     count = len(tiles)
     fine, mid, low = (keep_ref[k, 0:count] for k in range(3))
     place = lax.broadcasted_iota(jnp.int32, (count, LANES), 0)
@@ -389,9 +400,9 @@
         [vmem(*pieces)] + [vmem(strips + 2, *place[1:])] * 2 + [vmem(*place)] * 4,
         flops=40 * rows * cols,
     )
-    outside = call(
+    kept, sent = call(
         functools.partial(edge_kernel, per_chunk, doms),
-        [chunk(outer)] * SQUARE,
+        [(2, *chunk(outer))] * 2,
         (dom, me, weight, *tiles, state, near, far),
         2,
         [vmem(*pieces), vmem(3, strips, SLAB, LANES)]
@@ -405,22 +416,19 @@
         pairs = [(g * doms + d, (g ^ partners(d % 2)[meet]) * doms + d) for g, d in devices]
         return lax.ppermute(array, ("grp", "dom"), pairs)
 
-    def over_grids(own, *others):
-        theirs = [swap(array, meet) for meet, array in enumerate(others, 1)]
-        (total,) = call(sum_kernel, [own.shape], (own, *theirs))
+    def add(kernel, *parts):
+        return call(kernel, [parts[0].shape], parts)[0]
+
+    def over_squares(total):
         apart = SQUARE
         while apart < grids:
             other = lax.ppermute(total, "grp", [(g, g ^ apart) for g in range(grids)])
-            (total,) = call(sum_kernel, [own.shape], (total, other))
+            total = add(sum_kernel, total, other)
             apart *= 2
-        return [total] + [swap(total, meet) for meet in range(1, SQUARE)]
-
-    nodal, totals = None, []
-    for some, weighted in ((middle, inside), (outer, outside)):
-        if not some:
-            continue
-        totals = over_grids(*weighted) + totals
-        (nodal,) = call(
+        return total
+
+    def nodal_values(some, totals, onto, flops=0):
+        return call(
             functools.partial(nodal_kernel, per_chunk, some),
             [(many, strips, TILE, LANES)],
             (dom, me, keep, *totals),
@@ -429,9 +437,21 @@
                 vmem(SQUARE, len(some), per_chunk, TILE, LANES),
                 pltpu.SemaphoreType.DMA((SQUARE, len(some))),
             ],
+            flops=flops,
             out_space=pl.ANY,
-            onto=nodal,
-        )
+            onto=onto,
+        )[0]
+
+    nodal, inner_totals = None, []
+    if middle:
+        own, *others = inside
+        theirs = [swap(array, meet) for meet, array in enumerate(others, 1)]
+        total = over_squares(add(sum_kernel, own, *theirs))
+        inner_totals = [total] + [swap(total, meet) for meet in range(1, SQUARE)]
+        nodal = nodal_values(middle, inner_totals, None, MIDDLE_FLOPS * rows * cols)
+    kept = add(sum_kernel, kept, swap(sent, 1))
+    kept = over_squares(add(swapped_kernel, kept, swap(kept, 2)))
+    nodal = nodal_values(outer, [kept, swap(kept, 1), *inner_totals], nodal)
     return block_of(nodal)[None]
 
 

time: 34.1 us -> 36.8 us (1.079)
  the two profiles are of different devices: /device:TPU:0 before, /device:TPU:4 now
where the time goes in v18:
time: 36.8 us; the launch traced here: 36.7 us
  starting transfers between devices  15.1 us (41%)
  waiting for transfers between devices  14.9 us (40%)
  Pallas kernels  5.1 us (14%)
  between operations  1.57 us (4%)
    ppermute x9, waiting for transfers between devices, swap(): return lax.ppermute(array, ('grp', 'dom'), pairs)  12.3 us
    ppermute x9, starting transfers between devices, swap(): return lax.ppermute(array, ('grp', 'dom'), pairs)  9.37 us
    pallas_call x12, Pallas kernels, call(): pl.pallas_call(kernel, out_shape=[jax.ShapeDtypeStruct(shape, jnp.float32...  5.1 us
    ppermute x2, starting transfers between devices, over_squares(): other = lax.ppermute(total, 'grp', [(g, g ^ apart) for g in range(grids)])  3.75 us
    ppermute x2, waiting for transfers between devices, over_squares(): other = lax.ppermute(total, 'grp', [(g, g ^ apart) for g in range(grids)])  2.51 us
    ppermute x1, starting transfers between devices, on_device(): far = lax.ppermute(far, 'dom', far_pairs)  1.92 us
  transfers between devices with their start and end apart: 13, of which 7 were waited for; matrix products, arithmetic and copies ran while one was open for 0% of the time, Pallas kernels for 12%

profile of v18, /device:TPU:4, one launch (start us, length us, event | category | flops | bytes accessed | tf_op | source)
XLA Modules:
  0.0 36.7 jit_solution(14137659896295421611)
XLA Ops:
  0.0 0.0 copy-start
  0.0 0.0 copy-start.1
  0.0 0.0 copy-start.2
  1.4 0.0 copy-done
  1.5 0.0 copy-done.1
  1.5 0.0 copy-done.2
  1.5 0.1 shard_map.58
  1.5 0.1 collective-permute-start
  1.6 1.9 %collective-permute-start.1 = (f32[16,16,128]{2,1,0:T(8,128)S(1)}, f32[16,16,128]{2,1,0:T(8,128)S(1)}, u32[]{:S(2)}, u32[]{:S(2)}) collective-permute-start(f32[16,16,128]{2,1,0:T(8,128)S(1)} %get-tuple-element.20), channel_id=1, source_target_pairs={{0,0},{1,2},{2,1},{3,3},{4,4},{5,6},{6,5},{7,7},{8,8},{9,10},{10,9... | collective-permute-start | bytes 393224 | tf_op jit(solution)/shard_map/ppermute | solution.py:387
  3.6 2.1 %shard_map.57 = (f32[16,8,8,128]{3,2,1,0:T(8,128)S(1)}, f32[25,8,128]{2,1,0:T(8,128)S(1)}, f32[25,8,128]{2,1,0:T(8,128)S(1)}, f32[25,8,128]{2,1,0:T(8,128)S(1)}, f32[25,8,128]{2,1,0:T(8,128)S(1)}) custom-call(s32[1]{0:T(128)} %bitcast.dom_ref, s32[1]{0:T(128)} %bitcast.1.me_ref, f32[4,8,128]{2,1,0:T(8,128)S(1)} %get-tuple-element.17.weight_ref, ...), custom_call_target="tpu_custom_call" | custom-call | flops 5242880 | bytes 1589256 | tf_op jit(solution)/shard_map/pallas_call | solution.py:346
  5.6 2.1 %collective-permute-start.6 = (f32[25,8,128]{2,1,0:T(8,128)S(1)}, f32[25,8,128]{2,1,0:T(8,128)S(1)}, u32[]{:S(2)}, u32[]{:S(2)}) collective-permute-start(f32[25,8,128]{2,1,0:T(8,128)S(1)} %get-tuple-element.24), channel_id=1, source_target_pairs={{0,4},{1,9},{2,6},{3,11},{4,0},{5,13},{6,2},{7,15},{8,12},{9,1},{1... | collective-permute-start | bytes 307208 | tf_op jit(solution)/shard_map/ppermute | solution.py:417
  7.8 1.6 %collective-permute-start.7 = (f32[25,8,128]{2,1,0:T(8,128)S(1)}, f32[25,8,128]{2,1,0:T(8,128)S(1)}, u32[]{:S(2)}, u32[]{:S(2)}) collective-permute-start(f32[25,8,128]{2,1,0:T(8,128)S(1)} %get-tuple-element.25), channel_id=1, source_target_pairs={{0,8},{1,5},{2,10},{3,7},{4,12},{5,1},{6,14},{7,3},{8,0},{9,13},{1... | collective-permute-start | bytes 307208 | tf_op jit(solution)/shard_map/ppermute | solution.py:417
  9.3 0.0 collective-permute-start.8
  9.3 0.0 collective-permute-done.refs_3_
  9.3 0.0 collective-permute-done.1.refs_4_
  9.3 0.9 %shard_map.59 = (f32[2,9,8,128]{3,2,1,0:T(8,128)S(1)}, f32[2,9,8,128]{3,2,1,0:T(8,128)S(1)}) custom-call(s32[1]{0:T(128)} %bitcast.dom_ref, s32[1]{0:T(128)} %bitcast.1.me_ref, f32[4,8,128]{2,1,0:T(8,128)S(1)} %get-tuple-element.17.weight_ref, f32[8,16,8,128]{3,2,1,0:T(8,128)S(1)} %bitcast.16, f32[8,16,8,128]{3,2,1,0:T(8,128)S(1)} %bitcast.19, ...), custom_call_target="tpu_custom_call" | custom-call | flops 2621440 | bytes 2375688 | tf_op jit(solution)/shard_map/pallas_call | solution.py:346
  10.3 2.0 %collective-permute-start.2 = (f32[2,9,8,128]{3,2,1,0:T(8,128)S(1)}, f32[2,9,8,128]{3,2,1,0:T(8,128)S(1)}, u32[]{:S(2)}, u32[]{:S(2)}) collective-permute-start(f32[2,9,8,128]{3,2,1,0:T(8,128)S(1)} %get-tuple-element.22), channel_id=1, source_target_pairs={{0,4},{1,9},{2,6},{3,11},{4,0},{5,13},{6,2},{7,15},{8,12},{9,1},{1... | collective-permute-start | bytes 221192 | tf_op jit(solution)/shard_map/ppermute | solution.py:417
  12.2 0.0 collective-permute-done.6.refs_1_
  12.2 0.8 %collective-permute-done.7.refs_2_ = f32[25,8,128]{2,1,0:T(8,128)S(1)} collective-permute-done((f32[25,8,128]{2,1,0:T(8,128)S(1)}, f32[25,8,128]{2,1,0:T(8,128)S(1)}, u32[]{:S(2)}, u32[]{:S(2)}) %collective-permute-start.7) | collective-permute-done | bytes 102432 | tf_op jit(solution)/shard_map/ppermute | solution.py:417
  13.0 2.0 %collective-permute-done.8.refs_3_ = f32[25,8,128]{2,1,0:T(8,128)S(1)} collective-permute-done((f32[25,8,128]{2,1,0:T(8,128)S(1)}, f32[25,8,128]{2,1,0:T(8,128)S(1)}, u32[]{:S(2)}, u32[]{:S(2)}) %collective-permute-start.8) | collective-permute-done | bytes 102432 | tf_op jit(solution)/shard_map/ppermute | solution.py:417
  15.1 3.7 %collective-permute-start.9 = (f32[25,8,128]{2,1,0:T(8,128)S(1)}, f32[25,8,128]{2,1,0:T(8,128)S(1)}, u32[]{:S(2)}, u32[]{:S(2)}) collective-permute-start(f32[25,8,128]{2,1,0:T(8,128)S(1)} %shard_map.63.refs_0_), channel_id=1, source_target_pairs={{0,16},{4,20},{8,24},{12,28},{16,0},{20,4},{24,8},{28,12},{1,17},{... | collective-permute-start | bytes 307208 | tf_op jit(solution)/shard_map/ppermute | solution.py:425
  18.7 0.0 collective-permute-done.2.refs_1_
  18.8 0.1 collective-permute-start.3
  18.8 6.4 %collective-permute-done.3.theirs_ref = f32[2,9,8,128]{3,2,1,0:T(8,128)S(1)} collective-permute-done((f32[2,9,8,128]{3,2,1,0:T(8,128)S(1)}, f32[2,9,8,128]{3,2,1,0:T(8,128)S(1)}, u32[]{:S(2)}, u32[]{:S(2)}) %collective-permute-start.3) | collective-permute-done | bytes 73760 | tf_op jit(solution)/shard_map/ppermute | solution.py:417
  25.2 0.1 collective-permute-start.4
  25.3 0.0 collective-permute-done.9.refs_1_
  25.4 0.8 %collective-permute-start.12 = (f32[25,8,128]{2,1,0:T(8,128)S(1)}, f32[25,8,128]{2,1,0:T(8,128)S(1)}, u32[]{:S(2)}, u32[]{:S(2)}) collective-permute-start(f32[25,8,128]{2,1,0:T(8,128)S(1)} %shard_map.64.refs_0_.refs_2_), channel_id=1, source_target_pairs={{0,12},{1,13},{2,14},{3,15},{4,8},{5,9},{6,10},{7,11},{8,4},{9,5},... | collective-permute-start | bytes 307208 | tf_op jit(solution)/shard_map/ppermute | solution.py:417
  26.1 0.5 %collective-permute-start.11 = (f32[25,8,128]{2,1,0:T(8,128)S(1)}, f32[25,8,128]{2,1,0:T(8,128)S(1)}, u32[]{:S(2)}, u32[]{:S(2)}) collective-permute-start(f32[25,8,128]{2,1,0:T(8,128)S(1)} %shard_map.64.refs_0_.refs_2_), channel_id=1, source_target_pairs={{0,8},{1,5},{2,10},{3,7},{4,12},{5,1},{6,14},{7,3},{8,0},{9,13},{1... | collective-permute-start | bytes 307208 | tf_op jit(solution)/shard_map/ppermute | solution.py:417
  26.7 2.3 %collective-permute-start.10 = (f32[25,8,128]{2,1,0:T(8,128)S(1)}, f32[25,8,128]{2,1,0:T(8,128)S(1)}, u32[]{:S(2)}, u32[]{:S(2)}) collective-permute-start(f32[25,8,128]{2,1,0:T(8,128)S(1)} %shard_map.64.refs_0_.refs_2_), channel_id=1, source_target_pairs={{0,4},{1,9},{2,6},{3,11},{4,0},{5,13},{6,2},{7,15},{8,12},{9,1},{1... | collective-permute-start | bytes 307208 | tf_op jit(solution)/shard_map/ppermute | solution.py:417
  28.9 2.5 %collective-permute-done.4.refs_1_ = f32[2,9,8,128]{3,2,1,0:T(8,128)S(1)} collective-permute-done((f32[2,9,8,128]{3,2,1,0:T(8,128)S(1)}, f32[2,9,8,128]{3,2,1,0:T(8,128)S(1)}, u32[]{:S(2)}, u32[]{:S(2)}) %collective-permute-start.4) | collective-permute-done | bytes 73760 | tf_op jit(solution)/shard_map/ppermute | solution.py:425
  31.4 0.1 collective-permute-start.5
  31.5 0.0 collective-permute-done.12.refs_3_.refs_5_
  31.5 0.1 collective-permute-done.11.refs_2_.refs_4_
  31.6 0.5 %collective-permute-done.10.refs_1_.refs_3_ = f32[25,8,128]{2,1,0:T(8,128)S(1)} collective-permute-done((f32[25,8,128]{2,1,0:T(8,128)S(1)}, f32[25,8,128]{2,1,0:T(8,128)S(1)}, u32[]{:S(2)}, u32[]{:S(2)}) %collective-permute-start.10) | collective-permute-done | bytes 102432 | tf_op jit(solution)/shard_map/ppermute | solution.py:417
  32.1 1.2 %shard_map.65.refs_6_ = f32[8,16,8,128]{3,2,1,0:T(8,128)} custom-call(s32[1]{0:T(128)} %bitcast.dom_ref, s32[1]{0:T(128)} %bitcast.1.me_ref, f32[3,8,128]{2,1,0:T(8,128)S(1)} %get-tuple-element.16.keep_ref, f32[25,8,128]{2,1,0:T(8,128)S(1)} %shard_map.64.refs_0_.refs_2_, f32[25,8,128]{2,1,0:T(8,128)S(1)} %collective-permute-done.10.refs_1_.refs_3_, ...), custom_call_target="tpu_custom_call" | custom-call | flops 262144000 | bytes 421896 | tf_op jit(solution)/shard_map/pallas_call | solution.py:346
  33.3 2.6 %collective-permute-done.5.refs_1_ = f32[2,9,8,128]{3,2,1,0:T(8,128)S(1)} collective-permute-done((f32[2,9,8,128]{3,2,1,0:T(8,128)S(1)}, f32[2,9,8,128]{3,2,1,0:T(8,128)S(1)}, u32[]{:S(2)}, u32[]{:S(2)}) %collective-permute-start.5) | collective-permute-done | bytes 73760 | tf_op jit(solution)/shard_map/ppermute | solution.py:417
  35.8 0.8 %shard_map.66 = f32[8,16,8,128]{3,2,1,0:T(8,128)} custom-call(s32[1]{0:T(128)} %bitcast.dom_ref, s32[1]{0:T(128)} %bitcast.1.me_ref, f32[3,8,128]{2,1,0:T(8,128)S(1)} %get-tuple-element.16.keep_ref, f32[2,9,8,128]{3,2,1,0:T(8,128)S(1)} %shard_map.62.refs_0_, f32[2,9,8,128]{3,2,1,0:T(8,128)S(1)} %collective-permute-done.5.refs_1_, ...), custom_call_target="tpu_custom_call", output_to_operand_aliasing={{}: (9, {})} | custom-call | bytes 1093640 | tf_op jit(solution)/shard_map/pallas_call | solution.py:346
  (7 shorter events, 0.1 us)
Async XLA Ops:
  0.0 1.5 %copy-start = (f32[1,64,2048]{2,1,0:T(8,128)S(1)}, f32[1,64,2048]{2,1,0:T(8,128)}, u32[]{:S(2)}) copy-start(f32[1,64,2048]{2,1,0:T(8,128)} %param.5) | copy-start | bytes 1572868
  0.0 1.5 %copy-start.1 = (f32[1,64,2048]{2,1,0:T(8,128)S(1)}, f32[1,64,2048]{2,1,0:T(8,128)}, u32[]{:S(2)}) copy-start(f32[1,64,2048]{2,1,0:T(8,128)} %param.6) | copy-start | bytes 1572868
  0.0 1.5 %copy-start.2 = (f32[1,64,2048]{2,1,0:T(8,128)S(1)}, f32[1,64,2048]{2,1,0:T(8,128)}, u32[]{:S(2)}) copy-start(f32[1,64,2048]{2,1,0:T(8,128)} %param.7) | copy-start | bytes 1572868
  1.5 7.8 %collective-permute-start = (f32[16,16,128]{2,1,0:T(8,128)S(1)}, f32[16,16,128]{2,1,0:T(8,128)S(1)}, u32[]{:S(2)}, u32[]{:S(2)}) collective-permute-start(f32[16,16,128]{2,1,0:T(8,128)S(1)} %get-tuple-element.19), channel_id=1, source_target_pairs={{0,1},{1,0},{2,3},{3,2},{4,5},{5,4},{6,7},{7,6},{8,9},{9,8},{10,11... | collective-permute-start | bytes 393224 | tf_op jit(solution)/shard_map/ppermute | solution.py:386
  1.6 7.7 %collective-permute-start.1 = (f32[16,16,128]{2,1,0:T(8,128)S(1)}, f32[16,16,128]{2,1,0:T(8,128)S(1)}, u32[]{:S(2)}, u32[]{:S(2)}) collective-permute-start(f32[16,16,128]{2,1,0:T(8,128)S(1)} %get-tuple-element.20), channel_id=1, source_target_pairs={{0,0},{1,2},{2,1},{3,3},{4,4},{5,6},{6,5},{7,7},{8,8},{9,10},{10,9... | collective-permute-start | bytes 393224 | tf_op jit(solution)/shard_map/ppermute | solution.py:387
  5.6 6.6 %collective-permute-start.6 = (f32[25,8,128]{2,1,0:T(8,128)S(1)}, f32[25,8,128]{2,1,0:T(8,128)S(1)}, u32[]{:S(2)}, u32[]{:S(2)}) collective-permute-start(f32[25,8,128]{2,1,0:T(8,128)S(1)} %get-tuple-element.24), channel_id=1, source_target_pairs={{0,4},{1,9},{2,6},{3,11},{4,0},{5,13},{6,2},{7,15},{8,12},{9,1},{1... | collective-permute-start | bytes 307208 | tf_op jit(solution)/shard_map/ppermute | solution.py:417
  7.8 5.3 %collective-permute-start.7 = (f32[25,8,128]{2,1,0:T(8,128)S(1)}, f32[25,8,128]{2,1,0:T(8,128)S(1)}, u32[]{:S(2)}, u32[]{:S(2)}) collective-permute-start(f32[25,8,128]{2,1,0:T(8,128)S(1)} %get-tuple-element.25), channel_id=1, source_target_pairs={{0,8},{1,5},{2,10},{3,7},{4,12},{5,1},{6,14},{7,3},{8,0},{9,13},{1... | collective-permute-start | bytes 307208 | tf_op jit(solution)/shard_map/ppermute | solution.py:417
  9.3 5.7 %collective-permute-start.8 = (f32[25,8,128]{2,1,0:T(8,128)S(1)}, f32[25,8,128]{2,1,0:T(8,128)S(1)}, u32[]{:S(2)}, u32[]{:S(2)}) collective-permute-start(f32[25,8,128]{2,1,0:T(8,128)S(1)} %get-tuple-element.26), channel_id=1, source_target_pairs={{0,12},{1,13},{2,14},{3,15},{4,8},{5,9},{6,10},{7,11},{8,4},{9,5},... | collective-permute-start | bytes 307208 | tf_op jit(solution)/shard_map/ppermute | solution.py:417
  10.3 8.5 %collective-permute-start.2 = (f32[2,9,8,128]{3,2,1,0:T(8,128)S(1)}, f32[2,9,8,128]{3,2,1,0:T(8,128)S(1)}, u32[]{:S(2)}, u32[]{:S(2)}) collective-permute-start(f32[2,9,8,128]{3,2,1,0:T(8,128)S(1)} %get-tuple-element.22), channel_id=1, source_target_pairs={{0,4},{1,9},{2,6},{3,11},{4,0},{5,13},{6,2},{7,15},{8,12},{9,1},{1... | collective-permute-start | bytes 221192 | tf_op jit(solution)/shard_map/ppermute | solution.py:417
  15.1 10.2 %collective-permute-start.9 = (f32[25,8,128]{2,1,0:T(8,128)S(1)}, f32[25,8,128]{2,1,0:T(8,128)S(1)}, u32[]{:S(2)}, u32[]{:S(2)}) collective-permute-start(f32[25,8,128]{2,1,0:T(8,128)S(1)} %shard_map.63.refs_0_), channel_id=1, source_target_pairs={{0,16},{4,20},{8,24},{12,28},{16,0},{20,4},{24,8},{28,12},{1,17},{... | collective-permute-start | bytes 307208 | tf_op jit(solution)/shard_map/ppermute | solution.py:425
  18.8 6.5 %collective-permute-start.3 = (f32[2,9,8,128]{3,2,1,0:T(8,128)S(1)}, f32[2,9,8,128]{3,2,1,0:T(8,128)S(1)}, u32[]{:S(2)}, u32[]{:S(2)}) collective-permute-start(f32[2,9,8,128]{3,2,1,0:T(8,128)S(1)} %shard_map.60.mine_ref), channel_id=1, source_target_pairs={{0,8},{1,5},{2,10},{3,7},{4,12},{5,1},{6,14},{7,3},{8,0},{9,13},{1... | collective-permute-start | bytes 221192 | tf_op jit(solution)/shard_map/ppermute | solution.py:417
  25.2 6.2 %collective-permute-start.4 = (f32[2,9,8,128]{3,2,1,0:T(8,128)S(1)}, f32[2,9,8,128]{3,2,1,0:T(8,128)S(1)}, u32[]{:S(2)}, u32[]{:S(2)}) collective-permute-start(f32[2,9,8,128]{3,2,1,0:T(8,128)S(1)} %shard_map.61.refs_0_), channel_id=1, source_target_pairs={{0,16},{4,20},{8,24},{12,28},{16,0},{20,4},{24,8},{28,12},{1,17},{... | collective-permute-start | bytes 221192 | tf_op jit(solution)/shard_map/ppermute | solution.py:425
  25.4 6.2 %collective-permute-start.12 = (f32[25,8,128]{2,1,0:T(8,128)S(1)}, f32[25,8,128]{2,1,0:T(8,128)S(1)}, u32[]{:S(2)}, u32[]{:S(2)}) collective-permute-start(f32[25,8,128]{2,1,0:T(8,128)S(1)} %shard_map.64.refs_0_.refs_2_), channel_id=1, source_target_pairs={{0,12},{1,13},{2,14},{3,15},{4,8},{5,9},{6,10},{7,11},{8,4},{9,5},... | collective-permute-start | bytes 307208 | tf_op jit(solution)/shard_map/ppermute | solution.py:417
  26.1 5.5 %collective-permute-start.11 = (f32[25,8,128]{2,1,0:T(8,128)S(1)}, f32[25,8,128]{2,1,0:T(8,128)S(1)}, u32[]{:S(2)}, u32[]{:S(2)}) collective-permute-start(f32[25,8,128]{2,1,0:T(8,128)S(1)} %shard_map.64.refs_0_.refs_2_), channel_id=1, source_target_pairs={{0,8},{1,5},{2,10},{3,7},{4,12},{5,1},{6,14},{7,3},{8,0},{9,13},{1... | collective-permute-start | bytes 307208 | tf_op jit(solution)/shard_map/ppermute | solution.py:417
  26.7 5.4 %collective-permute-start.10 = (f32[25,8,128]{2,1,0:T(8,128)S(1)}, f32[25,8,128]{2,1,0:T(8,128)S(1)}, u32[]{:S(2)}, u32[]{:S(2)}) collective-permute-start(f32[25,8,128]{2,1,0:T(8,128)S(1)} %shard_map.64.refs_0_.refs_2_), channel_id=1, source_target_pairs={{0,4},{1,9},{2,6},{3,11},{4,0},{5,13},{6,2},{7,15},{8,12},{9,1},{1... | collective-permute-start | bytes 307208 | tf_op jit(solution)/shard_map/ppermute | solution.py:417
  31.4 4.4 %collective-permute-start.5 = (f32[2,9,8,128]{3,2,1,0:T(8,128)S(1)}, f32[2,9,8,128]{3,2,1,0:T(8,128)S(1)}, u32[]{:S(2)}, u32[]{:S(2)}) collective-permute-start(f32[2,9,8,128]{3,2,1,0:T(8,128)S(1)} %shard_map.62.refs_0_), channel_id=1, source_target_pairs={{0,4},{1,9},{2,6},{3,11},{4,0},{5,13},{6,2},{7,15},{8,12},{9,1},{1... | collective-permute-start | bytes 221192 | tf_op jit(solution)/shard_map/ppermute | solution.py:417

commit v19 on v17

--- a/solution.py
+++ b/solution.py
@@ -406,7 +406,7 @@
         return lax.ppermute(array, ("grp", "dom"), pairs)
 
     def over_grids(own, *others):
-        theirs = [swap(array, meet) for meet, array in enumerate(others, 1)]
+        theirs = [swap(others[meet - 1], meet) for meet in (3, 1, 2)]
         (total,) = call(sum_kernel, [own.shape], (own, *theirs))
         apart = SQUARE
         while apart < grids:

time: 34.1 us -> 33 us (0.968)
  waiting for transfers between devices: 6.06 us -> 4.87 us
    ppermute x12, waiting for transfers between devices: 5.42 us -> 3.94 us  [swap(): return lax.ppermute(array, ('grp', 'dom'), pairs)]
  transfers between devices with their start and end apart: 16 -> 16, of which waited for: 6 -> 7; matrix products, arithmetic and copies ran while one was open for 0% -> 0% of each run, Pallas kernels for 12% -> 12%
where the time goes in v19:
time: 33 us; the launch traced here: 32.8 us
  starting transfers between devices  21.4 us (65%)
  Pallas kernels  5.03 us (15%)
  waiting for transfers between devices  4.87 us (15%)
  between operations  1.51 us (5%)
    ppermute x12, starting transfers between devices, swap(): return lax.ppermute(array, ('grp', 'dom'), pairs)  14.9 us
    ppermute x2, starting transfers between devices, over_grids(): other = lax.ppermute(total, 'grp', [(g, g ^ apart) for g in range(grids)])  5.3 us
    pallas_call x11, Pallas kernels, call(): pl.pallas_call(kernel, out_shape=[jax.ShapeDtypeStruct(shape, jnp.float32...  5.03 us
    ppermute x12, waiting for transfers between devices, swap(): return lax.ppermute(array, ('grp', 'dom'), pairs)  3.94 us
    ppermute x2, waiting for transfers between devices, over_grids(): other = lax.ppermute(total, 'grp', [(g, g ^ apart) for g in range(grids)])  0.93 us
  transfers between devices with their start and end apart: 16, of which 7 were waited for; matrix products, arithmetic and copies ran while one was open for 0% of the time, Pallas kernels for 12%

profile of v19, /device:TPU:0, one launch (start us, length us, event | category | flops | bytes accessed | tf_op | source)
XLA Modules:
  0.0 32.8 jit_solution(5010814478983511923)
XLA Ops:
  0.0 0.0 copy-start
  0.0 0.0 copy-start.1
  0.0 0.0 copy-start.2
  1.4 0.0 copy-done
  1.5 0.0 copy-done.1
  1.5 0.0 copy-done.2
  1.5 0.1 shard_map.58
  1.5 0.5 %collective-permute-start = (f32[16,16,128]{2,1,0:T(8,128)S(1)}, f32[16,16,128]{2,1,0:T(8,128)S(1)}, u32[]{:S(2)}, u32[]{:S(2)}) collective-permute-start(f32[16,16,128]{2,1,0:T(8,128)S(1)} %get-tuple-element.21), channel_id=1, source_target_pairs={{0,1},{1,0},{2,3},{3,2},{4,5},{5,4},{6,7},{7,6},{8,9},{9,8},{10,11... | collective-permute-start | bytes 393224 | tf_op jit(solution)/shard_map/ppermute | solution.py:375
  2.1 0.7 %collective-permute-start.1 = (f32[16,16,128]{2,1,0:T(8,128)S(1)}, f32[16,16,128]{2,1,0:T(8,128)S(1)}, u32[]{:S(2)}, u32[]{:S(2)}) collective-permute-start(f32[16,16,128]{2,1,0:T(8,128)S(1)} %get-tuple-element.22), channel_id=1, source_target_pairs={{0,0},{1,2},{2,1},{3,3},{4,4},{5,6},{6,5},{7,7},{8,8},{9,10},{10,9... | collective-permute-start | bytes 393224 | tf_op jit(solution)/shard_map/ppermute | solution.py:376
  2.7 2.1 %shard_map.57 = (f32[16,8,8,128]{3,2,1,0:T(8,128)S(1)}, f32[17,8,128]{2,1,0:T(8,128)S(1)}, f32[17,8,128]{2,1,0:T(8,128)S(1)}, f32[17,8,128]{2,1,0:T(8,128)S(1)}, f32[17,8,128]{2,1,0:T(8,128)S(1)}) custom-call(s32[1]{0:T(128)} %bitcast.dom_ref, s32[1]{0:T(128)} %bitcast.1.me_ref, f32[4,8,128]{2,1,0:T(8,128)S(1)} %get-tuple-element.19.weight_ref, ...), custom_call_target="tpu_custom_call" | custom-call | flops 5242880 | bytes 1589256 | tf_op jit(solution)/shard_map/pallas_call | solution.py:335
  4.8 3.6 %collective-permute-start.9 = (f32[17,8,128]{2,1,0:T(8,128)S(1)}, f32[17,8,128]{2,1,0:T(8,128)S(1)}, u32[]{:S(2)}, u32[]{:S(2)}) collective-permute-start(f32[17,8,128]{2,1,0:T(8,128)S(1)} %get-tuple-element.28), channel_id=1, source_target_pairs={{0,12},{1,13},{2,14},{3,15},{4,8},{5,9},{6,10},{7,11},{8,4},{9,5},... | collective-permute-start | bytes 208904 | tf_op jit(solution)/shard_map/ppermute | solution.py:406
  8.4 0.5 %collective-permute-start.10 = (f32[17,8,128]{2,1,0:T(8,128)S(1)}, f32[17,8,128]{2,1,0:T(8,128)S(1)}, u32[]{:S(2)}, u32[]{:S(2)}) collective-permute-start(f32[17,8,128]{2,1,0:T(8,128)S(1)} %get-tuple-element.29), channel_id=1, source_target_pairs={{0,4},{1,9},{2,6},{3,11},{4,0},{5,13},{6,2},{7,15},{8,12},{9,1},{1... | collective-permute-start | bytes 208904 | tf_op jit(solution)/shard_map/ppermute | solution.py:406
  8.9 0.1 collective-permute-start.11
  9.0 0.0 collective-permute-done.refs_3_
  9.0 0.0 collective-permute-done.1.refs_4_
  9.0 0.9 %shard_map.59 = (f32[17,8,128]{2,1,0:T(8,128)S(1)}, f32[17,8,128]{2,1,0:T(8,128)S(1)}, f32[17,8,128]{2,1,0:T(8,128)S(1)}, f32[17,8,128]{2,1,0:T(8,128)S(1)}) custom-call(s32[1]{0:T(128)} %bitcast.dom_ref, s32[1]{0:T(128)} %bitcast.1.me_ref, f32[4,8,128]{2,1,0:T(8,128)S(1)} %get-tuple-element.19.weight_ref, f32[8,16,8,128]{3,2,1,0:T(8,128)S(1)} %bitcast.16, ...), custom_call_target="tpu_custom_call" | custom-call | flops 2621440 | bytes 2375688 | tf_op jit(solution)/shard_map/pallas_call | solution.py:335
  10.0 2.9 %collective-permute-start.2 = (f32[17,8,128]{2,1,0:T(8,128)S(1)}, f32[17,8,128]{2,1,0:T(8,128)S(1)}, u32[]{:S(2)}, u32[]{:S(2)}) collective-permute-start(f32[17,8,128]{2,1,0:T(8,128)S(1)} %get-tuple-element.24), channel_id=1, source_target_pairs={{0,12},{1,13},{2,14},{3,15},{4,8},{5,9},{6,10},{7,11},{8,4},{9,5},... | collective-permute-start | bytes 208904 | tf_op jit(solution)/shard_map/ppermute | solution.py:406
  12.9 0.5 %collective-permute-start.3 = (f32[17,8,128]{2,1,0:T(8,128)S(1)}, f32[17,8,128]{2,1,0:T(8,128)S(1)}, u32[]{:S(2)}, u32[]{:S(2)}) collective-permute-start(f32[17,8,128]{2,1,0:T(8,128)S(1)} %get-tuple-element.25), channel_id=1, source_target_pairs={{0,4},{1,9},{2,6},{3,11},{4,0},{5,13},{6,2},{7,15},{8,12},{9,1},{1... | collective-permute-start | bytes 208904 | tf_op jit(solution)/shard_map/ppermute | solution.py:406
  13.4 0.0 collective-permute-done.9.refs_1_
  13.4 0.1 collective-permute-start.4
  13.5 0.0 collective-permute-done.10.refs_2_
  13.5 0.4 %collective-permute-done.11.refs_3_ = f32[17,8,128]{2,1,0:T(8,128)S(1)} collective-permute-done((f32[17,8,128]{2,1,0:T(8,128)S(1)}, f32[17,8,128]{2,1,0:T(8,128)S(1)}, u32[]{:S(2)}, u32[]{:S(2)}) %collective-permute-start.11) | collective-permute-done | bytes 69664 | tf_op jit(solution)/shard_map/ppermute | solution.py:406
  14.0 2.7 %collective-permute-start.12 = (f32[17,8,128]{2,1,0:T(8,128)S(1)}, f32[17,8,128]{2,1,0:T(8,128)S(1)}, u32[]{:S(2)}, u32[]{:S(2)}) collective-permute-start(f32[17,8,128]{2,1,0:T(8,128)S(1)} %shard_map.62.refs_0_), channel_id=1, source_target_pairs={{0,16},{4,20},{8,24},{12,28},{16,0},{20,4},{24,8},{28,12},{1,17},{... | collective-permute-start | bytes 208904 | tf_op jit(solution)/shard_map/ppermute | solution.py:413
  16.6 0.0 collective-permute-done.2.refs_1_
  16.6 0.8 %collective-permute-done.3.refs_2_ = f32[17,8,128]{2,1,0:T(8,128)S(1)} collective-permute-done((f32[17,8,128]{2,1,0:T(8,128)S(1)}, f32[17,8,128]{2,1,0:T(8,128)S(1)}, u32[]{:S(2)}, u32[]{:S(2)}) %collective-permute-start.3) | collective-permute-done | bytes 69664 | tf_op jit(solution)/shard_map/ppermute | solution.py:406
  17.4 0.8 %collective-permute-done.4.refs_3_ = f32[17,8,128]{2,1,0:T(8,128)S(1)} collective-permute-done((f32[17,8,128]{2,1,0:T(8,128)S(1)}, f32[17,8,128]{2,1,0:T(8,128)S(1)}, u32[]{:S(2)}, u32[]{:S(2)}) %collective-permute-start.4) | collective-permute-done | bytes 69664 | tf_op jit(solution)/shard_map/ppermute | solution.py:406
  18.2 2.6 %collective-permute-start.5 = (f32[17,8,128]{2,1,0:T(8,128)S(1)}, f32[17,8,128]{2,1,0:T(8,128)S(1)}, u32[]{:S(2)}, u32[]{:S(2)}) collective-permute-start(f32[17,8,128]{2,1,0:T(8,128)S(1)} %shard_map.60.refs_0_), channel_id=1, source_target_pairs={{0,16},{4,20},{8,24},{12,28},{16,0},{20,4},{24,8},{28,12},{1,17},{... | collective-permute-start | bytes 208904 | tf_op jit(solution)/shard_map/ppermute | solution.py:413
  20.9 0.0 collective-permute-done.12.refs_1_
  20.9 2.1 %collective-permute-start.15 = (f32[17,8,128]{2,1,0:T(8,128)S(1)}, f32[17,8,128]{2,1,0:T(8,128)S(1)}, u32[]{:S(2)}, u32[]{:S(2)}) collective-permute-start(f32[17,8,128]{2,1,0:T(8,128)S(1)} %shard_map.63.refs_0_.refs_4_), channel_id=1, source_target_pairs={{0,12},{1,13},{2,14},{3,15},{4,8},{5,9},{6,10},{7,11},{8,4},{9,5},... | collective-permute-start | bytes 208904 | tf_op jit(solution)/shard_map/ppermute | solution.py:406
  23.1 0.6 %collective-permute-start.14 = (f32[17,8,128]{2,1,0:T(8,128)S(1)}, f32[17,8,128]{2,1,0:T(8,128)S(1)}, u32[]{:S(2)}, u32[]{:S(2)}) collective-permute-start(f32[17,8,128]{2,1,0:T(8,128)S(1)} %shard_map.63.refs_0_.refs_4_), channel_id=1, source_target_pairs={{0,8},{1,5},{2,10},{3,7},{4,12},{5,1},{6,14},{7,3},{8,0},{9,13},{1... | collective-permute-start | bytes 208904 | tf_op jit(solution)/shard_map/ppermute | solution.py:406
  23.6 0.8 %collective-permute-start.13 = (f32[17,8,128]{2,1,0:T(8,128)S(1)}, f32[17,8,128]{2,1,0:T(8,128)S(1)}, u32[]{:S(2)}, u32[]{:S(2)}) collective-permute-start(f32[17,8,128]{2,1,0:T(8,128)S(1)} %shard_map.63.refs_0_.refs_4_), channel_id=1, source_target_pairs={{0,4},{1,9},{2,6},{3,11},{4,0},{5,13},{6,2},{7,15},{8,12},{9,1},{1... | collective-permute-start | bytes 208904 | tf_op jit(solution)/shard_map/ppermute | solution.py:406
  24.5 0.9 %collective-permute-done.5.refs_1_ = f32[17,8,128]{2,1,0:T(8,128)S(1)} collective-permute-done((f32[17,8,128]{2,1,0:T(8,128)S(1)}, f32[17,8,128]{2,1,0:T(8,128)S(1)}, u32[]{:S(2)}, u32[]{:S(2)}) %collective-permute-start.5) | collective-permute-done | bytes 69664 | tf_op jit(solution)/shard_map/ppermute | solution.py:413
  25.4 1.2 %collective-permute-start.8 = (f32[17,8,128]{2,1,0:T(8,128)S(1)}, f32[17,8,128]{2,1,0:T(8,128)S(1)}, u32[]{:S(2)}, u32[]{:S(2)}) collective-permute-start(f32[17,8,128]{2,1,0:T(8,128)S(1)} %shard_map.61.refs_0_), channel_id=1, source_target_pairs={{0,12},{1,13},{2,14},{3,15},{4,8},{5,9},{6,10},{7,11},{8,4},{9,5},... | collective-permute-start | bytes 208904 | tf_op jit(solution)/shard_map/ppermute | solution.py:406
  26.6 0.9 %collective-permute-start.7 = (f32[17,8,128]{2,1,0:T(8,128)S(1)}, f32[17,8,128]{2,1,0:T(8,128)S(1)}, u32[]{:S(2)}, u32[]{:S(2)}) collective-permute-start(f32[17,8,128]{2,1,0:T(8,128)S(1)} %shard_map.61.refs_0_), channel_id=1, source_target_pairs={{0,8},{1,5},{2,10},{3,7},{4,12},{5,1},{6,14},{7,3},{8,0},{9,13},{1... | collective-permute-start | bytes 208904 | tf_op jit(solution)/shard_map/ppermute | solution.py:406
  27.5 0.0 collective-permute-done.15.refs_3_.refs_7_
  27.5 1.4 %collective-permute-start.6 = (f32[17,8,128]{2,1,0:T(8,128)S(1)}, f32[17,8,128]{2,1,0:T(8,128)S(1)}, u32[]{:S(2)}, u32[]{:S(2)}) collective-permute-start(f32[17,8,128]{2,1,0:T(8,128)S(1)} %shard_map.61.refs_0_), channel_id=1, source_target_pairs={{0,4},{1,9},{2,6},{3,11},{4,0},{5,13},{6,2},{7,15},{8,12},{9,1},{1... | collective-permute-start | bytes 208904 | tf_op jit(solution)/shard_map/ppermute | solution.py:406
  29.0 0.0 collective-permute-done.14.refs_2_.refs_6_
  29.0 0.0 collective-permute-done.13.refs_1_.refs_5_
  29.0 1.0 %shard_map.64.refs_8_ = f32[8,16,8,128]{3,2,1,0:T(8,128)} custom-call(s32[1]{0:T(128)} %bitcast.dom_ref, s32[1]{0:T(128)} %bitcast.1.me_ref, f32[3,8,128]{2,1,0:T(8,128)S(1)} %get-tuple-element.18.keep_ref, f32[17,8,128]{2,1,0:T(8,128)S(1)} %shard_map.63.refs_0_.refs_4_, f32[17,8,128]{2,1,0:T(8,128)S(1)} %collective-permute-done.13.refs_1_.refs_5_, ...), custom_call_target="tpu_custom_call" | custom-call | bytes 290824 | tf_op jit(solution)/shard_map/pallas_call | solution.py:335
  29.9 1.0 %collective-permute-done.8.refs_3_ = f32[17,8,128]{2,1,0:T(8,128)S(1)} collective-permute-done((f32[17,8,128]{2,1,0:T(8,128)S(1)}, f32[17,8,128]{2,1,0:T(8,128)S(1)}, u32[]{:S(2)}, u32[]{:S(2)}) %collective-permute-start.8) | collective-permute-done | bytes 69664 | tf_op jit(solution)/shard_map/ppermute | solution.py:406
  31.0 0.4 %collective-permute-done.7.refs_2_ = f32[17,8,128]{2,1,0:T(8,128)S(1)} collective-permute-done((f32[17,8,128]{2,1,0:T(8,128)S(1)}, f32[17,8,128]{2,1,0:T(8,128)S(1)}, u32[]{:S(2)}, u32[]{:S(2)}) %collective-permute-start.7) | collective-permute-done | bytes 69664 | tf_op jit(solution)/shard_map/ppermute | solution.py:406
  31.4 0.4 %collective-permute-done.6.refs_1_ = f32[17,8,128]{2,1,0:T(8,128)S(1)} collective-permute-done((f32[17,8,128]{2,1,0:T(8,128)S(1)}, f32[17,8,128]{2,1,0:T(8,128)S(1)}, u32[]{:S(2)}, u32[]{:S(2)}) %collective-permute-start.6) | collective-permute-done | bytes 69664 | tf_op jit(solution)/shard_map/ppermute | solution.py:406
  31.9 1.0 %shard_map.65 = f32[8,16,8,128]{3,2,1,0:T(8,128)} custom-call(s32[1]{0:T(128)} %bitcast.dom_ref, s32[1]{0:T(128)} %bitcast.1.me_ref, f32[3,8,128]{2,1,0:T(8,128)S(1)} %get-tuple-element.18.keep_ref, f32[17,8,128]{2,1,0:T(8,128)S(1)} %shard_map.61.refs_0_, f32[17,8,128]{2,1,0:T(8,128)S(1)} %collective-permute-done.6.refs_1_, ...), custom_call_target="tpu_custom_call", output_to_operand_aliasing={{}: (11, {})} | custom-call | bytes 1093640 | tf_op jit(solution)/shard_map/pallas_call | solution.py:335
  (6 shorter events, 0.1 us)
Async XLA Ops:
  0.0 1.4 %copy-start = (f32[1,64,2048]{2,1,0:T(8,128)S(1)}, f32[1,64,2048]{2,1,0:T(8,128)}, u32[]{:S(2)}) copy-start(f32[1,64,2048]{2,1,0:T(8,128)} %param.5) | copy-start | bytes 1572868
  0.0 1.5 %copy-start.1 = (f32[1,64,2048]{2,1,0:T(8,128)S(1)}, f32[1,64,2048]{2,1,0:T(8,128)}, u32[]{:S(2)}) copy-start(f32[1,64,2048]{2,1,0:T(8,128)} %param.6) | copy-start | bytes 1572868
  0.0 1.5 %copy-start.2 = (f32[1,64,2048]{2,1,0:T(8,128)S(1)}, f32[1,64,2048]{2,1,0:T(8,128)}, u32[]{:S(2)}) copy-start(f32[1,64,2048]{2,1,0:T(8,128)} %param.7) | copy-start | bytes 1572868
  1.5 7.5 %collective-permute-start = (f32[16,16,128]{2,1,0:T(8,128)S(1)}, f32[16,16,128]{2,1,0:T(8,128)S(1)}, u32[]{:S(2)}, u32[]{:S(2)}) collective-permute-start(f32[16,16,128]{2,1,0:T(8,128)S(1)} %get-tuple-element.21), channel_id=1, source_target_pairs={{0,1},{1,0},{2,3},{3,2},{4,5},{5,4},{6,7},{7,6},{8,9},{9,8},{10,11... | collective-permute-start | bytes 393224 | tf_op jit(solution)/shard_map/ppermute | solution.py:375
  2.1 7.0 %collective-permute-start.1 = (f32[16,16,128]{2,1,0:T(8,128)S(1)}, f32[16,16,128]{2,1,0:T(8,128)S(1)}, u32[]{:S(2)}, u32[]{:S(2)}) collective-permute-start(f32[16,16,128]{2,1,0:T(8,128)S(1)} %get-tuple-element.22), channel_id=1, source_target_pairs={{0,0},{1,2},{2,1},{3,3},{4,4},{5,6},{6,5},{7,7},{8,8},{9,10},{10,9... | collective-permute-start | bytes 393224 | tf_op jit(solution)/shard_map/ppermute | solution.py:376
  4.8 8.6 %collective-permute-start.9 = (f32[17,8,128]{2,1,0:T(8,128)S(1)}, f32[17,8,128]{2,1,0:T(8,128)S(1)}, u32[]{:S(2)}, u32[]{:S(2)}) collective-permute-start(f32[17,8,128]{2,1,0:T(8,128)S(1)} %get-tuple-element.28), channel_id=1, source_target_pairs={{0,12},{1,13},{2,14},{3,15},{4,8},{5,9},{6,10},{7,11},{8,4},{9,5},... | collective-permute-start | bytes 208904 | tf_op jit(solution)/shard_map/ppermute | solution.py:406
  8.4 5.1 %collective-permute-start.10 = (f32[17,8,128]{2,1,0:T(8,128)S(1)}, f32[17,8,128]{2,1,0:T(8,128)S(1)}, u32[]{:S(2)}, u32[]{:S(2)}) collective-permute-start(f32[17,8,128]{2,1,0:T(8,128)S(1)} %get-tuple-element.29), channel_id=1, source_target_pairs={{0,4},{1,9},{2,6},{3,11},{4,0},{5,13},{6,2},{7,15},{8,12},{9,1},{1... | collective-permute-start | bytes 208904 | tf_op jit(solution)/shard_map/ppermute | solution.py:406
  8.9 5.0 %collective-permute-start.11 = (f32[17,8,128]{2,1,0:T(8,128)S(1)}, f32[17,8,128]{2,1,0:T(8,128)S(1)}, u32[]{:S(2)}, u32[]{:S(2)}) collective-permute-start(f32[17,8,128]{2,1,0:T(8,128)S(1)} %get-tuple-element.30), channel_id=1, source_target_pairs={{0,8},{1,5},{2,10},{3,7},{4,12},{5,1},{6,14},{7,3},{8,0},{9,13},{1... | collective-permute-start | bytes 208904 | tf_op jit(solution)/shard_map/ppermute | solution.py:406
  10.0 6.7 %collective-permute-start.2 = (f32[17,8,128]{2,1,0:T(8,128)S(1)}, f32[17,8,128]{2,1,0:T(8,128)S(1)}, u32[]{:S(2)}, u32[]{:S(2)}) collective-permute-start(f32[17,8,128]{2,1,0:T(8,128)S(1)} %get-tuple-element.24), channel_id=1, source_target_pairs={{0,12},{1,13},{2,14},{3,15},{4,8},{5,9},{6,10},{7,11},{8,4},{9,5},... | collective-permute-start | bytes 208904 | tf_op jit(solution)/shard_map/ppermute | solution.py:406
  12.9 4.5 %collective-permute-start.3 = (f32[17,8,128]{2,1,0:T(8,128)S(1)}, f32[17,8,128]{2,1,0:T(8,128)S(1)}, u32[]{:S(2)}, u32[]{:S(2)}) collective-permute-start(f32[17,8,128]{2,1,0:T(8,128)S(1)} %get-tuple-element.25), channel_id=1, source_target_pairs={{0,4},{1,9},{2,6},{3,11},{4,0},{5,13},{6,2},{7,15},{8,12},{9,1},{1... | collective-permute-start | bytes 208904 | tf_op jit(solution)/shard_map/ppermute | solution.py:406
  13.4 4.8 %collective-permute-start.4 = (f32[17,8,128]{2,1,0:T(8,128)S(1)}, f32[17,8,128]{2,1,0:T(8,128)S(1)}, u32[]{:S(2)}, u32[]{:S(2)}) collective-permute-start(f32[17,8,128]{2,1,0:T(8,128)S(1)} %get-tuple-element.26), channel_id=1, source_target_pairs={{0,8},{1,5},{2,10},{3,7},{4,12},{5,1},{6,14},{7,3},{8,0},{9,13},{1... | collective-permute-start | bytes 208904 | tf_op jit(solution)/shard_map/ppermute | solution.py:406
  14.0 6.9 %collective-permute-start.12 = (f32[17,8,128]{2,1,0:T(8,128)S(1)}, f32[17,8,128]{2,1,0:T(8,128)S(1)}, u32[]{:S(2)}, u32[]{:S(2)}) collective-permute-start(f32[17,8,128]{2,1,0:T(8,128)S(1)} %shard_map.62.refs_0_), channel_id=1, source_target_pairs={{0,16},{4,20},{8,24},{12,28},{16,0},{20,4},{24,8},{28,12},{1,17},{... | collective-permute-start | bytes 208904 | tf_op jit(solution)/shard_map/ppermute | solution.py:413
  18.2 7.2 %collective-permute-start.5 = (f32[17,8,128]{2,1,0:T(8,128)S(1)}, f32[17,8,128]{2,1,0:T(8,128)S(1)}, u32[]{:S(2)}, u32[]{:S(2)}) collective-permute-start(f32[17,8,128]{2,1,0:T(8,128)S(1)} %shard_map.60.refs_0_), channel_id=1, source_target_pairs={{0,16},{4,20},{8,24},{12,28},{16,0},{20,4},{24,8},{28,12},{1,17},{... | collective-permute-start | bytes 208904 | tf_op jit(solution)/shard_map/ppermute | solution.py:413
  20.9 6.6 %collective-permute-start.15 = (f32[17,8,128]{2,1,0:T(8,128)S(1)}, f32[17,8,128]{2,1,0:T(8,128)S(1)}, u32[]{:S(2)}, u32[]{:S(2)}) collective-permute-start(f32[17,8,128]{2,1,0:T(8,128)S(1)} %shard_map.63.refs_0_.refs_4_), channel_id=1, source_target_pairs={{0,12},{1,13},{2,14},{3,15},{4,8},{5,9},{6,10},{7,11},{8,4},{9,5},... | collective-permute-start | bytes 208904 | tf_op jit(solution)/shard_map/ppermute | solution.py:406
  23.1 5.9 %collective-permute-start.14 = (f32[17,8,128]{2,1,0:T(8,128)S(1)}, f32[17,8,128]{2,1,0:T(8,128)S(1)}, u32[]{:S(2)}, u32[]{:S(2)}) collective-permute-start(f32[17,8,128]{2,1,0:T(8,128)S(1)} %shard_map.63.refs_0_.refs_4_), channel_id=1, source_target_pairs={{0,8},{1,5},{2,10},{3,7},{4,12},{5,1},{6,14},{7,3},{8,0},{9,13},{1... | collective-permute-start | bytes 208904 | tf_op jit(solution)/shard_map/ppermute | solution.py:406
  23.6 5.3 %collective-permute-start.13 = (f32[17,8,128]{2,1,0:T(8,128)S(1)}, f32[17,8,128]{2,1,0:T(8,128)S(1)}, u32[]{:S(2)}, u32[]{:S(2)}) collective-permute-start(f32[17,8,128]{2,1,0:T(8,128)S(1)} %shard_map.63.refs_0_.refs_4_), channel_id=1, source_target_pairs={{0,4},{1,9},{2,6},{3,11},{4,0},{5,13},{6,2},{7,15},{8,12},{9,1},{1... | collective-permute-start | bytes 208904 | tf_op jit(solution)/shard_map/ppermute | solution.py:406
  25.4 5.6 %collective-permute-start.8 = (f32[17,8,128]{2,1,0:T(8,128)S(1)}, f32[17,8,128]{2,1,0:T(8,128)S(1)}, u32[]{:S(2)}, u32[]{:S(2)}) collective-permute-start(f32[17,8,128]{2,1,0:T(8,128)S(1)} %shard_map.61.refs_0_), channel_id=1, source_target_pairs={{0,12},{1,13},{2,14},{3,15},{4,8},{5,9},{6,10},{7,11},{8,4},{9,5},... | collective-permute-start | bytes 208904 | tf_op jit(solution)/shard_map/ppermute | solution.py:406
  26.6 4.8 %collective-permute-start.7 = (f32[17,8,128]{2,1,0:T(8,128)S(1)}, f32[17,8,128]{2,1,0:T(8,128)S(1)}, u32[]{:S(2)}, u32[]{:S(2)}) collective-permute-start(f32[17,8,128]{2,1,0:T(8,128)S(1)} %shard_map.61.refs_0_), channel_id=1, source_target_pairs={{0,8},{1,5},{2,10},{3,7},{4,12},{5,1},{6,14},{7,3},{8,0},{9,13},{1... | collective-permute-start | bytes 208904 | tf_op jit(solution)/shard_map/ppermute | solution.py:406
  27.5 4.3 %collective-permute-start.6 = (f32[17,8,128]{2,1,0:T(8,128)S(1)}, f32[17,8,128]{2,1,0:T(8,128)S(1)}, u32[]{:S(2)}, u32[]{:S(2)}) collective-permute-start(f32[17,8,128]{2,1,0:T(8,128)S(1)} %shard_map.61.refs_0_), channel_id=1, source_target_pairs={{0,4},{1,9},{2,6},{3,11},{4,0},{5,13},{6,2},{7,15},{8,12},{9,1},{1... | collective-permute-start | bytes 208904 | tf_op jit(solution)/shard_map/ppermute | solution.py:406

commit v20 on v19

--- a/solution.py
+++ b/solution.py
@@ -154,7 +154,7 @@
 
 
 def middle_tiles(many):
-    return list(range(many // 4, many - many // 4)) if many >= 4 else []
+    return list(range(many // 4, many - 1)) if many >= 4 else []
 
 
 def outer_tiles(many):

time: 33 us -> 36.6 us (1.11)
  waiting for transfers between devices: 4.87 us -> 10.3 us
  starting transfers between devices: 21.4 us -> 19.6 us
    ppermute x12, waiting for transfers between devices: 3.94 us -> 7.08 us  [swap(): return lax.ppermute(array, ('grp', 'dom'), pairs)]
    ppermute x2, waiting for transfers between devices: 0.93 us -> 3.2 us  [over_grids(): other = lax.ppermute(total, 'grp', [(g, g ^ apart) for g in range(grids)])]
    ppermute x2, starting transfers between devices: 5.3 us -> 3.53 us  [over_grids(): other = lax.ppermute(total, 'grp', [(g, g ^ apart) for g in range(grids)])]
    ppermute x1, starting transfers between devices: 0.53 us -> 0.07 us  [on_device(): near = lax.ppermute(near, 'dom', near_pairs)]
    ppermute x12, starting transfers between devices: 14.9 us -> 15.3 us  [swap(): return lax.ppermute(array, ('grp', 'dom'), pairs)]
  transfers between devices with their start and end apart: 16 -> 16, of which waited for: 7 -> 10; matrix products, arithmetic and copies ran while one was open for 0% -> 0% of each run, Pallas kernels for 12% -> 6%
where the time goes in v20:
time: 36.6 us; the launch traced here: 36.4 us
  starting transfers between devices  19.6 us (54%)
  waiting for transfers between devices  10.3 us (28%)
  Pallas kernels  5.06 us (14%)
  between operations  1.51 us (4%)
    ppermute x12, starting transfers between devices, swap(): return lax.ppermute(array, ('grp', 'dom'), pairs)  15.3 us
    ppermute x12, waiting for transfers between devices, swap(): return lax.ppermute(array, ('grp', 'dom'), pairs)  7.08 us
    pallas_call x11, Pallas kernels, call(): pl.pallas_call(kernel, out_shape=[jax.ShapeDtypeStruct(shape, jnp.float32...  5.06 us
    ppermute x2, starting transfers between devices, over_grids(): other = lax.ppermute(total, 'grp', [(g, g ^ apart) for g in range(grids)])  3.53 us
    ppermute x2, waiting for transfers between devices, over_grids(): other = lax.ppermute(total, 'grp', [(g, g ^ apart) for g in range(grids)])  3.2 us
  transfers between devices with their start and end apart: 16, of which 10 were waited for; matrix products, arithmetic and copies ran while one was open for 0% of the time, Pallas kernels for 6%

profile of v20, /device:TPU:0, one launch (start us, length us, event | category | flops | bytes accessed | tf_op | source)
XLA Modules:
  0.0 36.4 jit_solution(9327318228694776339)
XLA Ops:
  0.0 0.0 copy-start
  0.0 0.0 copy-start.1
  0.0 0.0 copy-start.2
  1.4 0.0 copy-done
  1.5 0.0 copy-done.1
  1.5 0.0 copy-done.2
  1.5 2.1 %shard_map.57 = (f32[16,8,8,128]{3,2,1,0:T(8,128)S(1)}, f32[21,8,128]{2,1,0:T(8,128)S(1)}, f32[21,8,128]{2,1,0:T(8,128)S(1)}, f32[21,8,128]{2,1,0:T(8,128)S(1)}, f32[21,8,128]{2,1,0:T(8,128)S(1)}) custom-call(s32[1]{0:T(128)} %bitcast.dom_ref, s32[1]{0:T(128)} %bitcast.1.me_ref, f32[4,8,128]{2,1,0:T(8,128)S(1)} %get-tuple-element.19.weight_ref, ...), custom_call_target="tpu_custom_call" | custom-call | flops 5242880 | bytes 1589256 | tf_op jit(solution)/shard_map/pallas_call | solution.py:335
  3.5 4.0 %collective-permute-start.9 = (f32[21,8,128]{2,1,0:T(8,128)S(1)}, f32[21,8,128]{2,1,0:T(8,128)S(1)}, u32[]{:S(2)}, u32[]{:S(2)}) collective-permute-start(f32[21,8,128]{2,1,0:T(8,128)S(1)} %get-tuple-element.28), channel_id=1, source_target_pairs={{0,12},{1,13},{2,14},{3,15},{4,8},{5,9},{6,10},{7,11},{8,4},{9,5},... | collective-permute-start | bytes 258056 | tf_op jit(solution)/shard_map/ppermute | solution.py:406
  7.6 0.5 %collective-permute-start.10 = (f32[21,8,128]{2,1,0:T(8,128)S(1)}, f32[21,8,128]{2,1,0:T(8,128)S(1)}, u32[]{:S(2)}, u32[]{:S(2)}) collective-permute-start(f32[21,8,128]{2,1,0:T(8,128)S(1)} %get-tuple-element.29), channel_id=1, source_target_pairs={{0,4},{1,9},{2,6},{3,11},{4,0},{5,13},{6,2},{7,15},{8,12},{9,1},{1... | collective-permute-start | bytes 258056 | tf_op jit(solution)/shard_map/ppermute | solution.py:406
  8.1 0.1 collective-permute-start.11
  8.3 0.1 collective-permute-start
  8.3 0.7 %collective-permute-start.1 = (f32[16,16,128]{2,1,0:T(8,128)S(1)}, f32[16,16,128]{2,1,0:T(8,128)S(1)}, u32[]{:S(2)}, u32[]{:S(2)}) collective-permute-start(f32[16,16,128]{2,1,0:T(8,128)S(1)} %get-tuple-element.22), channel_id=1, source_target_pairs={{0,0},{1,2},{2,1},{3,3},{4,4},{5,6},{6,5},{7,7},{8,8},{9,10},{10,9... | collective-permute-start | bytes 393224 | tf_op jit(solution)/shard_map/ppermute | solution.py:376
  9.0 1.6 %collective-permute-done.9.refs_1_ = f32[21,8,128]{2,1,0:T(8,128)S(1)} collective-permute-done((f32[21,8,128]{2,1,0:T(8,128)S(1)}, f32[21,8,128]{2,1,0:T(8,128)S(1)}, u32[]{:S(2)}, u32[]{:S(2)}) %collective-permute-start.9) | collective-permute-done | bytes 86048 | tf_op jit(solution)/shard_map/ppermute | solution.py:406
  10.6 1.5 %collective-permute-done.10.refs_2_ = f32[21,8,128]{2,1,0:T(8,128)S(1)} collective-permute-done((f32[21,8,128]{2,1,0:T(8,128)S(1)}, f32[21,8,128]{2,1,0:T(8,128)S(1)}, u32[]{:S(2)}, u32[]{:S(2)}) %collective-permute-start.10) | collective-permute-done | bytes 86048 | tf_op jit(solution)/shard_map/ppermute | solution.py:406
  12.1 0.5 %collective-permute-done.11.refs_3_ = f32[21,8,128]{2,1,0:T(8,128)S(1)} collective-permute-done((f32[21,8,128]{2,1,0:T(8,128)S(1)}, f32[21,8,128]{2,1,0:T(8,128)S(1)}, u32[]{:S(2)}, u32[]{:S(2)}) %collective-permute-start.11) | collective-permute-done | bytes 86048 | tf_op jit(solution)/shard_map/ppermute | solution.py:406
  12.6 2.7 %collective-permute-start.12 = (f32[21,8,128]{2,1,0:T(8,128)S(1)}, f32[21,8,128]{2,1,0:T(8,128)S(1)}, u32[]{:S(2)}, u32[]{:S(2)}) collective-permute-start(f32[21,8,128]{2,1,0:T(8,128)S(1)} %shard_map.62.refs_0_), channel_id=1, source_target_pairs={{0,16},{4,20},{8,24},{12,28},{16,0},{20,4},{24,8},{28,12},{1,17},{... | collective-permute-start | bytes 258056 | tf_op jit(solution)/shard_map/ppermute | solution.py:413
  15.3 0.0 collective-permute-done.refs_3_
  15.3 0.0 collective-permute-done.1.refs_4_
  15.3 0.9 %shard_map.59 = (f32[13,8,128]{2,1,0:T(8,128)S(1)}, f32[13,8,128]{2,1,0:T(8,128)S(1)}, f32[13,8,128]{2,1,0:T(8,128)S(1)}, f32[13,8,128]{2,1,0:T(8,128)S(1)}) custom-call(s32[1]{0:T(128)} %bitcast.dom_ref, s32[1]{0:T(128)} %bitcast.1.me_ref, f32[4,8,128]{2,1,0:T(8,128)S(1)} %get-tuple-element.19.weight_ref, f32[8,16,8,128]{3,2,1,0:T(8,128)S(1)} %bitcast.16, ...), custom_call_target="tpu_custom_call" | custom-call | flops 2621440 | bytes 2375688 | tf_op jit(solution)/shard_map/pallas_call | solution.py:335
  16.2 2.1 %collective-permute-start.2 = (f32[13,8,128]{2,1,0:T(8,128)S(1)}, f32[13,8,128]{2,1,0:T(8,128)S(1)}, u32[]{:S(2)}, u32[]{:S(2)}) collective-permute-start(f32[13,8,128]{2,1,0:T(8,128)S(1)} %get-tuple-element.24), channel_id=1, source_target_pairs={{0,12},{1,13},{2,14},{3,15},{4,8},{5,9},{6,10},{7,11},{8,4},{9,5},... | collective-permute-start | bytes 159752 | tf_op jit(solution)/shard_map/ppermute | solution.py:406
  18.3 0.9 %collective-permute-start.3 = (f32[13,8,128]{2,1,0:T(8,128)S(1)}, f32[13,8,128]{2,1,0:T(8,128)S(1)}, u32[]{:S(2)}, u32[]{:S(2)}) collective-permute-start(f32[13,8,128]{2,1,0:T(8,128)S(1)} %get-tuple-element.25), channel_id=1, source_target_pairs={{0,4},{1,9},{2,6},{3,11},{4,0},{5,13},{6,2},{7,15},{8,12},{9,1},{1... | collective-permute-start | bytes 159752 | tf_op jit(solution)/shard_map/ppermute | solution.py:406
  19.2 0.6 %collective-permute-start.4 = (f32[13,8,128]{2,1,0:T(8,128)S(1)}, f32[13,8,128]{2,1,0:T(8,128)S(1)}, u32[]{:S(2)}, u32[]{:S(2)}) collective-permute-start(f32[13,8,128]{2,1,0:T(8,128)S(1)} %get-tuple-element.26), channel_id=1, source_target_pairs={{0,8},{1,5},{2,10},{3,7},{4,12},{5,1},{6,14},{7,3},{8,0},{9,13},{1... | collective-permute-start | bytes 159752 | tf_op jit(solution)/shard_map/ppermute | solution.py:406
  19.8 0.1 collective-permute-done.12.refs_1_
  19.9 1.9 %collective-permute-start.15 = (f32[21,8,128]{2,1,0:T(8,128)S(1)}, f32[21,8,128]{2,1,0:T(8,128)S(1)}, u32[]{:S(2)}, u32[]{:S(2)}) collective-permute-start(f32[21,8,128]{2,1,0:T(8,128)S(1)} %shard_map.63.refs_0_.refs_4_), channel_id=1, source_target_pairs={{0,12},{1,13},{2,14},{3,15},{4,8},{5,9},{6,10},{7,11},{8,4},{9,5},... | collective-permute-start | bytes 258056 | tf_op jit(solution)/shard_map/ppermute | solution.py:406
  21.8 0.0 collective-permute-done.2.refs_1_
  21.9 1.8 %collective-permute-done.3.refs_2_ = f32[13,8,128]{2,1,0:T(8,128)S(1)} collective-permute-done((f32[13,8,128]{2,1,0:T(8,128)S(1)}, f32[13,8,128]{2,1,0:T(8,128)S(1)}, u32[]{:S(2)}, u32[]{:S(2)}) %collective-permute-start.3) | collective-permute-done | bytes 53280 | tf_op jit(solution)/shard_map/ppermute | solution.py:406
  23.7 0.2 collective-permute-done.4.refs_3_
  23.9 0.9 %collective-permute-start.5 = (f32[13,8,128]{2,1,0:T(8,128)S(1)}, f32[13,8,128]{2,1,0:T(8,128)S(1)}, u32[]{:S(2)}, u32[]{:S(2)}) collective-permute-start(f32[13,8,128]{2,1,0:T(8,128)S(1)} %shard_map.60.refs_0_), channel_id=1, source_target_pairs={{0,16},{4,20},{8,24},{12,28},{16,0},{20,4},{24,8},{28,12},{1,17},{... | collective-permute-start | bytes 159752 | tf_op jit(solution)/shard_map/ppermute | solution.py:413
  24.8 0.6 %collective-permute-start.14 = (f32[21,8,128]{2,1,0:T(8,128)S(1)}, f32[21,8,128]{2,1,0:T(8,128)S(1)}, u32[]{:S(2)}, u32[]{:S(2)}) collective-permute-start(f32[21,8,128]{2,1,0:T(8,128)S(1)} %shard_map.63.refs_0_.refs_4_), channel_id=1, source_target_pairs={{0,8},{1,5},{2,10},{3,7},{4,12},{5,1},{6,14},{7,3},{8,0},{9,13},{1... | collective-permute-start | bytes 258056 | tf_op jit(solution)/shard_map/ppermute | solution.py:406
  25.4 1.1 %collective-permute-start.13 = (f32[21,8,128]{2,1,0:T(8,128)S(1)}, f32[21,8,128]{2,1,0:T(8,128)S(1)}, u32[]{:S(2)}, u32[]{:S(2)}) collective-permute-start(f32[21,8,128]{2,1,0:T(8,128)S(1)} %shard_map.63.refs_0_.refs_4_), channel_id=1, source_target_pairs={{0,4},{1,9},{2,6},{3,11},{4,0},{5,13},{6,2},{7,15},{8,12},{9,1},{1... | collective-permute-start | bytes 258056 | tf_op jit(solution)/shard_map/ppermute | solution.py:406
  26.4 3.1 %collective-permute-done.5.refs_1_ = f32[13,8,128]{2,1,0:T(8,128)S(1)} collective-permute-done((f32[13,8,128]{2,1,0:T(8,128)S(1)}, f32[13,8,128]{2,1,0:T(8,128)S(1)}, u32[]{:S(2)}, u32[]{:S(2)}) %collective-permute-start.5) | collective-permute-done | bytes 53280 | tf_op jit(solution)/shard_map/ppermute | solution.py:413
  29.5 1.4 %collective-permute-start.8 = (f32[13,8,128]{2,1,0:T(8,128)S(1)}, f32[13,8,128]{2,1,0:T(8,128)S(1)}, u32[]{:S(2)}, u32[]{:S(2)}) collective-permute-start(f32[13,8,128]{2,1,0:T(8,128)S(1)} %shard_map.61.refs_0_), channel_id=1, source_target_pairs={{0,12},{1,13},{2,14},{3,15},{4,8},{5,9},{6,10},{7,11},{8,4},{9,5},... | collective-permute-start | bytes 159752 | tf_op jit(solution)/shard_map/ppermute | solution.py:406
  30.9 0.5 %collective-permute-start.7 = (f32[13,8,128]{2,1,0:T(8,128)S(1)}, f32[13,8,128]{2,1,0:T(8,128)S(1)}, u32[]{:S(2)}, u32[]{:S(2)}) collective-permute-start(f32[13,8,128]{2,1,0:T(8,128)S(1)} %shard_map.61.refs_0_), channel_id=1, source_target_pairs={{0,8},{1,5},{2,10},{3,7},{4,12},{5,1},{6,14},{7,3},{8,0},{9,13},{1... | collective-permute-start | bytes 159752 | tf_op jit(solution)/shard_map/ppermute | solution.py:406
  31.4 0.0 collective-permute-done.15.refs_3_.refs_7_
  31.4 1.6 %collective-permute-start.6 = (f32[13,8,128]{2,1,0:T(8,128)S(1)}, f32[13,8,128]{2,1,0:T(8,128)S(1)}, u32[]{:S(2)}, u32[]{:S(2)}) collective-permute-start(f32[13,8,128]{2,1,0:T(8,128)S(1)} %shard_map.61.refs_0_), channel_id=1, source_target_pairs={{0,4},{1,9},{2,6},{3,11},{4,0},{5,13},{6,2},{7,15},{8,12},{9,1},{1... | collective-permute-start | bytes 159752 | tf_op jit(solution)/shard_map/ppermute | solution.py:406
  33.0 0.0 collective-permute-done.14.refs_2_.refs_6_
  33.0 0.0 collective-permute-done.13.refs_1_.refs_5_
  33.0 1.1 %shard_map.64.refs_8_ = f32[8,16,8,128]{3,2,1,0:T(8,128)} custom-call(s32[1]{0:T(128)} %bitcast.dom_ref, s32[1]{0:T(128)} %bitcast.1.me_ref, f32[3,8,128]{2,1,0:T(8,128)S(1)} %get-tuple-element.18.keep_ref, f32[21,8,128]{2,1,0:T(8,128)S(1)} %shard_map.63.refs_0_.refs_4_, f32[21,8,128]{2,1,0:T(8,128)S(1)} %collective-permute-done.13.refs_1_.refs_5_, ...), custom_call_target="tpu_custom_call" | custom-call | bytes 356360 | tf_op jit(solution)/shard_map/pallas_call | solution.py:335
  34.1 0.5 %collective-permute-done.8.refs_3_ = f32[13,8,128]{2,1,0:T(8,128)S(1)} collective-permute-done((f32[13,8,128]{2,1,0:T(8,128)S(1)}, f32[13,8,128]{2,1,0:T(8,128)S(1)}, u32[]{:S(2)}, u32[]{:S(2)}) %collective-permute-start.8) | collective-permute-done | bytes 53280 | tf_op jit(solution)/shard_map/ppermute | solution.py:406
  34.6 0.4 %collective-permute-done.7.refs_2_ = f32[13,8,128]{2,1,0:T(8,128)S(1)} collective-permute-done((f32[13,8,128]{2,1,0:T(8,128)S(1)}, f32[13,8,128]{2,1,0:T(8,128)S(1)}, u32[]{:S(2)}, u32[]{:S(2)}) %collective-permute-start.7) | collective-permute-done | bytes 53280 | tf_op jit(solution)/shard_map/ppermute | solution.py:406
  35.0 0.5 %collective-permute-done.6.refs_1_ = f32[13,8,128]{2,1,0:T(8,128)S(1)} collective-permute-done((f32[13,8,128]{2,1,0:T(8,128)S(1)}, f32[13,8,128]{2,1,0:T(8,128)S(1)}, u32[]{:S(2)}, u32[]{:S(2)}) %collective-permute-start.6) | collective-permute-done | bytes 53280 | tf_op jit(solution)/shard_map/ppermute | solution.py:406
  35.6 0.9 %shard_map.65 = f32[8,16,8,128]{3,2,1,0:T(8,128)} custom-call(s32[1]{0:T(128)} %bitcast.dom_ref, s32[1]{0:T(128)} %bitcast.1.me_ref, f32[3,8,128]{2,1,0:T(8,128)S(1)} %get-tuple-element.18.keep_ref, f32[13,8,128]{2,1,0:T(8,128)S(1)} %shard_map.61.refs_0_, f32[13,8,128]{2,1,0:T(8,128)S(1)} %collective-permute-done.6.refs_1_, ...), custom_call_target="tpu_custom_call", output_to_operand_aliasing={{}: (11, {})} | custom-call | bytes 1093640 | tf_op jit(solution)/shard_map/pallas_call | solution.py:335
  (7 shorter events, 0.1 us)
Async XLA Ops:
  0.0 1.4 %copy-start = (f32[1,64,2048]{2,1,0:T(8,128)S(1)}, f32[1,64,2048]{2,1,0:T(8,128)}, u32[]{:S(2)}) copy-start(f32[1,64,2048]{2,1,0:T(8,128)} %param.5) | copy-start | bytes 1572868
  0.0 1.5 %copy-start.1 = (f32[1,64,2048]{2,1,0:T(8,128)S(1)}, f32[1,64,2048]{2,1,0:T(8,128)}, u32[]{:S(2)}) copy-start(f32[1,64,2048]{2,1,0:T(8,128)} %param.6) | copy-start | bytes 1572868
  0.0 1.5 %copy-start.2 = (f32[1,64,2048]{2,1,0:T(8,128)S(1)}, f32[1,64,2048]{2,1,0:T(8,128)}, u32[]{:S(2)}) copy-start(f32[1,64,2048]{2,1,0:T(8,128)} %param.7) | copy-start | bytes 1572868
  3.5 7.0 %collective-permute-start.9 = (f32[21,8,128]{2,1,0:T(8,128)S(1)}, f32[21,8,128]{2,1,0:T(8,128)S(1)}, u32[]{:S(2)}, u32[]{:S(2)}) collective-permute-start(f32[21,8,128]{2,1,0:T(8,128)S(1)} %get-tuple-element.28), channel_id=1, source_target_pairs={{0,12},{1,13},{2,14},{3,15},{4,8},{5,9},{6,10},{7,11},{8,4},{9,5},... | collective-permute-start | bytes 258056 | tf_op jit(solution)/shard_map/ppermute | solution.py:406
  7.6 4.5 %collective-permute-start.10 = (f32[21,8,128]{2,1,0:T(8,128)S(1)}, f32[21,8,128]{2,1,0:T(8,128)S(1)}, u32[]{:S(2)}, u32[]{:S(2)}) collective-permute-start(f32[21,8,128]{2,1,0:T(8,128)S(1)} %get-tuple-element.29), channel_id=1, source_target_pairs={{0,4},{1,9},{2,6},{3,11},{4,0},{5,13},{6,2},{7,15},{8,12},{9,1},{1... | collective-permute-start | bytes 258056 | tf_op jit(solution)/shard_map/ppermute | solution.py:406
  8.1 4.5 %collective-permute-start.11 = (f32[21,8,128]{2,1,0:T(8,128)S(1)}, f32[21,8,128]{2,1,0:T(8,128)S(1)}, u32[]{:S(2)}, u32[]{:S(2)}) collective-permute-start(f32[21,8,128]{2,1,0:T(8,128)S(1)} %get-tuple-element.30), channel_id=1, source_target_pairs={{0,8},{1,5},{2,10},{3,7},{4,12},{5,1},{6,14},{7,3},{8,0},{9,13},{1... | collective-permute-start | bytes 258056 | tf_op jit(solution)/shard_map/ppermute | solution.py:406
  8.3 7.0 %collective-permute-start = (f32[16,16,128]{2,1,0:T(8,128)S(1)}, f32[16,16,128]{2,1,0:T(8,128)S(1)}, u32[]{:S(2)}, u32[]{:S(2)}) collective-permute-start(f32[16,16,128]{2,1,0:T(8,128)S(1)} %get-tuple-element.21), channel_id=1, source_target_pairs={{0,1},{1,0},{2,3},{3,2},{4,5},{5,4},{6,7},{7,6},{8,9},{9,8},{10,11... | collective-permute-start | bytes 393224 | tf_op jit(solution)/shard_map/ppermute | solution.py:375
  8.3 6.9 %collective-permute-start.1 = (f32[16,16,128]{2,1,0:T(8,128)S(1)}, f32[16,16,128]{2,1,0:T(8,128)S(1)}, u32[]{:S(2)}, u32[]{:S(2)}) collective-permute-start(f32[16,16,128]{2,1,0:T(8,128)S(1)} %get-tuple-element.22), channel_id=1, source_target_pairs={{0,0},{1,2},{2,1},{3,3},{4,4},{5,6},{6,5},{7,7},{8,8},{9,10},{10,9... | collective-permute-start | bytes 393224 | tf_op jit(solution)/shard_map/ppermute | solution.py:376
  12.6 7.3 %collective-permute-start.12 = (f32[21,8,128]{2,1,0:T(8,128)S(1)}, f32[21,8,128]{2,1,0:T(8,128)S(1)}, u32[]{:S(2)}, u32[]{:S(2)}) collective-permute-start(f32[21,8,128]{2,1,0:T(8,128)S(1)} %shard_map.62.refs_0_), channel_id=1, source_target_pairs={{0,16},{4,20},{8,24},{12,28},{16,0},{20,4},{24,8},{28,12},{1,17},{... | collective-permute-start | bytes 258056 | tf_op jit(solution)/shard_map/ppermute | solution.py:413
  16.2 5.7 %collective-permute-start.2 = (f32[13,8,128]{2,1,0:T(8,128)S(1)}, f32[13,8,128]{2,1,0:T(8,128)S(1)}, u32[]{:S(2)}, u32[]{:S(2)}) collective-permute-start(f32[13,8,128]{2,1,0:T(8,128)S(1)} %get-tuple-element.24), channel_id=1, source_target_pairs={{0,12},{1,13},{2,14},{3,15},{4,8},{5,9},{6,10},{7,11},{8,4},{9,5},... | collective-permute-start | bytes 159752 | tf_op jit(solution)/shard_map/ppermute | solution.py:406
  18.3 5.4 %collective-permute-start.3 = (f32[13,8,128]{2,1,0:T(8,128)S(1)}, f32[13,8,128]{2,1,0:T(8,128)S(1)}, u32[]{:S(2)}, u32[]{:S(2)}) collective-permute-start(f32[13,8,128]{2,1,0:T(8,128)S(1)} %get-tuple-element.25), channel_id=1, source_target_pairs={{0,4},{1,9},{2,6},{3,11},{4,0},{5,13},{6,2},{7,15},{8,12},{9,1},{1... | collective-permute-start | bytes 159752 | tf_op jit(solution)/shard_map/ppermute | solution.py:406
  19.2 4.7 %collective-permute-start.4 = (f32[13,8,128]{2,1,0:T(8,128)S(1)}, f32[13,8,128]{2,1,0:T(8,128)S(1)}, u32[]{:S(2)}, u32[]{:S(2)}) collective-permute-start(f32[13,8,128]{2,1,0:T(8,128)S(1)} %get-tuple-element.26), channel_id=1, source_target_pairs={{0,8},{1,5},{2,10},{3,7},{4,12},{5,1},{6,14},{7,3},{8,0},{9,13},{1... | collective-permute-start | bytes 159752 | tf_op jit(solution)/shard_map/ppermute | solution.py:406
  19.9 11.5 %collective-permute-start.15 = (f32[21,8,128]{2,1,0:T(8,128)S(1)}, f32[21,8,128]{2,1,0:T(8,128)S(1)}, u32[]{:S(2)}, u32[]{:S(2)}) collective-permute-start(f32[21,8,128]{2,1,0:T(8,128)S(1)} %shard_map.63.refs_0_.refs_4_), channel_id=1, source_target_pairs={{0,12},{1,13},{2,14},{3,15},{4,8},{5,9},{6,10},{7,11},{8,4},{9,5},... | collective-permute-start | bytes 258056 | tf_op jit(solution)/shard_map/ppermute | solution.py:406
  23.9 5.5 %collective-permute-start.5 = (f32[13,8,128]{2,1,0:T(8,128)S(1)}, f32[13,8,128]{2,1,0:T(8,128)S(1)}, u32[]{:S(2)}, u32[]{:S(2)}) collective-permute-start(f32[13,8,128]{2,1,0:T(8,128)S(1)} %shard_map.60.refs_0_), channel_id=1, source_target_pairs={{0,16},{4,20},{8,24},{12,28},{16,0},{20,4},{24,8},{28,12},{1,17},{... | collective-permute-start | bytes 159752 | tf_op jit(solution)/shard_map/ppermute | solution.py:413
  24.8 8.2 %collective-permute-start.14 = (f32[21,8,128]{2,1,0:T(8,128)S(1)}, f32[21,8,128]{2,1,0:T(8,128)S(1)}, u32[]{:S(2)}, u32[]{:S(2)}) collective-permute-start(f32[21,8,128]{2,1,0:T(8,128)S(1)} %shard_map.63.refs_0_.refs_4_), channel_id=1, source_target_pairs={{0,8},{1,5},{2,10},{3,7},{4,12},{5,1},{6,14},{7,3},{8,0},{9,13},{1... | collective-permute-start | bytes 258056 | tf_op jit(solution)/shard_map/ppermute | solution.py:406
  25.4 7.7 %collective-permute-start.13 = (f32[21,8,128]{2,1,0:T(8,128)S(1)}, f32[21,8,128]{2,1,0:T(8,128)S(1)}, u32[]{:S(2)}, u32[]{:S(2)}) collective-permute-start(f32[21,8,128]{2,1,0:T(8,128)S(1)} %shard_map.63.refs_0_.refs_4_), channel_id=1, source_target_pairs={{0,4},{1,9},{2,6},{3,11},{4,0},{5,13},{6,2},{7,15},{8,12},{9,1},{1... | collective-permute-start | bytes 258056 | tf_op jit(solution)/shard_map/ppermute | solution.py:406
  29.5 5.1 %collective-permute-start.8 = (f32[13,8,128]{2,1,0:T(8,128)S(1)}, f32[13,8,128]{2,1,0:T(8,128)S(1)}, u32[]{:S(2)}, u32[]{:S(2)}) collective-permute-start(f32[13,8,128]{2,1,0:T(8,128)S(1)} %shard_map.61.refs_0_), channel_id=1, source_target_pairs={{0,12},{1,13},{2,14},{3,15},{4,8},{5,9},{6,10},{7,11},{8,4},{9,5},... | collective-permute-start | bytes 159752 | tf_op jit(solution)/shard_map/ppermute | solution.py:406
  30.9 4.1 %collective-permute-start.7 = (f32[13,8,128]{2,1,0:T(8,128)S(1)}, f32[13,8,128]{2,1,0:T(8,128)S(1)}, u32[]{:S(2)}, u32[]{:S(2)}) collective-permute-start(f32[13,8,128]{2,1,0:T(8,128)S(1)} %shard_map.61.refs_0_), channel_id=1, source_target_pairs={{0,8},{1,5},{2,10},{3,7},{4,12},{5,1},{6,14},{7,3},{8,0},{9,13},{1... | collective-permute-start | bytes 159752 | tf_op jit(solution)/shard_map/ppermute | solution.py:406
  31.4 4.1 %collective-permute-start.6 = (f32[13,8,128]{2,1,0:T(8,128)S(1)}, f32[13,8,128]{2,1,0:T(8,128)S(1)}, u32[]{:S(2)}, u32[]{:S(2)}) collective-permute-start(f32[13,8,128]{2,1,0:T(8,128)S(1)} %shard_map.61.refs_0_), channel_id=1, source_target_pairs={{0,4},{1,9},{2,6},{3,11},{4,0},{5,13},{6,2},{7,15},{8,12},{9,1},{1... | collective-permute-start | bytes 159752 | tf_op jit(solution)/shard_map/ppermute | solution.py:406

commit v21 on v19

--- a/solution.py
+++ b/solution.py
@@ -49,15 +49,14 @@
     lax.fori_loop(0, strips, step, 0, unroll=unroll)
 
 
-def advance(first, count, classes, source, coefs, emit):
-    shape = source.shape[2:]
-    lanes = lax.broadcasted_iota(jnp.int32, shape, 1)
-    center, above_c, below_c, side = coefs
+def advance(first, count, classes, strip, coefs, emit):
+    prev, cur = strip(first - 1), strip(first)
+    lanes = lax.broadcasted_iota(jnp.int32, cur[0].shape, 1)
 
     def body(k, carry):
         j = first + k
         cur, right_prev, left_cur = carry
-        nxt = [source[j + 2, t] for t in range(classes)]
+        nxt = strip(j + 1)
         left_next = [pltpu.roll(x, LANES - 1, 1) for x in nxt]
         right_cur = [pltpu.roll(x, 1, 1) for x in cur]
         above = cur[1:] + [roll_rows(cur[0], -1)]
@@ -66,46 +65,52 @@
         for t in range(classes):
             left = jnp.where(lanes == 0, right_prev[t], right_cur[t])
             right = jnp.where(lanes == LANES - 1, left_next[t], left_cur[t])
+            center, above_c, below_c, side = coefs(j, t)
             new.append(
-                center[j, t] * cur[t]
-                + above_c[j, t] * above[t]
-                + below_c[j, t] * below[t]
-                + side[j, t] * (left + right)
+                center * cur[t] + above_c * above[t] + below_c * below[t] + side * (left + right)
             )
         emit(j, k, new)
         return nxt, right_cur, left_next
 
-    prev, cur = ([source[first + at, t] for t in range(classes)] for at in range(2))
     ends = [pltpu.roll(x, 1, 1) for x in prev], [pltpu.roll(x, LANES - 1, 1) for x in cur]
     lax.fori_loop(0, count, body, (cur, *ends), unroll=min(count, UNROLL))
 
 
 def run_steps(strips, classes, load, buffers, coefs, last):
-    center, above_c, below_c, side = coefs
     for buf in buffers:
         for edge in (0, strips + 1):
             buf[edge] = jnp.zeros(buf.shape[1:], jnp.float32)
 
-    def begin(j):
-        for t in range(classes):
-            state, diffuse, drifts = load(j, t)
-            half = 0.5 * drifts
-            buffers[0][j + 1, t] = state
-            center[j, t] = 1.0 - 4.0 * diffuse
-            above_c[j, t] = diffuse - half
-            below_c[j, t] = diffuse + half
-            side[j, t] = diffuse
-
-    per_strip(strips, begin, min(strips, UNROLL))
+    def first_strip(j):
+        if isinstance(j, int) and j < 0:
+            return [jnp.zeros(buffers[0].shape[2:], jnp.float32)] * classes
+        inside = jnp.minimum(j, strips - 1)
+        return [jnp.where(j < strips, load(0, inside, t), 0.0) for t in range(classes)]
+
+    def first_coefs(j, t):
+        diffuse, half = load(1, j, t), 0.5 * load(2, j, t)
+        made = 1.0 - 4.0 * diffuse, diffuse - half, diffuse + half, diffuse
+        for ref, value in zip(coefs, made):
+            ref[j, t] = value
+        return made
+
+    def kept_strip(buf):
+        return lambda j: [buf[j + 1, t] for t in range(classes)]
+
+    def kept_coefs(j, t):
+        return [ref[j, t] for ref in coefs]
+
+    strip, now = first_strip, first_coefs
     for step in range(STEPS - 1):
-        source, target = buffers[step % 2], buffers[1 - step % 2]
+        target = buffers[step % 2]
 
         def keep(j, _, new, target=target):
             for t in range(classes):
                 target[j + 1, t] = new[t]
 
-        advance(0, strips, classes, source, coefs, keep)
-    last(buffers[(STEPS - 1) % 2])
+        advance(0, strips, classes, strip, now, keep)
+        strip, now = kept_strip(target), kept_coefs
+    last(strip, now)
 
 
 def surpluses(s, prev, weights):
@@ -182,9 +187,8 @@
     weights = [weight_ref[k] for k in range(4)]
     tiles = middle_tiles(many)
 
-    def load(j, t):
-        at = spaced(j * TILE + t, many, strips * TILE)
-        return [ref[at, :] for ref in rows]
+    def load(k, j, t):
+        return rows[k][spaced(j * TILE + t, many, strips * TILE), :]
 
     def finish(out_ref, j, part, new):
         for t in range(TILE):
@@ -194,11 +198,11 @@
             before = weighted[7][tiles[0] - 1 : tiles[0]]
             emit_tiles(tiles, per_chunk, scratch, out_ref, j, part, weighted, before)
 
-    def last(source):
+    def last(strip, now):
         for out_ref, away in zip(out_refs or [None] * SQUARE, partners(dom_ref[0])):
             first = (me_ref[0] ^ away) * per_chunk
             emit = functools.partial(finish, out_ref)
-            advance(first, per_chunk, TILE, source, coefs, emit)
+            advance(first, per_chunk, TILE, strip, now, emit)
 
     run_steps(strips, TILE, load, (state_a, state_b), coefs, last)
 
@@ -238,10 +242,8 @@
     per_strip(strips, stage, 4)
     slabs = flat(slab)
 
-    def load(j, t):
-        return [
-            slabs[pl.ds((k * strips + j) * SLAB + t, TILE, stride=HALF), :] for k in range(3)
-        ]
+    def load(k, j, t):
+        return slabs[pl.ds((k * strips + j) * SLAB + t, TILE, stride=HALF), :]
 
     place = lax.broadcasted_iota(jnp.int32, (many, LANES), 0)
     weights = [weight_ref[k] for k in range(4)]
@@ -257,11 +259,11 @@
         tiles = outer_tiles(many)
         emit_tiles(tiles, per_chunk, scratch, out_ref, j, part, weighted, before)
 
-    def last(source):
+    def last(strip, now):
         for out_ref, away in zip(out_refs, partners(dom_ref[0])):
             first = (me_ref[0] ^ away) * per_chunk
             emit = functools.partial(finish, out_ref)
-            advance(first, per_chunk, HALF, source, coefs, emit)
+            advance(first, per_chunk, HALF, strip, now, emit)
 
     run_steps(strips, HALF, load, (state_a, state_b), coefs, last)
 

time: 33 us -> 33 us (level)
  no operation moved by 1% of the time
where the time goes in v21:
time: 33 us; the launch traced here: 32.8 us
  starting transfers between devices  21.4 us (65%)
  Pallas kernels  5.04 us (15%)
  waiting for transfers between devices  4.87 us (15%)
  between operations  1.51 us (5%)
    ppermute x12, starting transfers between devices, swap(): return lax.ppermute(array, ('grp', 'dom'), pairs)  14.9 us
    ppermute x2, starting transfers between devices, over_grids(): other = lax.ppermute(total, 'grp', [(g, g ^ apart) for g in range(grids)])  5.3 us
    pallas_call x11, Pallas kernels, call(): pl.pallas_call(kernel, out_shape=[jax.ShapeDtypeStruct(shape, jnp.float32...  5.04 us
    ppermute x12, waiting for transfers between devices, swap(): return lax.ppermute(array, ('grp', 'dom'), pairs)  3.94 us
    ppermute x2, waiting for transfers between devices, over_grids(): other = lax.ppermute(total, 'grp', [(g, g ^ apart) for g in range(grids)])  0.93 us
  transfers between devices with their start and end apart: 16, of which 7 were waited for; matrix products, arithmetic and copies ran while one was open for 0% of the time, Pallas kernels for 12%

profile of v21, /device:TPU:0, one launch (start us, length us, event | category | flops | bytes accessed | tf_op | source)
XLA Modules:
  0.0 32.8 jit_solution(9026291625332660973)
XLA Ops:
  0.0 0.0 copy-start
  0.0 0.0 copy-start.1
  0.0 0.0 copy-start.2
  1.4 0.0 copy-done
  1.5 0.0 copy-done.1
  1.5 0.0 copy-done.2
  1.5 0.1 shard_map.58
  1.5 0.5 %collective-permute-start = (f32[16,16,128]{2,1,0:T(8,128)S(1)}, f32[16,16,128]{2,1,0:T(8,128)S(1)}, u32[]{:S(2)}, u32[]{:S(2)}) collective-permute-start(f32[16,16,128]{2,1,0:T(8,128)S(1)} %get-tuple-element.21), channel_id=1, source_target_pairs={{0,1},{1,0},{2,3},{3,2},{4,5},{5,4},{6,7},{7,6},{8,9},{9,8},{10,11... | collective-permute-start | bytes 393224 | tf_op jit(solution)/shard_map/ppermute | solution.py:377
  2.1 0.7 %collective-permute-start.1 = (f32[16,16,128]{2,1,0:T(8,128)S(1)}, f32[16,16,128]{2,1,0:T(8,128)S(1)}, u32[]{:S(2)}, u32[]{:S(2)}) collective-permute-start(f32[16,16,128]{2,1,0:T(8,128)S(1)} %get-tuple-element.22), channel_id=1, source_target_pairs={{0,0},{1,2},{2,1},{3,3},{4,4},{5,6},{6,5},{7,7},{8,8},{9,10},{10,9... | collective-permute-start | bytes 393224 | tf_op jit(solution)/shard_map/ppermute | solution.py:378
  2.7 2.1 %shard_map.57 = (f32[16,8,8,128]{3,2,1,0:T(8,128)S(1)}, f32[17,8,128]{2,1,0:T(8,128)S(1)}, f32[17,8,128]{2,1,0:T(8,128)S(1)}, f32[17,8,128]{2,1,0:T(8,128)S(1)}, f32[17,8,128]{2,1,0:T(8,128)S(1)}) custom-call(s32[1]{0:T(128)} %bitcast.dom_ref, s32[1]{0:T(128)} %bitcast.1.me_ref, f32[4,8,128]{2,1,0:T(8,128)S(1)} %get-tuple-element.19.weight_ref, ...), custom_call_target="tpu_custom_call" | custom-call | flops 5242880 | bytes 1589256 | tf_op jit(solution)/shard_map/pallas_call | solution.py:337
  4.8 3.6 %collective-permute-start.9 = (f32[17,8,128]{2,1,0:T(8,128)S(1)}, f32[17,8,128]{2,1,0:T(8,128)S(1)}, u32[]{:S(2)}, u32[]{:S(2)}) collective-permute-start(f32[17,8,128]{2,1,0:T(8,128)S(1)} %get-tuple-element.28), channel_id=1, source_target_pairs={{0,12},{1,13},{2,14},{3,15},{4,8},{5,9},{6,10},{7,11},{8,4},{9,5},... | collective-permute-start | bytes 208904 | tf_op jit(solution)/shard_map/ppermute | solution.py:408
  8.4 0.5 %collective-permute-start.10 = (f32[17,8,128]{2,1,0:T(8,128)S(1)}, f32[17,8,128]{2,1,0:T(8,128)S(1)}, u32[]{:S(2)}, u32[]{:S(2)}) collective-permute-start(f32[17,8,128]{2,1,0:T(8,128)S(1)} %get-tuple-element.29), channel_id=1, source_target_pairs={{0,4},{1,9},{2,6},{3,11},{4,0},{5,13},{6,2},{7,15},{8,12},{9,1},{1... | collective-permute-start | bytes 208904 | tf_op jit(solution)/shard_map/ppermute | solution.py:408
  8.9 0.1 collective-permute-start.11
  9.0 0.0 collective-permute-done.refs_3_
  9.0 0.0 collective-permute-done.1.refs_4_
  9.0 0.9 %shard_map.59 = (f32[17,8,128]{2,1,0:T(8,128)S(1)}, f32[17,8,128]{2,1,0:T(8,128)S(1)}, f32[17,8,128]{2,1,0:T(8,128)S(1)}, f32[17,8,128]{2,1,0:T(8,128)S(1)}) custom-call(s32[1]{0:T(128)} %bitcast.dom_ref, s32[1]{0:T(128)} %bitcast.1.me_ref, f32[4,8,128]{2,1,0:T(8,128)S(1)} %get-tuple-element.19.weight_ref, f32[8,16,8,128]{3,2,1,0:T(8,128)S(1)} %bitcast.16, ...), custom_call_target="tpu_custom_call" | custom-call | flops 2621440 | bytes 2375688 | tf_op jit(solution)/shard_map/pallas_call | solution.py:337
  10.0 2.9 %collective-permute-start.2 = (f32[17,8,128]{2,1,0:T(8,128)S(1)}, f32[17,8,128]{2,1,0:T(8,128)S(1)}, u32[]{:S(2)}, u32[]{:S(2)}) collective-permute-start(f32[17,8,128]{2,1,0:T(8,128)S(1)} %get-tuple-element.24), channel_id=1, source_target_pairs={{0,12},{1,13},{2,14},{3,15},{4,8},{5,9},{6,10},{7,11},{8,4},{9,5},... | collective-permute-start | bytes 208904 | tf_op jit(solution)/shard_map/ppermute | solution.py:408
  12.9 0.5 %collective-permute-start.3 = (f32[17,8,128]{2,1,0:T(8,128)S(1)}, f32[17,8,128]{2,1,0:T(8,128)S(1)}, u32[]{:S(2)}, u32[]{:S(2)}) collective-permute-start(f32[17,8,128]{2,1,0:T(8,128)S(1)} %get-tuple-element.25), channel_id=1, source_target_pairs={{0,4},{1,9},{2,6},{3,11},{4,0},{5,13},{6,2},{7,15},{8,12},{9,1},{1... | collective-permute-start | bytes 208904 | tf_op jit(solution)/shard_map/ppermute | solution.py:408
  13.4 0.0 collective-permute-done.9.refs_1_
  13.4 0.1 collective-permute-start.4
  13.5 0.0 collective-permute-done.10.refs_2_
  13.5 0.4 %collective-permute-done.11.refs_3_ = f32[17,8,128]{2,1,0:T(8,128)S(1)} collective-permute-done((f32[17,8,128]{2,1,0:T(8,128)S(1)}, f32[17,8,128]{2,1,0:T(8,128)S(1)}, u32[]{:S(2)}, u32[]{:S(2)}) %collective-permute-start.11) | collective-permute-done | bytes 69664 | tf_op jit(solution)/shard_map/ppermute | solution.py:408
  14.0 2.7 %collective-permute-start.12 = (f32[17,8,128]{2,1,0:T(8,128)S(1)}, f32[17,8,128]{2,1,0:T(8,128)S(1)}, u32[]{:S(2)}, u32[]{:S(2)}) collective-permute-start(f32[17,8,128]{2,1,0:T(8,128)S(1)} %shard_map.62.refs_0_), channel_id=1, source_target_pairs={{0,16},{4,20},{8,24},{12,28},{16,0},{20,4},{24,8},{28,12},{1,17},{... | collective-permute-start | bytes 208904 | tf_op jit(solution)/shard_map/ppermute | solution.py:415
  16.6 0.0 collective-permute-done.2.refs_1_
  16.6 0.8 %collective-permute-done.3.refs_2_ = f32[17,8,128]{2,1,0:T(8,128)S(1)} collective-permute-done((f32[17,8,128]{2,1,0:T(8,128)S(1)}, f32[17,8,128]{2,1,0:T(8,128)S(1)}, u32[]{:S(2)}, u32[]{:S(2)}) %collective-permute-start.3) | collective-permute-done | bytes 69664 | tf_op jit(solution)/shard_map/ppermute | solution.py:408
  17.4 0.8 %collective-permute-done.4.refs_3_ = f32[17,8,128]{2,1,0:T(8,128)S(1)} collective-permute-done((f32[17,8,128]{2,1,0:T(8,128)S(1)}, f32[17,8,128]{2,1,0:T(8,128)S(1)}, u32[]{:S(2)}, u32[]{:S(2)}) %collective-permute-start.4) | collective-permute-done | bytes 69664 | tf_op jit(solution)/shard_map/ppermute | solution.py:408
  18.3 2.6 %collective-permute-start.5 = (f32[17,8,128]{2,1,0:T(8,128)S(1)}, f32[17,8,128]{2,1,0:T(8,128)S(1)}, u32[]{:S(2)}, u32[]{:S(2)}) collective-permute-start(f32[17,8,128]{2,1,0:T(8,128)S(1)} %shard_map.60.refs_0_), channel_id=1, source_target_pairs={{0,16},{4,20},{8,24},{12,28},{16,0},{20,4},{24,8},{28,12},{1,17},{... | collective-permute-start | bytes 208904 | tf_op jit(solution)/shard_map/ppermute | solution.py:415
  20.9 0.0 collective-permute-done.12.refs_1_
  20.9 2.1 %collective-permute-start.15 = (f32[17,8,128]{2,1,0:T(8,128)S(1)}, f32[17,8,128]{2,1,0:T(8,128)S(1)}, u32[]{:S(2)}, u32[]{:S(2)}) collective-permute-start(f32[17,8,128]{2,1,0:T(8,128)S(1)} %shard_map.63.refs_0_.refs_4_), channel_id=1, source_target_pairs={{0,12},{1,13},{2,14},{3,15},{4,8},{5,9},{6,10},{7,11},{8,4},{9,5},... | collective-permute-start | bytes 208904 | tf_op jit(solution)/shard_map/ppermute | solution.py:408
  23.1 0.6 %collective-permute-start.14 = (f32[17,8,128]{2,1,0:T(8,128)S(1)}, f32[17,8,128]{2,1,0:T(8,128)S(1)}, u32[]{:S(2)}, u32[]{:S(2)}) collective-permute-start(f32[17,8,128]{2,1,0:T(8,128)S(1)} %shard_map.63.refs_0_.refs_4_), channel_id=1, source_target_pairs={{0,8},{1,5},{2,10},{3,7},{4,12},{5,1},{6,14},{7,3},{8,0},{9,13},{1... | collective-permute-start | bytes 208904 | tf_op jit(solution)/shard_map/ppermute | solution.py:408
  23.6 0.8 %collective-permute-start.13 = (f32[17,8,128]{2,1,0:T(8,128)S(1)}, f32[17,8,128]{2,1,0:T(8,128)S(1)}, u32[]{:S(2)}, u32[]{:S(2)}) collective-permute-start(f32[17,8,128]{2,1,0:T(8,128)S(1)} %shard_map.63.refs_0_.refs_4_), channel_id=1, source_target_pairs={{0,4},{1,9},{2,6},{3,11},{4,0},{5,13},{6,2},{7,15},{8,12},{9,1},{1... | collective-permute-start | bytes 208904 | tf_op jit(solution)/shard_map/ppermute | solution.py:408
  24.5 0.9 %collective-permute-done.5.refs_1_ = f32[17,8,128]{2,1,0:T(8,128)S(1)} collective-permute-done((f32[17,8,128]{2,1,0:T(8,128)S(1)}, f32[17,8,128]{2,1,0:T(8,128)S(1)}, u32[]{:S(2)}, u32[]{:S(2)}) %collective-permute-start.5) | collective-permute-done | bytes 69664 | tf_op jit(solution)/shard_map/ppermute | solution.py:415
  25.4 1.2 %collective-permute-start.8 = (f32[17,8,128]{2,1,0:T(8,128)S(1)}, f32[17,8,128]{2,1,0:T(8,128)S(1)}, u32[]{:S(2)}, u32[]{:S(2)}) collective-permute-start(f32[17,8,128]{2,1,0:T(8,128)S(1)} %shard_map.61.refs_0_), channel_id=1, source_target_pairs={{0,12},{1,13},{2,14},{3,15},{4,8},{5,9},{6,10},{7,11},{8,4},{9,5},... | collective-permute-start | bytes 208904 | tf_op jit(solution)/shard_map/ppermute | solution.py:408
  26.6 0.9 %collective-permute-start.7 = (f32[17,8,128]{2,1,0:T(8,128)S(1)}, f32[17,8,128]{2,1,0:T(8,128)S(1)}, u32[]{:S(2)}, u32[]{:S(2)}) collective-permute-start(f32[17,8,128]{2,1,0:T(8,128)S(1)} %shard_map.61.refs_0_), channel_id=1, source_target_pairs={{0,8},{1,5},{2,10},{3,7},{4,12},{5,1},{6,14},{7,3},{8,0},{9,13},{1... | collective-permute-start | bytes 208904 | tf_op jit(solution)/shard_map/ppermute | solution.py:408
  27.5 0.0 collective-permute-done.15.refs_3_.refs_7_
  27.5 1.4 %collective-permute-start.6 = (f32[17,8,128]{2,1,0:T(8,128)S(1)}, f32[17,8,128]{2,1,0:T(8,128)S(1)}, u32[]{:S(2)}, u32[]{:S(2)}) collective-permute-start(f32[17,8,128]{2,1,0:T(8,128)S(1)} %shard_map.61.refs_0_), channel_id=1, source_target_pairs={{0,4},{1,9},{2,6},{3,11},{4,0},{5,13},{6,2},{7,15},{8,12},{9,1},{1... | collective-permute-start | bytes 208904 | tf_op jit(solution)/shard_map/ppermute | solution.py:408
  29.0 0.0 collective-permute-done.14.refs_2_.refs_6_
  29.0 0.0 collective-permute-done.13.refs_1_.refs_5_
  29.0 1.0 %shard_map.64.refs_8_ = f32[8,16,8,128]{3,2,1,0:T(8,128)} custom-call(s32[1]{0:T(128)} %bitcast.dom_ref, s32[1]{0:T(128)} %bitcast.1.me_ref, f32[3,8,128]{2,1,0:T(8,128)S(1)} %get-tuple-element.18.keep_ref, f32[17,8,128]{2,1,0:T(8,128)S(1)} %shard_map.63.refs_0_.refs_4_, f32[17,8,128]{2,1,0:T(8,128)S(1)} %collective-permute-done.13.refs_1_.refs_5_, ...), custom_call_target="tpu_custom_call" | custom-call | bytes 290824 | tf_op jit(solution)/shard_map/pallas_call | solution.py:337
  30.0 1.0 %collective-permute-done.8.refs_3_ = f32[17,8,128]{2,1,0:T(8,128)S(1)} collective-permute-done((f32[17,8,128]{2,1,0:T(8,128)S(1)}, f32[17,8,128]{2,1,0:T(8,128)S(1)}, u32[]{:S(2)}, u32[]{:S(2)}) %collective-permute-start.8) | collective-permute-done | bytes 69664 | tf_op jit(solution)/shard_map/ppermute | solution.py:408
  31.0 0.4 %collective-permute-done.7.refs_2_ = f32[17,8,128]{2,1,0:T(8,128)S(1)} collective-permute-done((f32[17,8,128]{2,1,0:T(8,128)S(1)}, f32[17,8,128]{2,1,0:T(8,128)S(1)}, u32[]{:S(2)}, u32[]{:S(2)}) %collective-permute-start.7) | collective-permute-done | bytes 69664 | tf_op jit(solution)/shard_map/ppermute | solution.py:408
  31.4 0.4 %collective-permute-done.6.refs_1_ = f32[17,8,128]{2,1,0:T(8,128)S(1)} collective-permute-done((f32[17,8,128]{2,1,0:T(8,128)S(1)}, f32[17,8,128]{2,1,0:T(8,128)S(1)}, u32[]{:S(2)}, u32[]{:S(2)}) %collective-permute-start.6) | collective-permute-done | bytes 69664 | tf_op jit(solution)/shard_map/ppermute | solution.py:408
  31.9 1.0 %shard_map.65 = f32[8,16,8,128]{3,2,1,0:T(8,128)} custom-call(s32[1]{0:T(128)} %bitcast.dom_ref, s32[1]{0:T(128)} %bitcast.1.me_ref, f32[3,8,128]{2,1,0:T(8,128)S(1)} %get-tuple-element.18.keep_ref, f32[17,8,128]{2,1,0:T(8,128)S(1)} %shard_map.61.refs_0_, f32[17,8,128]{2,1,0:T(8,128)S(1)} %collective-permute-done.6.refs_1_, ...), custom_call_target="tpu_custom_call", output_to_operand_aliasing={{}: (11, {})} | custom-call | bytes 1093640 | tf_op jit(solution)/shard_map/pallas_call | solution.py:337
  (6 shorter events, 0.1 us)
Async XLA Ops:
  0.0 1.4 %copy-start = (f32[1,64,2048]{2,1,0:T(8,128)S(1)}, f32[1,64,2048]{2,1,0:T(8,128)}, u32[]{:S(2)}) copy-start(f32[1,64,2048]{2,1,0:T(8,128)} %param.5) | copy-start | bytes 1572868
  0.0 1.5 %copy-start.1 = (f32[1,64,2048]{2,1,0:T(8,128)S(1)}, f32[1,64,2048]{2,1,0:T(8,128)}, u32[]{:S(2)}) copy-start(f32[1,64,2048]{2,1,0:T(8,128)} %param.6) | copy-start | bytes 1572868
  0.0 1.5 %copy-start.2 = (f32[1,64,2048]{2,1,0:T(8,128)S(1)}, f32[1,64,2048]{2,1,0:T(8,128)}, u32[]{:S(2)}) copy-start(f32[1,64,2048]{2,1,0:T(8,128)} %param.7) | copy-start | bytes 1572868
  1.5 7.5 %collective-permute-start = (f32[16,16,128]{2,1,0:T(8,128)S(1)}, f32[16,16,128]{2,1,0:T(8,128)S(1)}, u32[]{:S(2)}, u32[]{:S(2)}) collective-permute-start(f32[16,16,128]{2,1,0:T(8,128)S(1)} %get-tuple-element.21), channel_id=1, source_target_pairs={{0,1},{1,0},{2,3},{3,2},{4,5},{5,4},{6,7},{7,6},{8,9},{9,8},{10,11... | collective-permute-start | bytes 393224 | tf_op jit(solution)/shard_map/ppermute | solution.py:377
  2.1 7.0 %collective-permute-start.1 = (f32[16,16,128]{2,1,0:T(8,128)S(1)}, f32[16,16,128]{2,1,0:T(8,128)S(1)}, u32[]{:S(2)}, u32[]{:S(2)}) collective-permute-start(f32[16,16,128]{2,1,0:T(8,128)S(1)} %get-tuple-element.22), channel_id=1, source_target_pairs={{0,0},{1,2},{2,1},{3,3},{4,4},{5,6},{6,5},{7,7},{8,8},{9,10},{10,9... | collective-permute-start | bytes 393224 | tf_op jit(solution)/shard_map/ppermute | solution.py:378
  4.8 8.6 %collective-permute-start.9 = (f32[17,8,128]{2,1,0:T(8,128)S(1)}, f32[17,8,128]{2,1,0:T(8,128)S(1)}, u32[]{:S(2)}, u32[]{:S(2)}) collective-permute-start(f32[17,8,128]{2,1,0:T(8,128)S(1)} %get-tuple-element.28), channel_id=1, source_target_pairs={{0,12},{1,13},{2,14},{3,15},{4,8},{5,9},{6,10},{7,11},{8,4},{9,5},... | collective-permute-start | bytes 208904 | tf_op jit(solution)/shard_map/ppermute | solution.py:408
  8.4 5.1 %collective-permute-start.10 = (f32[17,8,128]{2,1,0:T(8,128)S(1)}, f32[17,8,128]{2,1,0:T(8,128)S(1)}, u32[]{:S(2)}, u32[]{:S(2)}) collective-permute-start(f32[17,8,128]{2,1,0:T(8,128)S(1)} %get-tuple-element.29), channel_id=1, source_target_pairs={{0,4},{1,9},{2,6},{3,11},{4,0},{5,13},{6,2},{7,15},{8,12},{9,1},{1... | collective-permute-start | bytes 208904 | tf_op jit(solution)/shard_map/ppermute | solution.py:408
  8.9 5.0 %collective-permute-start.11 = (f32[17,8,128]{2,1,0:T(8,128)S(1)}, f32[17,8,128]{2,1,0:T(8,128)S(1)}, u32[]{:S(2)}, u32[]{:S(2)}) collective-permute-start(f32[17,8,128]{2,1,0:T(8,128)S(1)} %get-tuple-element.30), channel_id=1, source_target_pairs={{0,8},{1,5},{2,10},{3,7},{4,12},{5,1},{6,14},{7,3},{8,0},{9,13},{1... | collective-permute-start | bytes 208904 | tf_op jit(solution)/shard_map/ppermute | solution.py:408
  10.0 6.7 %collective-permute-start.2 = (f32[17,8,128]{2,1,0:T(8,128)S(1)}, f32[17,8,128]{2,1,0:T(8,128)S(1)}, u32[]{:S(2)}, u32[]{:S(2)}) collective-permute-start(f32[17,8,128]{2,1,0:T(8,128)S(1)} %get-tuple-element.24), channel_id=1, source_target_pairs={{0,12},{1,13},{2,14},{3,15},{4,8},{5,9},{6,10},{7,11},{8,4},{9,5},... | collective-permute-start | bytes 208904 | tf_op jit(solution)/shard_map/ppermute | solution.py:408
  12.9 4.5 %collective-permute-start.3 = (f32[17,8,128]{2,1,0:T(8,128)S(1)}, f32[17,8,128]{2,1,0:T(8,128)S(1)}, u32[]{:S(2)}, u32[]{:S(2)}) collective-permute-start(f32[17,8,128]{2,1,0:T(8,128)S(1)} %get-tuple-element.25), channel_id=1, source_target_pairs={{0,4},{1,9},{2,6},{3,11},{4,0},{5,13},{6,2},{7,15},{8,12},{9,1},{1... | collective-permute-start | bytes 208904 | tf_op jit(solution)/shard_map/ppermute | solution.py:408
  13.4 4.8 %collective-permute-start.4 = (f32[17,8,128]{2,1,0:T(8,128)S(1)}, f32[17,8,128]{2,1,0:T(8,128)S(1)}, u32[]{:S(2)}, u32[]{:S(2)}) collective-permute-start(f32[17,8,128]{2,1,0:T(8,128)S(1)} %get-tuple-element.26), channel_id=1, source_target_pairs={{0,8},{1,5},{2,10},{3,7},{4,12},{5,1},{6,14},{7,3},{8,0},{9,13},{1... | collective-permute-start | bytes 208904 | tf_op jit(solution)/shard_map/ppermute | solution.py:408
  14.0 6.9 %collective-permute-start.12 = (f32[17,8,128]{2,1,0:T(8,128)S(1)}, f32[17,8,128]{2,1,0:T(8,128)S(1)}, u32[]{:S(2)}, u32[]{:S(2)}) collective-permute-start(f32[17,8,128]{2,1,0:T(8,128)S(1)} %shard_map.62.refs_0_), channel_id=1, source_target_pairs={{0,16},{4,20},{8,24},{12,28},{16,0},{20,4},{24,8},{28,12},{1,17},{... | collective-permute-start | bytes 208904 | tf_op jit(solution)/shard_map/ppermute | solution.py:415
  18.3 7.2 %collective-permute-start.5 = (f32[17,8,128]{2,1,0:T(8,128)S(1)}, f32[17,8,128]{2,1,0:T(8,128)S(1)}, u32[]{:S(2)}, u32[]{:S(2)}) collective-permute-start(f32[17,8,128]{2,1,0:T(8,128)S(1)} %shard_map.60.refs_0_), channel_id=1, source_target_pairs={{0,16},{4,20},{8,24},{12,28},{16,0},{20,4},{24,8},{28,12},{1,17},{... | collective-permute-start | bytes 208904 | tf_op jit(solution)/shard_map/ppermute | solution.py:415
  20.9 6.6 %collective-permute-start.15 = (f32[17,8,128]{2,1,0:T(8,128)S(1)}, f32[17,8,128]{2,1,0:T(8,128)S(1)}, u32[]{:S(2)}, u32[]{:S(2)}) collective-permute-start(f32[17,8,128]{2,1,0:T(8,128)S(1)} %shard_map.63.refs_0_.refs_4_), channel_id=1, source_target_pairs={{0,12},{1,13},{2,14},{3,15},{4,8},{5,9},{6,10},{7,11},{8,4},{9,5},... | collective-permute-start | bytes 208904 | tf_op jit(solution)/shard_map/ppermute | solution.py:408
  23.1 5.9 %collective-permute-start.14 = (f32[17,8,128]{2,1,0:T(8,128)S(1)}, f32[17,8,128]{2,1,0:T(8,128)S(1)}, u32[]{:S(2)}, u32[]{:S(2)}) collective-permute-start(f32[17,8,128]{2,1,0:T(8,128)S(1)} %shard_map.63.refs_0_.refs_4_), channel_id=1, source_target_pairs={{0,8},{1,5},{2,10},{3,7},{4,12},{5,1},{6,14},{7,3},{8,0},{9,13},{1... | collective-permute-start | bytes 208904 | tf_op jit(solution)/shard_map/ppermute | solution.py:408
  23.6 5.3 %collective-permute-start.13 = (f32[17,8,128]{2,1,0:T(8,128)S(1)}, f32[17,8,128]{2,1,0:T(8,128)S(1)}, u32[]{:S(2)}, u32[]{:S(2)}) collective-permute-start(f32[17,8,128]{2,1,0:T(8,128)S(1)} %shard_map.63.refs_0_.refs_4_), channel_id=1, source_target_pairs={{0,4},{1,9},{2,6},{3,11},{4,0},{5,13},{6,2},{7,15},{8,12},{9,1},{1... | collective-permute-start | bytes 208904 | tf_op jit(solution)/shard_map/ppermute | solution.py:408
  25.4 5.6 %collective-permute-start.8 = (f32[17,8,128]{2,1,0:T(8,128)S(1)}, f32[17,8,128]{2,1,0:T(8,128)S(1)}, u32[]{:S(2)}, u32[]{:S(2)}) collective-permute-start(f32[17,8,128]{2,1,0:T(8,128)S(1)} %shard_map.61.refs_0_), channel_id=1, source_target_pairs={{0,12},{1,13},{2,14},{3,15},{4,8},{5,9},{6,10},{7,11},{8,4},{9,5},... | collective-permute-start | bytes 208904 | tf_op jit(solution)/shard_map/ppermute | solution.py:408
  26.6 4.8 %collective-permute-start.7 = (f32[17,8,128]{2,1,0:T(8,128)S(1)}, f32[17,8,128]{2,1,0:T(8,128)S(1)}, u32[]{:S(2)}, u32[]{:S(2)}) collective-permute-start(f32[17,8,128]{2,1,0:T(8,128)S(1)} %shard_map.61.refs_0_), channel_id=1, source_target_pairs={{0,8},{1,5},{2,10},{3,7},{4,12},{5,1},{6,14},{7,3},{8,0},{9,13},{1... | collective-permute-start | bytes 208904 | tf_op jit(solution)/shard_map/ppermute | solution.py:408
  27.5 4.3 %collective-permute-start.6 = (f32[17,8,128]{2,1,0:T(8,128)S(1)}, f32[17,8,128]{2,1,0:T(8,128)S(1)}, u32[]{:S(2)}, u32[]{:S(2)}) collective-permute-start(f32[17,8,128]{2,1,0:T(8,128)S(1)} %shard_map.61.refs_0_), channel_id=1, source_target_pairs={{0,4},{1,9},{2,6},{3,11},{4,0},{5,13},{6,2},{7,15},{8,12},{9,1},{1... | collective-permute-start | bytes 208904 | tf_op jit(solution)/shard_map/ppermute | solution.py:408

commit v22 on v21

--- a/solution.py
+++ b/solution.py
@@ -282,6 +282,8 @@
     fine, mid, low = (keep_ref[k, 0:count] for k in range(3))
     place = lax.broadcasted_iota(jnp.int32, (count, LANES), 0)
     gaps = [k for k in range(1, count) if tiles[k] != tiles[k - 1] + 1]
+    starts = [0, *gaps]
+    runs = [end - start for start, end in zip(starts, [*gaps, count])]
     copies = []
     for k, (ref, away) in enumerate(zip(totals, partners(dom_ref[0]))):
         first = (me_ref[0] ^ away) * per_chunk
@@ -314,9 +316,11 @@
                 by_row[spaced(part * TILE + t, count, per_chunk * TILE), :] = rows[t]
 
         per_strip(per_chunk, body, min(per_chunk, 4))
-        for e, m in enumerate(tiles):
+        for e, run in zip(starts, runs):
             copy = pltpu.make_async_copy(
-                values.at[k, e], out_ref.at[m, pl.ds(first, per_chunk)], sems.at[k, e]
+                values.at[k, pl.ds(e, run)],
+                out_ref.at[pl.ds(tiles[e], run), pl.ds(first, per_chunk)],
+                sems.at[k, e],
             )
             copy.start()
             copies.append(copy)

time: 33 us -> 33 us (level)
  no operation moved by 1% of the time
where the time goes in v22:
time: 33 us; the launch traced here: 32.8 us
  starting transfers between devices  21.4 us (65%)
  Pallas kernels  5.05 us (15%)
  waiting for transfers between devices  4.87 us (15%)
  between operations  1.51 us (5%)
    ppermute x12, starting transfers between devices, swap(): return lax.ppermute(array, ('grp', 'dom'), pairs)  14.9 us
    ppermute x2, starting transfers between devices, over_grids(): other = lax.ppermute(total, 'grp', [(g, g ^ apart) for g in range(grids)])  5.3 us
    pallas_call x11, Pallas kernels, call(): pl.pallas_call(kernel, out_shape=[jax.ShapeDtypeStruct(shape, jnp.float32...  5.05 us
    ppermute x12, waiting for transfers between devices, swap(): return lax.ppermute(array, ('grp', 'dom'), pairs)  3.93 us
    ppermute x2, waiting for transfers between devices, over_grids(): other = lax.ppermute(total, 'grp', [(g, g ^ apart) for g in range(grids)])  0.93 us
  transfers between devices with their start and end apart: 16, of which 7 were waited for; matrix products, arithmetic and copies ran while one was open for 0% of the time, Pallas kernels for 12%

profile of v22, /device:TPU:0, one launch (start us, length us, event | category | flops | bytes accessed | tf_op | source)
XLA Modules:
  0.0 32.8 jit_solution(16649738541264926366)
XLA Ops:
  0.0 0.0 copy-start
  0.0 0.0 copy-start.1
  0.0 0.0 copy-start.2
  1.4 0.0 copy-done
  1.5 0.0 copy-done.1
  1.5 0.0 copy-done.2
  1.5 0.1 shard_map.58
  1.5 0.5 %collective-permute-start = (f32[16,16,128]{2,1,0:T(8,128)S(1)}, f32[16,16,128]{2,1,0:T(8,128)S(1)}, u32[]{:S(2)}, u32[]{:S(2)}) collective-permute-start(f32[16,16,128]{2,1,0:T(8,128)S(1)} %get-tuple-element.21), channel_id=1, source_target_pairs={{0,1},{1,0},{2,3},{3,2},{4,5},{5,4},{6,7},{7,6},{8,9},{9,8},{10,11... | collective-permute-start | bytes 393224 | tf_op jit(solution)/shard_map/ppermute | solution.py:381
  2.1 0.7 %collective-permute-start.1 = (f32[16,16,128]{2,1,0:T(8,128)S(1)}, f32[16,16,128]{2,1,0:T(8,128)S(1)}, u32[]{:S(2)}, u32[]{:S(2)}) collective-permute-start(f32[16,16,128]{2,1,0:T(8,128)S(1)} %get-tuple-element.22), channel_id=1, source_target_pairs={{0,0},{1,2},{2,1},{3,3},{4,4},{5,6},{6,5},{7,7},{8,8},{9,10},{10,9... | collective-permute-start | bytes 393224 | tf_op jit(solution)/shard_map/ppermute | solution.py:382
  2.7 2.1 %shard_map.57 = (f32[16,8,8,128]{3,2,1,0:T(8,128)S(1)}, f32[17,8,128]{2,1,0:T(8,128)S(1)}, f32[17,8,128]{2,1,0:T(8,128)S(1)}, f32[17,8,128]{2,1,0:T(8,128)S(1)}, f32[17,8,128]{2,1,0:T(8,128)S(1)}) custom-call(s32[1]{0:T(128)} %bitcast.dom_ref, s32[1]{0:T(128)} %bitcast.1.me_ref, f32[4,8,128]{2,1,0:T(8,128)S(1)} %get-tuple-element.19.weight_ref, ...), custom_call_target="tpu_custom_call" | custom-call | flops 5242880 | bytes 1589256 | tf_op jit(solution)/shard_map/pallas_call | solution.py:341
  4.8 3.6 %collective-permute-start.9 = (f32[17,8,128]{2,1,0:T(8,128)S(1)}, f32[17,8,128]{2,1,0:T(8,128)S(1)}, u32[]{:S(2)}, u32[]{:S(2)}) collective-permute-start(f32[17,8,128]{2,1,0:T(8,128)S(1)} %get-tuple-element.28), channel_id=1, source_target_pairs={{0,12},{1,13},{2,14},{3,15},{4,8},{5,9},{6,10},{7,11},{8,4},{9,5},... | collective-permute-start | bytes 208904 | tf_op jit(solution)/shard_map/ppermute | solution.py:412
  8.4 0.5 %collective-permute-start.10 = (f32[17,8,128]{2,1,0:T(8,128)S(1)}, f32[17,8,128]{2,1,0:T(8,128)S(1)}, u32[]{:S(2)}, u32[]{:S(2)}) collective-permute-start(f32[17,8,128]{2,1,0:T(8,128)S(1)} %get-tuple-element.29), channel_id=1, source_target_pairs={{0,4},{1,9},{2,6},{3,11},{4,0},{5,13},{6,2},{7,15},{8,12},{9,1},{1... | collective-permute-start | bytes 208904 | tf_op jit(solution)/shard_map/ppermute | solution.py:412
  8.9 0.1 collective-permute-start.11
  9.0 0.0 collective-permute-done.refs_3_
  9.0 0.0 collective-permute-done.1.refs_4_
  9.0 0.9 %shard_map.59 = (f32[17,8,128]{2,1,0:T(8,128)S(1)}, f32[17,8,128]{2,1,0:T(8,128)S(1)}, f32[17,8,128]{2,1,0:T(8,128)S(1)}, f32[17,8,128]{2,1,0:T(8,128)S(1)}) custom-call(s32[1]{0:T(128)} %bitcast.dom_ref, s32[1]{0:T(128)} %bitcast.1.me_ref, f32[4,8,128]{2,1,0:T(8,128)S(1)} %get-tuple-element.19.weight_ref, f32[8,16,8,128]{3,2,1,0:T(8,128)S(1)} %bitcast.16, ...), custom_call_target="tpu_custom_call" | custom-call | flops 2621440 | bytes 2375688 | tf_op jit(solution)/shard_map/pallas_call | solution.py:341
  10.0 2.9 %collective-permute-start.2 = (f32[17,8,128]{2,1,0:T(8,128)S(1)}, f32[17,8,128]{2,1,0:T(8,128)S(1)}, u32[]{:S(2)}, u32[]{:S(2)}) collective-permute-start(f32[17,8,128]{2,1,0:T(8,128)S(1)} %get-tuple-element.24), channel_id=1, source_target_pairs={{0,12},{1,13},{2,14},{3,15},{4,8},{5,9},{6,10},{7,11},{8,4},{9,5},... | collective-permute-start | bytes 208904 | tf_op jit(solution)/shard_map/ppermute | solution.py:412
  12.9 0.5 %collective-permute-start.3 = (f32[17,8,128]{2,1,0:T(8,128)S(1)}, f32[17,8,128]{2,1,0:T(8,128)S(1)}, u32[]{:S(2)}, u32[]{:S(2)}) collective-permute-start(f32[17,8,128]{2,1,0:T(8,128)S(1)} %get-tuple-element.25), channel_id=1, source_target_pairs={{0,4},{1,9},{2,6},{3,11},{4,0},{5,13},{6,2},{7,15},{8,12},{9,1},{1... | collective-permute-start | bytes 208904 | tf_op jit(solution)/shard_map/ppermute | solution.py:412
  13.4 0.0 collective-permute-done.9.refs_1_
  13.4 0.1 collective-permute-start.4
  13.5 0.0 collective-permute-done.10.refs_2_
  13.5 0.4 %collective-permute-done.11.refs_3_ = f32[17,8,128]{2,1,0:T(8,128)S(1)} collective-permute-done((f32[17,8,128]{2,1,0:T(8,128)S(1)}, f32[17,8,128]{2,1,0:T(8,128)S(1)}, u32[]{:S(2)}, u32[]{:S(2)}) %collective-permute-start.11) | collective-permute-done | bytes 69664 | tf_op jit(solution)/shard_map/ppermute | solution.py:412
  14.0 2.7 %collective-permute-start.12 = (f32[17,8,128]{2,1,0:T(8,128)S(1)}, f32[17,8,128]{2,1,0:T(8,128)S(1)}, u32[]{:S(2)}, u32[]{:S(2)}) collective-permute-start(f32[17,8,128]{2,1,0:T(8,128)S(1)} %shard_map.62.refs_0_), channel_id=1, source_target_pairs={{0,16},{4,20},{8,24},{12,28},{16,0},{20,4},{24,8},{28,12},{1,17},{... | collective-permute-start | bytes 208904 | tf_op jit(solution)/shard_map/ppermute | solution.py:419
  16.6 0.0 collective-permute-done.2.refs_1_
  16.6 0.8 %collective-permute-done.3.refs_2_ = f32[17,8,128]{2,1,0:T(8,128)S(1)} collective-permute-done((f32[17,8,128]{2,1,0:T(8,128)S(1)}, f32[17,8,128]{2,1,0:T(8,128)S(1)}, u32[]{:S(2)}, u32[]{:S(2)}) %collective-permute-start.3) | collective-permute-done | bytes 69664 | tf_op jit(solution)/shard_map/ppermute | solution.py:412
  17.4 0.8 %collective-permute-done.4.refs_3_ = f32[17,8,128]{2,1,0:T(8,128)S(1)} collective-permute-done((f32[17,8,128]{2,1,0:T(8,128)S(1)}, f32[17,8,128]{2,1,0:T(8,128)S(1)}, u32[]{:S(2)}, u32[]{:S(2)}) %collective-permute-start.4) | collective-permute-done | bytes 69664 | tf_op jit(solution)/shard_map/ppermute | solution.py:412
  18.3 2.6 %collective-permute-start.5 = (f32[17,8,128]{2,1,0:T(8,128)S(1)}, f32[17,8,128]{2,1,0:T(8,128)S(1)}, u32[]{:S(2)}, u32[]{:S(2)}) collective-permute-start(f32[17,8,128]{2,1,0:T(8,128)S(1)} %shard_map.60.refs_0_), channel_id=1, source_target_pairs={{0,16},{4,20},{8,24},{12,28},{16,0},{20,4},{24,8},{28,12},{1,17},{... | collective-permute-start | bytes 208904 | tf_op jit(solution)/shard_map/ppermute | solution.py:419
  20.9 0.0 collective-permute-done.12.refs_1_
  20.9 2.1 %collective-permute-start.15 = (f32[17,8,128]{2,1,0:T(8,128)S(1)}, f32[17,8,128]{2,1,0:T(8,128)S(1)}, u32[]{:S(2)}, u32[]{:S(2)}) collective-permute-start(f32[17,8,128]{2,1,0:T(8,128)S(1)} %shard_map.63.refs_0_.refs_4_), channel_id=1, source_target_pairs={{0,12},{1,13},{2,14},{3,15},{4,8},{5,9},{6,10},{7,11},{8,4},{9,5},... | collective-permute-start | bytes 208904 | tf_op jit(solution)/shard_map/ppermute | solution.py:412
  23.1 0.6 %collective-permute-start.14 = (f32[17,8,128]{2,1,0:T(8,128)S(1)}, f32[17,8,128]{2,1,0:T(8,128)S(1)}, u32[]{:S(2)}, u32[]{:S(2)}) collective-permute-start(f32[17,8,128]{2,1,0:T(8,128)S(1)} %shard_map.63.refs_0_.refs_4_), channel_id=1, source_target_pairs={{0,8},{1,5},{2,10},{3,7},{4,12},{5,1},{6,14},{7,3},{8,0},{9,13},{1... | collective-permute-start | bytes 208904 | tf_op jit(solution)/shard_map/ppermute | solution.py:412
  23.6 0.8 %collective-permute-start.13 = (f32[17,8,128]{2,1,0:T(8,128)S(1)}, f32[17,8,128]{2,1,0:T(8,128)S(1)}, u32[]{:S(2)}, u32[]{:S(2)}) collective-permute-start(f32[17,8,128]{2,1,0:T(8,128)S(1)} %shard_map.63.refs_0_.refs_4_), channel_id=1, source_target_pairs={{0,4},{1,9},{2,6},{3,11},{4,0},{5,13},{6,2},{7,15},{8,12},{9,1},{1... | collective-permute-start | bytes 208904 | tf_op jit(solution)/shard_map/ppermute | solution.py:412
  24.5 0.9 %collective-permute-done.5.refs_1_ = f32[17,8,128]{2,1,0:T(8,128)S(1)} collective-permute-done((f32[17,8,128]{2,1,0:T(8,128)S(1)}, f32[17,8,128]{2,1,0:T(8,128)S(1)}, u32[]{:S(2)}, u32[]{:S(2)}) %collective-permute-start.5) | collective-permute-done | bytes 69664 | tf_op jit(solution)/shard_map/ppermute | solution.py:419
  25.4 1.2 %collective-permute-start.8 = (f32[17,8,128]{2,1,0:T(8,128)S(1)}, f32[17,8,128]{2,1,0:T(8,128)S(1)}, u32[]{:S(2)}, u32[]{:S(2)}) collective-permute-start(f32[17,8,128]{2,1,0:T(8,128)S(1)} %shard_map.61.refs_0_), channel_id=1, source_target_pairs={{0,12},{1,13},{2,14},{3,15},{4,8},{5,9},{6,10},{7,11},{8,4},{9,5},... | collective-permute-start | bytes 208904 | tf_op jit(solution)/shard_map/ppermute | solution.py:412
  26.6 0.9 %collective-permute-start.7 = (f32[17,8,128]{2,1,0:T(8,128)S(1)}, f32[17,8,128]{2,1,0:T(8,128)S(1)}, u32[]{:S(2)}, u32[]{:S(2)}) collective-permute-start(f32[17,8,128]{2,1,0:T(8,128)S(1)} %shard_map.61.refs_0_), channel_id=1, source_target_pairs={{0,8},{1,5},{2,10},{3,7},{4,12},{5,1},{6,14},{7,3},{8,0},{9,13},{1... | collective-permute-start | bytes 208904 | tf_op jit(solution)/shard_map/ppermute | solution.py:412
  27.5 0.0 collective-permute-done.15.refs_3_.refs_7_
  27.5 1.4 %collective-permute-start.6 = (f32[17,8,128]{2,1,0:T(8,128)S(1)}, f32[17,8,128]{2,1,0:T(8,128)S(1)}, u32[]{:S(2)}, u32[]{:S(2)}) collective-permute-start(f32[17,8,128]{2,1,0:T(8,128)S(1)} %shard_map.61.refs_0_), channel_id=1, source_target_pairs={{0,4},{1,9},{2,6},{3,11},{4,0},{5,13},{6,2},{7,15},{8,12},{9,1},{1... | collective-permute-start | bytes 208904 | tf_op jit(solution)/shard_map/ppermute | solution.py:412
  29.0 0.0 collective-permute-done.14.refs_2_.refs_6_
  29.0 0.0 collective-permute-done.13.refs_1_.refs_5_
  29.0 1.0 %shard_map.64.refs_8_ = f32[8,16,8,128]{3,2,1,0:T(8,128)} custom-call(s32[1]{0:T(128)} %bitcast.dom_ref, s32[1]{0:T(128)} %bitcast.1.me_ref, f32[3,8,128]{2,1,0:T(8,128)S(1)} %get-tuple-element.18.keep_ref, f32[17,8,128]{2,1,0:T(8,128)S(1)} %shard_map.63.refs_0_.refs_4_, f32[17,8,128]{2,1,0:T(8,128)S(1)} %collective-permute-done.13.refs_1_.refs_5_, ...), custom_call_target="tpu_custom_call" | custom-call | bytes 290824 | tf_op jit(solution)/shard_map/pallas_call | solution.py:341
  30.0 1.0 %collective-permute-done.8.refs_3_ = f32[17,8,128]{2,1,0:T(8,128)S(1)} collective-permute-done((f32[17,8,128]{2,1,0:T(8,128)S(1)}, f32[17,8,128]{2,1,0:T(8,128)S(1)}, u32[]{:S(2)}, u32[]{:S(2)}) %collective-permute-start.8) | collective-permute-done | bytes 69664 | tf_op jit(solution)/shard_map/ppermute | solution.py:412
  31.0 0.4 %collective-permute-done.7.refs_2_ = f32[17,8,128]{2,1,0:T(8,128)S(1)} collective-permute-done((f32[17,8,128]{2,1,0:T(8,128)S(1)}, f32[17,8,128]{2,1,0:T(8,128)S(1)}, u32[]{:S(2)}, u32[]{:S(2)}) %collective-permute-start.7) | collective-permute-done | bytes 69664 | tf_op jit(solution)/shard_map/ppermute | solution.py:412
  31.4 0.4 %collective-permute-done.6.refs_1_ = f32[17,8,128]{2,1,0:T(8,128)S(1)} collective-permute-done((f32[17,8,128]{2,1,0:T(8,128)S(1)}, f32[17,8,128]{2,1,0:T(8,128)S(1)}, u32[]{:S(2)}, u32[]{:S(2)}) %collective-permute-start.6) | collective-permute-done | bytes 69664 | tf_op jit(solution)/shard_map/ppermute | solution.py:412
  31.9 1.0 %shard_map.65 = f32[8,16,8,128]{3,2,1,0:T(8,128)} custom-call(s32[1]{0:T(128)} %bitcast.dom_ref, s32[1]{0:T(128)} %bitcast.1.me_ref, f32[3,8,128]{2,1,0:T(8,128)S(1)} %get-tuple-element.18.keep_ref, f32[17,8,128]{2,1,0:T(8,128)S(1)} %shard_map.61.refs_0_, f32[17,8,128]{2,1,0:T(8,128)S(1)} %collective-permute-done.6.refs_1_, ...), custom_call_target="tpu_custom_call", output_to_operand_aliasing={{}: (11, {})} | custom-call | bytes 1093640 | tf_op jit(solution)/shard_map/pallas_call | solution.py:341
  (6 shorter events, 0.1 us)
Async XLA Ops:
  0.0 1.4 %copy-start = (f32[1,64,2048]{2,1,0:T(8,128)S(1)}, f32[1,64,2048]{2,1,0:T(8,128)}, u32[]{:S(2)}) copy-start(f32[1,64,2048]{2,1,0:T(8,128)} %param.5) | copy-start | bytes 1572868
  0.0 1.5 %copy-start.1 = (f32[1,64,2048]{2,1,0:T(8,128)S(1)}, f32[1,64,2048]{2,1,0:T(8,128)}, u32[]{:S(2)}) copy-start(f32[1,64,2048]{2,1,0:T(8,128)} %param.6) | copy-start | bytes 1572868
  0.0 1.5 %copy-start.2 = (f32[1,64,2048]{2,1,0:T(8,128)S(1)}, f32[1,64,2048]{2,1,0:T(8,128)}, u32[]{:S(2)}) copy-start(f32[1,64,2048]{2,1,0:T(8,128)} %param.7) | copy-start | bytes 1572868
  1.5 7.5 %collective-permute-start = (f32[16,16,128]{2,1,0:T(8,128)S(1)}, f32[16,16,128]{2,1,0:T(8,128)S(1)}, u32[]{:S(2)}, u32[]{:S(2)}) collective-permute-start(f32[16,16,128]{2,1,0:T(8,128)S(1)} %get-tuple-element.21), channel_id=1, source_target_pairs={{0,1},{1,0},{2,3},{3,2},{4,5},{5,4},{6,7},{7,6},{8,9},{9,8},{10,11... | collective-permute-start | bytes 393224 | tf_op jit(solution)/shard_map/ppermute | solution.py:381
  2.1 7.0 %collective-permute-start.1 = (f32[16,16,128]{2,1,0:T(8,128)S(1)}, f32[16,16,128]{2,1,0:T(8,128)S(1)}, u32[]{:S(2)}, u32[]{:S(2)}) collective-permute-start(f32[16,16,128]{2,1,0:T(8,128)S(1)} %get-tuple-element.22), channel_id=1, source_target_pairs={{0,0},{1,2},{2,1},{3,3},{4,4},{5,6},{6,5},{7,7},{8,8},{9,10},{10,9... | collective-permute-start | bytes 393224 | tf_op jit(solution)/shard_map/ppermute | solution.py:382
  4.8 8.6 %collective-permute-start.9 = (f32[17,8,128]{2,1,0:T(8,128)S(1)}, f32[17,8,128]{2,1,0:T(8,128)S(1)}, u32[]{:S(2)}, u32[]{:S(2)}) collective-permute-start(f32[17,8,128]{2,1,0:T(8,128)S(1)} %get-tuple-element.28), channel_id=1, source_target_pairs={{0,12},{1,13},{2,14},{3,15},{4,8},{5,9},{6,10},{7,11},{8,4},{9,5},... | collective-permute-start | bytes 208904 | tf_op jit(solution)/shard_map/ppermute | solution.py:412
  8.4 5.1 %collective-permute-start.10 = (f32[17,8,128]{2,1,0:T(8,128)S(1)}, f32[17,8,128]{2,1,0:T(8,128)S(1)}, u32[]{:S(2)}, u32[]{:S(2)}) collective-permute-start(f32[17,8,128]{2,1,0:T(8,128)S(1)} %get-tuple-element.29), channel_id=1, source_target_pairs={{0,4},{1,9},{2,6},{3,11},{4,0},{5,13},{6,2},{7,15},{8,12},{9,1},{1... | collective-permute-start | bytes 208904 | tf_op jit(solution)/shard_map/ppermute | solution.py:412
  8.9 5.0 %collective-permute-start.11 = (f32[17,8,128]{2,1,0:T(8,128)S(1)}, f32[17,8,128]{2,1,0:T(8,128)S(1)}, u32[]{:S(2)}, u32[]{:S(2)}) collective-permute-start(f32[17,8,128]{2,1,0:T(8,128)S(1)} %get-tuple-element.30), channel_id=1, source_target_pairs={{0,8},{1,5},{2,10},{3,7},{4,12},{5,1},{6,14},{7,3},{8,0},{9,13},{1... | collective-permute-start | bytes 208904 | tf_op jit(solution)/shard_map/ppermute | solution.py:412
  10.0 6.7 %collective-permute-start.2 = (f32[17,8,128]{2,1,0:T(8,128)S(1)}, f32[17,8,128]{2,1,0:T(8,128)S(1)}, u32[]{:S(2)}, u32[]{:S(2)}) collective-permute-start(f32[17,8,128]{2,1,0:T(8,128)S(1)} %get-tuple-element.24), channel_id=1, source_target_pairs={{0,12},{1,13},{2,14},{3,15},{4,8},{5,9},{6,10},{7,11},{8,4},{9,5},... | collective-permute-start | bytes 208904 | tf_op jit(solution)/shard_map/ppermute | solution.py:412
  12.9 4.5 %collective-permute-start.3 = (f32[17,8,128]{2,1,0:T(8,128)S(1)}, f32[17,8,128]{2,1,0:T(8,128)S(1)}, u32[]{:S(2)}, u32[]{:S(2)}) collective-permute-start(f32[17,8,128]{2,1,0:T(8,128)S(1)} %get-tuple-element.25), channel_id=1, source_target_pairs={{0,4},{1,9},{2,6},{3,11},{4,0},{5,13},{6,2},{7,15},{8,12},{9,1},{1... | collective-permute-start | bytes 208904 | tf_op jit(solution)/shard_map/ppermute | solution.py:412
  13.4 4.8 %collective-permute-start.4 = (f32[17,8,128]{2,1,0:T(8,128)S(1)}, f32[17,8,128]{2,1,0:T(8,128)S(1)}, u32[]{:S(2)}, u32[]{:S(2)}) collective-permute-start(f32[17,8,128]{2,1,0:T(8,128)S(1)} %get-tuple-element.26), channel_id=1, source_target_pairs={{0,8},{1,5},{2,10},{3,7},{4,12},{5,1},{6,14},{7,3},{8,0},{9,13},{1... | collective-permute-start | bytes 208904 | tf_op jit(solution)/shard_map/ppermute | solution.py:412
  14.0 6.9 %collective-permute-start.12 = (f32[17,8,128]{2,1,0:T(8,128)S(1)}, f32[17,8,128]{2,1,0:T(8,128)S(1)}, u32[]{:S(2)}, u32[]{:S(2)}) collective-permute-start(f32[17,8,128]{2,1,0:T(8,128)S(1)} %shard_map.62.refs_0_), channel_id=1, source_target_pairs={{0,16},{4,20},{8,24},{12,28},{16,0},{20,4},{24,8},{28,12},{1,17},{... | collective-permute-start | bytes 208904 | tf_op jit(solution)/shard_map/ppermute | solution.py:419
  18.3 7.2 %collective-permute-start.5 = (f32[17,8,128]{2,1,0:T(8,128)S(1)}, f32[17,8,128]{2,1,0:T(8,128)S(1)}, u32[]{:S(2)}, u32[]{:S(2)}) collective-permute-start(f32[17,8,128]{2,1,0:T(8,128)S(1)} %shard_map.60.refs_0_), channel_id=1, source_target_pairs={{0,16},{4,20},{8,24},{12,28},{16,0},{20,4},{24,8},{28,12},{1,17},{... | collective-permute-start | bytes 208904 | tf_op jit(solution)/shard_map/ppermute | solution.py:419
  20.9 6.6 %collective-permute-start.15 = (f32[17,8,128]{2,1,0:T(8,128)S(1)}, f32[17,8,128]{2,1,0:T(8,128)S(1)}, u32[]{:S(2)}, u32[]{:S(2)}) collective-permute-start(f32[17,8,128]{2,1,0:T(8,128)S(1)} %shard_map.63.refs_0_.refs_4_), channel_id=1, source_target_pairs={{0,12},{1,13},{2,14},{3,15},{4,8},{5,9},{6,10},{7,11},{8,4},{9,5},... | collective-permute-start | bytes 208904 | tf_op jit(solution)/shard_map/ppermute | solution.py:412
  23.1 5.9 %collective-permute-start.14 = (f32[17,8,128]{2,1,0:T(8,128)S(1)}, f32[17,8,128]{2,1,0:T(8,128)S(1)}, u32[]{:S(2)}, u32[]{:S(2)}) collective-permute-start(f32[17,8,128]{2,1,0:T(8,128)S(1)} %shard_map.63.refs_0_.refs_4_), channel_id=1, source_target_pairs={{0,8},{1,5},{2,10},{3,7},{4,12},{5,1},{6,14},{7,3},{8,0},{9,13},{1... | collective-permute-start | bytes 208904 | tf_op jit(solution)/shard_map/ppermute | solution.py:412
  23.6 5.3 %collective-permute-start.13 = (f32[17,8,128]{2,1,0:T(8,128)S(1)}, f32[17,8,128]{2,1,0:T(8,128)S(1)}, u32[]{:S(2)}, u32[]{:S(2)}) collective-permute-start(f32[17,8,128]{2,1,0:T(8,128)S(1)} %shard_map.63.refs_0_.refs_4_), channel_id=1, source_target_pairs={{0,4},{1,9},{2,6},{3,11},{4,0},{5,13},{6,2},{7,15},{8,12},{9,1},{1... | collective-permute-start | bytes 208904 | tf_op jit(solution)/shard_map/ppermute | solution.py:412
  25.4 5.6 %collective-permute-start.8 = (f32[17,8,128]{2,1,0:T(8,128)S(1)}, f32[17,8,128]{2,1,0:T(8,128)S(1)}, u32[]{:S(2)}, u32[]{:S(2)}) collective-permute-start(f32[17,8,128]{2,1,0:T(8,128)S(1)} %shard_map.61.refs_0_), channel_id=1, source_target_pairs={{0,12},{1,13},{2,14},{3,15},{4,8},{5,9},{6,10},{7,11},{8,4},{9,5},... | collective-permute-start | bytes 208904 | tf_op jit(solution)/shard_map/ppermute | solution.py:412
  26.6 4.8 %collective-permute-start.7 = (f32[17,8,128]{2,1,0:T(8,128)S(1)}, f32[17,8,128]{2,1,0:T(8,128)S(1)}, u32[]{:S(2)}, u32[]{:S(2)}) collective-permute-start(f32[17,8,128]{2,1,0:T(8,128)S(1)} %shard_map.61.refs_0_), channel_id=1, source_target_pairs={{0,8},{1,5},{2,10},{3,7},{4,12},{5,1},{6,14},{7,3},{8,0},{9,13},{1... | collective-permute-start | bytes 208904 | tf_op jit(solution)/shard_map/ppermute | solution.py:412
  27.5 4.3 %collective-permute-start.6 = (f32[17,8,128]{2,1,0:T(8,128)S(1)}, f32[17,8,128]{2,1,0:T(8,128)S(1)}, u32[]{:S(2)}, u32[]{:S(2)}) collective-permute-start(f32[17,8,128]{2,1,0:T(8,128)S(1)} %shard_map.61.refs_0_), channel_id=1, source_target_pairs={{0,4},{1,9},{2,6},{3,11},{4,0},{5,13},{6,2},{7,15},{8,12},{9,1},{1... | collective-permute-start | bytes 208904 | tf_op jit(solution)/shard_map/ppermute | solution.py:412

commit v23 on v21

--- a/solution.py
+++ b/solution.py
@@ -277,7 +277,9 @@
 
 
 def nodal_kernel(per_chunk, tiles, dom_ref, me_ref, keep_ref, *refs):
-    totals, middles, (out_ref, values, sems) = refs[:SQUARE], refs[SQUARE:-3], refs[-3:]
+    out_ref, values, sems = refs[-3:]
+    own, second, first, diagonal = refs[:SQUARE]
+    totals = own, first, second, diagonal
     count = len(tiles)
     fine, mid, low = (keep_ref[k, 0:count] for k in range(3))
     place = lax.broadcasted_iota(jnp.int32, (count, LANES), 0)
@@ -295,7 +297,8 @@
             prev = jnp.where(place == 0, before, roll_rows(w[7], 1))
             for gap in gaps:
                 across = tiles[gap] - tiles[gap - 1] - 1
-                before = middles[k][part * across + across - 1, TILE - 1 : TILE, :]
+                middle_ref = refs[SQUARE + (0, 2, 1, 3)[k]]
+                before = middle_ref[part * across + across - 1, TILE - 1 : TILE, :]
                 prev = jnp.where(place == gap, before, prev)
             v3 = 0.5 * (prev + w[7]) + low * w[3]
             v1 = 0.5 * (prev + v3) + mid * w[1]
@@ -415,7 +418,7 @@
             other = lax.ppermute(total, "grp", [(g, g ^ apart) for g in range(grids)])
             (total,) = call(sum_kernel, [own.shape], (total, other))
             apart *= 2
-        return [total] + [swap(total, meet) for meet in range(1, SQUARE)]
+        return [total] + [swap(total, meet) for meet in (2, 1, 3)]
 
     nodal, totals = None, []
     for some, weighted in ((middle, inside), (outer, outside)):

time: 33 us -> 33 us (level)
  transfers between devices with their start and end apart: 16 -> 16, of which waited for: 7 -> 6; matrix products, arithmetic and copies ran while one was open for 0% -> 0% of each run, Pallas kernels for 12% -> 12%
where the time goes in v23:
time: 33 us; the launch traced here: 32.8 us
  starting transfers between devices  21.4 us (65%)
  Pallas kernels  5.05 us (15%)
  waiting for transfers between devices  4.84 us (15%)
  between operations  1.51 us (5%)
    ppermute x12, starting transfers between devices, swap(): return lax.ppermute(array, ('grp', 'dom'), pairs)  14.9 us
    ppermute x2, starting transfers between devices, over_grids(): other = lax.ppermute(total, 'grp', [(g, g ^ apart) for g in range(grids)])  5.3 us
    pallas_call x11, Pallas kernels, call(): pl.pallas_call(kernel, out_shape=[jax.ShapeDtypeStruct(shape, jnp.float32...  5.05 us
    ppermute x12, waiting for transfers between devices, swap(): return lax.ppermute(array, ('grp', 'dom'), pairs)  3.9 us
    ppermute x2, waiting for transfers between devices, over_grids(): other = lax.ppermute(total, 'grp', [(g, g ^ apart) for g in range(grids)])  0.93 us
  transfers between devices with their start and end apart: 16, of which 6 were waited for; matrix products, arithmetic and copies ran while one was open for 0% of the time, Pallas kernels for 12%

profile of v23, /device:TPU:0, one launch (start us, length us, event | category | flops | bytes accessed | tf_op | source)
XLA Modules:
  0.0 32.8 jit_solution(11603976896934464676)
XLA Ops:
  0.0 0.0 copy-start
  0.0 0.0 copy-start.1
  0.0 0.0 copy-start.2
  1.4 0.0 copy-done
  1.5 0.0 copy-done.1
  1.5 0.0 copy-done.2
  1.5 0.1 shard_map.58
  1.5 0.5 %collective-permute-start = (f32[16,16,128]{2,1,0:T(8,128)S(1)}, f32[16,16,128]{2,1,0:T(8,128)S(1)}, u32[]{:S(2)}, u32[]{:S(2)}) collective-permute-start(f32[16,16,128]{2,1,0:T(8,128)S(1)} %get-tuple-element.21), channel_id=1, source_target_pairs={{0,1},{1,0},{2,3},{3,2},{4,5},{5,4},{6,7},{7,6},{8,9},{9,8},{10,11... | collective-permute-start | bytes 393224 | tf_op jit(solution)/shard_map/ppermute | solution.py:380
  2.1 0.7 %collective-permute-start.1 = (f32[16,16,128]{2,1,0:T(8,128)S(1)}, f32[16,16,128]{2,1,0:T(8,128)S(1)}, u32[]{:S(2)}, u32[]{:S(2)}) collective-permute-start(f32[16,16,128]{2,1,0:T(8,128)S(1)} %get-tuple-element.22), channel_id=1, source_target_pairs={{0,0},{1,2},{2,1},{3,3},{4,4},{5,6},{6,5},{7,7},{8,8},{9,10},{10,9... | collective-permute-start | bytes 393224 | tf_op jit(solution)/shard_map/ppermute | solution.py:381
  2.7 2.1 %shard_map.57 = (f32[16,8,8,128]{3,2,1,0:T(8,128)S(1)}, f32[17,8,128]{2,1,0:T(8,128)S(1)}, f32[17,8,128]{2,1,0:T(8,128)S(1)}, f32[17,8,128]{2,1,0:T(8,128)S(1)}, f32[17,8,128]{2,1,0:T(8,128)S(1)}) custom-call(s32[1]{0:T(128)} %bitcast.dom_ref, s32[1]{0:T(128)} %bitcast.1.me_ref, f32[4,8,128]{2,1,0:T(8,128)S(1)} %get-tuple-element.19.weight_ref, ...), custom_call_target="tpu_custom_call" | custom-call | flops 5242880 | bytes 1589256 | tf_op jit(solution)/shard_map/pallas_call | solution.py:340
  4.8 3.6 %collective-permute-start.9 = (f32[17,8,128]{2,1,0:T(8,128)S(1)}, f32[17,8,128]{2,1,0:T(8,128)S(1)}, u32[]{:S(2)}, u32[]{:S(2)}) collective-permute-start(f32[17,8,128]{2,1,0:T(8,128)S(1)} %get-tuple-element.28), channel_id=1, source_target_pairs={{0,12},{1,13},{2,14},{3,15},{4,8},{5,9},{6,10},{7,11},{8,4},{9,5},... | collective-permute-start | bytes 208904 | tf_op jit(solution)/shard_map/ppermute | solution.py:411
  8.4 0.5 %collective-permute-start.10 = (f32[17,8,128]{2,1,0:T(8,128)S(1)}, f32[17,8,128]{2,1,0:T(8,128)S(1)}, u32[]{:S(2)}, u32[]{:S(2)}) collective-permute-start(f32[17,8,128]{2,1,0:T(8,128)S(1)} %get-tuple-element.29), channel_id=1, source_target_pairs={{0,4},{1,9},{2,6},{3,11},{4,0},{5,13},{6,2},{7,15},{8,12},{9,1},{1... | collective-permute-start | bytes 208904 | tf_op jit(solution)/shard_map/ppermute | solution.py:411
  8.9 0.1 collective-permute-start.11
  9.0 0.0 collective-permute-done.refs_3_
  9.0 0.0 collective-permute-done.1.refs_4_
  9.0 0.9 %shard_map.59 = (f32[17,8,128]{2,1,0:T(8,128)S(1)}, f32[17,8,128]{2,1,0:T(8,128)S(1)}, f32[17,8,128]{2,1,0:T(8,128)S(1)}, f32[17,8,128]{2,1,0:T(8,128)S(1)}) custom-call(s32[1]{0:T(128)} %bitcast.dom_ref, s32[1]{0:T(128)} %bitcast.1.me_ref, f32[4,8,128]{2,1,0:T(8,128)S(1)} %get-tuple-element.19.weight_ref, f32[8,16,8,128]{3,2,1,0:T(8,128)S(1)} %bitcast.16, ...), custom_call_target="tpu_custom_call" | custom-call | flops 2621440 | bytes 2375688 | tf_op jit(solution)/shard_map/pallas_call | solution.py:340
  10.0 2.9 %collective-permute-start.2 = (f32[17,8,128]{2,1,0:T(8,128)S(1)}, f32[17,8,128]{2,1,0:T(8,128)S(1)}, u32[]{:S(2)}, u32[]{:S(2)}) collective-permute-start(f32[17,8,128]{2,1,0:T(8,128)S(1)} %get-tuple-element.24), channel_id=1, source_target_pairs={{0,12},{1,13},{2,14},{3,15},{4,8},{5,9},{6,10},{7,11},{8,4},{9,5},... | collective-permute-start | bytes 208904 | tf_op jit(solution)/shard_map/ppermute | solution.py:411
  12.9 0.5 %collective-permute-start.3 = (f32[17,8,128]{2,1,0:T(8,128)S(1)}, f32[17,8,128]{2,1,0:T(8,128)S(1)}, u32[]{:S(2)}, u32[]{:S(2)}) collective-permute-start(f32[17,8,128]{2,1,0:T(8,128)S(1)} %get-tuple-element.25), channel_id=1, source_target_pairs={{0,4},{1,9},{2,6},{3,11},{4,0},{5,13},{6,2},{7,15},{8,12},{9,1},{1... | collective-permute-start | bytes 208904 | tf_op jit(solution)/shard_map/ppermute | solution.py:411
  13.4 0.0 collective-permute-done.9.refs_1_
  13.4 0.1 collective-permute-start.4
  13.5 0.0 collective-permute-done.10.refs_2_
  13.5 0.4 %collective-permute-done.11.refs_3_ = f32[17,8,128]{2,1,0:T(8,128)S(1)} collective-permute-done((f32[17,8,128]{2,1,0:T(8,128)S(1)}, f32[17,8,128]{2,1,0:T(8,128)S(1)}, u32[]{:S(2)}, u32[]{:S(2)}) %collective-permute-start.11) | collective-permute-done | bytes 69664 | tf_op jit(solution)/shard_map/ppermute | solution.py:411
  14.0 2.7 %collective-permute-start.12 = (f32[17,8,128]{2,1,0:T(8,128)S(1)}, f32[17,8,128]{2,1,0:T(8,128)S(1)}, u32[]{:S(2)}, u32[]{:S(2)}) collective-permute-start(f32[17,8,128]{2,1,0:T(8,128)S(1)} %shard_map.62.refs_0_), channel_id=1, source_target_pairs={{0,16},{4,20},{8,24},{12,28},{16,0},{20,4},{24,8},{28,12},{1,17},{... | collective-permute-start | bytes 208904 | tf_op jit(solution)/shard_map/ppermute | solution.py:418
  16.6 0.0 collective-permute-done.2.refs_1_
  16.6 0.8 %collective-permute-done.3.refs_2_ = f32[17,8,128]{2,1,0:T(8,128)S(1)} collective-permute-done((f32[17,8,128]{2,1,0:T(8,128)S(1)}, f32[17,8,128]{2,1,0:T(8,128)S(1)}, u32[]{:S(2)}, u32[]{:S(2)}) %collective-permute-start.3) | collective-permute-done | bytes 69664 | tf_op jit(solution)/shard_map/ppermute | solution.py:411
  17.4 0.8 %collective-permute-done.4.refs_3_ = f32[17,8,128]{2,1,0:T(8,128)S(1)} collective-permute-done((f32[17,8,128]{2,1,0:T(8,128)S(1)}, f32[17,8,128]{2,1,0:T(8,128)S(1)}, u32[]{:S(2)}, u32[]{:S(2)}) %collective-permute-start.4) | collective-permute-done | bytes 69664 | tf_op jit(solution)/shard_map/ppermute | solution.py:411
  18.3 2.6 %collective-permute-start.5 = (f32[17,8,128]{2,1,0:T(8,128)S(1)}, f32[17,8,128]{2,1,0:T(8,128)S(1)}, u32[]{:S(2)}, u32[]{:S(2)}) collective-permute-start(f32[17,8,128]{2,1,0:T(8,128)S(1)} %shard_map.60.refs_0_), channel_id=1, source_target_pairs={{0,16},{4,20},{8,24},{12,28},{16,0},{20,4},{24,8},{28,12},{1,17},{... | collective-permute-start | bytes 208904 | tf_op jit(solution)/shard_map/ppermute | solution.py:418
  20.9 0.0 collective-permute-done.12.refs_1_
  20.9 2.1 %collective-permute-start.15 = (f32[17,8,128]{2,1,0:T(8,128)S(1)}, f32[17,8,128]{2,1,0:T(8,128)S(1)}, u32[]{:S(2)}, u32[]{:S(2)}) collective-permute-start(f32[17,8,128]{2,1,0:T(8,128)S(1)} %shard_map.63.refs_0_.refs_4_), channel_id=1, source_target_pairs={{0,12},{1,13},{2,14},{3,15},{4,8},{5,9},{6,10},{7,11},{8,4},{9,5},... | collective-permute-start | bytes 208904 | tf_op jit(solution)/shard_map/ppermute | solution.py:411
  23.1 0.8 %collective-permute-start.14 = (f32[17,8,128]{2,1,0:T(8,128)S(1)}, f32[17,8,128]{2,1,0:T(8,128)S(1)}, u32[]{:S(2)}, u32[]{:S(2)}) collective-permute-start(f32[17,8,128]{2,1,0:T(8,128)S(1)} %shard_map.63.refs_0_.refs_4_), channel_id=1, source_target_pairs={{0,4},{1,9},{2,6},{3,11},{4,0},{5,13},{6,2},{7,15},{8,12},{9,1},{1... | collective-permute-start | bytes 208904 | tf_op jit(solution)/shard_map/ppermute | solution.py:411
  23.9 0.6 %collective-permute-start.13 = (f32[17,8,128]{2,1,0:T(8,128)S(1)}, f32[17,8,128]{2,1,0:T(8,128)S(1)}, u32[]{:S(2)}, u32[]{:S(2)}) collective-permute-start(f32[17,8,128]{2,1,0:T(8,128)S(1)} %shard_map.63.refs_0_.refs_4_), channel_id=1, source_target_pairs={{0,8},{1,5},{2,10},{3,7},{4,12},{5,1},{6,14},{7,3},{8,0},{9,13},{1... | collective-permute-start | bytes 208904 | tf_op jit(solution)/shard_map/ppermute | solution.py:411
  24.5 0.9 %collective-permute-done.5.refs_1_ = f32[17,8,128]{2,1,0:T(8,128)S(1)} collective-permute-done((f32[17,8,128]{2,1,0:T(8,128)S(1)}, f32[17,8,128]{2,1,0:T(8,128)S(1)}, u32[]{:S(2)}, u32[]{:S(2)}) %collective-permute-start.5) | collective-permute-done | bytes 69664 | tf_op jit(solution)/shard_map/ppermute | solution.py:418
  25.4 1.2 %collective-permute-start.8 = (f32[17,8,128]{2,1,0:T(8,128)S(1)}, f32[17,8,128]{2,1,0:T(8,128)S(1)}, u32[]{:S(2)}, u32[]{:S(2)}) collective-permute-start(f32[17,8,128]{2,1,0:T(8,128)S(1)} %shard_map.61.refs_0_), channel_id=1, source_target_pairs={{0,12},{1,13},{2,14},{3,15},{4,8},{5,9},{6,10},{7,11},{8,4},{9,5},... | collective-permute-start | bytes 208904 | tf_op jit(solution)/shard_map/ppermute | solution.py:411
  26.6 0.8 %collective-permute-start.7 = (f32[17,8,128]{2,1,0:T(8,128)S(1)}, f32[17,8,128]{2,1,0:T(8,128)S(1)}, u32[]{:S(2)}, u32[]{:S(2)}) collective-permute-start(f32[17,8,128]{2,1,0:T(8,128)S(1)} %shard_map.61.refs_0_), channel_id=1, source_target_pairs={{0,4},{1,9},{2,6},{3,11},{4,0},{5,13},{6,2},{7,15},{8,12},{9,1},{1... | collective-permute-start | bytes 208904 | tf_op jit(solution)/shard_map/ppermute | solution.py:411
  27.4 0.0 collective-permute-done.15.refs_3_.refs_7_
  27.4 1.6 %collective-permute-start.6 = (f32[17,8,128]{2,1,0:T(8,128)S(1)}, f32[17,8,128]{2,1,0:T(8,128)S(1)}, u32[]{:S(2)}, u32[]{:S(2)}) collective-permute-start(f32[17,8,128]{2,1,0:T(8,128)S(1)} %shard_map.61.refs_0_), channel_id=1, source_target_pairs={{0,8},{1,5},{2,10},{3,7},{4,12},{5,1},{6,14},{7,3},{8,0},{9,13},{1... | collective-permute-start | bytes 208904 | tf_op jit(solution)/shard_map/ppermute | solution.py:411
  29.0 0.0 collective-permute-done.14.refs_2_.refs_6_
  29.0 0.0 collective-permute-done.13.refs_1_.refs_5_
  29.0 1.0 %shard_map.64.refs_8_ = f32[8,16,8,128]{3,2,1,0:T(8,128)} custom-call(s32[1]{0:T(128)} %bitcast.dom_ref, s32[1]{0:T(128)} %bitcast.1.me_ref, f32[3,8,128]{2,1,0:T(8,128)S(1)} %get-tuple-element.18.keep_ref, f32[17,8,128]{2,1,0:T(8,128)S(1)} %shard_map.63.refs_0_.refs_4_, f32[17,8,128]{2,1,0:T(8,128)S(1)} %collective-permute-done.13.refs_1_.refs_5_, ...), custom_call_target="tpu_custom_call" | custom-call | bytes 290824 | tf_op jit(solution)/shard_map/pallas_call | solution.py:340
  30.0 1.2 %collective-permute-done.8.refs_3_ = f32[17,8,128]{2,1,0:T(8,128)S(1)} collective-permute-done((f32[17,8,128]{2,1,0:T(8,128)S(1)}, f32[17,8,128]{2,1,0:T(8,128)S(1)}, u32[]{:S(2)}, u32[]{:S(2)}) %collective-permute-start.8) | collective-permute-done | bytes 69664 | tf_op jit(solution)/shard_map/ppermute | solution.py:411
  31.1 0.7 %collective-permute-done.7.refs_2_ = f32[17,8,128]{2,1,0:T(8,128)S(1)} collective-permute-done((f32[17,8,128]{2,1,0:T(8,128)S(1)}, f32[17,8,128]{2,1,0:T(8,128)S(1)}, u32[]{:S(2)}, u32[]{:S(2)}) %collective-permute-start.7) | collective-permute-done | bytes 69664 | tf_op jit(solution)/shard_map/ppermute | solution.py:411
  31.8 0.0 collective-permute-done.6.refs_1_
  31.8 1.0 %shard_map.65 = f32[8,16,8,128]{3,2,1,0:T(8,128)} custom-call(s32[1]{0:T(128)} %bitcast.dom_ref, s32[1]{0:T(128)} %bitcast.1.me_ref, f32[3,8,128]{2,1,0:T(8,128)S(1)} %get-tuple-element.18.keep_ref, f32[17,8,128]{2,1,0:T(8,128)S(1)} %shard_map.61.refs_0_, f32[17,8,128]{2,1,0:T(8,128)S(1)} %collective-permute-done.6.refs_1_, ...), custom_call_target="tpu_custom_call", output_to_operand_aliasing={{}: (11, {})} | custom-call | bytes 1093640 | tf_op jit(solution)/shard_map/pallas_call | solution.py:340
  (6 shorter events, 0.1 us)
Async XLA Ops:
  0.0 1.4 %copy-start = (f32[1,64,2048]{2,1,0:T(8,128)S(1)}, f32[1,64,2048]{2,1,0:T(8,128)}, u32[]{:S(2)}) copy-start(f32[1,64,2048]{2,1,0:T(8,128)} %param.5) | copy-start | bytes 1572868
  0.0 1.5 %copy-start.1 = (f32[1,64,2048]{2,1,0:T(8,128)S(1)}, f32[1,64,2048]{2,1,0:T(8,128)}, u32[]{:S(2)}) copy-start(f32[1,64,2048]{2,1,0:T(8,128)} %param.6) | copy-start | bytes 1572868
  0.0 1.5 %copy-start.2 = (f32[1,64,2048]{2,1,0:T(8,128)S(1)}, f32[1,64,2048]{2,1,0:T(8,128)}, u32[]{:S(2)}) copy-start(f32[1,64,2048]{2,1,0:T(8,128)} %param.7) | copy-start | bytes 1572868
  1.5 7.5 %collective-permute-start = (f32[16,16,128]{2,1,0:T(8,128)S(1)}, f32[16,16,128]{2,1,0:T(8,128)S(1)}, u32[]{:S(2)}, u32[]{:S(2)}) collective-permute-start(f32[16,16,128]{2,1,0:T(8,128)S(1)} %get-tuple-element.21), channel_id=1, source_target_pairs={{0,1},{1,0},{2,3},{3,2},{4,5},{5,4},{6,7},{7,6},{8,9},{9,8},{10,11... | collective-permute-start | bytes 393224 | tf_op jit(solution)/shard_map/ppermute | solution.py:380
  2.1 7.0 %collective-permute-start.1 = (f32[16,16,128]{2,1,0:T(8,128)S(1)}, f32[16,16,128]{2,1,0:T(8,128)S(1)}, u32[]{:S(2)}, u32[]{:S(2)}) collective-permute-start(f32[16,16,128]{2,1,0:T(8,128)S(1)} %get-tuple-element.22), channel_id=1, source_target_pairs={{0,0},{1,2},{2,1},{3,3},{4,4},{5,6},{6,5},{7,7},{8,8},{9,10},{10,9... | collective-permute-start | bytes 393224 | tf_op jit(solution)/shard_map/ppermute | solution.py:381
  4.8 8.6 %collective-permute-start.9 = (f32[17,8,128]{2,1,0:T(8,128)S(1)}, f32[17,8,128]{2,1,0:T(8,128)S(1)}, u32[]{:S(2)}, u32[]{:S(2)}) collective-permute-start(f32[17,8,128]{2,1,0:T(8,128)S(1)} %get-tuple-element.28), channel_id=1, source_target_pairs={{0,12},{1,13},{2,14},{3,15},{4,8},{5,9},{6,10},{7,11},{8,4},{9,5},... | collective-permute-start | bytes 208904 | tf_op jit(solution)/shard_map/ppermute | solution.py:411
  8.4 5.1 %collective-permute-start.10 = (f32[17,8,128]{2,1,0:T(8,128)S(1)}, f32[17,8,128]{2,1,0:T(8,128)S(1)}, u32[]{:S(2)}, u32[]{:S(2)}) collective-permute-start(f32[17,8,128]{2,1,0:T(8,128)S(1)} %get-tuple-element.29), channel_id=1, source_target_pairs={{0,4},{1,9},{2,6},{3,11},{4,0},{5,13},{6,2},{7,15},{8,12},{9,1},{1... | collective-permute-start | bytes 208904 | tf_op jit(solution)/shard_map/ppermute | solution.py:411
  8.9 5.0 %collective-permute-start.11 = (f32[17,8,128]{2,1,0:T(8,128)S(1)}, f32[17,8,128]{2,1,0:T(8,128)S(1)}, u32[]{:S(2)}, u32[]{:S(2)}) collective-permute-start(f32[17,8,128]{2,1,0:T(8,128)S(1)} %get-tuple-element.30), channel_id=1, source_target_pairs={{0,8},{1,5},{2,10},{3,7},{4,12},{5,1},{6,14},{7,3},{8,0},{9,13},{1... | collective-permute-start | bytes 208904 | tf_op jit(solution)/shard_map/ppermute | solution.py:411
  10.0 6.7 %collective-permute-start.2 = (f32[17,8,128]{2,1,0:T(8,128)S(1)}, f32[17,8,128]{2,1,0:T(8,128)S(1)}, u32[]{:S(2)}, u32[]{:S(2)}) collective-permute-start(f32[17,8,128]{2,1,0:T(8,128)S(1)} %get-tuple-element.24), channel_id=1, source_target_pairs={{0,12},{1,13},{2,14},{3,15},{4,8},{5,9},{6,10},{7,11},{8,4},{9,5},... | collective-permute-start | bytes 208904 | tf_op jit(solution)/shard_map/ppermute | solution.py:411
  12.9 4.5 %collective-permute-start.3 = (f32[17,8,128]{2,1,0:T(8,128)S(1)}, f32[17,8,128]{2,1,0:T(8,128)S(1)}, u32[]{:S(2)}, u32[]{:S(2)}) collective-permute-start(f32[17,8,128]{2,1,0:T(8,128)S(1)} %get-tuple-element.25), channel_id=1, source_target_pairs={{0,4},{1,9},{2,6},{3,11},{4,0},{5,13},{6,2},{7,15},{8,12},{9,1},{1... | collective-permute-start | bytes 208904 | tf_op jit(solution)/shard_map/ppermute | solution.py:411
  13.4 4.8 %collective-permute-start.4 = (f32[17,8,128]{2,1,0:T(8,128)S(1)}, f32[17,8,128]{2,1,0:T(8,128)S(1)}, u32[]{:S(2)}, u32[]{:S(2)}) collective-permute-start(f32[17,8,128]{2,1,0:T(8,128)S(1)} %get-tuple-element.26), channel_id=1, source_target_pairs={{0,8},{1,5},{2,10},{3,7},{4,12},{5,1},{6,14},{7,3},{8,0},{9,13},{1... | collective-permute-start | bytes 208904 | tf_op jit(solution)/shard_map/ppermute | solution.py:411
  14.0 6.9 %collective-permute-start.12 = (f32[17,8,128]{2,1,0:T(8,128)S(1)}, f32[17,8,128]{2,1,0:T(8,128)S(1)}, u32[]{:S(2)}, u32[]{:S(2)}) collective-permute-start(f32[17,8,128]{2,1,0:T(8,128)S(1)} %shard_map.62.refs_0_), channel_id=1, source_target_pairs={{0,16},{4,20},{8,24},{12,28},{16,0},{20,4},{24,8},{28,12},{1,17},{... | collective-permute-start | bytes 208904 | tf_op jit(solution)/shard_map/ppermute | solution.py:418
  18.3 7.2 %collective-permute-start.5 = (f32[17,8,128]{2,1,0:T(8,128)S(1)}, f32[17,8,128]{2,1,0:T(8,128)S(1)}, u32[]{:S(2)}, u32[]{:S(2)}) collective-permute-start(f32[17,8,128]{2,1,0:T(8,128)S(1)} %shard_map.60.refs_0_), channel_id=1, source_target_pairs={{0,16},{4,20},{8,24},{12,28},{16,0},{20,4},{24,8},{28,12},{1,17},{... | collective-permute-start | bytes 208904 | tf_op jit(solution)/shard_map/ppermute | solution.py:418
  20.9 6.5 %collective-permute-start.15 = (f32[17,8,128]{2,1,0:T(8,128)S(1)}, f32[17,8,128]{2,1,0:T(8,128)S(1)}, u32[]{:S(2)}, u32[]{:S(2)}) collective-permute-start(f32[17,8,128]{2,1,0:T(8,128)S(1)} %shard_map.63.refs_0_.refs_4_), channel_id=1, source_target_pairs={{0,12},{1,13},{2,14},{3,15},{4,8},{5,9},{6,10},{7,11},{8,4},{9,5},... | collective-permute-start | bytes 208904 | tf_op jit(solution)/shard_map/ppermute | solution.py:411
  23.1 5.9 %collective-permute-start.14 = (f32[17,8,128]{2,1,0:T(8,128)S(1)}, f32[17,8,128]{2,1,0:T(8,128)S(1)}, u32[]{:S(2)}, u32[]{:S(2)}) collective-permute-start(f32[17,8,128]{2,1,0:T(8,128)S(1)} %shard_map.63.refs_0_.refs_4_), channel_id=1, source_target_pairs={{0,4},{1,9},{2,6},{3,11},{4,0},{5,13},{6,2},{7,15},{8,12},{9,1},{1... | collective-permute-start | bytes 208904 | tf_op jit(solution)/shard_map/ppermute | solution.py:411
  23.9 5.1 %collective-permute-start.13 = (f32[17,8,128]{2,1,0:T(8,128)S(1)}, f32[17,8,128]{2,1,0:T(8,128)S(1)}, u32[]{:S(2)}, u32[]{:S(2)}) collective-permute-start(f32[17,8,128]{2,1,0:T(8,128)S(1)} %shard_map.63.refs_0_.refs_4_), channel_id=1, source_target_pairs={{0,8},{1,5},{2,10},{3,7},{4,12},{5,1},{6,14},{7,3},{8,0},{9,13},{1... | collective-permute-start | bytes 208904 | tf_op jit(solution)/shard_map/ppermute | solution.py:411
  25.4 5.7 %collective-permute-start.8 = (f32[17,8,128]{2,1,0:T(8,128)S(1)}, f32[17,8,128]{2,1,0:T(8,128)S(1)}, u32[]{:S(2)}, u32[]{:S(2)}) collective-permute-start(f32[17,8,128]{2,1,0:T(8,128)S(1)} %shard_map.61.refs_0_), channel_id=1, source_target_pairs={{0,12},{1,13},{2,14},{3,15},{4,8},{5,9},{6,10},{7,11},{8,4},{9,5},... | collective-permute-start | bytes 208904 | tf_op jit(solution)/shard_map/ppermute | solution.py:411
  26.6 5.2 %collective-permute-start.7 = (f32[17,8,128]{2,1,0:T(8,128)S(1)}, f32[17,8,128]{2,1,0:T(8,128)S(1)}, u32[]{:S(2)}, u32[]{:S(2)}) collective-permute-start(f32[17,8,128]{2,1,0:T(8,128)S(1)} %shard_map.61.refs_0_), channel_id=1, source_target_pairs={{0,4},{1,9},{2,6},{3,11},{4,0},{5,13},{6,2},{7,15},{8,12},{9,1},{1... | collective-permute-start | bytes 208904 | tf_op jit(solution)/shard_map/ppermute | solution.py:411
  27.4 4.4 %collective-permute-start.6 = (f32[17,8,128]{2,1,0:T(8,128)S(1)}, f32[17,8,128]{2,1,0:T(8,128)S(1)}, u32[]{:S(2)}, u32[]{:S(2)}) collective-permute-start(f32[17,8,128]{2,1,0:T(8,128)S(1)} %shard_map.61.refs_0_), channel_id=1, source_target_pairs={{0,8},{1,5},{2,10},{3,7},{4,12},{5,1},{6,14},{7,3},{8,0},{9,13},{1... | collective-permute-start | bytes 208904 | tf_op jit(solution)/shard_map/ppermute | solution.py:411

commit v24 on v21

--- a/solution.py
+++ b/solution.py
@@ -208,7 +208,7 @@
 
 
 def partners(dom):
-    return 0, 1 + dom % 2, 2 - dom % 2, 3
+    return 0, 2 - dom % 2, 1 + dom % 2, 3
 
 
 def edge_kernel(

time: 33 us -> 33.4 us (1.012)
    ppermute x12, waiting for transfers between devices: 3.94 us -> 4.34 us  [swap(): return lax.ppermute(array, ('grp', 'dom'), pairs)]
    ppermute x2, starting transfers between devices: 5.3 us -> 5.69 us  [over_grids(): other = lax.ppermute(total, 'grp', [(g, g ^ apart) for g in range(grids)])]
    ppermute x2, waiting for transfers between devices: 0.93 us -> 0.59 us  [over_grids(): other = lax.ppermute(total, 'grp', [(g, g ^ apart) for g in range(grids)])]
where the time goes in v24:
time: 33.4 us; the launch traced here: 33.2 us
  starting transfers between devices  21.7 us (65%)
  Pallas kernels  5.05 us (15%)
  waiting for transfers between devices  4.94 us (15%)
  between operations  1.51 us (5%)
    ppermute x12, starting transfers between devices, swap(): return lax.ppermute(array, ('grp', 'dom'), pairs)  14.8 us
    ppermute x2, starting transfers between devices, over_grids(): other = lax.ppermute(total, 'grp', [(g, g ^ apart) for g in range(grids)])  5.69 us
    pallas_call x11, Pallas kernels, call(): pl.pallas_call(kernel, out_shape=[jax.ShapeDtypeStruct(shape, jnp.float32...  5.05 us
    ppermute x12, waiting for transfers between devices, swap(): return lax.ppermute(array, ('grp', 'dom'), pairs)  4.34 us
  transfers between devices with their start and end apart: 16, of which 7 were waited for; matrix products, arithmetic and copies ran while one was open for 0% of the time, Pallas kernels for 12%

profile of v24, /device:TPU:0, one launch (start us, length us, event | category | flops | bytes accessed | tf_op | source)
XLA Modules:
  0.0 33.2 jit_solution(16696206703996875278)
XLA Ops:
  0.0 0.0 copy-start
  0.0 0.0 copy-start.1
  0.0 0.0 copy-start.2
  1.4 0.0 copy-done
  1.5 0.0 copy-done.1
  1.5 0.0 copy-done.2
  1.5 0.1 shard_map.58
  1.5 0.5 %collective-permute-start = (f32[16,16,128]{2,1,0:T(8,128)S(1)}, f32[16,16,128]{2,1,0:T(8,128)S(1)}, u32[]{:S(2)}, u32[]{:S(2)}) collective-permute-start(f32[16,16,128]{2,1,0:T(8,128)S(1)} %get-tuple-element.21), channel_id=1, source_target_pairs={{0,1},{1,0},{2,3},{3,2},{4,5},{5,4},{6,7},{7,6},{8,9},{9,8},{10,11... | collective-permute-start | bytes 393224 | tf_op jit(solution)/shard_map/ppermute | solution.py:377
  2.1 0.7 %collective-permute-start.1 = (f32[16,16,128]{2,1,0:T(8,128)S(1)}, f32[16,16,128]{2,1,0:T(8,128)S(1)}, u32[]{:S(2)}, u32[]{:S(2)}) collective-permute-start(f32[16,16,128]{2,1,0:T(8,128)S(1)} %get-tuple-element.22), channel_id=1, source_target_pairs={{0,0},{1,2},{2,1},{3,3},{4,4},{5,6},{6,5},{7,7},{8,8},{9,10},{10,9... | collective-permute-start | bytes 393224 | tf_op jit(solution)/shard_map/ppermute | solution.py:378
  2.7 2.1 %shard_map.57 = (f32[16,8,8,128]{3,2,1,0:T(8,128)S(1)}, f32[17,8,128]{2,1,0:T(8,128)S(1)}, f32[17,8,128]{2,1,0:T(8,128)S(1)}, f32[17,8,128]{2,1,0:T(8,128)S(1)}, f32[17,8,128]{2,1,0:T(8,128)S(1)}) custom-call(s32[1]{0:T(128)} %bitcast.dom_ref, s32[1]{0:T(128)} %bitcast.1.me_ref, f32[4,8,128]{2,1,0:T(8,128)S(1)} %get-tuple-element.19.weight_ref, ...), custom_call_target="tpu_custom_call" | custom-call | flops 5242880 | bytes 1589256 | tf_op jit(solution)/shard_map/pallas_call | solution.py:337
  4.8 3.6 %collective-permute-start.9 = (f32[17,8,128]{2,1,0:T(8,128)S(1)}, f32[17,8,128]{2,1,0:T(8,128)S(1)}, u32[]{:S(2)}, u32[]{:S(2)}) collective-permute-start(f32[17,8,128]{2,1,0:T(8,128)S(1)} %get-tuple-element.28), channel_id=1, source_target_pairs={{0,12},{1,13},{2,14},{3,15},{4,8},{5,9},{6,10},{7,11},{8,4},{9,5},... | collective-permute-start | bytes 208904 | tf_op jit(solution)/shard_map/ppermute | solution.py:408
  8.4 0.4 %collective-permute-start.10 = (f32[17,8,128]{2,1,0:T(8,128)S(1)}, f32[17,8,128]{2,1,0:T(8,128)S(1)}, u32[]{:S(2)}, u32[]{:S(2)}) collective-permute-start(f32[17,8,128]{2,1,0:T(8,128)S(1)} %get-tuple-element.29), channel_id=1, source_target_pairs={{0,8},{1,5},{2,10},{3,7},{4,12},{5,1},{6,14},{7,3},{8,0},{9,13},{1... | collective-permute-start | bytes 208904 | tf_op jit(solution)/shard_map/ppermute | solution.py:408
  8.8 0.2 collective-permute-start.11
  9.0 0.0 collective-permute-done.refs_3_
  9.0 0.0 collective-permute-done.1.refs_4_
  9.0 0.9 %shard_map.59 = (f32[17,8,128]{2,1,0:T(8,128)S(1)}, f32[17,8,128]{2,1,0:T(8,128)S(1)}, f32[17,8,128]{2,1,0:T(8,128)S(1)}, f32[17,8,128]{2,1,0:T(8,128)S(1)}) custom-call(s32[1]{0:T(128)} %bitcast.dom_ref, s32[1]{0:T(128)} %bitcast.1.me_ref, f32[4,8,128]{2,1,0:T(8,128)S(1)} %get-tuple-element.19.weight_ref, f32[8,16,8,128]{3,2,1,0:T(8,128)S(1)} %bitcast.16, ...), custom_call_target="tpu_custom_call" | custom-call | flops 2621440 | bytes 2375688 | tf_op jit(solution)/shard_map/pallas_call | solution.py:337
  10.0 2.9 %collective-permute-start.2 = (f32[17,8,128]{2,1,0:T(8,128)S(1)}, f32[17,8,128]{2,1,0:T(8,128)S(1)}, u32[]{:S(2)}, u32[]{:S(2)}) collective-permute-start(f32[17,8,128]{2,1,0:T(8,128)S(1)} %get-tuple-element.24), channel_id=1, source_target_pairs={{0,12},{1,13},{2,14},{3,15},{4,8},{5,9},{6,10},{7,11},{8,4},{9,5},... | collective-permute-start | bytes 208904 | tf_op jit(solution)/shard_map/ppermute | solution.py:408
  12.9 0.4 %collective-permute-start.3 = (f32[17,8,128]{2,1,0:T(8,128)S(1)}, f32[17,8,128]{2,1,0:T(8,128)S(1)}, u32[]{:S(2)}, u32[]{:S(2)}) collective-permute-start(f32[17,8,128]{2,1,0:T(8,128)S(1)} %get-tuple-element.25), channel_id=1, source_target_pairs={{0,8},{1,5},{2,10},{3,7},{4,12},{5,1},{6,14},{7,3},{8,0},{9,13},{1... | collective-permute-start | bytes 208904 | tf_op jit(solution)/shard_map/ppermute | solution.py:408
  13.3 0.0 collective-permute-done.9.refs_1_
  13.3 0.2 collective-permute-start.4
  13.5 0.0 collective-permute-done.10.refs_2_
  13.5 0.5 %collective-permute-done.11.refs_3_ = f32[17,8,128]{2,1,0:T(8,128)S(1)} collective-permute-done((f32[17,8,128]{2,1,0:T(8,128)S(1)}, f32[17,8,128]{2,1,0:T(8,128)S(1)}, u32[]{:S(2)}, u32[]{:S(2)}) %collective-permute-start.11) | collective-permute-done | bytes 69664 | tf_op jit(solution)/shard_map/ppermute | solution.py:408
  14.1 2.7 %collective-permute-start.12 = (f32[17,8,128]{2,1,0:T(8,128)S(1)}, f32[17,8,128]{2,1,0:T(8,128)S(1)}, u32[]{:S(2)}, u32[]{:S(2)}) collective-permute-start(f32[17,8,128]{2,1,0:T(8,128)S(1)} %shard_map.62.refs_0_), channel_id=1, source_target_pairs={{0,16},{4,20},{8,24},{12,28},{16,0},{20,4},{24,8},{28,12},{1,17},{... | collective-permute-start | bytes 208904 | tf_op jit(solution)/shard_map/ppermute | solution.py:415
  16.7 0.0 collective-permute-done.2.refs_1_
  16.7 0.7 %collective-permute-done.3.refs_2_ = f32[17,8,128]{2,1,0:T(8,128)S(1)} collective-permute-done((f32[17,8,128]{2,1,0:T(8,128)S(1)}, f32[17,8,128]{2,1,0:T(8,128)S(1)}, u32[]{:S(2)}, u32[]{:S(2)}) %collective-permute-start.3) | collective-permute-done | bytes 69664 | tf_op jit(solution)/shard_map/ppermute | solution.py:408
  17.4 0.7 %collective-permute-done.4.refs_3_ = f32[17,8,128]{2,1,0:T(8,128)S(1)} collective-permute-done((f32[17,8,128]{2,1,0:T(8,128)S(1)}, f32[17,8,128]{2,1,0:T(8,128)S(1)}, u32[]{:S(2)}, u32[]{:S(2)}) %collective-permute-start.4) | collective-permute-done | bytes 69664 | tf_op jit(solution)/shard_map/ppermute | solution.py:408
  18.2 3.0 %collective-permute-start.5 = (f32[17,8,128]{2,1,0:T(8,128)S(1)}, f32[17,8,128]{2,1,0:T(8,128)S(1)}, u32[]{:S(2)}, u32[]{:S(2)}) collective-permute-start(f32[17,8,128]{2,1,0:T(8,128)S(1)} %shard_map.60.refs_0_), channel_id=1, source_target_pairs={{0,16},{4,20},{8,24},{12,28},{16,0},{20,4},{24,8},{28,12},{1,17},{... | collective-permute-start | bytes 208904 | tf_op jit(solution)/shard_map/ppermute | solution.py:415
  21.2 0.0 collective-permute-done.12.refs_1_
  21.2 1.9 %collective-permute-start.15 = (f32[17,8,128]{2,1,0:T(8,128)S(1)}, f32[17,8,128]{2,1,0:T(8,128)S(1)}, u32[]{:S(2)}, u32[]{:S(2)}) collective-permute-start(f32[17,8,128]{2,1,0:T(8,128)S(1)} %shard_map.63.refs_0_.refs_4_), channel_id=1, source_target_pairs={{0,12},{1,13},{2,14},{3,15},{4,8},{5,9},{6,10},{7,11},{8,4},{9,5},... | collective-permute-start | bytes 208904 | tf_op jit(solution)/shard_map/ppermute | solution.py:408
  23.1 1.0 %collective-permute-start.14 = (f32[17,8,128]{2,1,0:T(8,128)S(1)}, f32[17,8,128]{2,1,0:T(8,128)S(1)}, u32[]{:S(2)}, u32[]{:S(2)}) collective-permute-start(f32[17,8,128]{2,1,0:T(8,128)S(1)} %shard_map.63.refs_0_.refs_4_), channel_id=1, source_target_pairs={{0,4},{1,9},{2,6},{3,11},{4,0},{5,13},{6,2},{7,15},{8,12},{9,1},{1... | collective-permute-start | bytes 208904 | tf_op jit(solution)/shard_map/ppermute | solution.py:408
  24.0 0.7 %collective-permute-start.13 = (f32[17,8,128]{2,1,0:T(8,128)S(1)}, f32[17,8,128]{2,1,0:T(8,128)S(1)}, u32[]{:S(2)}, u32[]{:S(2)}) collective-permute-start(f32[17,8,128]{2,1,0:T(8,128)S(1)} %shard_map.63.refs_0_.refs_4_), channel_id=1, source_target_pairs={{0,8},{1,5},{2,10},{3,7},{4,12},{5,1},{6,14},{7,3},{8,0},{9,13},{1... | collective-permute-start | bytes 208904 | tf_op jit(solution)/shard_map/ppermute | solution.py:408
  24.8 0.6 %collective-permute-done.5.refs_1_ = f32[17,8,128]{2,1,0:T(8,128)S(1)} collective-permute-done((f32[17,8,128]{2,1,0:T(8,128)S(1)}, f32[17,8,128]{2,1,0:T(8,128)S(1)}, u32[]{:S(2)}, u32[]{:S(2)}) %collective-permute-start.5) | collective-permute-done | bytes 69664 | tf_op jit(solution)/shard_map/ppermute | solution.py:415
  25.4 1.3 %collective-permute-start.8 = (f32[17,8,128]{2,1,0:T(8,128)S(1)}, f32[17,8,128]{2,1,0:T(8,128)S(1)}, u32[]{:S(2)}, u32[]{:S(2)}) collective-permute-start(f32[17,8,128]{2,1,0:T(8,128)S(1)} %shard_map.61.refs_0_), channel_id=1, source_target_pairs={{0,12},{1,13},{2,14},{3,15},{4,8},{5,9},{6,10},{7,11},{8,4},{9,5},... | collective-permute-start | bytes 208904 | tf_op jit(solution)/shard_map/ppermute | solution.py:408
  26.7 1.0 %collective-permute-start.7 = (f32[17,8,128]{2,1,0:T(8,128)S(1)}, f32[17,8,128]{2,1,0:T(8,128)S(1)}, u32[]{:S(2)}, u32[]{:S(2)}) collective-permute-start(f32[17,8,128]{2,1,0:T(8,128)S(1)} %shard_map.61.refs_0_), channel_id=1, source_target_pairs={{0,4},{1,9},{2,6},{3,11},{4,0},{5,13},{6,2},{7,15},{8,12},{9,1},{1... | collective-permute-start | bytes 208904 | tf_op jit(solution)/shard_map/ppermute | solution.py:408
  27.6 0.1 collective-permute-done.15.refs_3_.refs_7_
  27.7 1.3 %collective-permute-start.6 = (f32[17,8,128]{2,1,0:T(8,128)S(1)}, f32[17,8,128]{2,1,0:T(8,128)S(1)}, u32[]{:S(2)}, u32[]{:S(2)}) collective-permute-start(f32[17,8,128]{2,1,0:T(8,128)S(1)} %shard_map.61.refs_0_), channel_id=1, source_target_pairs={{0,8},{1,5},{2,10},{3,7},{4,12},{5,1},{6,14},{7,3},{8,0},{9,13},{1... | collective-permute-start | bytes 208904 | tf_op jit(solution)/shard_map/ppermute | solution.py:408
  28.9 0.0 collective-permute-done.14.refs_2_.refs_6_
  28.9 0.0 collective-permute-done.13.refs_1_.refs_5_
  28.9 1.0 %shard_map.64.refs_8_ = f32[8,16,8,128]{3,2,1,0:T(8,128)} custom-call(s32[1]{0:T(128)} %bitcast.dom_ref, s32[1]{0:T(128)} %bitcast.1.me_ref, f32[3,8,128]{2,1,0:T(8,128)S(1)} %get-tuple-element.18.keep_ref, f32[17,8,128]{2,1,0:T(8,128)S(1)} %shard_map.63.refs_0_.refs_4_, f32[17,8,128]{2,1,0:T(8,128)S(1)} %collective-permute-done.13.refs_1_.refs_5_, ...), custom_call_target="tpu_custom_call" | custom-call | bytes 290824 | tf_op jit(solution)/shard_map/pallas_call | solution.py:337
  29.9 1.2 %collective-permute-done.8.refs_3_ = f32[17,8,128]{2,1,0:T(8,128)S(1)} collective-permute-done((f32[17,8,128]{2,1,0:T(8,128)S(1)}, f32[17,8,128]{2,1,0:T(8,128)S(1)}, u32[]{:S(2)}, u32[]{:S(2)}) %collective-permute-start.8) | collective-permute-done | bytes 69664 | tf_op jit(solution)/shard_map/ppermute | solution.py:408
  31.1 1.1 %collective-permute-done.7.refs_2_ = f32[17,8,128]{2,1,0:T(8,128)S(1)} collective-permute-done((f32[17,8,128]{2,1,0:T(8,128)S(1)}, f32[17,8,128]{2,1,0:T(8,128)S(1)}, u32[]{:S(2)}, u32[]{:S(2)}) %collective-permute-start.7) | collective-permute-done | bytes 69664 | tf_op jit(solution)/shard_map/ppermute | solution.py:408
  32.2 0.0 collective-permute-done.6.refs_1_
  32.2 1.0 %shard_map.65 = f32[8,16,8,128]{3,2,1,0:T(8,128)} custom-call(s32[1]{0:T(128)} %bitcast.dom_ref, s32[1]{0:T(128)} %bitcast.1.me_ref, f32[3,8,128]{2,1,0:T(8,128)S(1)} %get-tuple-element.18.keep_ref, f32[17,8,128]{2,1,0:T(8,128)S(1)} %shard_map.61.refs_0_, f32[17,8,128]{2,1,0:T(8,128)S(1)} %collective-permute-done.6.refs_1_, ...), custom_call_target="tpu_custom_call", output_to_operand_aliasing={{}: (11, {})} | custom-call | bytes 1093640 | tf_op jit(solution)/shard_map/pallas_call | solution.py:337
  (6 shorter events, 0.1 us)
Async XLA Ops:
  0.0 1.4 %copy-start = (f32[1,64,2048]{2,1,0:T(8,128)S(1)}, f32[1,64,2048]{2,1,0:T(8,128)}, u32[]{:S(2)}) copy-start(f32[1,64,2048]{2,1,0:T(8,128)} %param.5) | copy-start | bytes 1572868
  0.0 1.5 %copy-start.1 = (f32[1,64,2048]{2,1,0:T(8,128)S(1)}, f32[1,64,2048]{2,1,0:T(8,128)}, u32[]{:S(2)}) copy-start(f32[1,64,2048]{2,1,0:T(8,128)} %param.6) | copy-start | bytes 1572868
  0.0 1.5 %copy-start.2 = (f32[1,64,2048]{2,1,0:T(8,128)S(1)}, f32[1,64,2048]{2,1,0:T(8,128)}, u32[]{:S(2)}) copy-start(f32[1,64,2048]{2,1,0:T(8,128)} %param.7) | copy-start | bytes 1572868
  1.5 7.5 %collective-permute-start = (f32[16,16,128]{2,1,0:T(8,128)S(1)}, f32[16,16,128]{2,1,0:T(8,128)S(1)}, u32[]{:S(2)}, u32[]{:S(2)}) collective-permute-start(f32[16,16,128]{2,1,0:T(8,128)S(1)} %get-tuple-element.21), channel_id=1, source_target_pairs={{0,1},{1,0},{2,3},{3,2},{4,5},{5,4},{6,7},{7,6},{8,9},{9,8},{10,11... | collective-permute-start | bytes 393224 | tf_op jit(solution)/shard_map/ppermute | solution.py:377
  2.1 7.0 %collective-permute-start.1 = (f32[16,16,128]{2,1,0:T(8,128)S(1)}, f32[16,16,128]{2,1,0:T(8,128)S(1)}, u32[]{:S(2)}, u32[]{:S(2)}) collective-permute-start(f32[16,16,128]{2,1,0:T(8,128)S(1)} %get-tuple-element.22), channel_id=1, source_target_pairs={{0,0},{1,2},{2,1},{3,3},{4,4},{5,6},{6,5},{7,7},{8,8},{9,10},{10,9... | collective-permute-start | bytes 393224 | tf_op jit(solution)/shard_map/ppermute | solution.py:378
  4.8 8.5 %collective-permute-start.9 = (f32[17,8,128]{2,1,0:T(8,128)S(1)}, f32[17,8,128]{2,1,0:T(8,128)S(1)}, u32[]{:S(2)}, u32[]{:S(2)}) collective-permute-start(f32[17,8,128]{2,1,0:T(8,128)S(1)} %get-tuple-element.28), channel_id=1, source_target_pairs={{0,12},{1,13},{2,14},{3,15},{4,8},{5,9},{6,10},{7,11},{8,4},{9,5},... | collective-permute-start | bytes 208904 | tf_op jit(solution)/shard_map/ppermute | solution.py:408
  8.4 5.1 %collective-permute-start.10 = (f32[17,8,128]{2,1,0:T(8,128)S(1)}, f32[17,8,128]{2,1,0:T(8,128)S(1)}, u32[]{:S(2)}, u32[]{:S(2)}) collective-permute-start(f32[17,8,128]{2,1,0:T(8,128)S(1)} %get-tuple-element.29), channel_id=1, source_target_pairs={{0,8},{1,5},{2,10},{3,7},{4,12},{5,1},{6,14},{7,3},{8,0},{9,13},{1... | collective-permute-start | bytes 208904 | tf_op jit(solution)/shard_map/ppermute | solution.py:408
  8.8 5.2 %collective-permute-start.11 = (f32[17,8,128]{2,1,0:T(8,128)S(1)}, f32[17,8,128]{2,1,0:T(8,128)S(1)}, u32[]{:S(2)}, u32[]{:S(2)}) collective-permute-start(f32[17,8,128]{2,1,0:T(8,128)S(1)} %get-tuple-element.30), channel_id=1, source_target_pairs={{0,4},{1,9},{2,6},{3,11},{4,0},{5,13},{6,2},{7,15},{8,12},{9,1},{1... | collective-permute-start | bytes 208904 | tf_op jit(solution)/shard_map/ppermute | solution.py:408
  10.0 6.7 %collective-permute-start.2 = (f32[17,8,128]{2,1,0:T(8,128)S(1)}, f32[17,8,128]{2,1,0:T(8,128)S(1)}, u32[]{:S(2)}, u32[]{:S(2)}) collective-permute-start(f32[17,8,128]{2,1,0:T(8,128)S(1)} %get-tuple-element.24), channel_id=1, source_target_pairs={{0,12},{1,13},{2,14},{3,15},{4,8},{5,9},{6,10},{7,11},{8,4},{9,5},... | collective-permute-start | bytes 208904 | tf_op jit(solution)/shard_map/ppermute | solution.py:408
  12.9 4.5 %collective-permute-start.3 = (f32[17,8,128]{2,1,0:T(8,128)S(1)}, f32[17,8,128]{2,1,0:T(8,128)S(1)}, u32[]{:S(2)}, u32[]{:S(2)}) collective-permute-start(f32[17,8,128]{2,1,0:T(8,128)S(1)} %get-tuple-element.25), channel_id=1, source_target_pairs={{0,8},{1,5},{2,10},{3,7},{4,12},{5,1},{6,14},{7,3},{8,0},{9,13},{1... | collective-permute-start | bytes 208904 | tf_op jit(solution)/shard_map/ppermute | solution.py:408
  13.3 4.8 %collective-permute-start.4 = (f32[17,8,128]{2,1,0:T(8,128)S(1)}, f32[17,8,128]{2,1,0:T(8,128)S(1)}, u32[]{:S(2)}, u32[]{:S(2)}) collective-permute-start(f32[17,8,128]{2,1,0:T(8,128)S(1)} %get-tuple-element.26), channel_id=1, source_target_pairs={{0,4},{1,9},{2,6},{3,11},{4,0},{5,13},{6,2},{7,15},{8,12},{9,1},{1... | collective-permute-start | bytes 208904 | tf_op jit(solution)/shard_map/ppermute | solution.py:408
  14.1 7.2 %collective-permute-start.12 = (f32[17,8,128]{2,1,0:T(8,128)S(1)}, f32[17,8,128]{2,1,0:T(8,128)S(1)}, u32[]{:S(2)}, u32[]{:S(2)}) collective-permute-start(f32[17,8,128]{2,1,0:T(8,128)S(1)} %shard_map.62.refs_0_), channel_id=1, source_target_pairs={{0,16},{4,20},{8,24},{12,28},{16,0},{20,4},{24,8},{28,12},{1,17},{... | collective-permute-start | bytes 208904 | tf_op jit(solution)/shard_map/ppermute | solution.py:415
  18.2 7.2 %collective-permute-start.5 = (f32[17,8,128]{2,1,0:T(8,128)S(1)}, f32[17,8,128]{2,1,0:T(8,128)S(1)}, u32[]{:S(2)}, u32[]{:S(2)}) collective-permute-start(f32[17,8,128]{2,1,0:T(8,128)S(1)} %shard_map.60.refs_0_), channel_id=1, source_target_pairs={{0,16},{4,20},{8,24},{12,28},{16,0},{20,4},{24,8},{28,12},{1,17},{... | collective-permute-start | bytes 208904 | tf_op jit(solution)/shard_map/ppermute | solution.py:415
  21.2 6.5 %collective-permute-start.15 = (f32[17,8,128]{2,1,0:T(8,128)S(1)}, f32[17,8,128]{2,1,0:T(8,128)S(1)}, u32[]{:S(2)}, u32[]{:S(2)}) collective-permute-start(f32[17,8,128]{2,1,0:T(8,128)S(1)} %shard_map.63.refs_0_.refs_4_), channel_id=1, source_target_pairs={{0,12},{1,13},{2,14},{3,15},{4,8},{5,9},{6,10},{7,11},{8,4},{9,5},... | collective-permute-start | bytes 208904 | tf_op jit(solution)/shard_map/ppermute | solution.py:408
  23.1 5.9 %collective-permute-start.14 = (f32[17,8,128]{2,1,0:T(8,128)S(1)}, f32[17,8,128]{2,1,0:T(8,128)S(1)}, u32[]{:S(2)}, u32[]{:S(2)}) collective-permute-start(f32[17,8,128]{2,1,0:T(8,128)S(1)} %shard_map.63.refs_0_.refs_4_), channel_id=1, source_target_pairs={{0,4},{1,9},{2,6},{3,11},{4,0},{5,13},{6,2},{7,15},{8,12},{9,1},{1... | collective-permute-start | bytes 208904 | tf_op jit(solution)/shard_map/ppermute | solution.py:408
  24.0 4.9 %collective-permute-start.13 = (f32[17,8,128]{2,1,0:T(8,128)S(1)}, f32[17,8,128]{2,1,0:T(8,128)S(1)}, u32[]{:S(2)}, u32[]{:S(2)}) collective-permute-start(f32[17,8,128]{2,1,0:T(8,128)S(1)} %shard_map.63.refs_0_.refs_4_), channel_id=1, source_target_pairs={{0,8},{1,5},{2,10},{3,7},{4,12},{5,1},{6,14},{7,3},{8,0},{9,13},{1... | collective-permute-start | bytes 208904 | tf_op jit(solution)/shard_map/ppermute | solution.py:408
  25.4 5.7 %collective-permute-start.8 = (f32[17,8,128]{2,1,0:T(8,128)S(1)}, f32[17,8,128]{2,1,0:T(8,128)S(1)}, u32[]{:S(2)}, u32[]{:S(2)}) collective-permute-start(f32[17,8,128]{2,1,0:T(8,128)S(1)} %shard_map.61.refs_0_), channel_id=1, source_target_pairs={{0,12},{1,13},{2,14},{3,15},{4,8},{5,9},{6,10},{7,11},{8,4},{9,5},... | collective-permute-start | bytes 208904 | tf_op jit(solution)/shard_map/ppermute | solution.py:408
  26.7 5.6 %collective-permute-start.7 = (f32[17,8,128]{2,1,0:T(8,128)S(1)}, f32[17,8,128]{2,1,0:T(8,128)S(1)}, u32[]{:S(2)}, u32[]{:S(2)}) collective-permute-start(f32[17,8,128]{2,1,0:T(8,128)S(1)} %shard_map.61.refs_0_), channel_id=1, source_target_pairs={{0,4},{1,9},{2,6},{3,11},{4,0},{5,13},{6,2},{7,15},{8,12},{9,1},{1... | collective-permute-start | bytes 208904 | tf_op jit(solution)/shard_map/ppermute | solution.py:408
  27.7 4.5 %collective-permute-start.6 = (f32[17,8,128]{2,1,0:T(8,128)S(1)}, f32[17,8,128]{2,1,0:T(8,128)S(1)}, u32[]{:S(2)}, u32[]{:S(2)}) collective-permute-start(f32[17,8,128]{2,1,0:T(8,128)S(1)} %shard_map.61.refs_0_), channel_id=1, source_target_pairs={{0,8},{1,5},{2,10},{3,7},{4,12},{5,1},{6,14},{7,3},{8,0},{9,13},{1... | collective-permute-start | bytes 208904 | tf_op jit(solution)/shard_map/ppermute | solution.py:408

commit v25 on v21

--- a/solution.py
+++ b/solution.py
@@ -155,7 +155,7 @@
             far_ref[j, at] = jnp.where(odd, to_next[k], to_prev[k])
             near_ref[j, at] = jnp.where(odd, to_prev[k], to_next[k])
 
-    per_strip(strips, body, 4)
+    per_strip(strips, body, min(strips, UNROLL))
 
 
 def middle_tiles(many):
@@ -239,7 +239,7 @@
             for e, tile in enumerate(column):
                 slab[k, j, e * TILE : (e + 1) * TILE] = tile
 
-    per_strip(strips, stage, 4)
+    per_strip(strips, stage, min(strips, UNROLL))
     slabs = flat(slab)
 
     def load(k, j, t):

time: 33 us -> 32.9 us (level)
  no operation moved by 1% of the time
where the time goes in v25:
time: 32.9 us; the launch traced here: 32.8 us
  starting transfers between devices  21.4 us (65%)
  Pallas kernels  5 us (15%)
  waiting for transfers between devices  4.87 us (15%)
  between operations  1.52 us (5%)
    ppermute x12, starting transfers between devices, swap(): return lax.ppermute(array, ('grp', 'dom'), pairs)  14.9 us
    ppermute x2, starting transfers between devices, over_grids(): other = lax.ppermute(total, 'grp', [(g, g ^ apart) for g in range(grids)])  5.3 us
    pallas_call x11, Pallas kernels, call(): pl.pallas_call(kernel, out_shape=[jax.ShapeDtypeStruct(shape, jnp.float32...  5 us
    ppermute x12, waiting for transfers between devices, swap(): return lax.ppermute(array, ('grp', 'dom'), pairs)  3.94 us
    ppermute x2, waiting for transfers between devices, over_grids(): other = lax.ppermute(total, 'grp', [(g, g ^ apart) for g in range(grids)])  0.93 us
  transfers between devices with their start and end apart: 16, of which 7 were waited for; matrix products, arithmetic and copies ran while one was open for 0% of the time, Pallas kernels for 12%

profile of v25, /device:TPU:0, one launch (start us, length us, event | category | flops | bytes accessed | tf_op | source)
XLA Modules:
  0.0 32.8 jit_solution(2187625964856846078)
XLA Ops:
  0.0 0.0 copy-start
  0.0 0.0 copy-start.1
  0.0 0.0 copy-start.2
  1.4 0.0 copy-done
  1.5 0.0 copy-done.1
  1.5 0.0 copy-done.2
  1.5 0.5 %collective-permute-start = (f32[16,16,128]{2,1,0:T(8,128)S(1)}, f32[16,16,128]{2,1,0:T(8,128)S(1)}, u32[]{:S(2)}, u32[]{:S(2)}) collective-permute-start(f32[16,16,128]{2,1,0:T(8,128)S(1)} %get-tuple-element.21), channel_id=1, source_target_pairs={{0,1},{1,0},{2,3},{3,2},{4,5},{5,4},{6,7},{7,6},{8,9},{9,8},{10,11... | collective-permute-start | bytes 393224 | tf_op jit(solution)/shard_map/ppermute | solution.py:377
  2.0 0.7 %collective-permute-start.1 = (f32[16,16,128]{2,1,0:T(8,128)S(1)}, f32[16,16,128]{2,1,0:T(8,128)S(1)}, u32[]{:S(2)}, u32[]{:S(2)}) collective-permute-start(f32[16,16,128]{2,1,0:T(8,128)S(1)} %get-tuple-element.22), channel_id=1, source_target_pairs={{0,0},{1,2},{2,1},{3,3},{4,4},{5,6},{6,5},{7,7},{8,8},{9,10},{10,9... | collective-permute-start | bytes 393224 | tf_op jit(solution)/shard_map/ppermute | solution.py:378
  2.7 2.1 %shard_map.57 = (f32[16,8,8,128]{3,2,1,0:T(8,128)S(1)}, f32[17,8,128]{2,1,0:T(8,128)S(1)}, f32[17,8,128]{2,1,0:T(8,128)S(1)}, f32[17,8,128]{2,1,0:T(8,128)S(1)}, f32[17,8,128]{2,1,0:T(8,128)S(1)}) custom-call(s32[1]{0:T(128)} %bitcast.dom_ref, s32[1]{0:T(128)} %bitcast.1.me_ref, f32[4,8,128]{2,1,0:T(8,128)S(1)} %get-tuple-element.19.weight_ref, ...), custom_call_target="tpu_custom_call" | custom-call | flops 5242880 | bytes 1589256 | tf_op jit(solution)/shard_map/pallas_call | solution.py:337
  4.8 3.6 %collective-permute-start.9 = (f32[17,8,128]{2,1,0:T(8,128)S(1)}, f32[17,8,128]{2,1,0:T(8,128)S(1)}, u32[]{:S(2)}, u32[]{:S(2)}) collective-permute-start(f32[17,8,128]{2,1,0:T(8,128)S(1)} %get-tuple-element.28), channel_id=1, source_target_pairs={{0,12},{1,13},{2,14},{3,15},{4,8},{5,9},{6,10},{7,11},{8,4},{9,5},... | collective-permute-start | bytes 208904 | tf_op jit(solution)/shard_map/ppermute | solution.py:408
  8.4 0.5 %collective-permute-start.10 = (f32[17,8,128]{2,1,0:T(8,128)S(1)}, f32[17,8,128]{2,1,0:T(8,128)S(1)}, u32[]{:S(2)}, u32[]{:S(2)}) collective-permute-start(f32[17,8,128]{2,1,0:T(8,128)S(1)} %get-tuple-element.29), channel_id=1, source_target_pairs={{0,4},{1,9},{2,6},{3,11},{4,0},{5,13},{6,2},{7,15},{8,12},{9,1},{1... | collective-permute-start | bytes 208904 | tf_op jit(solution)/shard_map/ppermute | solution.py:408
  8.9 0.1 collective-permute-start.11
  9.0 0.0 collective-permute-done.refs_3_
  9.0 0.0 collective-permute-done.1.refs_4_
  9.0 0.9 %shard_map.59 = (f32[17,8,128]{2,1,0:T(8,128)S(1)}, f32[17,8,128]{2,1,0:T(8,128)S(1)}, f32[17,8,128]{2,1,0:T(8,128)S(1)}, f32[17,8,128]{2,1,0:T(8,128)S(1)}) custom-call(s32[1]{0:T(128)} %bitcast.dom_ref, s32[1]{0:T(128)} %bitcast.1.me_ref, f32[4,8,128]{2,1,0:T(8,128)S(1)} %get-tuple-element.19.weight_ref, f32[8,16,8,128]{3,2,1,0:T(8,128)S(1)} %bitcast.16, ...), custom_call_target="tpu_custom_call" | custom-call | flops 2621440 | bytes 2375688 | tf_op jit(solution)/shard_map/pallas_call | solution.py:337
  9.9 2.9 %collective-permute-start.2 = (f32[17,8,128]{2,1,0:T(8,128)S(1)}, f32[17,8,128]{2,1,0:T(8,128)S(1)}, u32[]{:S(2)}, u32[]{:S(2)}) collective-permute-start(f32[17,8,128]{2,1,0:T(8,128)S(1)} %get-tuple-element.24), channel_id=1, source_target_pairs={{0,12},{1,13},{2,14},{3,15},{4,8},{5,9},{6,10},{7,11},{8,4},{9,5},... | collective-permute-start | bytes 208904 | tf_op jit(solution)/shard_map/ppermute | solution.py:408
  12.8 0.5 %collective-permute-start.3 = (f32[17,8,128]{2,1,0:T(8,128)S(1)}, f32[17,8,128]{2,1,0:T(8,128)S(1)}, u32[]{:S(2)}, u32[]{:S(2)}) collective-permute-start(f32[17,8,128]{2,1,0:T(8,128)S(1)} %get-tuple-element.25), channel_id=1, source_target_pairs={{0,4},{1,9},{2,6},{3,11},{4,0},{5,13},{6,2},{7,15},{8,12},{9,1},{1... | collective-permute-start | bytes 208904 | tf_op jit(solution)/shard_map/ppermute | solution.py:408
  13.4 0.0 collective-permute-done.9.refs_1_
  13.4 0.1 collective-permute-start.4
  13.5 0.0 collective-permute-done.10.refs_2_
  13.5 0.4 %collective-permute-done.11.refs_3_ = f32[17,8,128]{2,1,0:T(8,128)S(1)} collective-permute-done((f32[17,8,128]{2,1,0:T(8,128)S(1)}, f32[17,8,128]{2,1,0:T(8,128)S(1)}, u32[]{:S(2)}, u32[]{:S(2)}) %collective-permute-start.11) | collective-permute-done | bytes 69664 | tf_op jit(solution)/shard_map/ppermute | solution.py:408
  14.0 2.7 %collective-permute-start.12 = (f32[17,8,128]{2,1,0:T(8,128)S(1)}, f32[17,8,128]{2,1,0:T(8,128)S(1)}, u32[]{:S(2)}, u32[]{:S(2)}) collective-permute-start(f32[17,8,128]{2,1,0:T(8,128)S(1)} %shard_map.62.refs_0_), channel_id=1, source_target_pairs={{0,16},{4,20},{8,24},{12,28},{16,0},{20,4},{24,8},{28,12},{1,17},{... | collective-permute-start | bytes 208904 | tf_op jit(solution)/shard_map/ppermute | solution.py:415
  16.6 0.0 collective-permute-done.2.refs_1_
  16.6 0.7 %collective-permute-done.3.refs_2_ = f32[17,8,128]{2,1,0:T(8,128)S(1)} collective-permute-done((f32[17,8,128]{2,1,0:T(8,128)S(1)}, f32[17,8,128]{2,1,0:T(8,128)S(1)}, u32[]{:S(2)}, u32[]{:S(2)}) %collective-permute-start.3) | collective-permute-done | bytes 69664 | tf_op jit(solution)/shard_map/ppermute | solution.py:408
  17.4 0.8 %collective-permute-done.4.refs_3_ = f32[17,8,128]{2,1,0:T(8,128)S(1)} collective-permute-done((f32[17,8,128]{2,1,0:T(8,128)S(1)}, f32[17,8,128]{2,1,0:T(8,128)S(1)}, u32[]{:S(2)}, u32[]{:S(2)}) %collective-permute-start.4) | collective-permute-done | bytes 69664 | tf_op jit(solution)/shard_map/ppermute | solution.py:408
  18.2 2.6 %collective-permute-start.5 = (f32[17,8,128]{2,1,0:T(8,128)S(1)}, f32[17,8,128]{2,1,0:T(8,128)S(1)}, u32[]{:S(2)}, u32[]{:S(2)}) collective-permute-start(f32[17,8,128]{2,1,0:T(8,128)S(1)} %shard_map.60.refs_0_), channel_id=1, source_target_pairs={{0,16},{4,20},{8,24},{12,28},{16,0},{20,4},{24,8},{28,12},{1,17},{... | collective-permute-start | bytes 208904 | tf_op jit(solution)/shard_map/ppermute | solution.py:415
  20.9 0.0 collective-permute-done.12.refs_1_
  20.9 2.1 %collective-permute-start.15 = (f32[17,8,128]{2,1,0:T(8,128)S(1)}, f32[17,8,128]{2,1,0:T(8,128)S(1)}, u32[]{:S(2)}, u32[]{:S(2)}) collective-permute-start(f32[17,8,128]{2,1,0:T(8,128)S(1)} %shard_map.63.refs_0_.refs_4_), channel_id=1, source_target_pairs={{0,12},{1,13},{2,14},{3,15},{4,8},{5,9},{6,10},{7,11},{8,4},{9,5},... | collective-permute-start | bytes 208904 | tf_op jit(solution)/shard_map/ppermute | solution.py:408
  23.0 0.6 %collective-permute-start.14 = (f32[17,8,128]{2,1,0:T(8,128)S(1)}, f32[17,8,128]{2,1,0:T(8,128)S(1)}, u32[]{:S(2)}, u32[]{:S(2)}) collective-permute-start(f32[17,8,128]{2,1,0:T(8,128)S(1)} %shard_map.63.refs_0_.refs_4_), channel_id=1, source_target_pairs={{0,8},{1,5},{2,10},{3,7},{4,12},{5,1},{6,14},{7,3},{8,0},{9,13},{1... | collective-permute-start | bytes 208904 | tf_op jit(solution)/shard_map/ppermute | solution.py:408
  23.6 0.8 %collective-permute-start.13 = (f32[17,8,128]{2,1,0:T(8,128)S(1)}, f32[17,8,128]{2,1,0:T(8,128)S(1)}, u32[]{:S(2)}, u32[]{:S(2)}) collective-permute-start(f32[17,8,128]{2,1,0:T(8,128)S(1)} %shard_map.63.refs_0_.refs_4_), channel_id=1, source_target_pairs={{0,4},{1,9},{2,6},{3,11},{4,0},{5,13},{6,2},{7,15},{8,12},{9,1},{1... | collective-permute-start | bytes 208904 | tf_op jit(solution)/shard_map/ppermute | solution.py:408
  24.4 0.9 %collective-permute-done.5.refs_1_ = f32[17,8,128]{2,1,0:T(8,128)S(1)} collective-permute-done((f32[17,8,128]{2,1,0:T(8,128)S(1)}, f32[17,8,128]{2,1,0:T(8,128)S(1)}, u32[]{:S(2)}, u32[]{:S(2)}) %collective-permute-start.5) | collective-permute-done | bytes 69664 | tf_op jit(solution)/shard_map/ppermute | solution.py:415
  25.4 1.2 %collective-permute-start.8 = (f32[17,8,128]{2,1,0:T(8,128)S(1)}, f32[17,8,128]{2,1,0:T(8,128)S(1)}, u32[]{:S(2)}, u32[]{:S(2)}) collective-permute-start(f32[17,8,128]{2,1,0:T(8,128)S(1)} %shard_map.61.refs_0_), channel_id=1, source_target_pairs={{0,12},{1,13},{2,14},{3,15},{4,8},{5,9},{6,10},{7,11},{8,4},{9,5},... | collective-permute-start | bytes 208904 | tf_op jit(solution)/shard_map/ppermute | solution.py:408
  26.6 0.9 %collective-permute-start.7 = (f32[17,8,128]{2,1,0:T(8,128)S(1)}, f32[17,8,128]{2,1,0:T(8,128)S(1)}, u32[]{:S(2)}, u32[]{:S(2)}) collective-permute-start(f32[17,8,128]{2,1,0:T(8,128)S(1)} %shard_map.61.refs_0_), channel_id=1, source_target_pairs={{0,8},{1,5},{2,10},{3,7},{4,12},{5,1},{6,14},{7,3},{8,0},{9,13},{1... | collective-permute-start | bytes 208904 | tf_op jit(solution)/shard_map/ppermute | solution.py:408
  27.5 0.0 collective-permute-done.15.refs_3_.refs_7_
  27.5 1.4 %collective-permute-start.6 = (f32[17,8,128]{2,1,0:T(8,128)S(1)}, f32[17,8,128]{2,1,0:T(8,128)S(1)}, u32[]{:S(2)}, u32[]{:S(2)}) collective-permute-start(f32[17,8,128]{2,1,0:T(8,128)S(1)} %shard_map.61.refs_0_), channel_id=1, source_target_pairs={{0,4},{1,9},{2,6},{3,11},{4,0},{5,13},{6,2},{7,15},{8,12},{9,1},{1... | collective-permute-start | bytes 208904 | tf_op jit(solution)/shard_map/ppermute | solution.py:408
  28.9 0.0 collective-permute-done.14.refs_2_.refs_6_
  28.9 0.0 collective-permute-done.13.refs_1_.refs_5_
  28.9 1.0 %shard_map.64.refs_8_ = f32[8,16,8,128]{3,2,1,0:T(8,128)} custom-call(s32[1]{0:T(128)} %bitcast.dom_ref, s32[1]{0:T(128)} %bitcast.1.me_ref, f32[3,8,128]{2,1,0:T(8,128)S(1)} %get-tuple-element.18.keep_ref, f32[17,8,128]{2,1,0:T(8,128)S(1)} %shard_map.63.refs_0_.refs_4_, f32[17,8,128]{2,1,0:T(8,128)S(1)} %collective-permute-done.13.refs_1_.refs_5_, ...), custom_call_target="tpu_custom_call" | custom-call | bytes 290824 | tf_op jit(solution)/shard_map/pallas_call | solution.py:337
  29.9 1.0 %collective-permute-done.8.refs_3_ = f32[17,8,128]{2,1,0:T(8,128)S(1)} collective-permute-done((f32[17,8,128]{2,1,0:T(8,128)S(1)}, f32[17,8,128]{2,1,0:T(8,128)S(1)}, u32[]{:S(2)}, u32[]{:S(2)}) %collective-permute-start.8) | collective-permute-done | bytes 69664 | tf_op jit(solution)/shard_map/ppermute | solution.py:408
  31.0 0.4 %collective-permute-done.7.refs_2_ = f32[17,8,128]{2,1,0:T(8,128)S(1)} collective-permute-done((f32[17,8,128]{2,1,0:T(8,128)S(1)}, f32[17,8,128]{2,1,0:T(8,128)S(1)}, u32[]{:S(2)}, u32[]{:S(2)}) %collective-permute-start.7) | collective-permute-done | bytes 69664 | tf_op jit(solution)/shard_map/ppermute | solution.py:408
  31.4 0.4 %collective-permute-done.6.refs_1_ = f32[17,8,128]{2,1,0:T(8,128)S(1)} collective-permute-done((f32[17,8,128]{2,1,0:T(8,128)S(1)}, f32[17,8,128]{2,1,0:T(8,128)S(1)}, u32[]{:S(2)}, u32[]{:S(2)}) %collective-permute-start.6) | collective-permute-done | bytes 69664 | tf_op jit(solution)/shard_map/ppermute | solution.py:408
  31.8 1.0 %shard_map.65 = f32[8,16,8,128]{3,2,1,0:T(8,128)} custom-call(s32[1]{0:T(128)} %bitcast.dom_ref, s32[1]{0:T(128)} %bitcast.1.me_ref, f32[3,8,128]{2,1,0:T(8,128)S(1)} %get-tuple-element.18.keep_ref, f32[17,8,128]{2,1,0:T(8,128)S(1)} %shard_map.61.refs_0_, f32[17,8,128]{2,1,0:T(8,128)S(1)} %collective-permute-done.6.refs_1_, ...), custom_call_target="tpu_custom_call", output_to_operand_aliasing={{}: (11, {})} | custom-call | bytes 1093640 | tf_op jit(solution)/shard_map/pallas_call | solution.py:337
  (7 shorter events, 0.1 us)
Async XLA Ops:
  0.0 1.4 %copy-start = (f32[1,64,2048]{2,1,0:T(8,128)S(1)}, f32[1,64,2048]{2,1,0:T(8,128)}, u32[]{:S(2)}) copy-start(f32[1,64,2048]{2,1,0:T(8,128)} %param.5) | copy-start | bytes 1572868
  0.0 1.5 %copy-start.1 = (f32[1,64,2048]{2,1,0:T(8,128)S(1)}, f32[1,64,2048]{2,1,0:T(8,128)}, u32[]{:S(2)}) copy-start(f32[1,64,2048]{2,1,0:T(8,128)} %param.6) | copy-start | bytes 1572868
  0.0 1.5 %copy-start.2 = (f32[1,64,2048]{2,1,0:T(8,128)S(1)}, f32[1,64,2048]{2,1,0:T(8,128)}, u32[]{:S(2)}) copy-start(f32[1,64,2048]{2,1,0:T(8,128)} %param.7) | copy-start | bytes 1572868
  1.5 7.5 %collective-permute-start = (f32[16,16,128]{2,1,0:T(8,128)S(1)}, f32[16,16,128]{2,1,0:T(8,128)S(1)}, u32[]{:S(2)}, u32[]{:S(2)}) collective-permute-start(f32[16,16,128]{2,1,0:T(8,128)S(1)} %get-tuple-element.21), channel_id=1, source_target_pairs={{0,1},{1,0},{2,3},{3,2},{4,5},{5,4},{6,7},{7,6},{8,9},{9,8},{10,11... | collective-permute-start | bytes 393224 | tf_op jit(solution)/shard_map/ppermute | solution.py:377
  2.0 7.0 %collective-permute-start.1 = (f32[16,16,128]{2,1,0:T(8,128)S(1)}, f32[16,16,128]{2,1,0:T(8,128)S(1)}, u32[]{:S(2)}, u32[]{:S(2)}) collective-permute-start(f32[16,16,128]{2,1,0:T(8,128)S(1)} %get-tuple-element.22), channel_id=1, source_target_pairs={{0,0},{1,2},{2,1},{3,3},{4,4},{5,6},{6,5},{7,7},{8,8},{9,10},{10,9... | collective-permute-start | bytes 393224 | tf_op jit(solution)/shard_map/ppermute | solution.py:378
  4.8 8.6 %collective-permute-start.9 = (f32[17,8,128]{2,1,0:T(8,128)S(1)}, f32[17,8,128]{2,1,0:T(8,128)S(1)}, u32[]{:S(2)}, u32[]{:S(2)}) collective-permute-start(f32[17,8,128]{2,1,0:T(8,128)S(1)} %get-tuple-element.28), channel_id=1, source_target_pairs={{0,12},{1,13},{2,14},{3,15},{4,8},{5,9},{6,10},{7,11},{8,4},{9,5},... | collective-permute-start | bytes 208904 | tf_op jit(solution)/shard_map/ppermute | solution.py:408
  8.4 5.1 %collective-permute-start.10 = (f32[17,8,128]{2,1,0:T(8,128)S(1)}, f32[17,8,128]{2,1,0:T(8,128)S(1)}, u32[]{:S(2)}, u32[]{:S(2)}) collective-permute-start(f32[17,8,128]{2,1,0:T(8,128)S(1)} %get-tuple-element.29), channel_id=1, source_target_pairs={{0,4},{1,9},{2,6},{3,11},{4,0},{5,13},{6,2},{7,15},{8,12},{9,1},{1... | collective-permute-start | bytes 208904 | tf_op jit(solution)/shard_map/ppermute | solution.py:408
  8.9 5.0 %collective-permute-start.11 = (f32[17,8,128]{2,1,0:T(8,128)S(1)}, f32[17,8,128]{2,1,0:T(8,128)S(1)}, u32[]{:S(2)}, u32[]{:S(2)}) collective-permute-start(f32[17,8,128]{2,1,0:T(8,128)S(1)} %get-tuple-element.30), channel_id=1, source_target_pairs={{0,8},{1,5},{2,10},{3,7},{4,12},{5,1},{6,14},{7,3},{8,0},{9,13},{1... | collective-permute-start | bytes 208904 | tf_op jit(solution)/shard_map/ppermute | solution.py:408
  9.9 6.7 %collective-permute-start.2 = (f32[17,8,128]{2,1,0:T(8,128)S(1)}, f32[17,8,128]{2,1,0:T(8,128)S(1)}, u32[]{:S(2)}, u32[]{:S(2)}) collective-permute-start(f32[17,8,128]{2,1,0:T(8,128)S(1)} %get-tuple-element.24), channel_id=1, source_target_pairs={{0,12},{1,13},{2,14},{3,15},{4,8},{5,9},{6,10},{7,11},{8,4},{9,5},... | collective-permute-start | bytes 208904 | tf_op jit(solution)/shard_map/ppermute | solution.py:408
  12.8 4.5 %collective-permute-start.3 = (f32[17,8,128]{2,1,0:T(8,128)S(1)}, f32[17,8,128]{2,1,0:T(8,128)S(1)}, u32[]{:S(2)}, u32[]{:S(2)}) collective-permute-start(f32[17,8,128]{2,1,0:T(8,128)S(1)} %get-tuple-element.25), channel_id=1, source_target_pairs={{0,4},{1,9},{2,6},{3,11},{4,0},{5,13},{6,2},{7,15},{8,12},{9,1},{1... | collective-permute-start | bytes 208904 | tf_op jit(solution)/shard_map/ppermute | solution.py:408
  13.4 4.8 %collective-permute-start.4 = (f32[17,8,128]{2,1,0:T(8,128)S(1)}, f32[17,8,128]{2,1,0:T(8,128)S(1)}, u32[]{:S(2)}, u32[]{:S(2)}) collective-permute-start(f32[17,8,128]{2,1,0:T(8,128)S(1)} %get-tuple-element.26), channel_id=1, source_target_pairs={{0,8},{1,5},{2,10},{3,7},{4,12},{5,1},{6,14},{7,3},{8,0},{9,13},{1... | collective-permute-start | bytes 208904 | tf_op jit(solution)/shard_map/ppermute | solution.py:408
  14.0 6.9 %collective-permute-start.12 = (f32[17,8,128]{2,1,0:T(8,128)S(1)}, f32[17,8,128]{2,1,0:T(8,128)S(1)}, u32[]{:S(2)}, u32[]{:S(2)}) collective-permute-start(f32[17,8,128]{2,1,0:T(8,128)S(1)} %shard_map.62.refs_0_), channel_id=1, source_target_pairs={{0,16},{4,20},{8,24},{12,28},{16,0},{20,4},{24,8},{28,12},{1,17},{... | collective-permute-start | bytes 208904 | tf_op jit(solution)/shard_map/ppermute | solution.py:415
  18.2 7.2 %collective-permute-start.5 = (f32[17,8,128]{2,1,0:T(8,128)S(1)}, f32[17,8,128]{2,1,0:T(8,128)S(1)}, u32[]{:S(2)}, u32[]{:S(2)}) collective-permute-start(f32[17,8,128]{2,1,0:T(8,128)S(1)} %shard_map.60.refs_0_), channel_id=1, source_target_pairs={{0,16},{4,20},{8,24},{12,28},{16,0},{20,4},{24,8},{28,12},{1,17},{... | collective-permute-start | bytes 208904 | tf_op jit(solution)/shard_map/ppermute | solution.py:415
  20.9 6.6 %collective-permute-start.15 = (f32[17,8,128]{2,1,0:T(8,128)S(1)}, f32[17,8,128]{2,1,0:T(8,128)S(1)}, u32[]{:S(2)}, u32[]{:S(2)}) collective-permute-start(f32[17,8,128]{2,1,0:T(8,128)S(1)} %shard_map.63.refs_0_.refs_4_), channel_id=1, source_target_pairs={{0,12},{1,13},{2,14},{3,15},{4,8},{5,9},{6,10},{7,11},{8,4},{9,5},... | collective-permute-start | bytes 208904 | tf_op jit(solution)/shard_map/ppermute | solution.py:408
  23.0 5.9 %collective-permute-start.14 = (f32[17,8,128]{2,1,0:T(8,128)S(1)}, f32[17,8,128]{2,1,0:T(8,128)S(1)}, u32[]{:S(2)}, u32[]{:S(2)}) collective-permute-start(f32[17,8,128]{2,1,0:T(8,128)S(1)} %shard_map.63.refs_0_.refs_4_), channel_id=1, source_target_pairs={{0,8},{1,5},{2,10},{3,7},{4,12},{5,1},{6,14},{7,3},{8,0},{9,13},{1... | collective-permute-start | bytes 208904 | tf_op jit(solution)/shard_map/ppermute | solution.py:408
  23.6 5.3 %collective-permute-start.13 = (f32[17,8,128]{2,1,0:T(8,128)S(1)}, f32[17,8,128]{2,1,0:T(8,128)S(1)}, u32[]{:S(2)}, u32[]{:S(2)}) collective-permute-start(f32[17,8,128]{2,1,0:T(8,128)S(1)} %shard_map.63.refs_0_.refs_4_), channel_id=1, source_target_pairs={{0,4},{1,9},{2,6},{3,11},{4,0},{5,13},{6,2},{7,15},{8,12},{9,1},{1... | collective-permute-start | bytes 208904 | tf_op jit(solution)/shard_map/ppermute | solution.py:408
  25.4 5.6 %collective-permute-start.8 = (f32[17,8,128]{2,1,0:T(8,128)S(1)}, f32[17,8,128]{2,1,0:T(8,128)S(1)}, u32[]{:S(2)}, u32[]{:S(2)}) collective-permute-start(f32[17,8,128]{2,1,0:T(8,128)S(1)} %shard_map.61.refs_0_), channel_id=1, source_target_pairs={{0,12},{1,13},{2,14},{3,15},{4,8},{5,9},{6,10},{7,11},{8,4},{9,5},... | collective-permute-start | bytes 208904 | tf_op jit(solution)/shard_map/ppermute | solution.py:408
  26.6 4.8 %collective-permute-start.7 = (f32[17,8,128]{2,1,0:T(8,128)S(1)}, f32[17,8,128]{2,1,0:T(8,128)S(1)}, u32[]{:S(2)}, u32[]{:S(2)}) collective-permute-start(f32[17,8,128]{2,1,0:T(8,128)S(1)} %shard_map.61.refs_0_), channel_id=1, source_target_pairs={{0,8},{1,5},{2,10},{3,7},{4,12},{5,1},{6,14},{7,3},{8,0},{9,13},{1... | collective-permute-start | bytes 208904 | tf_op jit(solution)/shard_map/ppermute | solution.py:408
  27.5 4.3 %collective-permute-start.6 = (f32[17,8,128]{2,1,0:T(8,128)S(1)}, f32[17,8,128]{2,1,0:T(8,128)S(1)}, u32[]{:S(2)}, u32[]{:S(2)}) collective-permute-start(f32[17,8,128]{2,1,0:T(8,128)S(1)} %shard_map.61.refs_0_), channel_id=1, source_target_pairs={{0,4},{1,9},{2,6},{3,11},{4,0},{5,13},{6,2},{7,15},{8,12},{9,1},{1... | collective-permute-start | bytes 208904 | tf_op jit(solution)/shard_map/ppermute | solution.py:408
